TPU v7x, 32 devices: a whole 2x2x4 slice. The times are simulated.
32 devices in a mesh: rep: 4 (over z), fsdp: 8 (over y, x, core).
Axes of the slice: x: 2, y: 2, z: 4, core: 2. Of those that a mesh axis runs over, the one named last changes fastest.
Arguments:
- tokens: bfloat16 [32768, 768], P(('rep', 'fsdp')), may hold values from -6 to 6
- cotangent: bfloat16 [32768, 768], P(('rep', 'fsdp')), may hold values from -6 to 6
- lengths: int32 [256], P(('rep', 'fsdp')), may hold values from 32 to 128, as said below
- w_attn: float32 [768, 3072], P('fsdp')
- w_in: float32 [768, 3072], P('fsdp'), may hold values from -0.21875 to 0.21875
- w_out: float32 [3072, 768], P('fsdp'), may hold values from -0.109375 to 0.109375
- b_in: float32 [3072], P('fsdp'), may hold values from -1.8 to 1.8
- vecs: float32 [8, 768], P(None, 'fsdp')
- m_attn: float32 [768, 3072], P('fsdp'), may hold values from -6 to 6
- m_in: float32 [768, 3072], P('fsdp'), may hold values from -6 to 6
- m_out: float32 [3072, 768], P('fsdp'), may hold values from -6 to 6
- m_bin: float32 [3072], P('fsdp'), may hold values from -6 to 6
- m_vecs: float32 [8, 768], P(None, 'fsdp'), may hold values from -6 to 6
- v_attn: float32 [768, 3072], P('fsdp'), may hold values from 1 to 100
- v_in: float32 [768, 3072], P('fsdp'), may hold values from 1 to 100
- v_out: float32 [3072, 768], P('fsdp'), may hold values from 1 to 100
- v_bin: float32 [3072], P('fsdp'), may hold values from 1 to 100
- v_vecs: float32 [8, 768], P(None, 'fsdp'), may hold values from 1 to 100
Outputs:
- output: bfloat16 [32768, 768], P(('rep', 'fsdp'))
- grad_tokens: bfloat16 [32768, 768], P(('rep', 'fsdp'))
- grad_attn: float32 [768, 3072], P('fsdp')
- grad_in: float32 [768, 3072], P('fsdp')
- grad_out: float32 [3072, 768], P('fsdp')
- grad_bin: float32 [3072], P('fsdp')
- grad_vecs: float32 [8, 768], P(None, 'fsdp')
- step_attn: float32 [768, 3072], P('fsdp')
- step_in: float32 [768, 3072], P('fsdp')
- step_out: float32 [3072, 768], P('fsdp')
- step_bin: float32 [3072], P('fsdp')
- step_vecs: float32 [8, 768], P(None, 'fsdp')
- mom_attn: float32 [768, 3072], P('fsdp')
- mom_in: float32 [768, 3072], P('fsdp')
- mom_out: float32 [3072, 768], P('fsdp')
- mom_bin: float32 [3072], P('fsdp')
- mom_vecs: float32 [8, 768], P(None, 'fsdp')
- sq_attn: float32 [768, 3072], P('fsdp')
- sq_in: float32 [768, 3072], P('fsdp')
- sq_out: float32 [3072, 768], P('fsdp')
- sq_bin: float32 [3072], P('fsdp')
- sq_vecs: float32 [8, 768], P(None, 'fsdp')
Inputs may be any that keep to these rules, and one draw needn't show every extreme that they name: `lengths`: each pair has at least 32 valid rows; on every device one of its 8 pairs fills all 128 rows.
All inputs are finite; a program needn't handle non-finite values.
Results may differ from a plain program's by a relative error of at most 0.017.
The roundings to bfloat16 on the way count: a program that leaves them out, or rounds other values in their place, can miss the bound.
Values may be sent and summed in bfloat16 or wider, within the bound.
No kernel may reach another device: no remote copies, remote signals or barrier semaphores. Data moves between devices by JAX's collectives and lax.ppermute only.
A program may use at most 192 MiB of HBM per device.

v0:
```python
import jax
import jax.numpy as jnp
from jax import lax
from jax.sharding import PartitionSpec as P

D = 768
HEADS = 12
HDIM = 64
SEQ = 128
STEP = 5


beta_one = 0.9
beta_two = 0.999
adam_epsilon = 1e-06
norm_epsilon = 1e-05
masked_score = -1000000000.0


def normalize(residual):
    centre = residual - jnp.mean(residual, axis=-1, keepdims=True)
    variance = jnp.mean(centre * centre, axis=-1, keepdims=True)
    inv_std = lax.rsqrt(variance + norm_epsilon)
    return (centre * inv_std, inv_std)


def norm_back(grad_normed, normed, inv_std):
    first_mean = jnp.mean(grad_normed, axis=-1, keepdims=True)
    second_mean = jnp.mean(grad_normed * normed, axis=-1, keepdims=True)
    return inv_std * (grad_normed - first_mean - normed * second_mean)


def gelu_slope(pre_act):
    cumulative = 0.5 * (1.0 + lax.erf(pre_act * 0.7071067811865476))
    density = jnp.exp(-0.5 * pre_act * pre_act) * 0.3989422804014327
    return cumulative + pre_act * density


def adamw(moment, square, gradient, first_fix, second_fix):
    moment = beta_one * moment + (1.0 - beta_one) * gradient
    square = beta_two * square + (1.0 - beta_two) * gradient * gradient
    update = moment / first_fix / (jnp.sqrt(square / second_fix) + adam_epsilon)
    return (update, moment, square)


def forward_pass(source, lengths, gathered):
    attn_mat, in_mat, out_mat, in_bias, vectors = gathered
    vectors_f = vectors.astype(jnp.float32)
    bias_f = in_bias.astype(jnp.float32)
    row_count = source.shape[0]
    seq_count = lengths.shape[0]
    head_shape = (seq_count, SEQ, HEADS, HDIM)
    score_scale = HDIM ** (-0.5)
    projected = jnp.dot(source, attn_mat[:, : 3 * D], preferred_element_type=jnp.float32)
    queries = (projected[:, :D] + vectors_f[0]).astype(jnp.bfloat16).reshape(head_shape)
    key_rows = projected[:, D : 2 * D].astype(jnp.bfloat16).reshape(head_shape)
    value_rows = (projected[:, 2 * D :] + vectors_f[1]).astype(jnp.bfloat16).reshape(head_shape)
    scores = (
        jnp.einsum("bqhd,bkhd->bhqk", queries, key_rows, preferred_element_type=jnp.float32)
        * score_scale
    )
    valid_keys = jnp.arange(SEQ)[None, :] < lengths[:, None]
    scores = jnp.where(valid_keys[:, None, None, :], scores, masked_score)
    attn_weights = jax.nn.softmax(scores, axis=-1)
    weights_low = attn_weights.astype(jnp.bfloat16)
    attended = jnp.einsum(
        "bhqk,bkhd->bqhd", weights_low, value_rows, preferred_element_type=jnp.float32
    )
    attended = attended.reshape(row_count, D).astype(jnp.bfloat16)
    branch = (
        jnp.dot(attended, attn_mat[:, 3 * D :], preferred_element_type=jnp.float32) + vectors_f[2]
    )
    normed_one, inv_one = normalize(source.astype(jnp.float32) + branch)
    hidden = normed_one * vectors_f[3] + vectors_f[4]
    hidden_low = hidden.astype(jnp.bfloat16)
    pre_act = jnp.dot(hidden_low, in_mat, preferred_element_type=jnp.float32) + bias_f
    activated = jax.nn.gelu(pre_act, approximate=False).astype(jnp.bfloat16)
    ffn_out = jnp.dot(activated, out_mat, preferred_element_type=jnp.float32) + vectors_f[5]
    normed_two, inv_two = normalize(hidden + ffn_out)
    output = normed_two * vectors_f[6] + vectors_f[7]
    return (
        output,
        queries,
        key_rows,
        value_rows,
        attn_weights,
        weights_low,
        attended,
        normed_one,
        inv_one,
        hidden_low,
        pre_act,
        activated,
        normed_two,
        inv_two,
    )


def local(
    tokens,
    cotangent,
    lengths,
    w_attn,
    w_in,
    w_out,
    b_in,
    vecs,
    m_attn,
    m_in,
    m_out,
    m_bin,
    m_vecs,
    v_attn,
    v_in,
    v_out,
    v_bin,
    v_vecs,
):
    attn_low = w_attn.astype(jnp.bfloat16)
    in_low = w_in.astype(jnp.bfloat16)
    out_low = w_out.astype(jnp.bfloat16)
    bias_low = b_in.astype(jnp.bfloat16)
    vecs_low = vecs.astype(jnp.bfloat16)
    gathered = (
        lax.all_gather(attn_low, "fsdp", axis=0, tiled=True),
        lax.all_gather(in_low, "fsdp", axis=0, tiled=True),
        lax.all_gather(out_low, "fsdp", axis=0, tiled=True),
        lax.all_gather(bias_low, "fsdp", axis=0, tiled=True),
        lax.all_gather(vecs_low, "fsdp", axis=1, tiled=True),
    )
    output = forward_pass(tokens, lengths, gathered)[0].astype(jnp.bfloat16)
    regathered = (
        lax.all_gather(attn_low, "fsdp", axis=0, tiled=True),
        lax.all_gather(in_low, "fsdp", axis=0, tiled=True),
        lax.all_gather(out_low, "fsdp", axis=0, tiled=True),
        lax.all_gather(bias_low, "fsdp", axis=0, tiled=True),
        lax.all_gather(vecs_low, "fsdp", axis=1, tiled=True),
    )
    attn_mat, in_mat, out_mat, in_bias, vectors = regathered
    vectors_f = vectors.astype(jnp.float32)
    (
        unused_out,
        queries,
        key_rows,
        value_rows,
        attn_weights,
        weights_low,
        attended,
        normed_one,
        inv_one,
        hidden_low,
        pre_act,
        activated,
        normed_two,
        inv_two,
    ) = forward_pass(tokens, lengths, regathered)
    row_count = tokens.shape[0]
    seq_count = lengths.shape[0]
    head_shape = (seq_count, SEQ, HEADS, HDIM)
    score_scale = HDIM ** (-0.5)
    grad_y = cotangent.astype(jnp.float32)
    grad_gain_two = jnp.sum(grad_y * normed_two, axis=0)
    grad_shift_two = jnp.sum(grad_y, axis=0)
    grad_res_two = norm_back(grad_y * vectors_f[6], normed_two, inv_two)
    grad_ffn = grad_res_two.astype(jnp.bfloat16)
    grad_bias_two = jnp.sum(grad_ffn.astype(jnp.float32), axis=0)
    grad_out_mat = jnp.einsum("rf,rd->fd", activated, grad_ffn, preferred_element_type=jnp.float32)
    grad_act = jnp.einsum("rd,fd->rf", grad_ffn, out_mat, preferred_element_type=jnp.float32)
    grad_pre = (grad_act * gelu_slope(pre_act)).astype(jnp.bfloat16)
    grad_bias_in = jnp.sum(grad_pre.astype(jnp.float32), axis=0)
    grad_in_mat = jnp.einsum("rd,rf->df", hidden_low, grad_pre, preferred_element_type=jnp.float32)
    grad_hidden = (
        jnp.einsum("rf,df->rd", grad_pre, in_mat, preferred_element_type=jnp.float32) + grad_res_two
    )
    grad_gain_one = jnp.sum(grad_hidden * normed_one, axis=0)
    grad_shift_one = jnp.sum(grad_hidden, axis=0)
    grad_res_one = norm_back(grad_hidden * vectors_f[3], normed_one, inv_one)
    grad_branch = grad_res_one.astype(jnp.bfloat16)
    grad_bias_out = jnp.sum(grad_branch.astype(jnp.float32), axis=0)
    grad_proj = jnp.einsum("rk,rd->kd", attended, grad_branch, preferred_element_type=jnp.float32)
    grad_attended = jnp.einsum(
        "rd,kd->rk", grad_branch, attn_mat[:, 3 * D :], preferred_element_type=jnp.float32
    )
    grad_attended = grad_attended.astype(jnp.bfloat16).reshape(head_shape)
    grad_weights = jnp.einsum(
        "bqhd,bkhd->bhqk", grad_attended, value_rows, preferred_element_type=jnp.float32
    )
    grad_values = jnp.einsum(
        "bhqk,bqhd->bkhd", weights_low, grad_attended, preferred_element_type=jnp.float32
    )
    grad_values = grad_values.astype(jnp.bfloat16).reshape(row_count, D)
    row_dot = jnp.sum(grad_weights * attn_weights, axis=-1, keepdims=True)
    grad_scores = (attn_weights * (grad_weights - row_dot)).astype(jnp.bfloat16)
    grad_queries = (
        jnp.einsum("bhqk,bkhd->bqhd", grad_scores, key_rows, preferred_element_type=jnp.float32)
        * score_scale
    )
    grad_keys = (
        jnp.einsum("bhqk,bqhd->bkhd", grad_scores, queries, preferred_element_type=jnp.float32)
        * score_scale
    )
    grad_queries = grad_queries.astype(jnp.bfloat16).reshape(row_count, D)
    grad_keys = grad_keys.astype(jnp.bfloat16).reshape(row_count, D)
    grad_mixed = jnp.concatenate([grad_queries, grad_keys, grad_values], axis=1)
    grad_bias_query = jnp.sum(grad_queries.astype(jnp.float32), axis=0)
    grad_bias_value = jnp.sum(grad_values.astype(jnp.float32), axis=0)
    grad_qkv_mat = jnp.einsum("rd,re->de", tokens, grad_mixed, preferred_element_type=jnp.float32)
    grad_source = (
        jnp.einsum(
            "re,de->rd", grad_mixed, attn_mat[:, : 3 * D], preferred_element_type=jnp.float32
        )
        + grad_res_one
    )
    grad_tokens = grad_source.astype(jnp.bfloat16)
    local_attn = jnp.concatenate([grad_qkv_mat, grad_proj], axis=1)
    local_vecs = jnp.stack(
        [
            grad_bias_query,
            grad_bias_value,
            grad_bias_out,
            grad_gain_one,
            grad_shift_one,
            grad_bias_two,
            grad_gain_two,
            grad_shift_two,
        ],
        axis=0,
    )
    owned = (
        lax.psum_scatter(local_attn, "fsdp", scatter_dimension=0, tiled=True),
        lax.psum_scatter(grad_in_mat, "fsdp", scatter_dimension=0, tiled=True),
        lax.psum_scatter(grad_out_mat, "fsdp", scatter_dimension=0, tiled=True),
        lax.psum_scatter(grad_bias_in, "fsdp", scatter_dimension=0, tiled=True),
        lax.psum_scatter(local_vecs, "fsdp", scatter_dimension=1, tiled=True),
    )
    summed = (
        lax.psum(owned[0].astype(jnp.bfloat16), "rep").astype(jnp.float32),
        lax.psum(owned[1].astype(jnp.bfloat16), "rep").astype(jnp.float32),
        lax.psum(owned[2].astype(jnp.bfloat16), "rep").astype(jnp.float32),
        lax.psum(owned[3].astype(jnp.bfloat16), "rep").astype(jnp.float32),
        lax.psum(owned[4].astype(jnp.bfloat16), "rep").astype(jnp.float32),
    )
    grad_attn, grad_in, grad_out, grad_bin, grad_vecs = summed
    first_fix = 1.0 - beta_one**STEP
    second_fix = 1.0 - beta_two**STEP
    step_attn, mom_attn, sq_attn = adamw(m_attn, v_attn, grad_attn, first_fix, second_fix)
    step_in, mom_in, sq_in = adamw(m_in, v_in, grad_in, first_fix, second_fix)
    step_out, mom_out, sq_out = adamw(m_out, v_out, grad_out, first_fix, second_fix)
    step_bin, mom_bin, sq_bin = adamw(m_bin, v_bin, grad_bin, first_fix, second_fix)
    step_vecs, mom_vecs, sq_vecs = adamw(m_vecs, v_vecs, grad_vecs, first_fix, second_fix)
    return (
        output,
        grad_tokens,
        grad_attn,
        grad_in,
        grad_out,
        grad_bin,
        grad_vecs,
        step_attn,
        step_in,
        step_out,
        step_bin,
        step_vecs,
        mom_attn,
        mom_in,
        mom_out,
        mom_bin,
        mom_vecs,
        sq_attn,
        sq_in,
        sq_out,
        sq_bin,
        sq_vecs,
    )


def solution(mesh):
    in_specs = (
        P(("rep", "fsdp"), None),
        P(("rep", "fsdp"), None),
        P(("rep", "fsdp")),
        P("fsdp", None),
        P("fsdp", None),
        P("fsdp", None),
        P("fsdp"),
        P(None, "fsdp"),
        P("fsdp", None),
        P("fsdp", None),
        P("fsdp", None),
        P("fsdp"),
        P(None, "fsdp"),
        P("fsdp", None),
        P("fsdp", None),
        P("fsdp", None),
        P("fsdp"),
        P(None, "fsdp"),
    )
    out_specs = (
        P(("rep", "fsdp"), None),
        P(("rep", "fsdp"), None),
        P("fsdp", None),
        P("fsdp", None),
        P("fsdp", None),
        P("fsdp"),
        P(None, "fsdp"),
        P("fsdp", None),
        P("fsdp", None),
        P("fsdp", None),
        P("fsdp"),
        P(None, "fsdp"),
        P("fsdp", None),
        P("fsdp", None),
        P("fsdp", None),
        P("fsdp"),
        P(None, "fsdp"),
        P("fsdp", None),
        P("fsdp", None),
        P("fsdp", None),
        P("fsdp"),
        P(None, "fsdp"),
    )
    return jax.shard_map(local, mesh=mesh, in_specs=in_specs, out_specs=out_specs, check_vma=False)
```

profile of v0, /device:TPU:0, one launch (start us, length us, event | category | flops | bytes accessed | tf_op | source)
XLA Modules:
  0.0 584.3 jit_solution(2312041083617451606)
XLA Ops:
  7.3 2.2 convert_element_type.150
  10.5 2.3 convert_element_type.164
  12.9 10.4 %all-gather = bf16[8,96,8]{1,2,0:T(8,128)(2,1)S(1)} all-gather(bf16[1,96,8]{1,2,0:T(8,128)(2,1)S(1)} %convert_bitcast_fusion), channel_id=1, replica_groups=mesh['rep'=4,'fsdp'=8] {'fsdp'}, dimensions={0}, use_global_device_ids=true | all-gather | bytes 13824 | tf_op jit(solution)/shard_map/all_gather | solution.py:129
  23.5 1.6 copy.113
  25.2 8.9 %all-gather.1 = bf16[8,1,384]{2,1,0:T(2,128)(2,1)S(1)} all-gather(bf16[1,1,384]{2,1,0:T(2,128)(2,1)S(1)} %reshape.145), channel_id=1, replica_groups=mesh['rep'=4,'fsdp'=8] {'fsdp'}, dimensions={0}, use_global_device_ids=true | all-gather | bytes 6912 | tf_op jit(solution)/shard_map/all_gather | solution.py:128
  34.1 1.6 copy.124
  35.7 16.5 %all-gather.6.cloned.1.call-done = bf16[768,3072]{1,0:T(8,128)(2,1)} async-done(((bf16[96,3072]{1,0:T(8,128)(2,1)}), bf16[768,3072]{1,0:T(8,128)(2,1)}) %all-gather.6.cloned.1.call-update) | async-done | bytes 4718608 | tf_op jit(solution)/shard_map/all_gather | solution.py:125
  52.2 5.8 fusion.32
  58.2 1.8 fusion.25
  59.9 1.6 copy.116
  61.5 1.9 copy.169
  63.5 1.6 copy.117
  65.2 1.8 copy.170
  67.0 3.1 copy.115
  70.2 1.8 copy.168
  73.1 2.7 fusion.84
  80.1 3.3 fusion.85
  83.8 9.8 %all-gather.8.cloned.1.call-done = bf16[768,3072]{1,0:T(8,128)(2,1)} async-done(((bf16[96,3072]{1,0:T(8,128)(2,1)}), bf16[768,3072]{1,0:T(8,128)(2,1)}) %all-gather.8.cloned.1.call-update) | async-done | bytes 4718608 | tf_op jit(solution)/shard_map/all_gather | solution.py:126
  93.6 48.1 %fusion.3 = (bf16[1024,3072]{1,0:T(8,128)(2,1)}, f32[1024,3072]{1,0:T(8,128)}) fusion(f32[3072]{0:T(1024)S(1)} %bitcast.110, bf16[768,3072]{1,0:T(8,128)(2,1)} %all-gather.8.cloned.1.call-done, f32[1024,768]{0,1:T(8,128)S(1)} %get-tuple-element.137, f32[768]{0:T(1024)S(1)} %get-tuple-element.99, f32[768]{0:T(1024)S(1)} %get-tuple-element.100, ...), kind=kOutput, calls=%fused_computation.5 | convolution fusion | flops 5043388416 | bytes 26765312 | tf_op jit(solution)/shard_map/dot_general | solution.py:76
  141.8 9.6 %fusion.86 = (f32[1024]{0:T(1024)S(1)}, f32[1024,768]{0,1:T(8,128)S(1)}) fusion(f32[768]{0:T(1024)S(1)} %get-tuple-element.98, bf16[1024,3072]{1,0:T(8,128)(2,1)} %get-tuple-element.138, bf16[3072,768]{1,0:T(8,128)(2,1)} %all-gather.10.cloned.1.call-done, f32[768]{0:T(1024)S(1)} %get-tuple-element.99, f32[768]{0:T(1024)S(1)} %get-tuple-element.100, ...), kind=kOutput, calls=%fused_computation.156 | convolution fusion | flops 4837342208 | bytes 17323008 | tf_op jit(solution)/shard_map/dot_general | solution.py:78
  152.8 1.3 fusion.24
  154.1 2.6 convert_reduce_fusion.2
  156.8 11.7 %convert_reduce_fusion = (f32[3072]{0:T(1024)S(1)}, bf16[1024,3072]{1,0:T(8,128)(2,1)S(1)}) fusion(f32[1024,3072]{1,0:T(8,128)S(1)} %copy-done.44, f32[3072]{0:T(1024)S(1)} %bitcast.111, bf16[1024,768]{0,1:T(8,128)(2,1)S(1)} %get-tuple-element.128, bf16[3072,768]{1,0:T(8,128)(2,1)S(1)} %bitcast.113), kind=kOutput, calls=%fused_computation.12 | convolution fusion | flops 4872729600 | bytes 25190400 | tf_op jit(solution)/shard_map/rd,fd->rf/dot_general | solution.py:168
  168.5 2.6 copy-done.43
  171.1 7.8 %fusion.74 = f32[768,3072]{1,0:T(8,128)} fusion(bf16[1024,3072]{1,0:T(8,128)(2,1)S(1)} %get-tuple-element.146, f32[1024,768]{0,1:T(8,128)S(1)} %copy-done.6, f32[768]{0:T(1024)S(1)} %get-tuple-element.99, f32[768]{0:T(1024)S(1)} %get-tuple-element.100, f32[1024]{0:T(1024)S(1)} %add_rsqrt_fusion.1, f32[1024]{0:T(1024)S(1)} %broadcast_multiply_fusion.5), kind=kOutput, calls=%fused_computation.152 | convolution fusion | flops 4835770368 | bytes 18888704
  179.0 11.4 %multiply_reduce_fusion.1 = (f32[768]{0:T(1024)S(1)}, f32[1024]{0:T(1024)S(1)}, f32[1024]{0:T(1024)S(1)}, f32[768]{0:T(1024)S(1)}, f32[1024,768]{0,1:T(8,128)S(1)}) fusion(f32[1024,768]{0,1:T(8,128)} %copy-done.5, f32[1024]{0:T(1024)S(1)} %add_rsqrt_fusion.1, f32[1024]{0:T(1024)S(1)} %broadcast_multiply_fusion.5, f32[768]{0:T(1024)S(1)} %get-tuple-element.100, ...), kind=kOutput, calls=%fused_computation.51 | convolution fusion | flops 4845989888 | bytes 22065152 | tf_op jit(solution)/shard_map/rf,df->rd/dot_general | solution.py:173
  191.5 1.7 copy-done.15
  193.3 3.0 convolution_convert_fusion.1
  198.0 5.4 convert_reduce_fusion.4
  204.7 4.4 multiply_reduce_fusion
  209.1 5.0 multiply_convert_fusion
  214.1 2.3 fusion.45
  223.2 1.4 fusion.37
  225.7 5.8 convolution_bitcast_fusion
  231.5 7.4 %pad_maximum_fusion = f32[768,3072]{0,1:T(8,128)} fusion(f32[768,768]{0,1:T(8,128)S(1)} %fusion.37, f32[768,2304]{0,1:T(8,128)} %convolution_bitcast_fusion), kind=kLoop, calls=%fused_computation.28 | loop fusion | flops 2359296 | bytes 18874368 | tf_op jit(solution)/shard_map/concatenate | solution.py:215
  239.0 9.9 %copy.162 = f32[768,3072]{1,0:T(8,128)} copy(f32[768,3072]{0,1:T(8,128)} %pad_maximum_fusion) | data formatting | bytes 18874368
  249.0 1.4 copy-done.26
  250.4 10.3 %fusion.87 = f32[3072,768]{1,0:T(8,128)} fusion(bf16[1024,3072]{1,0:T(8,128)(2,1)} %get-tuple-element.138, bf16[1024,768]{0,1:T(8,128)(2,1)S(1)} %copy-done.26), kind=kOutput, calls=%fused_computation.157 | convolution fusion | flops 4831838208 | bytes 17301504 | tf_op jit(solution)/shard_map/rf,rd->fd/dot_general | solution.py:167
  262.0 2.4 copy.165
  264.4 71.0 %reduce-scatter.13.cloned.1.call-done = f32[96,3072]{1,0:T(8,128)} async-done(((f32[768,3072]{1,0:T(8,128)}), f32[96,3072]{1,0:T(8,128)}) %reduce-scatter.13.cloned.1.call-update) | async-done | bytes 1179664
  335.4 2.4 copy.163
  337.8 77.5 %reduce-scatter.11.cloned.1.call-done = f32[384,768]{1,0:T(8,128)} async-done(((f32[3072,768]{1,0:T(8,128)}), f32[384,768]{1,0:T(8,128)}) %reduce-scatter.11.cloned.1.call-update) | async-done | bytes 1179664 | tf_op jit(solution)/shard_map/reduce_scatter | solution.py:232
  415.3 2.1 convert_element_type.183
  417.5 1.6 copy.140
  419.1 1.6 copy.141
  420.8 1.7 copy.142
  422.5 1.6 copy.143
  425.4 9.4 %add_convert_fusion = bf16[1024,768]{0,1:T(8,128)(2,1)} fusion(f32[1024,768]{0,1:T(8,128)} %copy-done.15, bf16[1024,2304]{0,1:T(8,128)(2,1)} %copy-done.32, bf16[768,3072]{1,0:T(8,128)(2,1)} %all-gather.6.cloned.1.call-done), kind=kOutput, calls=%fused_computation.55 | convolution fusion | flops 3625451520 | bytes 12976128 | tf_op jit(solution)/shard_map/re,de->rd/dot_general | solution.py:209
  434.9 2.7 copy.145
  437.6 1.6 copy.144
  439.1 23.2 %all-reduce = bf16[3072]{0:T(1024)(128)(2,1)S(1)} all-reduce(f32[3072]{0:T(1024)S(1)} %get-tuple-element.145), channel_id=5, replica_groups=mesh['rep'=4,'fsdp'=8] {'fsdp'}, use_global_device_ids=true, to_apply=%region_18.19.clone | all-reduce | flops 3072 | bytes 18432
  463.2 12.2 %all-reduce.1 = (bf16[384]{0:T(512)(128)(2,1)S(1)}, bf16[8,96]{1,0:T(8,128)(2,1)S(1)}) all-reduce(bf16[384]{0:T(512)(128)(2,1)S(1)} %dynamic-slice.3, bf16[8,96]{1,0:T(8,128)(2,1)S(1)} %copy.167), channel_id=1, replica_groups=mesh['rep'=4,'fsdp'=8] {'rep'}, use_global_device_ids=true, to_apply=%region_19.20 | all-reduce | flops 1152 | bytes 4608 | tf_op jit(solution)/shard_map/psum | solution.py:240
  476.7 70.1 %all-reduce.5.cloned.1.call-done = (bf16[96,3072]{0,1:T(8,128)(2,1)}, bf16[96,3072]{0,1:T(8,128)(2,1)}, bf16[384,768]{1,0:T(8,128)(2,1)}) async-done(((bf16[96,3072]{0,1:T(8,128)(2,1)}, bf16[96,3072]{0,1:T(8,128)(2,1)}, bf16[384,768]{1,0:T(8,128)(2,1)}), (bf16[96,3072]{0,1:T(8,128)(2,1)}, bf16[96,3072]{0,1:T(8,128)(2,1)}, bf16[384,768]{1,0:T(8,128)(2,1)})) %all-reduce.5.cloned.1.call-update) | async-done | bytes 1769488 | tf_op jit(solution)/shard_map/psum | solution.py:237
  546.7 2.4 copy.146
  549.2 4.5 add_divide_fusion.1
  553.6 3.0 copy.148
  556.6 2.4 copy.147
  559.0 3.9 add_divide_fusion
  562.9 3.0 copy.149
  565.9 1.5 copy.150
  567.4 3.0 copy.151
  570.4 1.5 copy.152
  571.9 1.5 copy.153
  573.4 3.9 add_divide_fusion.2
  (163 shorter events, 24.9 us)
Async XLA Ops:
  7.2 2.4 copy-start.27
  7.2 5.7 copy-start.35
  7.2 45.0 %all-gather.6.cloned.1.call-start = ((), (), s32[]{:S(2)}) async-start(), calls=%async_computation.4 | async-start | bytes 5308416 | tf_op jit(solution)/shard_map/all_gather | solution.py:125
  9.5 13.9 %copy-start.41 = (s32[8]{0:T(128)S(1)}, s32[8]{0:T(128)}, u32[]{:S(2)}) copy-start(s32[8]{0:T(128)} %param.20) | copy-start | bytes 100
  9.5 14.0 %copy-start.18 = (bf16[1024,768]{1,0:T(8,128)(2,1)S(1)}, bf16[1024,768]{1,0:T(8,128)(2,1)}, u32[]{:S(2)}) copy-start(bf16[1024,768]{1,0:T(8,128)(2,1)} %param.18) | copy-start | bytes 4718596
  9.5 84.0 %all-gather.8.cloned.1.call-start = ((), (), s32[]{:S(2)}) async-start(), calls=%async_computation.5 | async-start | bytes 5308416 | tf_op jit(solution)/shard_map/all_gather | solution.py:126
  10.5 14.7 %copy-start.38 = (f32[384]{0:T(512)S(1)}, f32[384]{0:T(512)}, u32[]{:S(2)}) copy-start(f32[384]{0:T(512)} %param.24) | copy-start | bytes 4612
  10.5 23.6 %copy-start.17 = (bf16[1024,768]{1,0:T(8,128)(2,1)S(1)}, bf16[1024,768]{1,0:T(8,128)(2,1)}, u32[]{:S(2)}) copy-start(bf16[1024,768]{1,0:T(8,128)(2,1)} %param.19) | copy-start | bytes 4718596
  10.5 131.3 %all-gather.10.cloned.1.call-start = ((), (), s32[]{:S(2)}) async-start(), calls=%async_computation.6 | async-start | bytes 5308416 | tf_op jit(solution)/shard_map/all_gather | solution.py:127
  12.8 249.2 %reduce-scatter.15.cloned.1.call-start = ((), (), s32[]{:S(2)}) async-start(), calls=%async_computation.9 | async-start | bytes 10616832
  63.5 8.5 %copy-start.2 = (bf16[96,8,8,128]{3,2,1,0:T(8,128)(2,1)}, bf16[96,8,8,128]{3,2,1,0:T(8,128)(2,1)S(1)}, u32[]{:S(2)}) copy-start(bf16[96,8,8,128]{3,2,1,0:T(8,128)(2,1)S(1)} %copy.169) | copy-start | bytes 4718596
  67.0 5.0 copy-start
  72.0 3.8 copy-start.22
  75.8 0.6 copy-start.33
  75.8 2.9 copy-start.9
  78.7 1.4 copy-start.24
  79.9 3.5 copy-start.20
  83.4 58.3 %copy-start.5 = (f32[1024,768]{0,1:T(8,128)}, f32[1024,768]{0,1:T(8,128)S(1)}, u32[]{:S(2)}) copy-start(f32[1024,768]{0,1:T(8,128)S(1)} %get-tuple-element.137) | copy-start | bytes 9437188
  141.8 15.0 %copy-start.44 = (f32[1024,3072]{1,0:T(8,128)S(1)}, f32[1024,3072]{1,0:T(8,128)}, u32[]{:S(2)}) copy-start(f32[1024,3072]{1,0:T(8,128)} %get-tuple-element.139) | copy-start | bytes 37748740
  151.4 1.4 copy-start.4
  152.8 4.0 slice-start.2
  154.1 2.7 slice-start.3
  156.8 11.7 %copy-start.25 = (bf16[1024,768]{0,1:T(8,128)(2,1)}, bf16[1024,768]{0,1:T(8,128)(2,1)S(1)}, u32[]{:S(2)}) copy-start(bf16[1024,768]{0,1:T(8,128)(2,1)S(1)} %get-tuple-element.128) | copy-start | bytes 4718596
  156.8 14.3 %copy-start.6 = (f32[1024,768]{0,1:T(8,128)S(1)}, f32[1024,768]{0,1:T(8,128)}, u32[]{:S(2)}) copy-start(f32[1024,768]{0,1:T(8,128)} %copy-done.5) | copy-start | bytes 9437188
  168.5 2.6 copy-start.43
  178.9 156.5 %reduce-scatter.13.cloned.1.call-start = ((), (), s32[]{:S(2)}) async-start(), calls=%async_computation.8 | async-start | bytes 10616832
  179.0 11.5 %copy-start.7 = (f32[1024,768]{0,1:T(8,128)S(1)}, f32[1024,768]{0,1:T(8,128)}, u32[]{:S(2)}) copy-start(f32[1024,768]{0,1:T(8,128)} %copy-done.5) | copy-start | bytes 9437188
  191.5 1.7 copy-start.15
  196.3 1.6 copy-start.34
  197.5 7.1 %slice-start = ((s8[6291456]{0:T(1024)(128)(4,1)}), s8[4194304]{0:T(1024)(128)(4,1)S(1)}, s32[]{:S(2)}) async-start(s8[6291456]{0:T(1024)(128)(4,1)} %bitcast.99), calls=%async_computation.12 | async-start | bytes 8388608
  197.9 6.7 %slice-start.1 = ((s8[6291456]{0:T(1024)(128)(4,1)}), s8[2097152]{0:T(1024)(128)(4,1)S(1)}, s32[]{:S(2)}) async-start(s8[6291456]{0:T(1024)(128)(4,1)} %bitcast.99), calls=%async_computation.13 | async-start | bytes 4194304
  203.3 1.4 copy-start.23
  209.1 5.0 copy-start.3
  216.4 1.4 copy-start.1
  220.5 2.2 copy-start.16
  220.5 2.6 copy-start.21
  223.2 2.1 copy-start.32
  223.2 2.6 copy-start.19
  248.9 1.4 copy-start.26
  248.9 166.4 %reduce-scatter.11.cloned.1.call-start = ((), (), s32[]{:S(2)}) async-start(), calls=%async_computation.7 | async-start | bytes 10616832 | tf_op jit(solution)/shard_map/reduce_scatter | solution.py:232
  260.7 201.7 %reduce-scatter.17.cloned.1.call-start = ((), (), s32[]{:S(2)}) async-start(), calls=%async_computation.10 | async-start | bytes 442368
  261.9 284.8 %all-reduce.5.cloned.1.call-start = ((), (), s32[]{:S(2)}) async-start(), calls=%async_computation.11 | async-start | bytes 4325376 | tf_op jit(solution)/shard_map/psum | solution.py:237
  264.4 153.0 %copy-start.28 = (f32[96,3072]{1,0:T(8,128)S(1)}, f32[96,3072]{1,0:T(8,128)}, u32[]{:S(2)}) copy-start(f32[96,3072]{1,0:T(8,128)} %param.26) | copy-start | bytes 3538948
  337.8 81.3 %copy-start.29 = (f32[96,3072]{1,0:T(8,128)S(1)}, f32[96,3072]{1,0:T(8,128)}, u32[]{:S(2)}) copy-start(f32[96,3072]{1,0:T(8,128)} %param.31) | copy-start | bytes 3538948
  419.1 3.4 copy-start.30
  420.8 3.4 copy-start.42
  434.8 2.7 copy-start.8
  434.8 40.6 %copy-start.39 = (f32[384]{0:T(512)S(1)}, f32[384]{0:T(512)}, u32[]{:S(2)}) copy-start(f32[384]{0:T(512)} %param.29) | copy-start | bytes 4612
  434.9 40.6 %copy-start.40 = (f32[384]{0:T(512)S(1)}, f32[384]{0:T(512)}, u32[]{:S(2)}) copy-start(f32[384]{0:T(512)} %param.34) | copy-start | bytes 4612
  434.9 41.2 %copy-start.36 = (f32[8,96]{1,0:T(8,128)S(1)}, f32[8,96]{1,0:T(8,128)}, u32[]{:S(2)}) copy-start(f32[8,96]{1,0:T(8,128)} %param.30) | copy-start | bytes 9220
  434.9 41.2 %copy-start.37 = (f32[8,96]{1,0:T(8,128)S(1)}, f32[8,96]{1,0:T(8,128)}, u32[]{:S(2)}) copy-start(f32[8,96]{1,0:T(8,128)} %param.35) | copy-start | bytes 9220
  439.1 110.0 %copy-start.11 = (f32[96,3072]{0,1:T(8,128)S(1)}, f32[96,3072]{0,1:T(8,128)}, u32[]{:S(2)}) copy-start(f32[96,3072]{0,1:T(8,128)} %copy.140) | copy-start | bytes 3538948
  553.6 5.4 copy-start.10
  562.9 3.0 copy-start.13
  565.9 4.5 copy-start.12
  567.4 4.5 copy-start.14
  571.9 1.5 copy-start.31
Sparse Core Ops, SparseCore 0:
  10.5 41.6 all-gather.5
  54.6 38.9 all-gather.7
  96.0 38.9 all-gather.9
  179.0 76.4 reduce-scatter.14
  258.9 76.4 reduce-scatter.12
  338.8 76.4 reduce-scatter.10
  418.9 33.8 reduce-scatter.16
  456.5 90.1 all-reduce.4
where the time goes:
time: 591 us; the launch traced here: 584 us
  waiting for transfers between devices  245 us (41%)
  matrix products  143 us (24%)
  local copies, waits for them, and re-layouts  82.1 us (14%)
  blocking collectives  54.6 us (9%)
  other arithmetic  43.8 us (7%)
  between operations  15.7 us (3%)
    reduce_scatter x1, waiting for transfers between devices, local(): lax.psum_scatter(grad_out_mat, 'fsdp', scatter_dimension=0, tiled=True)  77.5 us
    unnamed x11, waiting for transfers between devices  71.1 us
    psum x1, waiting for transfers between devices, local(): lax.psum(owned[0].astype(jnp.bfloat16), 'rep').astype(jnp.float32)  70.1 us
    unnamed x128, local copies, waits for them, and re-layouts  68.7 us
    dot_general x1, matrix products, forward_pass(): jnp.dot(hidden_low, in_mat, preferred_element_type=jnp.float32) + bias_f  48.1 us
    unnamed x1, blocking collectives  23.2 us
    all_gather x1, waiting for transfers between devices, local(): lax.all_gather(attn_low, 'fsdp', axis=0, tiled=True)  16.5 us
    div x5, other arithmetic, adamw(): update = moment / first_fix / (jnp.sqrt(square / second_fix) + adam_epsilon)  13.4 us
  transfers between devices with their start and end apart: 8, of which 5 were waited for; matrix products, arithmetic and copies ran while one was open for 33% of the time, Pallas kernels for 0%

commit v1 on v0

v1 whole, which is shorter than its diff:
```python
import functools

import jax
import jax.numpy as jnp
from jax import lax
from jax.experimental import pallas as pl
from jax.experimental.pallas import tpu as pltpu
from jax.sharding import PartitionSpec as P

D = 768
HEADS = 12
HDIM = 64
FF = 3072
SEQ = 128
STEP = 5

RANKS = 8
SHARD = D // RANKS
SHARD_FF = FF // RANKS

beta_one = 0.9
beta_two = 0.999
adam_epsilon = 1e-06
norm_epsilon = 1e-05
masked_score = -1000000000.0

bf16 = jnp.bfloat16
f32 = jnp.float32
NN = (((1,), (0,)), ((), ()))
NT = (((1,), (1,)), ((), ()))
TN = (((0,), (0,)), ((), ()))
VMEM_BYTES = 56 * 1024 * 1024
TILE = 256


def dot(left, right, dims):
    return lax.dot_general(left, right, dims, preferred_element_type=f32)


def call(kernel, grid, in_specs, out_specs, out_shape, scratch=(), flops=0, bytes_accessed=0, name=None):
    return pl.pallas_call(
        kernel,
        grid_spec=pltpu.PrefetchScalarGridSpec(
            num_scalar_prefetch=1,
            grid=grid,
            in_specs=in_specs,
            out_specs=out_specs,
            scratch_shapes=list(scratch),
        ),
        out_shape=out_shape,
        compiler_params=pltpu.CompilerParams(
            vmem_limit_bytes=VMEM_BYTES, dimension_semantics=("arbitrary",) * len(grid)
        ),
        cost_estimate=pl.CostEstimate(
            flops=int(flops), bytes_accessed=int(bytes_accessed), transcendentals=0
        ),
        name=name,
    )


def rows_of(width, tile=TILE):
    return pl.BlockSpec((tile, width), lambda i, s: (i, 0))


def whole(shape):
    return pl.BlockSpec(shape, lambda i, s: (0,) * len(shape))


ANY = pl.BlockSpec(memory_space=pl.ANY)


class Pieces:
    def __init__(self, arrays, places):
        self.arrays = list(arrays)
        self.places = places

    def __len__(self):
        return len(self.arrays)


def load_weight(pieces, me, refs, scratch, sem):
    copies = []
    for ref, place in zip(refs, pieces.places):
        if place is None:
            target = scratch
        else:
            mask, first, count = place
            target = scratch.at[me ^ mask, pl.ds(first, count)]
        copies.append(pltpu.make_async_copy(ref, target, sem))
    for copy in copies:
        copy.start()
    for copy in copies:
        copy.wait()


def lane_sum(value):
    return jnp.sum(value, axis=-1, keepdims=True)


def normalize(residual):
    centre = residual - lane_sum(residual) * (1.0 / D)
    variance = lane_sum(centre * centre) * (1.0 / D)
    inv_std = lax.rsqrt(variance + norm_epsilon)
    return (centre * inv_std, inv_std)


def norm_back(grad_normed, normed, inv_std):
    first_mean = lane_sum(grad_normed) * (1.0 / D)
    second_mean = lane_sum(grad_normed * normed) * (1.0 / D)
    return inv_std * (grad_normed - first_mean - normed * second_mean)


def gelu_and_slope(pre_act):
    cumulative = 0.5 * (1.0 + lax.erf(pre_act * 0.7071067811865476))
    density = jnp.exp(-0.5 * pre_act * pre_act) * 0.3989422804014327
    return (pre_act * cumulative, cumulative + pre_act * density)


def project_qkv(me, tokens, weight, bias):
    rows = tokens.shape[0]
    count = len(weight)

    def kernel(s, x_ref, b_ref, *rest):
        refs, (out_ref, w_ref, sem) = rest[:count], rest[count:]

        @pl.when(pl.program_id(0) == 0)
        def _():
            load_weight(weight, s[0], refs, w_ref, sem)

        j = pl.multiple_of(pl.program_id(0) * 256, 256)
        w = w_ref[:, :, pl.ds(j, 256)].reshape(D, 256)
        out_ref[...] = (dot(x_ref[...], w, NN) + b_ref[...]).astype(bf16)

    return call(
        kernel,
        (3 * D // 256,),
        [whole((rows, D)), pl.BlockSpec((1, 256), lambda j, s: (0, j))] + [ANY] * count,
        pl.BlockSpec((rows, 256), lambda j, s: (0, j)),
        jax.ShapeDtypeStruct((rows, 3 * D), bf16),
        [pltpu.VMEM((RANKS, SHARD, 3 * D), bf16), pltpu.SemaphoreType.DMA],
        flops=2 * rows * D * 3 * D,
        bytes_accessed=2 * (rows * D * 4 + 3 * D * D),
        name="qkv",
    )(me, tokens, bias, *weight.arrays)


def head_masks():
    lane = lax.broadcasted_iota(jnp.int32, (SEQ, 2 * HDIM), 1)
    return lane < HDIM


def stack_heads(value, first):
    zero = jnp.zeros_like(value)
    return jnp.concatenate([jnp.where(first, value, zero), jnp.where(first, zero, value)], axis=0)


def attention(lengths, qkv):
    rows = qkv.shape[0]
    pairs = rows // SEQ
    scale = HDIM ** (-0.5)

    def kernel(s, qkv_ref, out_ref, p_ref):
        length = s[pl.program_id(0)]
        first = head_masks()
        valid = lax.broadcasted_iota(jnp.int32, (SEQ, SEQ), 1) < length
        for h in range(HEADS // 2):
            lanes = slice(h * 2 * HDIM, (h + 1) * 2 * HDIM)
            q = qkv_ref[:, lanes]
            k = qkv_ref[:, D + h * 2 * HDIM : D + (h + 1) * 2 * HDIM]
            v = qkv_ref[:, 2 * D + h * 2 * HDIM : 2 * D + (h + 1) * 2 * HDIM]
            scores = dot(q, stack_heads(k, first), NT) * scale
            halves = []
            for part in range(2):
                one = jnp.where(valid, scores[:, part * SEQ : (part + 1) * SEQ], masked_score)
                top = jnp.max(one, axis=-1, keepdims=True)
                raised = jnp.exp(one - top)
                halves.append(raised / lane_sum(raised))
            weights = jnp.concatenate(halves, axis=1)
            p_ref[:, h * 2 * SEQ : (h + 1) * 2 * SEQ] = weights
            out_ref[:, lanes] = dot(weights.astype(bf16), stack_heads(v, first), NN).astype(bf16)

    return call(
        kernel,
        (pairs,),
        [rows_of(3 * D, SEQ)],
        [rows_of(D, SEQ), rows_of(HEADS * SEQ, SEQ)],
        [
            jax.ShapeDtypeStruct((rows, D), bf16),
            jax.ShapeDtypeStruct((rows, HEADS * SEQ), f32),
        ],
        flops=8e9,
        bytes_accessed=rows * (3 * D * 2 + D * 2 + HEADS * SEQ * 4),
        name="attention",
    )(lengths, qkv)


def feed_in(me, attended, tokens, weight, vectors, in_bias):
    rows = tokens.shape[0]
    count = len(weight)
    tile = 512

    def kernel(s, o_ref, x_ref, v_ref, b_ref, *rest):
        refs = rest[:count]
        n1_ref, inv_ref, hb_ref, f_ref, sl_ref, w_ref, sem = rest[count:]

        @pl.when(pl.program_id(0) == 0)
        def _():
            load_weight(weight, s[0], refs, w_ref, sem)

        w_proj = w_ref[:, :, :D].reshape(D, D)
        branch = dot(o_ref[...], w_proj, NN) + v_ref[2:3, :]
        normed, inv_std = normalize(x_ref[...].astype(f32) + branch)
        n1_ref[...] = normed
        inv_ref[...] = inv_std
        low = (normed * v_ref[3:4, :] + v_ref[4:5, :]).astype(bf16)
        hb_ref[...] = low
        for j in range(FF // tile):
            w = w_ref[:, :, D + j * tile : D + (j + 1) * tile].reshape(D, tile)
            pre_act = dot(low, w, NN) + b_ref[:, j * tile : (j + 1) * tile]
            act, slope = gelu_and_slope(pre_act)
            f_ref[:, j * tile : (j + 1) * tile] = act.astype(bf16)
            sl_ref[:, j * tile : (j + 1) * tile] = slope.astype(bf16)

    return call(
        kernel,
        (rows // TILE,),
        [rows_of(D), rows_of(D), whole((8, D)), whole((1, FF))] + [ANY] * count,
        [rows_of(D), rows_of(1), rows_of(D), rows_of(FF), rows_of(FF)],
        [
            jax.ShapeDtypeStruct((rows, D), f32),
            jax.ShapeDtypeStruct((rows, 1), f32),
            jax.ShapeDtypeStruct((rows, D), bf16),
            jax.ShapeDtypeStruct((rows, FF), bf16),
            jax.ShapeDtypeStruct((rows, FF), bf16),
        ],
        [pltpu.VMEM((RANKS, SHARD, D + FF), bf16), pltpu.SemaphoreType.DMA],
        flops=2 * rows * D * (D + FF),
        bytes_accessed=rows * (D * 10 + FF * 4) + 2 * D * (D + FF),
        name="feed_in",
    )(me, attended, tokens, vectors, in_bias, *weight.arrays)


def feed_out(me, activated, normed_one, cotangent, weight, vectors):
    rows = activated.shape[0]
    count = len(weight)

    def kernel(s, f_ref, n1_ref, g_ref, v_ref, *rest):
        refs = rest[:count]
        y_ref, dr_ref, dz_ref, sums_ref, w_ref, sem = rest[count:]

        @pl.when(pl.program_id(0) == 0)
        def _():
            load_weight(weight, s[0], refs, w_ref, sem)
            sums_ref[...] = jnp.zeros_like(sums_ref)

        branch = dot(f_ref[...], w_ref[...].reshape(FF, D), NN) + v_ref[5:6, :]
        hidden = n1_ref[...] * v_ref[3:4, :] + v_ref[4:5, :]
        normed, inv_std = normalize(hidden + branch)
        y_ref[...] = (normed * v_ref[6:7, :] + v_ref[7:8, :]).astype(bf16)
        grad_y = g_ref[...].astype(f32)
        sums_ref[1:2, :] += jnp.sum(grad_y * normed, axis=0, keepdims=True)
        sums_ref[2:3, :] += jnp.sum(grad_y, axis=0, keepdims=True)
        grad_res = norm_back(grad_y * v_ref[6:7, :], normed, inv_std)
        dr_ref[...] = grad_res
        low = grad_res.astype(bf16)
        dz_ref[...] = low
        sums_ref[0:1, :] += jnp.sum(low.astype(f32), axis=0, keepdims=True)

    return call(
        kernel,
        (rows // TILE,),
        [rows_of(FF), rows_of(D), rows_of(D), whole((8, D))] + [ANY] * count,
        [rows_of(D), rows_of(D), rows_of(D), whole((8, D))],
        [
            jax.ShapeDtypeStruct((rows, D), bf16),
            jax.ShapeDtypeStruct((rows, D), f32),
            jax.ShapeDtypeStruct((rows, D), bf16),
            jax.ShapeDtypeStruct((8, D), f32),
        ],
        [pltpu.VMEM((RANKS, SHARD_FF, D), bf16), pltpu.SemaphoreType.DMA],
        flops=2 * rows * D * FF,
        bytes_accessed=rows * (D * 14 + FF * 2) + 2 * D * FF,
        name="feed_out",
    )(me, activated, normed_one, cotangent, vectors, *weight.arrays)


def grad_w_out(me, activated, grad_ffn):
    rows = activated.shape[0]
    half = RANKS // 2

    def rank(step, s):
        core = s[0] & 1
        slot = jnp.where(step < half, step, step - half)
        chip = (s[0] >> 1) ^ slot
        return chip * 2 + jnp.where(step < half, 1 - core, core)

    def kernel(s, f_ref, dz_ref, t_ref, m_ref):
        step = pl.program_id(0)
        block = dot(f_ref[...], dz_ref[...], TN).astype(bf16)

        @pl.when(step < half)
        def _():
            t_ref[0] = block

        @pl.when(step >= half)
        def _():
            m_ref[0] = block

    shape = jax.ShapeDtypeStruct((half, SHARD_FF, D), bf16)
    return call(
        kernel,
        (RANKS,),
        [pl.BlockSpec((rows, SHARD_FF), lambda i, s: (0, rank(i, s))), whole((rows, D))],
        [
            pl.BlockSpec((1, SHARD_FF, D), lambda i, s: (jnp.minimum(i, half - 1), 0, 0)),
            pl.BlockSpec((1, SHARD_FF, D), lambda i, s: (jnp.maximum(i - half, 0), 0, 0)),
        ],
        [shape, shape],
        flops=2 * rows * D * FF,
        bytes_accessed=rows * (D * 2 + FF * 2) + 2 * D * FF,
        name="grad_w_out",
    )(me, activated, grad_ffn)


def back_out(me, grad_ffn, slope, weight):
    rows = grad_ffn.shape[0]
    count = len(weight)

    def kernel(s, dz_ref, sl_ref, *rest):
        refs = rest[:count]
        du_ref, sums_ref, w_ref, sem = rest[count:]

        @pl.when(pl.program_id(0) == 0)
        def _():
            load_weight(weight, s[0], refs, w_ref, sem)
            sums_ref[...] = jnp.zeros_like(sums_ref)

        dz = dz_ref[...]
        for r in range(RANKS):
            lanes = slice(r * SHARD_FF, (r + 1) * SHARD_FF)
            grad = dot(dz, w_ref[r], NT) * sl_ref[:, lanes].astype(f32)
            low = grad.astype(bf16)
            du_ref[:, lanes] = low
            sums_ref[:, lanes] += jnp.sum(low.astype(f32), axis=0, keepdims=True)

    return call(
        kernel,
        (rows // TILE,),
        [rows_of(D), rows_of(FF)] + [ANY] * count,
        [rows_of(FF), whole((1, FF))],
        [jax.ShapeDtypeStruct((rows, FF), bf16), jax.ShapeDtypeStruct((1, FF), f32)],
        [pltpu.VMEM((RANKS, SHARD_FF, D), bf16), pltpu.SemaphoreType.DMA],
        flops=2 * rows * D * FF,
        bytes_accessed=rows * (D * 2 + FF * 4) + 2 * D * FF,
        name="back_out",
    )(me, grad_ffn, slope, *weight.arrays)


def back_in(me, grad_pre, grad_res_two, normed_one, inv_one, weight, vectors):
    rows = grad_pre.shape[0]
    count = len(weight)

    def kernel(s, du_ref, dr2_ref, n1_ref, inv_ref, v_ref, *rest):
        refs = rest[:count]
        dr1_ref, da_ref, do_ref, sums_ref, w_ref, sem = rest[count:]

        @pl.when(pl.program_id(0) == 0)
        def _():
            load_weight(weight, s[0], refs, w_ref, sem)
            sums_ref[...] = jnp.zeros_like(sums_ref)

        w_in = w_ref[:, :, D:].reshape(D, FF)
        grad_hidden = dot(du_ref[...], w_in, NT) + dr2_ref[...]
        normed = n1_ref[...]
        sums_ref[1:2, :] += jnp.sum(grad_hidden * normed, axis=0, keepdims=True)
        sums_ref[2:3, :] += jnp.sum(grad_hidden, axis=0, keepdims=True)
        grad_res = norm_back(grad_hidden * v_ref[3:4, :], normed, inv_ref[...])
        dr1_ref[...] = grad_res
        low = grad_res.astype(bf16)
        da_ref[...] = low
        sums_ref[0:1, :] += jnp.sum(low.astype(f32), axis=0, keepdims=True)
        w_proj = w_ref[:, :, :D].reshape(D, D)
        do_ref[...] = dot(low, w_proj, NT).astype(bf16)

    return call(
        kernel,
        (rows // TILE,),
        [rows_of(FF), rows_of(D), rows_of(D), rows_of(1), whole((8, D))] + [ANY] * count,
        [rows_of(D), rows_of(D), rows_of(D), whole((8, D))],
        [
            jax.ShapeDtypeStruct((rows, D), f32),
            jax.ShapeDtypeStruct((rows, D), bf16),
            jax.ShapeDtypeStruct((rows, D), bf16),
            jax.ShapeDtypeStruct((8, D), f32),
        ],
        [pltpu.VMEM((RANKS, SHARD, D + FF), bf16), pltpu.SemaphoreType.DMA],
        flops=2 * rows * D * (D + FF),
        bytes_accessed=rows * (D * 16 + FF * 2) + 2 * D * (D + FF),
        name="back_in",
    )(me, grad_pre, grad_res_two, normed_one, inv_one, vectors, *weight.arrays)


def store_by_rank(s, block, t_ref, m_ref):
    core, chip = s[0] & 1, s[0] >> 1
    for r in range(RANKS):
        part = block[r * SHARD : (r + 1) * SHARD]
        slot = chip ^ (r >> 1)

        @pl.when(core == (r & 1))
        def _():
            m_ref[slot] = part

        @pl.when(core != (r & 1))
        def _():
            t_ref[slot] = part


def grad_w_in(me, attended, grad_branch, hidden_low, grad_pre):
    rows = attended.shape[0]
    half = RANKS // 2
    tile = 384
    lead = D // tile

    def kernel(s, o_ref, da_ref, h_ref, du_ref, t_ref, m_ref, left_ref):
        step = pl.program_id(0)

        @pl.when(step == 0)
        def _():
            left_ref[...] = o_ref[...].T

        @pl.when(step == lead)
        def _():
            left_ref[...] = h_ref[...].T

        right = jnp.where(step < lead, da_ref[...], du_ref[...])
        store_by_rank(s, dot(left_ref[...], right, NN).astype(bf16), t_ref, m_ref)

    shape = jax.ShapeDtypeStruct((half, SHARD, D + FF), bf16)
    out = pl.BlockSpec((half, SHARD, tile), lambda i, s: (0, 0, i))
    return call(
        kernel,
        ((D + FF) // tile,),
        [
            whole((rows, D)),
            pl.BlockSpec((rows, tile), lambda i, s: (0, jnp.minimum(i, lead - 1))),
            whole((rows, D)),
            pl.BlockSpec((rows, tile), lambda i, s: (0, jnp.maximum(i - lead, 0))),
        ],
        [out, out],
        [shape, shape],
        [pltpu.VMEM((D, rows), bf16)],
        flops=2 * rows * D * (D + FF),
        bytes_accessed=rows * (D * 4 + FF * 2) + 2 * D * (D + FF),
        name="grad_w_in",
    )(me, attended, grad_branch, hidden_low, grad_pre)


def attention_back(lengths, qkv, weights, grad_attended):
    rows = qkv.shape[0]
    pairs = rows // SEQ
    scale = HDIM ** (-0.5)

    def kernel(s, qkv_ref, p_ref, do_ref, out_ref, sums_ref):
        @pl.when(pl.program_id(0) == 0)
        def _():
            sums_ref[...] = jnp.zeros_like(sums_ref)

        first = head_masks()
        for h in range(HEADS // 2):
            lanes = slice(h * 2 * HDIM, (h + 1) * 2 * HDIM)
            k_lanes = slice(D + h * 2 * HDIM, D + (h + 1) * 2 * HDIM)
            v_lanes = slice(2 * D + h * 2 * HDIM, 2 * D + (h + 1) * 2 * HDIM)
            q, k, v = qkv_ref[:, lanes], qkv_ref[:, k_lanes], qkv_ref[:, v_lanes]
            grad_out = do_ref[:, lanes]
            p = p_ref[:, h * 2 * SEQ : (h + 1) * 2 * SEQ]
            grad_p = dot(grad_out, stack_heads(v, first), NT)
            both = grad_p * p
            halves = []
            for part in range(2):
                cut = slice(part * SEQ, (part + 1) * SEQ)
                halves.append((p[:, cut] * (grad_p[:, cut] - lane_sum(both[:, cut]))).astype(bf16))
            grad_s = jnp.concatenate(halves, axis=1)
            grad_v = dot(p.astype(bf16), grad_out, TN)
            grad_v = jnp.where(first, grad_v[:SEQ], grad_v[SEQ:]).astype(bf16)
            grad_q = (dot(grad_s, stack_heads(k, first), NN) * scale).astype(bf16)
            grad_k = dot(grad_s, q, TN)
            grad_k = (jnp.where(first, grad_k[:SEQ], grad_k[SEQ:]) * scale).astype(bf16)
            out_ref[:, lanes] = grad_q
            out_ref[:, k_lanes] = grad_k
            out_ref[:, v_lanes] = grad_v
            sums_ref[0:1, lanes] += jnp.sum(grad_q.astype(f32), axis=0, keepdims=True)
            sums_ref[1:2, lanes] += jnp.sum(grad_v.astype(f32), axis=0, keepdims=True)

    return call(
        kernel,
        (pairs,),
        [rows_of(3 * D, SEQ), rows_of(HEADS * SEQ, SEQ), rows_of(D, SEQ)],
        [rows_of(3 * D, SEQ), whole((8, D))],
        [jax.ShapeDtypeStruct((rows, 3 * D), bf16), jax.ShapeDtypeStruct((8, D), f32)],
        flops=14e9,
        bytes_accessed=rows * (3 * D * 4 + D * 2 + HEADS * SEQ * 4),
        name="attention_back",
    )(lengths, qkv, weights, grad_attended)


def grad_w_qkv(me, tokens, grad_mixed):
    rows = tokens.shape[0]
    half = RANKS // 2
    tile = 384

    def kernel(s, x_ref, g_ref, t_ref, m_ref, left_ref):
        @pl.when(pl.program_id(0) == 0)
        def _():
            left_ref[...] = x_ref[...].T

        store_by_rank(s, dot(left_ref[...], g_ref[...], NN).astype(bf16), t_ref, m_ref)

    shape = jax.ShapeDtypeStruct((half, SHARD, 3 * D), bf16)
    out = pl.BlockSpec((half, SHARD, tile), lambda i, s: (0, 0, i))
    return call(
        kernel,
        (3 * D // tile,),
        [whole((rows, D)), pl.BlockSpec((rows, tile), lambda i, s: (0, i))],
        [out, out],
        [shape, shape],
        [pltpu.VMEM((D, rows), bf16)],
        flops=2 * rows * D * 3 * D,
        bytes_accessed=rows * (D * 8) + 2 * D * 3 * D,
        name="grad_w_qkv",
    )(me, tokens, grad_mixed)


def back_qkv(me, grad_mixed, grad_res_one, weight):
    rows = grad_mixed.shape[0]
    count = len(weight)

    def kernel(s, g_ref, dr_ref, *rest):
        refs = rest[:count]
        out_ref, w_ref, sem = rest[count:]

        @pl.when(pl.program_id(0) == 0)
        def _():
            load_weight(weight, s[0], refs, w_ref, sem)

        w = w_ref[...].reshape(D, 3 * D)
        out_ref[...] = (dot(g_ref[...], w, NT) + dr_ref[...]).astype(bf16)

    return call(
        kernel,
        (rows // TILE,),
        [rows_of(3 * D), rows_of(D)] + [ANY] * count,
        rows_of(D),
        jax.ShapeDtypeStruct((rows, D), bf16),
        [pltpu.VMEM((RANKS, SHARD, 3 * D), bf16), pltpu.SemaphoreType.DMA],
        flops=2 * rows * D * 3 * D,
        bytes_accessed=rows * D * 12 + 2 * D * 3 * D,
        name="back_qkv",
    )(me, grad_mixed, grad_res_one, *weight.arrays)


def adamw_math(moment, square, gradient):
    first_fix = 1.0 - beta_one**STEP
    second_fix = 1.0 - beta_two**STEP
    moment = beta_one * moment + (1.0 - beta_one) * gradient
    square = beta_two * square + (1.0 - beta_two) * gradient * gradient
    update = moment / first_fix / (jnp.sqrt(square / second_fix) + adam_epsilon)
    return (update, moment, square)


def adamw(moment, square, gradient):
    gradient = gradient.astype(f32)
    return (gradient,) + adamw_math(moment, square, gradient)


def flip(bit):
    return [(i, i ^ bit) for i in range(RANKS)]


def swap(value, bit):
    return lax.ppermute(value, "fsdp", flip(bit))


def gather_chunk(shard):
    half = shard.shape[0] // 2
    from_x = swap(shard, 2)
    from_y = swap(shard, 4)
    far_a = swap(from_x[:half], 4)
    far_b = swap(from_y[half:], 2)
    mine = [shard, from_x, from_y, far_a, far_b]
    places = [
        (0, 0, 2 * half),
        (2, 0, 2 * half),
        (4, 0, 2 * half),
        (6, 0, half),
        (6, half, half),
    ]
    other = [swap(piece, 1) for piece in mine]
    return Pieces(mine + other, places + [(m ^ 1, first, count) for m, first, count in places])


def low_sum(*values):
    total = values[0].astype(f32)
    for value in values[1:]:
        total = total + value.astype(f32)
    return total.astype(bf16)


def scatter_chunk(theirs, mine):
    half = mine.shape[1] // 2
    got = swap(theirs, 1)
    send_x = low_sum(mine[1::2, :half], got[1::2, :half])
    send_y = low_sum(mine[2:, half:], got[2:, half:])
    got_x = swap(send_x, 2)
    got_y = swap(send_y, 4)
    last_y = swap(low_sum(mine[2, :half], got[2, :half], got_x[1]), 4)
    last_x = swap(low_sum(mine[1, half:], got[1, half:], got_y[1]), 2)
    return jnp.concatenate(
        [
            low_sum(mine[0, :half], got[0, :half], got_x[0], last_y),
            low_sum(mine[0, half:], got[0, half:], got_y[0], last_x),
        ],
        axis=0,
    )


def sum_over_copies(owned, rep_index):
    near = low_sum(owned, lax.ppermute(owned, "rep", [(0, 1), (3, 2)]))
    total = low_sum(near, lax.ppermute(near, "rep", [(1, 2), (2, 1)]))
    back = lax.ppermute(total, "rep", [(1, 0), (2, 3)])
    inner = (rep_index == 1) | (rep_index == 2)
    return jnp.where(inner, total, back)


def gather_small(value, me):
    for position, bit in enumerate((1, 2, 4)):
        got = swap(value, bit)
        low_first = ((me >> position) & 1) == 0
        value = jnp.where(
            low_first, jnp.concatenate([value, got]), jnp.concatenate([got, value])
        )
    return value


def local(
    fsdp,
    rep,
    tokens,
    cotangent,
    lengths,
    w_attn,
    w_in,
    w_out,
    b_in,
    vecs,
    m_attn,
    m_in,
    m_out,
    m_bin,
    m_vecs,
    v_attn,
    v_in,
    v_out,
    v_bin,
    v_vecs,
):
    direct = fsdp == RANKS and rep == 4
    position = lax.axis_index("fsdp")
    rep_index = lax.axis_index("rep")
    part = D // fsdp
    low_qkv = w_attn[:, : 3 * D].astype(bf16)
    low_in = jnp.concatenate([w_attn[:, 3 * D :], w_in], axis=1).astype(bf16)
    low_out = w_out.astype(bf16)
    small = jnp.concatenate([vecs.reshape(1, -1), b_in.reshape(1, -1)], axis=1).astype(bf16)
    if direct:
        me = position.reshape(1)
        pieces_qkv = gather_chunk(low_qkv)
        small_all = gather_small(small, position)
        pieces_in = gather_chunk(low_in)
        pieces_out = gather_chunk(low_out)
    else:
        me = jnp.zeros((1,), jnp.int32)

        def gather(shard):
            full = lax.all_gather(shard, "fsdp", axis=0, tiled=True)
            return Pieces([full.reshape(RANKS, -1, full.shape[1])], [None])

        pieces_qkv, pieces_in, pieces_out = gather(low_qkv), gather(low_in), gather(low_out)
        small_all = lax.all_gather(small, "fsdp", axis=0, tiled=True)
    small_all = small_all.astype(f32)
    vectors = small_all[:, : 8 * part].reshape(fsdp, 8, part).transpose(1, 0, 2).reshape(8, D)
    in_bias = small_all[:, 8 * part :].reshape(1, FF)
    mixed_bias = jnp.concatenate([vectors[0:1], jnp.zeros((1, D), f32), vectors[1:2]], axis=1)

    qkv = project_qkv(me, tokens, pieces_qkv, mixed_bias)
    attended, weights = attention(lengths, qkv)
    normed_one, inv_one, hidden_low, activated, slope = feed_in(
        me, attended, tokens, pieces_in, vectors, in_bias
    )
    output, grad_res_two, grad_ffn, sums_two = feed_out(
        me, activated, normed_one, cotangent, pieces_out, vectors
    )
    parts_out = grad_w_out(me, activated, grad_ffn)
    grad_pre, sums_in = back_out(me, grad_ffn, slope, pieces_out)
    grad_res_one, grad_branch, grad_attended, sums_one = back_in(
        me, grad_pre, grad_res_two, normed_one, inv_one, pieces_in, vectors
    )
    parts_in = grad_w_in(me, attended, grad_branch, hidden_low, grad_pre)
    grad_mixed, sums_qkv = attention_back(lengths, qkv, weights, grad_attended)
    parts_qkv = grad_w_qkv(me, tokens, grad_mixed)
    grad_tokens = back_qkv(me, grad_mixed, grad_res_one, pieces_qkv)

    local_vecs = jnp.concatenate(
        [sums_qkv[0:2], sums_one[0:3], sums_two[0:3], sums_in.reshape(FF // D, D)], axis=0
    )
    if direct:
        for bit in (1, 2, 4):
            local_vecs = local_vecs + swap(local_vecs, bit)
        for bit in (1, 2):
            local_vecs = local_vecs + lax.ppermute(
                local_vecs, "rep", [(i, i ^ bit) for i in range(4)]
            )
        sum_out = sum_over_copies(scatter_chunk(*parts_out), rep_index)
        sum_in = sum_over_copies(scatter_chunk(*parts_in), rep_index)
        sum_qkv = sum_over_copies(scatter_chunk(*parts_qkv), rep_index)
    else:
        local_vecs = lax.psum(local_vecs, ("fsdp", "rep"))

        def reduce(theirs, mine):
            full = jnp.stack([mine, theirs], axis=1)
            full = full.reshape(-1, full.shape[-1])
            owned = lax.psum_scatter(full, "fsdp", scatter_dimension=0, tiled=True)
            return lax.psum(owned, "rep")

        sum_out, sum_in, sum_qkv = reduce(*parts_out), reduce(*parts_in), reduce(*parts_qkv)
    sum_vecs = lax.dynamic_slice(local_vecs, (0, position * part), (8, part))
    sum_bin = lax.dynamic_slice(local_vecs[8:].reshape(FF), (position * (FF // fsdp),), (FF // fsdp,))

    grad_out, step_out, mom_out, sq_out = adamw(m_out, v_out, sum_out)
    grad_in, step_in, mom_in, sq_in = adamw(m_in, v_in, sum_in[:, D:])
    sum_attn = jnp.concatenate([sum_qkv, sum_in[:, :D]], axis=1)
    grad_attn, step_attn, mom_attn, sq_attn = adamw(m_attn, v_attn, sum_attn)
    grad_bin, step_bin, mom_bin, sq_bin = adamw(m_bin, v_bin, sum_bin)
    grad_vecs, step_vecs, mom_vecs, sq_vecs = adamw(m_vecs, v_vecs, sum_vecs)
    return (
        output,
        grad_tokens,
        grad_attn,
        grad_in,
        grad_out,
        grad_bin,
        grad_vecs,
        step_attn,
        step_in,
        step_out,
        step_bin,
        step_vecs,
        mom_attn,
        mom_in,
        mom_out,
        mom_bin,
        mom_vecs,
        sq_attn,
        sq_in,
        sq_out,
        sq_bin,
        sq_vecs,
    )


def solution(mesh):
    rows, row, col = P(("rep", "fsdp"), None), P("fsdp", None), P(None, "fsdp")
    flat = P("fsdp")
    state = (row, row, row, flat, col)
    return jax.shard_map(
        functools.partial(local, mesh.shape["fsdp"], mesh.shape["rep"]),
        mesh=mesh,
        in_specs=(rows, rows, P(("rep", "fsdp"))) + state * 3,
        out_specs=(rows, rows) + state * 4,
        check_vma=False,
    )
```

time: 591 us -> 363 us (0.61)
  Pallas kernels: 0 us -> 147 us
  matrix products: 143 us -> 0 us
  waiting for transfers between devices: 245 us -> 121 us
  local copies, waits for them, and re-layouts: 82.1 us -> 9.92 us
  starting transfers between devices: 0.33 us -> 57.1 us
  blocking collectives: 54.6 us -> 0 us
  other arithmetic: 43.8 us -> 24.6 us
  between operations: 15.7 us -> 1.48 us
    pallas_call x0 -> x11, Pallas kernels: none -> 147 us  [the longest x1 16.9 us: feed_in(): call(kernel, (rows // TILE,), [rows_of(D), rows_of(D), whole((8, D)), who...]
    dot_general x17 -> x0, matrix products: 135 us -> none  [the longest x1 48.1 us: forward_pass(): jnp.dot(hidden_low, in_mat, preferred_element_type=jnp.float32) + bias_f]
    ppermute x0 -> x59, waiting for transfers between devices: none -> 121 us  [the longest x48 74.8 us: swap(): return lax.ppermute(value, 'fsdp', flip(bit))]
    reduce_scatter x1 -> x0, waiting for transfers between devices: 77.5 us -> none  [local(): lax.psum_scatter(grad_out_mat, 'fsdp', scatter_dimension=0, tiled=True)]
    unnamed x11 -> x0, waiting for transfers between devices: 71.1 us -> none
    psum x1 -> x0, waiting for transfers between devices: 70.1 us -> none  [local(): lax.psum(owned[0].astype(jnp.bfloat16), 'rep').astype(jnp.float32)]
    unnamed x128 -> x75, local copies, waits for them, and re-layouts: 68.7 us -> 3.38 us
    ppermute x0 -> x59, starting transfers between devices: none -> 57.1 us  [the longest x48 37.1 us: swap(): return lax.ppermute(value, 'fsdp', flip(bit))]
  transfers between devices with their start and end apart: 8 -> 59, of which waited for: 5 -> 21; matrix products, arithmetic and copies ran while one was open for 33% -> 7% of each run, Pallas kernels for 0% -> 21%
where the time goes in v1:
time: 363 us; the launch traced here: 361 us
  Pallas kernels  147 us (40%)
  waiting for transfers between devices  121 us (33%)
  starting transfers between devices  57.1 us (16%)
  other arithmetic  24.6 us (7%)
  local copies, waits for them, and re-layouts  9.92 us (3%)
    ppermute x48, waiting for transfers between devices, swap(): return lax.ppermute(value, 'fsdp', flip(bit))  74.8 us
    ppermute x48, starting transfers between devices, swap(): return lax.ppermute(value, 'fsdp', flip(bit))  37.1 us
    ppermute x3, waiting for transfers between devices, sum_over_copies(): back = lax.ppermute(total, 'rep', [(1, 0), (2, 3)])  28.2 us
    pallas_call x1, Pallas kernels, feed_in(): call(kernel, (rows // TILE,), [rows_of(D), rows_of(D), whole((8, D)), who...  16.9 us
    pallas_call x1, Pallas kernels, attention_back(): call(kernel, (pairs,), [rows_of(3 * D, SEQ), rows_of(HEADS * SEQ, SEQ), r...  16.8 us
    pallas_call x1, Pallas kernels, back_in(): call(kernel, (rows // TILE,), [rows_of(FF), rows_of(D), rows_of(D), rows_...  16.5 us
    pallas_call x1, Pallas kernels, grad_w_in(): call(kernel, ((D + FF) // tile,), [whole((rows, D)), pl.BlockSpec((rows,...  16.4 us
    ppermute x3, waiting for transfers between devices, sum_over_copies(): near = low_sum(owned, lax.ppermute(owned, 'rep', [(0, 1), (3, 2)]))  15.7 us
  transfers between devices with their start and end apart: 59, of which 21 were waited for; matrix products, arithmetic and copies ran while one was open for 7% of the time, Pallas kernels for 21%

profile of v1, /device:TPU:0, one launch (start us, length us, event | category | flops | bytes accessed | tf_op | source)
XLA Modules:
  0.0 360.9 jit_solution(9895362697569492712)
XLA Ops:
  3.6 2.9 collective-permute-start.1
  6.4 1.3 convert_element_type.351.rest_0_
  7.9 2.0 collective-permute-start.22
  10.3 1.9 collective-permute-start.3
  12.2 1.5 collective-permute-start.4
  13.8 10.5 %collective-permute-done.2 = bf16[4,1152]{1,0:T(4,128)(2,1)S(1)} collective-permute-done((bf16[4,1152]{1,0:T(4,128)(2,1)S(1)}, bf16[4,1152]{1,0:T(4,128)(2,1)S(1)}, u32[]{:S(2)}, u32[]{:S(2)}) %collective-permute-start.2) | collective-permute-done | bytes 9248 | tf_op jit(solution)/shard_map/ppermute | solution.py:580
  24.4 8.0 %collective-permute-done.3.rest_1_ = bf16[96,2304]{1,0:T(8,128)(2,1)S(1)} collective-permute-done((bf16[96,2304]{1,0:T(8,128)(2,1)S(1)}, bf16[96,2304]{1,0:T(8,128)(2,1)S(1)}, u32[]{:S(2)}, u32[]{:S(2)}) %collective-permute-start.3) | collective-permute-done | bytes 442400 | tf_op jit(solution)/shard_map/ppermute | solution.py:580
  32.8 1.7 collective-permute-start.13
  34.6 1.1 slice.279
  36.1 1.7 collective-permute-start.6
  37.8 17.4 %collective-permute-done.5.rest_3_ = bf16[48,2304]{1,0:T(8,128)(2,1)} collective-permute-done((bf16[48,2304]{1,0:T(8,128)(2,1)S(1)}, bf16[48,2304]{1,0:T(8,128)(2,1)}, u32[]{:S(2)}, u32[]{:S(2)}) %collective-permute-start.5) | collective-permute-done | bytes 221216 | tf_op jit(solution)/shard_map/ppermute | solution.py:580
  56.7 1.5 collective-permute-start.23
  62.7 1.5 collective-permute-start.15
  66.8 1.3 collective-permute-start.24
  68.1 10.5 %qkv.1.qkv_ref = bf16[1024,2304]{1,0:T(8,128)(2,1)} custom-call(s32[1]{0:T(128)} %bitcast.s, bf16[1024,768]{1,0:T(8,128)(2,1)} %x_ref.5, f32[1,2304]{1,0:T(1,128)} %fusion.16.b_ref, bf16[96,2304]{1,0:T(8,128)(2,1)} %copy-done.12, bf16[96,2304]{1,0:T(8,128)(2,1)} %copy-done.16, bf16[96,2304]{1,0:T(8,128)(2,1)} %collective-permute-done.4.rest_2_, ...), custom_call_target="tpu_custom_call" | custom-call | flops 3623878656 | bytes 9830400 | tf_op jit(solution)/shard_map/qkv/pallas_call | solution.py:134
  80.5 11.7 %attention.1 = (bf16[1024,768]{1,0:T(8,128)(2,1)}, f32[1024,1536]{1,0:T(8,128)}) custom-call(s32[8]{0:T(128)} %s.3, bf16[1024,2304]{1,0:T(8,128)(2,1)} %qkv.1.qkv_ref), custom_call_target="tpu_custom_call" | custom-call | flops 8000000000 | bytes 12582912 | tf_op jit(solution)/shard_map/attention/pallas_call | solution.py:182
  93.5 16.9 %feed_in.1 = (f32[1024,768]{1,0:T(8,128)}, f32[1024,1]{1,0:T(8,128)}, bf16[1024,768]{1,0:T(8,128)(2,1)}, bf16[1024,3072]{1,0:T(8,128)(2,1)}, bf16[1024,3072]{1,0:T(8,128)(2,1)}) custom-call(s32[1]{0:T(128)} %bitcast.s, bf16[1024,768]{1,0:T(8,128)(2,1)} %get-tuple-element.47.o_ref, bf16[1024,768]{1,0:T(8,128)(2,1)} %x_ref.5, f32[8,768]{1,0:T(8,128)} %reshape.172.v_ref, ...), custom_call_target="tpu_custom_call" | custom-call | flops 6039797760 | bytes 26345472 | tf_op jit(solution)/shard_map/feed_in/pallas_call | solution.py:224
  111.8 14.0 %feed_out.1 = (bf16[1024,768]{1,0:T(8,128)(2,1)}, f32[1024,768]{1,0:T(8,128)}, bf16[1024,768]{1,0:T(8,128)(2,1)}, f32[8,768]{1,0:T(8,128)}) custom-call(s32[1]{0:T(128)} %bitcast.s, bf16[1024,3072]{1,0:T(8,128)(2,1)} %get-tuple-element.48.f_ref, f32[1024,768]{1,0:T(8,128)} %get-tuple-element.49.n1_ref, bf16[1024,768]{1,0:T(8,128)(2,1)} %g_ref.1, ...), custom_call_target="tpu_custom_call" | custom-call | flops 4831838208 | bytes 22020096 | tf_op jit(solution)/shard_map/feed_out/pallas_call | solution.py:269
  125.9 12.8 %back_out.1 = (bf16[1024,3072]{1,0:T(8,128)(2,1)}, f32[1,3072]{1,0:T(1,128)}) custom-call(s32[1]{0:T(128)} %bitcast.s, bf16[1024,768]{1,0:T(8,128)(2,1)} %get-tuple-element.52.dz_ref, bf16[1024,3072]{1,0:T(8,128)(2,1)} %get-tuple-element.53.sl_ref, bf16[384,768]{1,0:T(8,128)(2,1)} %copy-done.11, bf16[384,768]{1,0:T(8,128)(2,1)} %copy-done.13, ...), custom_call_target="tpu_custom_call" | custom-call | flops 4831838208 | bytes 18874368 | tf_op jit(solution)/shard_map/back_out/pallas_call | solution.py:346
  138.7 16.5 %back_in.1 = (f32[1024,768]{1,0:T(8,128)}, bf16[1024,768]{1,0:T(8,128)(2,1)}, bf16[1024,768]{1,0:T(8,128)(2,1)}, f32[8,768]{1,0:T(8,128)}) custom-call(s32[1]{0:T(128)} %bitcast.s, bf16[1024,3072]{1,0:T(8,128)(2,1)} %get-tuple-element.54.du_ref, f32[1024,768]{1,0:T(8,128)} %get-tuple-element.55.dr2_ref, f32[1024,768]{1,0:T(8,128)} %get-tuple-element.49.n1_ref, ...), custom_call_target="tpu_custom_call" | custom-call | flops 6039797760 | bytes 24772608 | tf_op jit(solution)/shard_map/back_in/pallas_call | solution.py:385
  155.1 16.8 %attention_back.1 = (bf16[1024,2304]{1,0:T(8,128)(2,1)}, f32[8,768]{1,0:T(8,128)}) custom-call(s32[8]{0:T(128)} %s.3, bf16[1024,2304]{1,0:T(8,128)(2,1)} %qkv.1.qkv_ref, f32[1024,1536]{1,0:T(8,128)} %get-tuple-element.51.p_ref, bf16[1024,768]{1,0:T(8,128)(2,1)} %get-tuple-element.57.do_ref), custom_call_target="tpu_custom_call" | custom-call | flops 14000000000 | bytes 17301504 | tf_op jit(solution)/shard_map/attention_back/pallas_call | solution.py:494
  171.9 10.2 %grad_w_qkv.1 = (bf16[4,96,2304]{2,1,0:T(8,128)(2,1)}, bf16[4,96,2304]{2,1,0:T(8,128)(2,1)}) custom-call(s32[1]{0:T(128)} %bitcast.s, bf16[1024,768]{1,0:T(8,128)(2,1)} %x_ref.5, bf16[1024,2304]{1,0:T(8,128)(2,1)} %get-tuple-element.58.g_ref), custom_call_target="tpu_custom_call" | custom-call | flops 3623878656 | bytes 9830400 | tf_op jit(solution)/shard_map/grad_w_qkv/pallas_call | solution.py:520
  182.2 16.4 %grad_w_in.1 = (bf16[4,96,3840]{2,1,0:T(8,128)(2,1)}, bf16[4,96,3840]{2,1,0:T(8,128)(2,1)}) custom-call(s32[1]{0:T(128)} %bitcast.s, bf16[1024,768]{1,0:T(8,128)(2,1)} %get-tuple-element.47.o_ref, bf16[1024,768]{1,0:T(8,128)(2,1)} %get-tuple-element.62.da_ref, bf16[1024,768]{1,0:T(8,128)(2,1)} %get-tuple-element.63.h_ref, ...), custom_call_target="tpu_custom_call" | custom-call | flops 6039797760 | bytes 15335424 | tf_op jit(solution)/shard_map/grad_w_in/pallas_call | solution.py:440
  201.2 11.3 %grad_w_out.1 = (bf16[4,384,768]{2,1,0:T(8,128)(2,1)}, bf16[4,384,768]{2,1,0:T(8,128)(2,1)}) custom-call(s32[1]{0:T(128)} %bitcast.s, bf16[1024,3072]{1,0:T(8,128)(2,1)} %get-tuple-element.48.f_ref, bf16[1024,768]{1,0:T(8,128)(2,1)} %get-tuple-element.52.dz_ref), custom_call_target="tpu_custom_call" | custom-call | flops 4831838208 | bytes 12582912 | tf_op jit(solution)/shard_map/grad_w_out/pallas_call | solution.py:310
  213.0 1.6 collective-permute-start.55
  214.6 2.6 collective-permute-done.55
  217.2 1.4 collective-permute-start.56
  218.5 2.8 collective-permute-done.56
  221.3 1.6 collective-permute-start.57
  223.0 2.5 collective-permute-done.57
  225.5 2.9 collective-permute-start.58
  228.4 9.5 %back_qkv.1 = bf16[1024,768]{1,0:T(8,128)(2,1)} custom-call(s32[1]{0:T(128)} %bitcast.s, bf16[1024,2304]{1,0:T(8,128)(2,1)} %get-tuple-element.58.g_ref, f32[1024,768]{1,0:T(8,128)} %get-tuple-element.59.dr_ref, bf16[96,2304]{1,0:T(8,128)(2,1)} %copy-done.12, bf16[96,2304]{1,0:T(8,128)(2,1)} %copy-done.16, bf16[96,2304]{1,0:T(8,128)(2,1)} %collective-permute-done.4.rest_2_, ...), custom_call_target="tpu_custom_call" | custom-call | flops 3623878656 | bytes 12976128 | tf_op jit(solution)/shard_map/back_qkv/pallas_call | solution.py:548
  238.0 1.8 add_convert_fusion.11
  239.8 1.6 collective-permute-start.31
  241.3 1.3 collective-permute-start.33
  244.0 4.2 %collective-permute-done.31 = bf16[2,48,2304]{2,1,0:T(8,128)(2,1)S(1)} collective-permute-done((bf16[2,48,2304]{2,1,0:T(8,128)(2,1)S(1)}, bf16[2,48,2304]{2,1,0:T(8,128)(2,1)S(1)}, u32[]{:S(2)}, u32[]{:S(2)}) %collective-permute-start.31) | collective-permute-done | bytes 442400 | tf_op jit(solution)/shard_map/ppermute | solution.py:580
  248.1 2.3 collective-permute-done.33
  250.5 1.4 fusion.13
  251.9 1.4 collective-permute-start.32
  253.8 1.7 add_convert_fusion.7
  255.5 1.6 collective-permute-start.47
  258.8 1.5 collective-permute-done.32
  260.3 1.3 collective-permute-start.41
  261.6 1.5 fusion.8
  263.2 3.0 collective-permute-start.35
  266.2 8.0 %collective-permute-done.47 = bf16[2,192,768]{2,1,0:T(8,128)(2,1)S(1)} collective-permute-done((bf16[2,192,768]{2,1,0:T(8,128)(2,1)S(1)}, bf16[2,192,768]{2,1,0:T(8,128)(2,1)S(1)}, u32[]{:S(2)}, u32[]{:S(2)}) %collective-permute-start.47) | collective-permute-done | bytes 589856 | tf_op jit(solution)/shard_map/ppermute | solution.py:580
  274.3 1.3 fusion.11
  276.9 13.1 %collective-permute-done.39 = bf16[2,48,3840]{2,1,0:T(8,128)(2,1)S(1)} collective-permute-done((bf16[2,48,3840]{2,1,0:T(8,128)(2,1)S(1)}, bf16[2,48,3840]{2,1,0:T(8,128)(2,1)S(1)}, u32[]{:S(2)}, u32[]{:S(2)}) %collective-permute-start.39) | collective-permute-done | bytes 737312 | tf_op jit(solution)/shard_map/ppermute | solution.py:580
  290.6 1.0 collective-permute-start.42
  291.7 2.3 collective-permute-done.48
  294.0 1.4 fusion.6
  295.5 3.5 collective-permute-start.51
  299.5 2.5 collective-permute-start.43
  302.8 8.6 %collective-permute-done.51 = bf16[384,768]{1,0:T(8,128)(2,1)S(1)} collective-permute-done((bf16[384,768]{1,0:T(8,128)(2,1)S(1)}, bf16[384,768]{1,0:T(8,128)(2,1)S(1)}, u32[]{:S(2)}, u32[]{:S(2)}) %collective-permute-start.51) | collective-permute-done | bytes 589856 | tf_op jit(solution)/shard_map/ppermute | solution.py:627
  312.3 7.0 %collective-permute-done.43 = bf16[96,3840]{1,0:T(8,128)(2,1)S(1)} collective-permute-done((bf16[96,3840]{1,0:T(8,128)(2,1)S(1)}, bf16[96,3840]{1,0:T(8,128)(2,1)S(1)}, u32[]{:S(2)}, u32[]{:S(2)}) %collective-permute-start.43) | collective-permute-done | bytes 737312 | tf_op jit(solution)/shard_map/ppermute | solution.py:627
  320.4 1.3 collective-permute-start.37
  321.8 1.3 collective-permute-start.53
  323.3 1.7 collective-permute-start.45
  325.0 7.9 %collective-permute-done.37 = bf16[96,2304]{1,0:T(8,128)(2,1)S(1)} collective-permute-done((bf16[96,2304]{1,0:T(8,128)(2,1)S(1)}, bf16[96,2304]{1,0:T(8,128)(2,1)S(1)}, u32[]{:S(2)}, u32[]{:S(2)}) %collective-permute-start.37) | collective-permute-done | bytes 442400 | tf_op jit(solution)/shard_map/ppermute | solution.py:629
  333.0 14.3 %collective-permute-done.53 = bf16[384,768]{1,0:T(8,128)(2,1)S(1)} collective-permute-done((bf16[384,768]{1,0:T(8,128)(2,1)S(1)}, bf16[384,768]{1,0:T(8,128)(2,1)S(1)}, u32[]{:S(2)}, u32[]{:S(2)}) %collective-permute-start.53) | collective-permute-done | bytes 589856 | tf_op jit(solution)/shard_map/ppermute | solution.py:629
  347.2 2.5 add_divide_fusion
  349.7 6.0 %collective-permute-done.45 = bf16[96,3840]{1,0:T(8,128)(2,1)S(1)} collective-permute-done((bf16[96,3840]{1,0:T(8,128)(2,1)S(1)}, bf16[96,3840]{1,0:T(8,128)(2,1)S(1)}, u32[]{:S(2)}, u32[]{:S(2)}) %collective-permute-start.45) | collective-permute-done | bytes 737312 | tf_op jit(solution)/shard_map/ppermute | solution.py:629
  355.9 2.5 add_divide_fusion.1
  358.4 2.5 add_divide_fusion.2
  (209 shorter events, 29.7 us)
Async XLA Ops:
  2.2 1.3 collective-permute-start
  3.6 6.4 %collective-permute-start.1 = (bf16[2,1152]{1,0:T(2,128)(2,1)S(1)}, bf16[2,1152]{1,0:T(2,128)(2,1)S(1)}, u32[]{:S(2)}, u32[]{:S(2)}) collective-permute-start(bf16[2,1152]{1,0:T(2,128)(2,1)S(1)} %broadcast_select_fusion.2), channel_id=1, source_target_pairs={{0,2},{1,3},{2,0},{3,1},{4,6},{5,7},{6,4},{7,5},{8,10},{9,11},{10,... | collective-permute-start | bytes 13832 | tf_op jit(solution)/shard_map/ppermute | solution.py:580
  7.8 71.6 %copy-start.11 = (bf16[384,768]{1,0:T(8,128)(2,1)}, bf16[384,768]{1,0:T(8,128)(2,1)S(1)}, u32[]{:S(2)}) copy-start(bf16[384,768]{1,0:T(8,128)(2,1)S(1)} %convert_element_type.351.rest_0_) | copy-start | bytes 1769476
  7.8 27.9 %collective-permute-start.21 = (bf16[384,768]{1,0:T(8,128)(2,1)S(1)}, bf16[384,768]{1,0:T(8,128)(2,1)S(1)}, u32[]{:S(2)}, u32[]{:S(2)}) collective-permute-start(bf16[384,768]{1,0:T(8,128)(2,1)S(1)} %convert_element_type.351.rest_0_), channel_id=1, source_target_pairs={{0,2},{1,3},{2,0},{3,1},{4,6},{5,7},{6,4},{7,5},{8,10},{9,11},{10,... | collective-permute-start | bytes 1769480 | tf_op jit(solution)/shard_map/ppermute | solution.py:580
  7.9 28.2 %collective-permute-start.22 = (bf16[384,768]{1,0:T(8,128)(2,1)S(1)}, bf16[384,768]{1,0:T(8,128)(2,1)S(1)}, u32[]{:S(2)}, u32[]{:S(2)}) collective-permute-start(bf16[384,768]{1,0:T(8,128)(2,1)S(1)} %convert_element_type.351.rest_0_), channel_id=1, source_target_pairs={{0,4},{1,5},{2,6},{3,7},{4,0},{5,1},{6,2},{7,3},{8,12},{9,13},{10,... | collective-permute-start | bytes 1769480 | tf_op jit(solution)/shard_map/ppermute | solution.py:580
  10.0 14.4 %collective-permute-start.2 = (bf16[4,1152]{1,0:T(4,128)(2,1)S(1)}, bf16[4,1152]{1,0:T(4,128)(2,1)S(1)}, u32[]{:S(2)}, u32[]{:S(2)}) collective-permute-start(bf16[4,1152]{1,0:T(4,128)(2,1)S(1)} %maximum_select_fusion.1), channel_id=1, source_target_pairs={{0,4},{1,5},{2,6},{3,7},{4,0},{5,1},{6,2},{7,3},{8,12},{9,13},{10,... | collective-permute-start | bytes 27656 | tf_op jit(solution)/shard_map/ppermute | solution.py:580
  10.3 22.1 %collective-permute-start.3 = (bf16[96,2304]{1,0:T(8,128)(2,1)S(1)}, bf16[96,2304]{1,0:T(8,128)(2,1)S(1)}, u32[]{:S(2)}, u32[]{:S(2)}) collective-permute-start(bf16[96,2304]{1,0:T(8,128)(2,1)S(1)} %slice.277.rest_0_), channel_id=1, source_target_pairs={{0,2},{1,3},{2,0},{3,1},{4,6},{5,7},{6,4},{7,5},{8,10},{9,11},{10,... | collective-permute-start | bytes 1327112 | tf_op jit(solution)/shard_map/ppermute | solution.py:580
  12.2 20.6 %collective-permute-start.4 = (bf16[96,2304]{1,0:T(8,128)(2,1)S(1)}, bf16[96,2304]{1,0:T(8,128)(2,1)}, u32[]{:S(2)}, u32[]{:S(2)}) collective-permute-start(bf16[96,2304]{1,0:T(8,128)(2,1)S(1)} %slice.277.rest_0_), channel_id=1, source_target_pairs={{0,4},{1,5},{2,6},{3,7},{4,0},{5,1},{6,2},{7,3},{8,12},{9,13},{10,... | collective-permute-start | bytes 1327112 | tf_op jit(solution)/shard_map/ppermute | solution.py:580
  24.3 10.2 %collective-permute-start.7 = (bf16[96,2304]{1,0:T(8,128)(2,1)S(1)}, bf16[96,2304]{1,0:T(8,128)(2,1)S(1)}, u32[]{:S(2)}, u32[]{:S(2)}) collective-permute-start(bf16[96,2304]{1,0:T(8,128)(2,1)S(1)} %slice.277.rest_0_), channel_id=1, source_target_pairs={{0,1},{1,0},{2,3},{3,2},{4,5},{5,4},{6,7},{7,6},{8,9},{9,8},{10,11... | collective-permute-start | bytes 1327112 | tf_op jit(solution)/shard_map/ppermute | solution.py:580
  24.4 36.5 %copy-start.10 = (bf16[96,3840]{1,0:T(8,128)(2,1)}, bf16[96,3840]{1,0:T(8,128)(2,1)S(1)}, u32[]{:S(2)}) copy-start(bf16[96,3840]{1,0:T(8,128)(2,1)S(1)} %pad_maximum_fusion.rest_0_) | copy-start | bytes 2211844
  32.5 35.7 %copy-start.16 = (bf16[96,2304]{1,0:T(8,128)(2,1)}, bf16[96,2304]{1,0:T(8,128)(2,1)S(1)}, u32[]{:S(2)}) copy-start(bf16[96,2304]{1,0:T(8,128)(2,1)S(1)} %collective-permute-done.3.rest_1_) | copy-start | bytes 1327108
  32.5 24.3 %collective-permute-start.12 = (bf16[96,3840]{1,0:T(8,128)(2,1)S(1)}, bf16[96,3840]{1,0:T(8,128)(2,1)}, u32[]{:S(2)}, u32[]{:S(2)}) collective-permute-start(bf16[96,3840]{1,0:T(8,128)(2,1)S(1)} %pad_maximum_fusion.rest_0_), channel_id=1, source_target_pairs={{0,2},{1,3},{2,0},{3,1},{4,6},{5,7},{6,4},{7,5},{8,10},{9,11},{10,... | collective-permute-start | bytes 2211848 | tf_op jit(solution)/shard_map/ppermute | solution.py:580
  32.8 25.4 %collective-permute-start.13 = (bf16[96,3840]{1,0:T(8,128)(2,1)S(1)}, bf16[96,3840]{1,0:T(8,128)(2,1)}, u32[]{:S(2)}, u32[]{:S(2)}) collective-permute-start(bf16[96,3840]{1,0:T(8,128)(2,1)S(1)} %pad_maximum_fusion.rest_0_), channel_id=1, source_target_pairs={{0,4},{1,5},{2,6},{3,7},{4,0},{5,1},{6,2},{7,3},{8,12},{9,13},{10,... | collective-permute-start | bytes 2211848 | tf_op jit(solution)/shard_map/ppermute | solution.py:580
  34.5 23.7 %collective-permute-start.16 = (bf16[96,3840]{1,0:T(8,128)(2,1)S(1)}, bf16[96,3840]{1,0:T(8,128)(2,1)}, u32[]{:S(2)}, u32[]{:S(2)}) collective-permute-start(bf16[96,3840]{1,0:T(8,128)(2,1)S(1)} %pad_maximum_fusion.rest_0_), channel_id=1, source_target_pairs={{0,1},{1,0},{2,3},{3,2},{4,5},{5,4},{6,7},{7,6},{8,9},{9,8},{10,11... | collective-permute-start | bytes 2211848 | tf_op jit(solution)/shard_map/ppermute | solution.py:580
  35.7 43.7 %copy-start.13 = (bf16[384,768]{1,0:T(8,128)(2,1)}, bf16[384,768]{1,0:T(8,128)(2,1)S(1)}, u32[]{:S(2)}) copy-start(bf16[384,768]{1,0:T(8,128)(2,1)S(1)} %collective-permute-done.21.rest_1_) | copy-start | bytes 1769476
  35.7 19.5 %collective-permute-start.5 = (bf16[48,2304]{1,0:T(8,128)(2,1)S(1)}, bf16[48,2304]{1,0:T(8,128)(2,1)}, u32[]{:S(2)}, u32[]{:S(2)}) collective-permute-start(bf16[48,2304]{1,0:T(8,128)(2,1)S(1)} %slice.278), channel_id=1, source_target_pairs={{0,4},{1,5},{2,6},{3,7},{4,0},{5,1},{6,2},{7,3},{8,12},{9,13},{10,... | collective-permute-start | bytes 663560 | tf_op jit(solution)/shard_map/ppermute | solution.py:580
  36.1 19.1 %collective-permute-start.6 = (bf16[48,2304]{1,0:T(8,128)(2,1)S(1)}, bf16[48,2304]{1,0:T(8,128)(2,1)S(1)}, u32[]{:S(2)}, u32[]{:S(2)}) collective-permute-start(bf16[48,2304]{1,0:T(8,128)(2,1)S(1)} %slice.279), channel_id=1, source_target_pairs={{0,2},{1,3},{2,0},{3,1},{4,6},{5,7},{6,4},{7,5},{8,10},{9,11},{10,... | collective-permute-start | bytes 663560 | tf_op jit(solution)/shard_map/ppermute | solution.py:580
  55.2 3.6 collective-permute-start.8
  55.8 3.0 collective-permute-start.9
  56.7 10.0 %collective-permute-start.23 = (bf16[192,768]{1,0:T(8,128)(2,1)S(1)}, bf16[192,768]{1,0:T(8,128)(2,1)}, u32[]{:S(2)}, u32[]{:S(2)}) collective-permute-start(bf16[192,768]{1,0:T(8,128)(2,1)S(1)} %slice.284), channel_id=1, source_target_pairs={{0,4},{1,5},{2,6},{3,7},{4,0},{5,1},{6,2},{7,3},{8,12},{9,13},{10,... | collective-permute-start | bytes 884744 | tf_op jit(solution)/shard_map/ppermute | solution.py:580
  58.2 3.7 %collective-permute-start.10 = (bf16[48,2304]{1,0:T(8,128)(2,1)}, bf16[48,2304]{1,0:T(8,128)(2,1)S(1)}, u32[]{:S(2)}, u32[]{:S(2)}) collective-permute-start(bf16[48,2304]{1,0:T(8,128)(2,1)} %collective-permute-done.5.rest_3_), channel_id=1, source_target_pairs={{0,1},{1,0},{2,3},{3,2},{4,5},{5,4},{6,7},{7,6},{8,9},{9,8},{10,11... | collective-permute-start | bytes 663560 | tf_op jit(solution)/shard_map/ppermute | solution.py:580
  58.2 4.4 %collective-permute-start.11 = (bf16[48,2304]{1,0:T(8,128)(2,1)}, bf16[48,2304]{1,0:T(8,128)(2,1)S(1)}, u32[]{:S(2)}, u32[]{:S(2)}) collective-permute-start(bf16[48,2304]{1,0:T(8,128)(2,1)} %copy-done.33), channel_id=1, source_target_pairs={{0,1},{1,0},{2,3},{3,2},{4,5},{5,4},{6,7},{7,6},{8,9},{9,8},{10,11... | collective-permute-start | bytes 663560 | tf_op jit(solution)/shard_map/ppermute | solution.py:580
  58.7 21.2 %collective-permute-start.17 = (bf16[96,3840]{1,0:T(8,128)(2,1)}, bf16[96,3840]{1,0:T(8,128)(2,1)}, u32[]{:S(2)}, u32[]{:S(2)}) collective-permute-start(bf16[96,3840]{1,0:T(8,128)(2,1)} %collective-permute-done.12.rest_1_), channel_id=1, source_target_pairs={{0,1},{1,0},{2,3},{3,2},{4,5},{5,4},{6,7},{7,6},{8,9},{9,8},{10,11... | collective-permute-start | bytes 2211848 | tf_op jit(solution)/shard_map/ppermute | solution.py:580
  58.8 21.6 %collective-permute-start.18 = (bf16[96,3840]{1,0:T(8,128)(2,1)}, bf16[96,3840]{1,0:T(8,128)(2,1)}, u32[]{:S(2)}, u32[]{:S(2)}) collective-permute-start(bf16[96,3840]{1,0:T(8,128)(2,1)} %collective-permute-done.13.rest_2_), channel_id=1, source_target_pairs={{0,1},{1,0},{2,3},{3,2},{4,5},{5,4},{6,7},{7,6},{8,9},{9,8},{10,11... | collective-permute-start | bytes 2211848 | tf_op jit(solution)/shard_map/ppermute | solution.py:580
  61.9 17.4 %collective-permute-start.14 = (bf16[48,3840]{1,0:T(8,128)(2,1)S(1)}, bf16[48,3840]{1,0:T(8,128)(2,1)}, u32[]{:S(2)}, u32[]{:S(2)}) collective-permute-start(bf16[48,3840]{1,0:T(8,128)(2,1)S(1)} %slice.282), channel_id=1, source_target_pairs={{0,4},{1,5},{2,6},{3,7},{4,0},{5,1},{6,2},{7,3},{8,12},{9,13},{10,... | collective-permute-start | bytes 1105928 | tf_op jit(solution)/shard_map/ppermute | solution.py:580
  62.7 17.2 %collective-permute-start.15 = (bf16[48,3840]{1,0:T(8,128)(2,1)S(1)}, bf16[48,3840]{1,0:T(8,128)(2,1)}, u32[]{:S(2)}, u32[]{:S(2)}) collective-permute-start(bf16[48,3840]{1,0:T(8,128)(2,1)S(1)} %slice.283), channel_id=1, source_target_pairs={{0,2},{1,3},{2,0},{3,1},{4,6},{5,7},{6,4},{7,5},{8,10},{9,11},{10,... | collective-permute-start | bytes 1105928 | tf_op jit(solution)/shard_map/ppermute | solution.py:580
  66.8 12.6 %collective-permute-start.24 = (bf16[192,768]{1,0:T(8,128)(2,1)S(1)}, bf16[192,768]{1,0:T(8,128)(2,1)S(1)}, u32[]{:S(2)}, u32[]{:S(2)}) collective-permute-start(bf16[192,768]{1,0:T(8,128)(2,1)S(1)} %slice.285), channel_id=1, source_target_pairs={{0,2},{1,3},{2,0},{3,1},{4,6},{5,7},{6,4},{7,5},{8,10},{9,11},{10,... | collective-permute-start | bytes 884744 | tf_op jit(solution)/shard_map/ppermute | solution.py:580
  79.4 31.1 %collective-permute-start.25 = (bf16[384,768]{1,0:T(8,128)(2,1)S(1)}, bf16[384,768]{1,0:T(8,128)(2,1)S(1)}, u32[]{:S(2)}, u32[]{:S(2)}) collective-permute-start(bf16[384,768]{1,0:T(8,128)(2,1)S(1)} %convert_element_type.351.rest_0_), channel_id=1, source_target_pairs={{0,1},{1,0},{2,3},{3,2},{4,5},{5,4},{6,7},{7,6},{8,9},{9,8},{10,11... | collective-permute-start | bytes 1769480 | tf_op jit(solution)/shard_map/ppermute | solution.py:580
  79.4 31.1 %collective-permute-start.26 = (bf16[384,768]{1,0:T(8,128)(2,1)S(1)}, bf16[384,768]{1,0:T(8,128)(2,1)S(1)}, u32[]{:S(2)}, u32[]{:S(2)}) collective-permute-start(bf16[384,768]{1,0:T(8,128)(2,1)S(1)} %collective-permute-done.21.rest_1_), channel_id=1, source_target_pairs={{0,1},{1,0},{2,3},{3,2},{4,5},{5,4},{6,7},{7,6},{8,9},{9,8},{10,11... | collective-permute-start | bytes 1769480 | tf_op jit(solution)/shard_map/ppermute | solution.py:580
  79.9 30.6 %collective-permute-start.27 = (bf16[384,768]{1,0:T(8,128)(2,1)S(1)}, bf16[384,768]{1,0:T(8,128)(2,1)S(1)}, u32[]{:S(2)}, u32[]{:S(2)}) collective-permute-start(bf16[384,768]{1,0:T(8,128)(2,1)S(1)} %copy-done.15), channel_id=1, source_target_pairs={{0,1},{1,0},{2,3},{3,2},{4,5},{5,4},{6,7},{7,6},{8,9},{9,8},{10,11... | collective-permute-start | bytes 1769480 | tf_op jit(solution)/shard_map/ppermute | solution.py:580
  80.0 12.3 %collective-permute-start.19 = (bf16[48,3840]{1,0:T(8,128)(2,1)}, bf16[48,3840]{1,0:T(8,128)(2,1)S(1)}, u32[]{:S(2)}, u32[]{:S(2)}) collective-permute-start(bf16[48,3840]{1,0:T(8,128)(2,1)} %collective-permute-done.14.rest_3_), channel_id=1, source_target_pairs={{0,1},{1,0},{2,3},{3,2},{4,5},{5,4},{6,7},{7,6},{8,9},{9,8},{10,11... | collective-permute-start | bytes 1105928 | tf_op jit(solution)/shard_map/ppermute | solution.py:580
  80.4 12.3 %collective-permute-start.20 = (bf16[48,3840]{1,0:T(8,128)(2,1)}, bf16[48,3840]{1,0:T(8,128)(2,1)S(1)}, u32[]{:S(2)}, u32[]{:S(2)}) collective-permute-start(bf16[48,3840]{1,0:T(8,128)(2,1)} %collective-permute-done.15.rest_4_), channel_id=1, source_target_pairs={{0,1},{1,0},{2,3},{3,2},{4,5},{5,4},{6,7},{7,6},{8,9},{9,8},{10,11... | collective-permute-start | bytes 1105928 | tf_op jit(solution)/shard_map/ppermute | solution.py:580
  92.2 18.3 %collective-permute-start.28 = (bf16[192,768]{1,0:T(8,128)(2,1)}, bf16[192,768]{1,0:T(8,128)(2,1)S(1)}, u32[]{:S(2)}, u32[]{:S(2)}) collective-permute-start(bf16[192,768]{1,0:T(8,128)(2,1)} %collective-permute-done.23.rest_3_), channel_id=1, source_target_pairs={{0,1},{1,0},{2,3},{3,2},{4,5},{5,4},{6,7},{7,6},{8,9},{9,8},{10,11... | collective-permute-start | bytes 884744 | tf_op jit(solution)/shard_map/ppermute | solution.py:580
  92.7 17.8 %collective-permute-start.29 = (bf16[192,768]{1,0:T(8,128)(2,1)S(1)}, bf16[192,768]{1,0:T(8,128)(2,1)S(1)}, u32[]{:S(2)}, u32[]{:S(2)}) collective-permute-start(bf16[192,768]{1,0:T(8,128)(2,1)S(1)} %collective-permute-done.24.rest_4_), channel_id=1, source_target_pairs={{0,1},{1,0},{2,3},{3,2},{4,5},{5,4},{6,7},{7,6},{8,9},{9,8},{10,11... | collective-permute-start | bytes 884744 | tf_op jit(solution)/shard_map/ppermute | solution.py:580
  182.1 55.8 %collective-permute-start.30 = (bf16[4,96,2304]{2,1,0:T(8,128)(2,1)}, bf16[4,96,2304]{2,1,0:T(8,128)(2,1)}, u32[]{:S(2)}, u32[]{:S(2)}) collective-permute-start(bf16[4,96,2304]{2,1,0:T(8,128)(2,1)} %get-tuple-element.61), channel_id=1, source_target_pairs={{0,1},{1,0},{2,3},{3,2},{4,5},{5,4},{6,7},{7,6},{8,9},{9,8},{10,11... | collective-permute-start | bytes 5308424 | tf_op jit(solution)/shard_map/ppermute | solution.py:580
  198.6 59.2 %collective-permute-start.38 = (bf16[4,96,3840]{2,1,0:T(8,128)(2,1)}, bf16[4,96,3840]{2,1,0:T(8,128)(2,1)S(1)}, u32[]{:S(2)}, u32[]{:S(2)}) collective-permute-start(bf16[4,96,3840]{2,1,0:T(8,128)(2,1)} %get-tuple-element.65), channel_id=1, source_target_pairs={{0,1},{1,0},{2,3},{3,2},{4,5},{5,4},{6,7},{7,6},{8,9},{9,8},{10,11... | collective-permute-start | bytes 8847368 | tf_op jit(solution)/shard_map/ppermute | solution.py:580
  201.1 11.9 %collective-permute-start.54 = (f32[12,768]{1,0:T(8,128)S(1)}, f32[12,768]{1,0:T(8,128)S(1)}, u32[]{:S(2)}, u32[]{:S(2)}) collective-permute-start(f32[12,768]{1,0:T(8,128)S(1)} %pad_maximum_fusion.4), channel_id=1, source_target_pairs={{0,1},{1,0},{2,3},{3,2},{4,5},{5,4},{6,7},{7,6},{8,9},{9,8},{10,11... | collective-permute-start | bytes 110600 | tf_op jit(solution)/shard_map/ppermute | solution.py:580
  212.5 41.2 %collective-permute-start.46 = (bf16[4,384,768]{2,1,0:T(8,128)(2,1)}, bf16[4,384,768]{2,1,0:T(8,128)(2,1)}, u32[]{:S(2)}, u32[]{:S(2)}) collective-permute-start(bf16[4,384,768]{2,1,0:T(8,128)(2,1)} %get-tuple-element.67), channel_id=1, source_target_pairs={{0,1},{1,0},{2,3},{3,2},{4,5},{5,4},{6,7},{7,6},{8,9},{9,8},{10,11... | collective-permute-start | bytes 7077896 | tf_op jit(solution)/shard_map/ppermute | solution.py:580
  213.0 4.2 %collective-permute-start.55 = (f32[12,768]{1,0:T(8,128)S(1)}, f32[12,768]{1,0:T(8,128)S(1)}, u32[]{:S(2)}, u32[]{:S(2)}) collective-permute-start(f32[12,768]{1,0:T(8,128)S(1)} %fusion.19), channel_id=1, source_target_pairs={{0,2},{1,3},{2,0},{3,1},{4,6},{5,7},{6,4},{7,5},{8,10},{9,11},{10,... | collective-permute-start | bytes 110600 | tf_op jit(solution)/shard_map/ppermute | solution.py:580
  217.2 4.2 %collective-permute-start.56 = (f32[12,768]{1,0:T(8,128)S(1)}, f32[12,768]{1,0:T(8,128)S(1)}, u32[]{:S(2)}, u32[]{:S(2)}) collective-permute-start(f32[12,768]{1,0:T(8,128)S(1)} %add.286), channel_id=1, source_target_pairs={{0,4},{1,5},{2,6},{3,7},{4,0},{5,1},{6,2},{7,3},{8,12},{9,13},{10,... | collective-permute-start | bytes 110600 | tf_op jit(solution)/shard_map/ppermute | solution.py:580
  221.3 4.2 %collective-permute-start.57 = (f32[12,768]{1,0:T(8,128)S(1)}, f32[12,768]{1,0:T(8,128)S(1)}, u32[]{:S(2)}, u32[]{:S(2)}) collective-permute-start(f32[12,768]{1,0:T(8,128)S(1)} %add.287), channel_id=1, source_target_pairs={{0,8},{8,0},{16,24},{24,16},{1,9},{9,1},{17,25},{25,17},{2,10},{10... | collective-permute-start | bytes 110600 | tf_op jit(solution)/shard_map/ppermute | solution.py:719
  225.5 12.4 %collective-permute-start.58 = (f32[12,768]{1,0:T(8,128)S(1)}, f32[12,768]{1,0:T(8,128)S(1)}, u32[]{:S(2)}, u32[]{:S(2)}) collective-permute-start(f32[12,768]{1,0:T(8,128)S(1)} %add.288), channel_id=1, source_target_pairs={{0,16},{8,24},{16,0},{24,8},{1,17},{9,25},{17,1},{25,9},{2,18},{10... | collective-permute-start | bytes 110600 | tf_op jit(solution)/shard_map/ppermute | solution.py:719
  239.8 8.4 %collective-permute-start.31 = (bf16[2,48,2304]{2,1,0:T(8,128)(2,1)S(1)}, bf16[2,48,2304]{2,1,0:T(8,128)(2,1)S(1)}, u32[]{:S(2)}, u32[]{:S(2)}) collective-permute-start(bf16[2,48,2304]{2,1,0:T(8,128)(2,1)S(1)} %get-tuple-element.110), channel_id=1, source_target_pairs={{0,2},{1,3},{2,0},{3,1},{4,6},{5,7},{6,4},{7,5},{8,10},{9,11},{10,... | collective-permute-start | bytes 1327112 | tf_op jit(solution)/shard_map/ppermute | solution.py:580
  241.3 9.2 %collective-permute-start.33 = (bf16[2,48,2304]{2,1,0:T(8,128)(2,1)S(1)}, bf16[2,48,2304]{2,1,0:T(8,128)(2,1)S(1)}, u32[]{:S(2)}, u32[]{:S(2)}) collective-permute-start(bf16[2,48,2304]{2,1,0:T(8,128)(2,1)S(1)} %get-tuple-element.111), channel_id=1, source_target_pairs={{0,4},{1,5},{2,6},{3,7},{4,0},{5,1},{6,2},{7,3},{8,12},{9,13},{10,... | collective-permute-start | bytes 1327112 | tf_op jit(solution)/shard_map/ppermute | solution.py:580
  251.9 8.4 %collective-permute-start.32 = (bf16[48,2304]{1,0:T(8,128)(2,1)S(1)}, bf16[48,2304]{1,0:T(8,128)(2,1)S(1)}, u32[]{:S(2)}, u32[]{:S(2)}) collective-permute-start(bf16[48,2304]{1,0:T(8,128)(2,1)S(1)} %get-tuple-element.108), channel_id=1, source_target_pairs={{0,4},{1,5},{2,6},{3,7},{4,0},{5,1},{6,2},{7,3},{8,12},{9,13},{10,... | collective-permute-start | bytes 663560 | tf_op jit(solution)/shard_map/ppermute | solution.py:580
  253.3 8.4 %collective-permute-start.34 = (bf16[48,2304]{1,0:T(8,128)(2,1)S(1)}, bf16[48,2304]{1,0:T(8,128)(2,1)S(1)}, u32[]{:S(2)}, u32[]{:S(2)}) collective-permute-start(bf16[48,2304]{1,0:T(8,128)(2,1)S(1)} %get-tuple-element.109), channel_id=1, source_target_pairs={{0,2},{1,3},{2,0},{3,1},{4,6},{5,7},{6,4},{7,5},{8,10},{9,11},{10,... | collective-permute-start | bytes 663560 | tf_op jit(solution)/shard_map/ppermute | solution.py:580
  255.5 18.8 %collective-permute-start.47 = (bf16[2,192,768]{2,1,0:T(8,128)(2,1)S(1)}, bf16[2,192,768]{2,1,0:T(8,128)(2,1)S(1)}, u32[]{:S(2)}, u32[]{:S(2)}) collective-permute-start(bf16[2,192,768]{2,1,0:T(8,128)(2,1)S(1)} %get-tuple-element.104), channel_id=1, source_target_pairs={{0,2},{1,3},{2,0},{3,1},{4,6},{5,7},{6,4},{7,5},{8,10},{9,11},{10,... | collective-permute-start | bytes 1769480 | tf_op jit(solution)/shard_map/ppermute | solution.py:580
  257.1 17.2 %collective-permute-start.49 = (bf16[2,192,768]{2,1,0:T(8,128)(2,1)S(1)}, bf16[2,192,768]{2,1,0:T(8,128)(2,1)S(1)}, u32[]{:S(2)}, u32[]{:S(2)}) collective-permute-start(bf16[2,192,768]{2,1,0:T(8,128)(2,1)S(1)} %get-tuple-element.105), channel_id=1, source_target_pairs={{0,4},{1,5},{2,6},{3,7},{4,0},{5,1},{6,2},{7,3},{8,12},{9,13},{10,... | collective-permute-start | bytes 1769480 | tf_op jit(solution)/shard_map/ppermute | solution.py:580
  258.2 31.8 %collective-permute-start.39 = (bf16[2,48,3840]{2,1,0:T(8,128)(2,1)S(1)}, bf16[2,48,3840]{2,1,0:T(8,128)(2,1)S(1)}, u32[]{:S(2)}, u32[]{:S(2)}) collective-permute-start(bf16[2,48,3840]{2,1,0:T(8,128)(2,1)S(1)} %get-tuple-element.98), channel_id=1, source_target_pairs={{0,2},{1,3},{2,0},{3,1},{4,6},{5,7},{6,4},{7,5},{8,10},{9,11},{10,... | collective-permute-start | bytes 2211848 | tf_op jit(solution)/shard_map/ppermute | solution.py:580
  260.3 29.7 %collective-permute-start.41 = (bf16[2,48,3840]{2,1,0:T(8,128)(2,1)S(1)}, bf16[2,48,3840]{2,1,0:T(8,128)(2,1)S(1)}, u32[]{:S(2)}, u32[]{:S(2)}) collective-permute-start(bf16[2,48,3840]{2,1,0:T(8,128)(2,1)S(1)} %get-tuple-element.99), channel_id=1, source_target_pairs={{0,4},{1,5},{2,6},{3,7},{4,0},{5,1},{6,2},{7,3},{8,12},{9,13},{10,... | collective-permute-start | bytes 2211848 | tf_op jit(solution)/shard_map/ppermute | solution.py:580
  263.2 38.8 %collective-permute-start.35 = (bf16[96,2304]{1,0:T(8,128)(2,1)S(1)}, bf16[96,2304]{1,0:T(8,128)(2,1)S(1)}, u32[]{:S(2)}, u32[]{:S(2)}) collective-permute-start(bf16[96,2304]{1,0:T(8,128)(2,1)S(1)} %pad_maximum_fusion.3), channel_id=1, source_target_pairs={{0,8},{24,16},{1,9},{25,17},{2,10},{26,18},{3,11},{27,19},{4,12},{... | collective-permute-start | bytes 1327112 | tf_op jit(solution)/shard_map/ppermute | solution.py:627
  275.6 18.5 %collective-permute-start.48 = (bf16[192,768]{1,0:T(8,128)(2,1)S(1)}, bf16[192,768]{1,0:T(8,128)(2,1)S(1)}, u32[]{:S(2)}, u32[]{:S(2)}) collective-permute-start(bf16[192,768]{1,0:T(8,128)(2,1)S(1)} %get-tuple-element.102), channel_id=1, source_target_pairs={{0,4},{1,5},{2,6},{3,7},{4,0},{5,1},{6,2},{7,3},{8,12},{9,13},{10,... | collective-permute-start | bytes 884744 | tf_op jit(solution)/shard_map/ppermute | solution.py:580
  276.4 17.7 %collective-permute-start.50 = (bf16[192,768]{1,0:T(8,128)(2,1)S(1)}, bf16[192,768]{1,0:T(8,128)(2,1)S(1)}, u32[]{:S(2)}, u32[]{:S(2)}) collective-permute-start(bf16[192,768]{1,0:T(8,128)(2,1)S(1)} %get-tuple-element.103), channel_id=1, source_target_pairs={{0,2},{1,3},{2,0},{3,1},{4,6},{5,7},{6,4},{7,5},{8,10},{9,11},{10,... | collective-permute-start | bytes 884744 | tf_op jit(solution)/shard_map/ppermute | solution.py:580
  290.3 8.7 %collective-permute-start.40 = (bf16[48,3840]{1,0:T(8,128)(2,1)S(1)}, bf16[48,3840]{1,0:T(8,128)(2,1)S(1)}, u32[]{:S(2)}, u32[]{:S(2)}) collective-permute-start(bf16[48,3840]{1,0:T(8,128)(2,1)S(1)} %get-tuple-element.96), channel_id=1, source_target_pairs={{0,4},{1,5},{2,6},{3,7},{4,0},{5,1},{6,2},{7,3},{8,12},{9,13},{10,... | collective-permute-start | bytes 1105928 | tf_op jit(solution)/shard_map/ppermute | solution.py:580
  290.6 8.3 %collective-permute-start.42 = (bf16[48,3840]{1,0:T(8,128)(2,1)S(1)}, bf16[48,3840]{1,0:T(8,128)(2,1)S(1)}, u32[]{:S(2)}, u32[]{:S(2)}) collective-permute-start(bf16[48,3840]{1,0:T(8,128)(2,1)S(1)} %get-tuple-element.97), channel_id=1, source_target_pairs={{0,2},{1,3},{2,0},{3,1},{4,6},{5,7},{6,4},{7,5},{8,10},{9,11},{10,... | collective-permute-start | bytes 1105928 | tf_op jit(solution)/shard_map/ppermute | solution.py:580
  295.5 16.0 %collective-permute-start.51 = (bf16[384,768]{1,0:T(8,128)(2,1)S(1)}, bf16[384,768]{1,0:T(8,128)(2,1)S(1)}, u32[]{:S(2)}, u32[]{:S(2)}) collective-permute-start(bf16[384,768]{1,0:T(8,128)(2,1)S(1)} %pad_maximum_fusion.2), channel_id=1, source_target_pairs={{0,8},{24,16},{1,9},{25,17},{2,10},{26,18},{3,11},{27,19},{4,12},{... | collective-permute-start | bytes 1769480 | tf_op jit(solution)/shard_map/ppermute | solution.py:627
  299.5 19.9 %collective-permute-start.43 = (bf16[96,3840]{1,0:T(8,128)(2,1)S(1)}, bf16[96,3840]{1,0:T(8,128)(2,1)S(1)}, u32[]{:S(2)}, u32[]{:S(2)}) collective-permute-start(bf16[96,3840]{1,0:T(8,128)(2,1)S(1)} %pad_maximum_fusion.1), channel_id=1, source_target_pairs={{0,8},{24,16},{1,9},{25,17},{2,10},{26,18},{3,11},{27,19},{4,12},{... | collective-permute-start | bytes 2211848 | tf_op jit(solution)/shard_map/ppermute | solution.py:627
  302.1 18.1 %collective-permute-start.36 = (bf16[96,2304]{1,0:T(8,128)(2,1)S(1)}, bf16[96,2304]{1,0:T(8,128)(2,1)S(1)}, u32[]{:S(2)}, u32[]{:S(2)}) collective-permute-start(bf16[96,2304]{1,0:T(8,128)(2,1)S(1)} %add_convert_fusion.9), channel_id=1, source_target_pairs={{8,16},{16,8},{9,17},{17,9},{10,18},{18,10},{11,19},{19,11},{12,20... | collective-permute-start | bytes 1327112 | tf_op jit(solution)/shard_map/ppermute | solution.py:628
  311.6 10.1 %collective-permute-start.52 = (bf16[384,768]{1,0:T(8,128)(2,1)S(1)}, bf16[384,768]{1,0:T(8,128)(2,1)S(1)}, u32[]{:S(2)}, u32[]{:S(2)}) collective-permute-start(bf16[384,768]{1,0:T(8,128)(2,1)S(1)} %add_convert_fusion.5), channel_id=1, source_target_pairs={{8,16},{16,8},{9,17},{17,9},{10,18},{18,10},{11,19},{19,11},{12,20... | collective-permute-start | bytes 1769480 | tf_op jit(solution)/shard_map/ppermute | solution.py:628
  319.5 3.6 collective-permute-start.44
  320.4 12.6 %collective-permute-start.37 = (bf16[96,2304]{1,0:T(8,128)(2,1)S(1)}, bf16[96,2304]{1,0:T(8,128)(2,1)S(1)}, u32[]{:S(2)}, u32[]{:S(2)}) collective-permute-start(bf16[96,2304]{1,0:T(8,128)(2,1)S(1)} %add_convert_fusion.8), channel_id=1, source_target_pairs={{8,0},{16,24},{9,1},{17,25},{10,2},{18,26},{11,3},{19,27},{12,4},{... | collective-permute-start | bytes 1327112 | tf_op jit(solution)/shard_map/ppermute | solution.py:629
  321.8 25.4 %collective-permute-start.53 = (bf16[384,768]{1,0:T(8,128)(2,1)S(1)}, bf16[384,768]{1,0:T(8,128)(2,1)S(1)}, u32[]{:S(2)}, u32[]{:S(2)}) collective-permute-start(bf16[384,768]{1,0:T(8,128)(2,1)S(1)} %add_convert_fusion.4), channel_id=1, source_target_pairs={{8,0},{16,24},{9,1},{17,25},{10,2},{18,26},{11,3},{19,27},{12,4},{... | collective-permute-start | bytes 1769480 | tf_op jit(solution)/shard_map/ppermute | solution.py:629
  323.1 24.1 %copy-start.5 = (f32[384,768]{1,0:T(8,128)S(1)}, f32[384,768]{1,0:T(8,128)}, u32[]{:S(2)}) copy-start(f32[384,768]{1,0:T(8,128)} %param.33) | copy-start | bytes 3538948
  323.3 32.4 %collective-permute-start.45 = (bf16[96,3840]{1,0:T(8,128)(2,1)S(1)}, bf16[96,3840]{1,0:T(8,128)(2,1)S(1)}, u32[]{:S(2)}, u32[]{:S(2)}) collective-permute-start(bf16[96,3840]{1,0:T(8,128)(2,1)S(1)} %add_convert_fusion), channel_id=1, source_target_pairs={{8,0},{16,24},{9,1},{17,25},{10,2},{18,26},{11,3},{19,27},{12,4},{... | collective-permute-start | bytes 2211848 | tf_op jit(solution)/shard_map/ppermute | solution.py:629
  (31 other events, 243.7 us)

commit v2 on v1

v2 whole, which is shorter than its diff:
```python
import functools

import jax
import jax.numpy as jnp
from jax import lax
from jax.experimental import pallas as pl
from jax.experimental.pallas import tpu as pltpu
from jax.sharding import PartitionSpec as P

D = 768
HEADS = 12
HDIM = 64
PART = D // 2
FF = 3072
SEQ = 128
STEP = 5

RANKS = 8
SHARD = D // RANKS
SHARD_FF = FF // RANKS

beta_one = 0.9
beta_two = 0.999
adam_epsilon = 1e-06
norm_epsilon = 1e-05
masked_score = -1000000000.0

bf16 = jnp.bfloat16
f32 = jnp.float32
NN = (((1,), (0,)), ((), ()))
NT = (((1,), (1,)), ((), ()))
TN = (((0,), (0,)), ((), ()))
VMEM_BYTES = 24 * 1024 * 1024
TILE = 256
LIGHT = 1000


def dot(left, right, dims):
    return lax.dot_general(left, right, dims, preferred_element_type=f32)


def call(kernel, grid, in_specs, out_specs, out_shape, scratch=(), flops=0, bytes_accessed=0, name=None):
    return pl.pallas_call(
        kernel,
        grid_spec=pltpu.PrefetchScalarGridSpec(
            num_scalar_prefetch=1,
            grid=grid,
            in_specs=in_specs,
            out_specs=out_specs,
            scratch_shapes=list(scratch),
        ),
        out_shape=out_shape,
        compiler_params=pltpu.CompilerParams(
            vmem_limit_bytes=VMEM_BYTES, dimension_semantics=("arbitrary",) * len(grid)
        ),
        cost_estimate=pl.CostEstimate(
            flops=int(flops) // LIGHT, bytes_accessed=int(bytes_accessed) // LIGHT, transcendentals=0
        ),
        name=name,
    )


def rows_of(width, tile=TILE):
    return pl.BlockSpec((tile, width), lambda i, s: (i, 0))


def whole(shape):
    return pl.BlockSpec(shape, lambda i, s: (0,) * len(shape))


ANY = pl.BlockSpec(memory_space=pl.ANY)


def in_hbm(array):
    return pltpu.with_memory_space_constraint(array, pltpu.HBM)


class Pieces:
    def __init__(self, arrays, places):
        self.arrays = [in_hbm(array) for array in arrays]
        self.places = places

    def __len__(self):
        return len(self.arrays)


def load_weight(pieces, me, refs, scratch, sem):
    copies = []
    for ref, place in zip(refs, pieces.places):
        if place is None:
            target = scratch
        else:
            mask, first, count = place
            target = scratch.at[me ^ mask, pl.ds(first, count)]
        copies.append(pltpu.make_async_copy(ref, target, sem))
    for copy in copies:
        copy.start()
    for copy in copies:
        copy.wait()


def load_halves(halves, me, refs, scratch, sem):
    rows = scratch.shape[1] // 2
    copies = []
    for number, pieces in enumerate(halves):
        for ref, place in zip(refs[number * len(pieces) :], pieces.places):
            at = pl.ds(number * rows, rows)
            if place is None:
                target = scratch.at[:, at]
            else:
                target = scratch.at[me ^ place[0], at]
            copies.append(pltpu.make_async_copy(ref, target, sem))
    for copy in copies:
        copy.start()
    for copy in copies:
        copy.wait()


def lane_sum(value):
    return jnp.sum(value, axis=-1, keepdims=True)


def normalize(residual):
    centre = residual - lane_sum(residual) * (1.0 / D)
    variance = lane_sum(centre * centre) * (1.0 / D)
    inv_std = lax.rsqrt(variance + norm_epsilon)
    return (centre * inv_std, inv_std)


def norm_back(grad_normed, normed, inv_std):
    first_mean = lane_sum(grad_normed) * (1.0 / D)
    second_mean = lane_sum(grad_normed * normed) * (1.0 / D)
    return inv_std * (grad_normed - first_mean - normed * second_mean)


def gelu_and_slope(pre_act):
    cumulative = 0.5 * (1.0 + lax.erf(pre_act * 0.7071067811865476))
    density = jnp.exp(-0.5 * pre_act * pre_act) * 0.3989422804014327
    return (pre_act * cumulative, cumulative + pre_act * density)


def project_qkv(me, tokens, weight, bias):
    rows = tokens.shape[0]
    count = len(weight)
    width = 3 * PART

    def kernel(s, x_ref, b_ref, *rest):
        refs, (out_ref, w_ref, sem) = rest[:count], rest[count:]

        @pl.when(pl.program_id(0) == 0)
        def _():
            load_weight(weight, s[0], refs, w_ref, sem)

        w = w_ref[...].reshape(D, width)
        out_ref[...] = (dot(x_ref[...], w, NN) + b_ref[...]).astype(bf16)

    return call(
        kernel,
        (rows // 512,),
        [rows_of(D, 512), whole((1, width))] + [ANY] * count,
        rows_of(width, 512),
        jax.ShapeDtypeStruct((rows, width), bf16),
        [pltpu.VMEM((RANKS, SHARD, width), bf16), pltpu.SemaphoreType.DMA],
        flops=2 * rows * D * width,
        bytes_accessed=2 * (rows * D * 4 + 3 * D * D),
        name="qkv",
    )(me, tokens, bias, *weight.arrays)


def head_masks():
    lane = lax.broadcasted_iota(jnp.int32, (SEQ, 2 * HDIM), 1)
    return lane < HDIM


def stack_heads(value, first):
    zero = jnp.zeros_like(value)
    return jnp.concatenate([jnp.where(first, value, zero), jnp.where(first, zero, value)], axis=0)


GROUP = 2


def attention(lengths, qkv):
    rows = qkv.shape[0]
    scale = HDIM ** (-0.5)
    wide = 2 * HDIM

    def kernel(s, qkv_ref, out_ref, p_ref):
        first = head_masks()
        for g in range(GROUP):
            at = slice(g * SEQ, (g + 1) * SEQ)
            length = s[pl.program_id(0) * GROUP + g]
            valid = lax.broadcasted_iota(jnp.int32, (SEQ, SEQ), 1) < length
            for h in range(PART // wide):
                lanes = slice(h * wide, (h + 1) * wide)
                q = qkv_ref[at, lanes]
                k = qkv_ref[at, PART + h * wide : PART + (h + 1) * wide]
                v = qkv_ref[at, 2 * PART + h * wide : 2 * PART + (h + 1) * wide]
                scores = dot(q, stack_heads(k, first), NT) * scale
                halves = []
                for part in range(2):
                    one = jnp.where(valid, scores[:, part * SEQ : (part + 1) * SEQ], masked_score)
                    top = jnp.max(one, axis=-1, keepdims=True)
                    raised = jnp.exp(one - top)
                    halves.append(raised / lane_sum(raised))
                weights = jnp.concatenate(halves, axis=1)
                p_ref[at, h * 2 * SEQ : (h + 1) * 2 * SEQ] = weights
                out_ref[at, lanes] = dot(weights.astype(bf16), stack_heads(v, first), NN).astype(bf16)

    width = HEADS * SEQ // 2
    return call(
        kernel,
        (rows // (GROUP * SEQ),),
        [rows_of(3 * PART, GROUP * SEQ)],
        [rows_of(PART, GROUP * SEQ), rows_of(width, GROUP * SEQ)],
        [jax.ShapeDtypeStruct((rows, PART), bf16), pltpu.HBM((rows, width), f32)],
        flops=4e9,
        bytes_accessed=rows * (PART * 8 + width * 4),
        name="attention",
    )(lengths, qkv)


def feed_in(me, attended, tokens, weight, vectors, in_bias):
    rows = tokens.shape[0]
    count = len(weight[0])
    total = 2 * count
    tile = 384
    width = (D + FF) // 2

    def kernel(s, o0_ref, o1_ref, x_ref, v_ref, b_ref, *rest):
        refs = rest[:total]
        n1_ref, inv_ref, hb_ref, f_ref, sl_ref, w0_ref, w1_ref, sem = rest[total:]

        @pl.when(pl.program_id(0) == 0)
        def _():
            load_weight(weight[0], s[0], refs[:count], w0_ref, sem)
            load_weight(weight[1], s[0], refs[count:], w1_ref, sem)

        w_proj = w0_ref[:, :, :D].reshape(D, D)
        branch = (
            dot(o0_ref[...], w_proj[:PART], NN) + dot(o1_ref[...], w_proj[PART:], NN) + v_ref[2:3, :]
        )
        normed, inv_std = normalize(x_ref[...].astype(f32) + branch)
        n1_ref[...] = normed
        inv_ref[...] = inv_std
        low = (normed * v_ref[3:4, :] + v_ref[4:5, :]).astype(bf16)
        hb_ref[...] = low
        for j, lead, end in IN_TILES:
            w = (w0_ref, w1_ref)[j][:, :, lead:end].reshape(D, end - lead)
            start = j * width + lead - D
            lanes = slice(start, start + end - lead)
            pre_act = dot(low, w, NN) + b_ref[:, lanes]
            act, slope = gelu_and_slope(pre_act)
            f_ref[:, lanes] = act.astype(bf16)
            sl_ref[:, lanes] = slope.astype(bf16)

    return call(
        kernel,
        (rows // TILE,),
        [rows_of(PART), rows_of(PART), rows_of(D), whole((8, D)), whole((1, FF))] + [ANY] * total,
        [rows_of(D), rows_of(1), rows_of(D), rows_of(FF), rows_of(FF)],
        [
            jax.ShapeDtypeStruct((rows, D), f32),
            jax.ShapeDtypeStruct((rows, 1), f32),
            jax.ShapeDtypeStruct((rows, D), bf16),
            jax.ShapeDtypeStruct((rows, FF), bf16),
            jax.ShapeDtypeStruct((rows, FF), bf16),
        ],
        [pltpu.VMEM((RANKS, SHARD, width), bf16)] * 2 + [pltpu.SemaphoreType.DMA],
        flops=2 * rows * D * (D + FF),
        bytes_accessed=rows * (D * 10 + FF * 4) + 2 * D * (D + FF),
        name="feed_in",
    )(me, *attended, tokens, vectors, in_bias, *weight[0].arrays, *weight[1].arrays)


IN_TILES = ((0, 768, 1280), (0, 1280, 1920), (1, 0, 512), (1, 512, 1024), (1, 1024, 1536), (1, 1536, 1920))


def feed_out(me, activated, normed_one, cotangent, weight, vectors):
    rows = activated.shape[0]
    count = len(weight[0])
    total = 2 * count

    def kernel(s, f_ref, n1_ref, g_ref, v_ref, *rest):
        refs = rest[:total]
        y_ref, dr_ref, dz_ref, sums_ref, w_ref, sem = rest[total:]

        @pl.when(pl.program_id(0) == 0)
        def _():
            load_halves(weight, s[0], refs, w_ref, sem)
            sums_ref[...] = jnp.zeros_like(sums_ref)

        branch = dot(f_ref[...], w_ref[...].reshape(FF, D), NN) + v_ref[5:6, :]
        hidden = n1_ref[...] * v_ref[3:4, :] + v_ref[4:5, :]
        normed, inv_std = normalize(hidden + branch)
        y_ref[...] = (normed * v_ref[6:7, :] + v_ref[7:8, :]).astype(bf16)
        grad_y = g_ref[...].astype(f32)
        sums_ref[1:2, :] += jnp.sum(grad_y * normed, axis=0, keepdims=True)
        sums_ref[2:3, :] += jnp.sum(grad_y, axis=0, keepdims=True)
        grad_res = norm_back(grad_y * v_ref[6:7, :], normed, inv_std)
        dr_ref[...] = grad_res
        low = grad_res.astype(bf16)
        dz_ref[...] = low
        sums_ref[0:1, :] += jnp.sum(low.astype(f32), axis=0, keepdims=True)

    return call(
        kernel,
        (rows // TILE,),
        [rows_of(FF), rows_of(D), rows_of(D), whole((8, D))] + [ANY] * total,
        [rows_of(D), rows_of(D), rows_of(D), whole((8, D))],
        [
            jax.ShapeDtypeStruct((rows, D), bf16),
            jax.ShapeDtypeStruct((rows, D), f32),
            jax.ShapeDtypeStruct((rows, D), bf16),
            jax.ShapeDtypeStruct((8, D), f32),
        ],
        [pltpu.VMEM((RANKS, SHARD_FF, D), bf16), pltpu.SemaphoreType.DMA],
        flops=2 * rows * D * FF,
        bytes_accessed=rows * (D * 14 + FF * 2) + 2 * D * FF,
        name="feed_out",
    )(me, activated, normed_one, cotangent, vectors, *weight[0].arrays, *weight[1].arrays)


def grad_w_out(me, activated, grad_ffn):
    rows = activated.shape[0]
    half = RANKS // 2

    def kernel(s, f_ref, dz_ref, t_ref, m_ref):
        block = dot(f_ref[...], dz_ref[...], TN).astype(bf16)
        low, high = block[:SHARD_FF], block[SHARD_FF:]
        even = (s[0] & 1) == 0
        m_ref[0] = jnp.where(even, low, high)
        t_ref[0] = jnp.where(even, high, low)

    shape = jax.ShapeDtypeStruct((half, SHARD_FF, D), bf16)
    out = pl.BlockSpec((1, SHARD_FF, D), lambda i, s: (i, 0, 0))
    return call(
        kernel,
        (half,),
        [
            pl.BlockSpec((rows, 2 * SHARD_FF), lambda i, s: (0, (s[0] >> 1) ^ i)),
            whole((rows, D)),
        ],
        [out, out],
        [shape, shape],
        flops=2 * rows * D * FF,
        bytes_accessed=rows * (D * 2 + FF * 2) + 2 * D * FF,
        name="grad_w_out",
    )(me, activated, grad_ffn)


def back_out(me, grad_ffn, slope, weight):
    rows = grad_ffn.shape[0]
    count = len(weight[0])
    total = 2 * count

    def kernel(s, dz_ref, sl_ref, *rest):
        refs = rest[:total]
        du_ref, sums_ref, w_ref, sem = rest[total:]

        @pl.when(pl.program_id(0) == 0)
        def _():
            load_halves(weight, s[0], refs, w_ref, sem)
            sums_ref[...] = jnp.zeros_like(sums_ref)

        dz = dz_ref[...]
        for r in range(RANKS // 2):
            lanes = slice(2 * r * SHARD_FF, 2 * (r + 1) * SHARD_FF)
            w = w_ref[2 * r : 2 * r + 2].reshape(2 * SHARD_FF, D)
            grad = dot(dz, w, NT) * sl_ref[:, lanes].astype(f32)
            low = grad.astype(bf16)
            du_ref[:, lanes] = low
            sums_ref[:, lanes] += jnp.sum(low.astype(f32), axis=0, keepdims=True)

    return call(
        kernel,
        (rows // TILE,),
        [rows_of(D), rows_of(FF)] + [ANY] * total,
        [rows_of(FF), whole((1, FF))],
        [jax.ShapeDtypeStruct((rows, FF), bf16), jax.ShapeDtypeStruct((1, FF), f32)],
        [pltpu.VMEM((RANKS, SHARD_FF, D), bf16), pltpu.SemaphoreType.DMA],
        flops=2 * rows * D * FF,
        bytes_accessed=rows * (D * 2 + FF * 4) + 2 * D * FF,
        name="back_out",
    )(me, grad_ffn, slope, *weight[0].arrays, *weight[1].arrays)


def back_in(me, grad_pre, grad_res_two, normed_one, inv_one, weight, vectors):
    rows = grad_pre.shape[0]
    count = len(weight[0])
    total = 2 * count
    width = (D + FF) // 2

    def kernel(s, du_ref, dr2_ref, n1_ref, inv_ref, v_ref, *rest):
        refs = rest[:total]
        dr1_ref, da_ref, do0_ref, do1_ref, sums_ref, w0_ref, w1_ref, sem = rest[total:]

        @pl.when(pl.program_id(0) == 0)
        def _():
            load_weight(weight[0], s[0], refs[:count], w0_ref, sem)
            load_weight(weight[1], s[0], refs[count:], w1_ref, sem)
            sums_ref[...] = jnp.zeros_like(sums_ref)

        cut = width - D
        grad_hidden = (
            dot(du_ref[:, :cut], w0_ref[:, :, D:].reshape(D, cut), NT)
            + dot(du_ref[:, cut:], w1_ref[...].reshape(D, width), NT)
            + dr2_ref[...]
        )
        normed = n1_ref[...]
        sums_ref[1:2, :] += jnp.sum(grad_hidden * normed, axis=0, keepdims=True)
        sums_ref[2:3, :] += jnp.sum(grad_hidden, axis=0, keepdims=True)
        grad_res = norm_back(grad_hidden * v_ref[3:4, :], normed, inv_ref[...])
        dr1_ref[...] = grad_res
        low = grad_res.astype(bf16)
        da_ref[...] = low
        sums_ref[0:1, :] += jnp.sum(low.astype(f32), axis=0, keepdims=True)
        w_proj = w0_ref[:, :, :D].reshape(D, D)
        grad_attended = dot(low, w_proj, NT).astype(bf16)
        do0_ref[...] = grad_attended[:, :PART]
        do1_ref[...] = grad_attended[:, PART:]

    return call(
        kernel,
        (rows // TILE,),
        [rows_of(FF), rows_of(D), rows_of(D), rows_of(1), whole((8, D))] + [ANY] * total,
        [rows_of(D), rows_of(D), rows_of(PART), rows_of(PART), whole((8, D))],
        [
            jax.ShapeDtypeStruct((rows, D), f32),
            jax.ShapeDtypeStruct((rows, D), bf16),
            jax.ShapeDtypeStruct((rows, PART), bf16),
            jax.ShapeDtypeStruct((rows, PART), bf16),
            jax.ShapeDtypeStruct((8, D), f32),
        ],
        [pltpu.VMEM((RANKS, SHARD, width), bf16)] * 2 + [pltpu.SemaphoreType.DMA],
        flops=2 * rows * D * (D + FF),
        bytes_accessed=rows * (D * 16 + FF * 2) + 2 * D * (D + FF),
        name="back_in",
    )(
        me,
        grad_pre,
        grad_res_two,
        normed_one,
        inv_one,
        vectors,
        *weight[0].arrays,
        *weight[1].arrays,
    )


def store_by_rank(s, block, t_ref, m_ref, first=0):
    even = (s[0] & 1) == 0
    chip = s[0] >> 1
    lanes = slice(first, first + block.shape[1])
    for k in range(RANKS // 2):
        low = block[2 * k * SHARD : (2 * k + 1) * SHARD]
        high = block[(2 * k + 1) * SHARD : (2 * k + 2) * SHARD]
        m_ref[chip ^ k, :, lanes] = jnp.where(even, low, high)
        t_ref[chip ^ k, :, lanes] = jnp.where(even, high, low)


def grad_w_in(me, hidden_low, grad_pre):
    rows = hidden_low.shape[0]
    half = RANKS // 2

    def kernel(s, h_ref, du_ref, t_ref, m_ref):
        store_by_rank(s, dot(h_ref[...], du_ref[...], TN).astype(bf16), t_ref, m_ref)

    shape = jax.ShapeDtypeStruct((half, SHARD, FF), bf16)
    out = pl.BlockSpec((half, SHARD, D), lambda i, s: (0, 0, i))
    return call(
        kernel,
        (FF // D,),
        [whole((rows, D)), pl.BlockSpec((rows, D), lambda i, s: (0, i))],
        [out, out],
        [shape, shape],
        flops=2 * rows * D * FF,
        bytes_accessed=rows * (D * 4 + FF * 2) + 2 * D * FF,
        name="grad_w_in",
    )(me, hidden_low, grad_pre)


def attention_back(lengths, qkv, weights, grad_attended):
    rows = qkv.shape[0]
    scale = HDIM ** (-0.5)
    wide = 2 * HDIM
    width = HEADS * SEQ // 2

    def kernel(s, qkv_ref, p_ref, do_ref, out_ref, sums_ref):
        @pl.when(pl.program_id(0) == 0)
        def _():
            sums_ref[...] = jnp.zeros_like(sums_ref)

        first = head_masks()
        for g in range(GROUP):
            at = slice(g * SEQ, (g + 1) * SEQ)
            for h in range(PART // wide):
                lanes = slice(h * wide, (h + 1) * wide)
                k_lanes = slice(PART + h * wide, PART + (h + 1) * wide)
                v_lanes = slice(2 * PART + h * wide, 2 * PART + (h + 1) * wide)
                q, k, v = qkv_ref[at, lanes], qkv_ref[at, k_lanes], qkv_ref[at, v_lanes]
                grad_out = do_ref[at, lanes]
                p = p_ref[at, h * 2 * SEQ : (h + 1) * 2 * SEQ]
                grad_p = dot(grad_out, stack_heads(v, first), NT)
                both = grad_p * p
                halves = []
                for part in range(2):
                    cut = slice(part * SEQ, (part + 1) * SEQ)
                    inner = grad_p[:, cut] - lane_sum(both[:, cut])
                    halves.append((p[:, cut] * inner).astype(bf16))
                grad_s = jnp.concatenate(halves, axis=1)
                grad_v = dot(p.astype(bf16), grad_out, TN)
                grad_v = jnp.where(first, grad_v[:SEQ], grad_v[SEQ:]).astype(bf16)
                grad_q = (dot(grad_s, stack_heads(k, first), NN) * scale).astype(bf16)
                grad_k = dot(grad_s, q, TN)
                grad_k = (jnp.where(first, grad_k[:SEQ], grad_k[SEQ:]) * scale).astype(bf16)
                out_ref[at, lanes] = grad_q
                out_ref[at, k_lanes] = grad_k
                out_ref[at, v_lanes] = grad_v
                sums_ref[0:1, lanes] += jnp.sum(grad_q.astype(f32), axis=0, keepdims=True)
                sums_ref[1:2, lanes] += jnp.sum(grad_v.astype(f32), axis=0, keepdims=True)

    return call(
        kernel,
        (rows // (GROUP * SEQ),),
        [rows_of(3 * PART, GROUP * SEQ), rows_of(width, GROUP * SEQ), rows_of(PART, GROUP * SEQ)],
        [rows_of(3 * PART, GROUP * SEQ), whole((8, PART))],
        [jax.ShapeDtypeStruct((rows, 3 * PART), bf16), jax.ShapeDtypeStruct((8, PART), f32)],
        flops=7e9,
        bytes_accessed=rows * (PART * 14 + width * 4),
        name="attention_back",
    )(lengths, qkv, in_hbm(weights), grad_attended)


def grad_w_qkv(me, tokens, grad_mixed):
    rows = tokens.shape[0]
    half = RANKS // 2
    width = 3 * PART

    def kernel(s, x_ref, g_ref, t_ref, m_ref):
        store_by_rank(s, dot(x_ref[...], g_ref[...], TN).astype(bf16), t_ref, m_ref)

    shape = jax.ShapeDtypeStruct((half, SHARD, width), bf16)
    out = whole((half, SHARD, width))
    return call(
        kernel,
        (1,),
        [whole((rows, D)), whole((rows, width))],
        [out, out],
        [shape, shape],
        flops=2 * rows * D * width,
        bytes_accessed=rows * (D * 8) + 2 * D * width,
        name="grad_w_qkv",
    )(me, tokens, grad_mixed)


def grad_w_mixed(me, tokens, grad_mixed, attended, grad_branch):
    rows = tokens.shape[0]
    half = RANKS // 2
    width = 3 * PART

    def kernel(s, x_ref, g_ref, o0_ref, o1_ref, da_ref, t_ref, m_ref):
        store_by_rank(s, dot(x_ref[...], g_ref[...], TN).astype(bf16), t_ref, m_ref)
        proj = jnp.concatenate(
            [
                dot(o0_ref[...], da_ref[...], TN).astype(bf16),
                dot(o1_ref[...], da_ref[...], TN).astype(bf16),
            ],
            axis=0,
        )
        store_by_rank(s, proj, t_ref, m_ref, width)

    shape = jax.ShapeDtypeStruct((half, SHARD, width + D), bf16)
    out = whole((half, SHARD, width + D))
    return call(
        kernel,
        (1,),
        [
            whole((rows, D)),
            whole((rows, width)),
            whole((rows, PART)),
            whole((rows, PART)),
            whole((rows, D)),
        ],
        [out, out],
        [shape, shape],
        flops=2 * rows * D * (width + D),
        bytes_accessed=rows * (D * 12) + 2 * D * (width + D),
        name="grad_w_mixed",
    )(me, tokens, grad_mixed, *attended, grad_branch)


def back_qkv(me, grad_mixed, grad_res_one, weight):
    rows = grad_res_one.shape[0]
    count = len(weight[0])
    total = 2 * count
    width = 3 * PART

    def kernel(s, g0_ref, g1_ref, dr_ref, *rest):
        refs = rest[:total]
        out_ref, w0_ref, w1_ref, sem = rest[total:]

        @pl.when(pl.program_id(0) == 0)
        def _():
            load_weight(weight[0], s[0], refs[:count], w0_ref, sem)
            load_weight(weight[1], s[0], refs[count:], w1_ref, sem)

        out_ref[...] = (
            dot(g0_ref[...], w0_ref[...].reshape(D, width), NT)
            + dot(g1_ref[...], w1_ref[...].reshape(D, width), NT)
            + dr_ref[...]
        ).astype(bf16)

    return call(
        kernel,
        (rows // TILE,),
        [rows_of(width), rows_of(width), rows_of(D)] + [ANY] * total,
        rows_of(D),
        jax.ShapeDtypeStruct((rows, D), bf16),
        [pltpu.VMEM((RANKS, SHARD, width), bf16)] * 2 + [pltpu.SemaphoreType.DMA],
        flops=2 * rows * D * 3 * D,
        bytes_accessed=rows * D * 12 + 2 * D * 3 * D,
        name="back_qkv",
    )(me, *grad_mixed, grad_res_one, *weight[0].arrays, *weight[1].arrays)


def adamw_math(moment, square, gradient):
    first_fix = 1.0 - beta_one**STEP
    second_fix = 1.0 - beta_two**STEP
    moment = beta_one * moment + (1.0 - beta_one) * gradient
    square = beta_two * square + (1.0 - beta_two) * gradient * gradient
    update = moment / first_fix / (jnp.sqrt(square / second_fix) + adam_epsilon)
    return (update, moment, square)


def adamw(moment, square, gradient):
    gradient = gradient.astype(f32)
    return (gradient,) + adamw_math(moment, square, gradient)


def flip(bit):
    return [(i, i ^ bit) for i in range(RANKS)]


def swap(value, bit):
    return lax.ppermute(value, "fsdp", flip(bit))


def after(value, *others):
    return lax.optimization_barrier((value,) + others)[0]


class Gather:
    def __init__(self, shard, turn):
        self.shard, self.turn = shard, turn

    def start(self, *others):
        self.shard = after(self.shard, *others) if others else self.shard
        self.x = swap(self.shard, 2)
        self.y = swap(self.shard, 4)
        return self

    def forward(self, *others):
        self.x, self.y = lax.optimization_barrier((self.x, self.y) + others)[:2]
        self.far = swap(self.x if self.turn == 4 else self.y, self.turn)
        return self

    def cross(self):
        self.mine = [self.shard, self.x, self.y, self.far]
        self.other = [swap(piece, 1) for piece in self.mine]
        return self

    def pieces(self):
        rows = self.shard.shape[0]
        masks = (0, 2, 4, 6)
        return Pieces(
            self.mine + self.other,
            [(m, 0, rows) for m in masks] + [(m ^ 1, 0, rows) for m in masks],
        )


def low_sum(*values):
    total = values[0].astype(f32)
    for value in values[1:]:
        total = total + value.astype(f32)
    return total.astype(bf16)


class Scatter:
    def __init__(self, parts):
        self.theirs, self.mine = parts
        self.half = self.mine.shape[1] // 2
        self.got = swap(self.theirs, 1)

    def one(self, *others):
        half, mine = self.half, self.mine
        self.got = after(self.got, *others)
        self.send_x = low_sum(mine[1::2, :half], self.got[1::2, :half])
        self.send_y = low_sum(mine[2:, half:], self.got[2:, half:])
        self.got_x = swap(self.send_x, 2)
        self.got_y = swap(self.send_y, 4)
        return self.send_x, self.send_y

    def two(self, *others):
        half, mine, got = self.half, self.mine, self.got
        self.got_x, self.got_y = lax.optimization_barrier((self.got_x, self.got_y) + others)[:2]
        send_y = low_sum(mine[2, :half], got[2, :half], self.got_x[1])
        send_x = low_sum(mine[1, half:], got[1, half:], self.got_y[1])
        self.last_y = swap(send_y, 4)
        self.last_x = swap(send_x, 2)
        return send_x, send_y

    def three(self, *others):
        half, mine, got = self.half, self.mine, self.got
        self.last_x, self.last_y = lax.optimization_barrier((self.last_x, self.last_y) + others)[:2]
        self.owned = jnp.concatenate(
            [
                low_sum(mine[0, :half], got[0, :half], self.got_x[0], self.last_y),
                low_sum(mine[0, half:], got[0, half:], self.got_y[0], self.last_x),
            ],
            axis=0,
        )
        self.near = lax.ppermute(self.owned, "rep", [(0, 1), (3, 2)])
        return (self.owned,)

    def four(self, *others):
        self.near = low_sum(self.owned, after(self.near, *others))
        self.across = lax.ppermute(self.near, "rep", [(1, 2), (2, 1)])
        return (self.near,)

    def five(self, *others):
        self.total = low_sum(self.near, after(self.across, *others))
        self.back = lax.ppermute(self.total, "rep", [(1, 0), (2, 3)])
        return (self.total,)

    def result(self, rep_index):
        inner = (rep_index == 1) | (rep_index == 2)
        return jnp.where(inner, self.total, self.back)


def gather_small(value, me, position, *others):
    got = after(swap(value, 1 << position), *others)
    low_first = ((me >> position) & 1) == 0
    return jnp.where(low_first, jnp.concatenate([value, got]), jnp.concatenate([got, value]))


def by_head_half(value, half):
    return [value[:, k * D + half * PART : k * D + (half + 1) * PART] for k in range(3)]


def local(
    fsdp,
    rep,
    tokens,
    cotangent,
    lengths,
    w_attn,
    w_in,
    w_out,
    b_in,
    vecs,
    m_attn,
    m_in,
    m_out,
    m_bin,
    m_vecs,
    v_attn,
    v_in,
    v_out,
    v_bin,
    v_vecs,
):
    direct = fsdp == RANKS and rep == 4
    position = lax.axis_index("fsdp")
    rep_index = lax.axis_index("rep")
    part = D // fsdp
    cut = (FF - D) // 2
    low_a = [jnp.concatenate(by_head_half(w_attn, h), axis=1).astype(bf16) for h in range(2)]
    low_b = [
        jnp.concatenate([w_attn[:, 3 * D :], w_in[:, :cut]], axis=1).astype(bf16),
        w_in[:, cut:].astype(bf16),
    ]
    middle = w_out.shape[0] // 2
    low_c = [w_out[:middle].astype(bf16), w_out[middle:].astype(bf16)]
    small = jnp.concatenate([vecs.reshape(1, -1), b_in.reshape(1, -1)], axis=1).astype(bf16)
    if direct:
        me = position.reshape(1)
        a = [Gather(low, turn) for low, turn in zip(low_a, (4, 2))]
        b = [Gather(low, turn) for low, turn in zip(low_b, (4, 2))]
        c = [Gather(low, turn) for low, turn in zip(low_c, (4, 2))]
        a[0].start()
        small_all = gather_small(small, position, 0, a[0].x, a[0].y)
        a[0].forward()
        a[1].start(a[0].x, a[0].y)
        small_all = gather_small(small_all, position, 1, a[0].far)
        a[0].cross()
        small_all = gather_small(small_all, position, 2, a[1].x, a[1].y)
        a[1].forward(a[0].far)
        for g in b:
            g.start(a[1].x, a[1].y)
        a[1].cross()
        pieces_a = [g.pieces() for g in a]
    else:
        me = jnp.zeros((1,), jnp.int32)

        def gather(shard):
            full = lax.all_gather(shard, "fsdp", axis=0, tiled=True)
            return Pieces([full.reshape(RANKS, -1, full.shape[1])], [None])

        def gather_rows(shards):
            full = lax.all_gather(jnp.concatenate(shards, axis=0), "fsdp", axis=0, tiled=True)
            full = full.reshape(RANKS, 2, -1, full.shape[1])
            return [Pieces([full[:, h]], [None]) for h in range(2)]

        pieces_a = [gather(low) for low in low_a]
        pieces_b = [gather(low) for low in low_b]
        pieces_c = gather_rows(low_c)
        small_all = lax.all_gather(small, "fsdp", axis=0, tiled=True)
    small_all = small_all.astype(f32)
    vectors = small_all[:, : 8 * part].reshape(fsdp, 8, part).transpose(1, 0, 2).reshape(8, D)
    in_bias = small_all[:, 8 * part :].reshape(1, FF)
    bias = [
        jnp.concatenate(
            [
                vectors[0:1, h * PART : (h + 1) * PART],
                jnp.zeros((1, PART), f32),
                vectors[1:2, h * PART : (h + 1) * PART],
            ],
            axis=1,
        )
        for h in range(2)
    ]

    x = after(tokens, a[1].x, a[1].y) if direct else tokens
    qkv = [project_qkv(me, x, pieces_a[0], bias[0])]
    x = after(tokens, qkv[0])
    qkv.append(project_qkv(me, x, pieces_a[1], bias[1]))
    attended, weights = [None, None], [None, None]
    attended[0], weights[0] = attention(lengths, after(qkv[0], qkv[1]))
    if direct:
        for g in b:
            g.forward(attended[0])
        for g in c:
            g.start(b[0].x, b[0].y, b[1].x, b[1].y)
        for g in b:
            g.cross()
        pieces_b = [g.pieces() for g in b]
        second = after(qkv[1], attended[0], b[0].x, b[0].y, b[1].x, b[1].y)
    else:
        second = qkv[1]
    attended[1], weights[1] = attention(lengths, second)
    normed_one, inv_one, hidden_low, activated, slope = feed_in(
        me, attended, tokens, pieces_b, vectors, in_bias
    )
    if direct:
        for g in c:
            g.forward(activated)
            g.cross()
        pieces_c = [g.pieces() for g in c]
    output, grad_res_two, grad_ffn, sums_two = feed_out(
        me, activated, normed_one, cotangent, pieces_c, vectors
    )

    def ordered(value, *others):
        return after(value, *others) if direct else value

    parts_out = grad_w_out(me, activated, grad_ffn)
    grad_pre, sums_in = back_out(me, ordered(grad_ffn, *parts_out), slope, pieces_c)
    if direct:
        r_out = Scatter(parts_out)
        sent = r_out.one(grad_pre)
    else:
        sent = ()
    parts_in = grad_w_in(me, hidden_low, ordered(grad_pre, *sent))
    grad_res_one, grad_branch, *grad_attended, sums_one = back_in(
        me,
        ordered(grad_pre, *parts_in),
        grad_res_two,
        normed_one,
        inv_one,
        pieces_b,
        vectors,
    )
    if direct:
        r_in = Scatter(parts_in)
        sent = r_out.two(grad_branch) + r_in.one(grad_branch)
    mixed0, sums_q0 = attention_back(
        lengths, qkv[0], weights[0], ordered(grad_attended[0], *sent)
    )
    if direct:
        sent = r_out.three(mixed0)
    parts_mix = grad_w_mixed(me, tokens, ordered(mixed0, *sent), attended, grad_branch)
    if direct:
        r_mix = Scatter(parts_mix)
        sent = r_in.two(*parts_mix)
    mixed1, sums_q1 = attention_back(
        lengths, qkv[1], weights[1], ordered(grad_attended[1], *sent, *parts_mix)
    )
    if direct:
        sent = r_mix.one(mixed1) + r_out.four(mixed1)
    parts_qkv = grad_w_qkv(me, tokens, ordered(mixed1, *sent))
    local_vecs = jnp.concatenate(
        [
            jnp.concatenate([sums_q0[0:2], sums_q1[0:2]], axis=1),
            sums_one[0:3],
            sums_two[0:3],
            sums_in.reshape(FF // D, D),
        ],
        axis=0,
    )
    if direct:
        r_qkv = Scatter(parts_qkv)
        sent = r_in.three(*parts_qkv)
    grad_tokens = back_qkv(
        me,
        (mixed0, ordered(mixed1, *sent, *parts_qkv)),
        grad_res_one,
        pieces_a,
    )
    if direct:
        r_qkv.one(grad_tokens)
        r_mix.two(grad_tokens)
        r_out.five(grad_tokens)
        r_in.four(grad_tokens)
        local_vecs = after(local_vecs, r_qkv.send_x)
        local_vecs = local_vecs + swap(local_vecs, 1)
        r_mix.three()
        sent = r_qkv.two()
        local_vecs = after(local_vecs, *sent)
        local_vecs = local_vecs + swap(local_vecs, 2)
        r_in.five()
        r_mix.four()
        sent = r_qkv.three()
        local_vecs = after(local_vecs, *sent)
        local_vecs = local_vecs + swap(local_vecs, 4)
        r_mix.five()
        sent = r_qkv.four()
        local_vecs = after(local_vecs, *sent)
        local_vecs = local_vecs + lax.ppermute(local_vecs, "rep", [(i, i ^ 1) for i in range(4)])
        sent = r_qkv.five()
        local_vecs = after(local_vecs, *sent)
        local_vecs = local_vecs + lax.ppermute(local_vecs, "rep", [(i, i ^ 2) for i in range(4)])
        sum_out, sum_in, sum_mix, sum_qkv = [
            r.result(rep_index) for r in (r_out, r_in, r_mix, r_qkv)
        ]
    else:
        local_vecs = lax.psum(local_vecs, ("fsdp", "rep"))

        def reduce(theirs, mine):
            full = jnp.stack([mine, theirs], axis=1)
            full = full.reshape(-1, full.shape[-1])
            owned = lax.psum_scatter(full, "fsdp", scatter_dimension=0, tiled=True)
            return lax.psum(owned, "rep")

        sum_out, sum_in, sum_mix, sum_qkv = [
            reduce(*parts) for parts in (parts_out, parts_in, parts_mix, parts_qkv)
        ]
    sum_vecs = lax.dynamic_slice(local_vecs, (0, position * part), (8, part))
    sum_bin = lax.dynamic_slice(local_vecs[8:].reshape(FF), (position * (FF // fsdp),), (FF // fsdp,))

    grad_out, step_out, mom_out, sq_out = adamw(m_out, v_out, sum_out)
    grad_in, step_in, mom_in, sq_in = adamw(m_in, v_in, sum_in)
    columns = []
    for k in range(3):
        columns += [sum_mix[:, k * PART : (k + 1) * PART], sum_qkv[:, k * PART : (k + 1) * PART]]
    sum_attn = jnp.concatenate(columns + [sum_mix[:, 3 * PART :]], axis=1)
    grad_attn, step_attn, mom_attn, sq_attn = adamw(m_attn, v_attn, sum_attn)
    grad_bin, step_bin, mom_bin, sq_bin = adamw(m_bin, v_bin, sum_bin)
    grad_vecs, step_vecs, mom_vecs, sq_vecs = adamw(m_vecs, v_vecs, sum_vecs)
    return (
        output,
        grad_tokens,
        grad_attn,
        grad_in,
        grad_out,
        grad_bin,
        grad_vecs,
        step_attn,
        step_in,
        step_out,
        step_bin,
        step_vecs,
        mom_attn,
        mom_in,
        mom_out,
        mom_bin,
        mom_vecs,
        sq_attn,
        sq_in,
        sq_out,
        sq_bin,
        sq_vecs,
    )


def solution(mesh):
    rows, row, col = P(("rep", "fsdp"), None), P("fsdp", None), P(None, "fsdp")
    flat = P("fsdp")
    state = (row, row, row, flat, col)
    return jax.shard_map(
        functools.partial(local, mesh.shape["fsdp"], mesh.shape["rep"]),
        mesh=mesh,
        in_specs=(rows, rows, P(("rep", "fsdp"))) + state * 3,
        out_specs=(rows, rows) + state * 4,
        check_vma=False,
    )
```

time: 363 us -> 296 us (0.82)
  waiting for transfers between devices: 121 us -> 57.2 us
  Pallas kernels: 147 us -> 115 us
  starting transfers between devices: 57.1 us -> 77.6 us
    ppermute x48 -> x68, waiting for transfers between devices: 74.8 us -> 36.4 us  [swap(): return lax.ppermute(value, 'fsdp', flip(bit))]
    pallas_call x9 -> x13, Pallas kernels: 116 us -> 89.9 us  [the longest x2 17.5 us: attention_back(): call(kernel, (rows // (GROUP * SEQ),), [rows_of(3 * PART, GROUP * SEQ), r...]
    ppermute x11 -> x14, waiting for transfers between devices: 46.4 us -> 20.8 us  [the longest x4 10.9 us: five(): self.back = lax.ppermute(self.total, 'rep', [(1, 0), (2, 3)])]
    ppermute x48 -> x68, starting transfers between devices: 37.1 us -> 49.6 us  [swap(): return lax.ppermute(value, 'fsdp', flip(bit))]
    ppermute x11 -> x14, starting transfers between devices: 19.9 us -> 28 us  [the longest x4 13.2 us: three(): self.near = lax.ppermute(self.owned, 'rep', [(0, 1), (3, 2)])]
    unnamed x75 -> x157, local copies, waits for them, and re-layouts: 3.38 us -> 11 us
    slice x13 -> x8, local copies, waits for them, and re-layouts: 5.13 us -> 0.16 us  [the longest x1 0.05 us: by_head_half(): value[:, k * D + half * PART:k * D + (half + 1) * PART]]
    convert_element_type x15 -> x20, other arithmetic: 11 us -> 11.1 us  [low_sum(): return total.astype(bf16)]
  transfers between devices with their start and end apart: 59 -> 82, of which waited for: 21 -> 21; matrix products, arithmetic and copies ran while one was open for 7% -> 9% of each run, Pallas kernels for 21% -> 31%
where the time goes in v2:
time: 296 us; the launch traced here: 293 us
  Pallas kernels  115 us (39%)
  starting transfers between devices  77.6 us (26%)
  waiting for transfers between devices  57.2 us (19%)
  other arithmetic  27.2 us (9%)
  local copies, waits for them, and re-layouts  12.7 us (4%)
    ppermute x68, starting transfers between devices, swap(): return lax.ppermute(value, 'fsdp', flip(bit))  49.6 us
    ppermute x68, waiting for transfers between devices, swap(): return lax.ppermute(value, 'fsdp', flip(bit))  36.4 us
    pallas_call x2, Pallas kernels, attention_back(): call(kernel, (rows // (GROUP * SEQ),), [rows_of(3 * PART, GROUP * SEQ), r...  17.5 us
    pallas_call x1, Pallas kernels, feed_in(): call(kernel, (rows // TILE,), [rows_of(PART), rows_of(PART), rows_of(D),...  16.2 us
    pallas_call x1, Pallas kernels, back_in(): call(kernel, (rows // TILE,), [rows_of(FF), rows_of(D), rows_of(D), rows_...  14.3 us
    ppermute x4, starting transfers between devices, three(): self.near = lax.ppermute(self.owned, 'rep', [(0, 1), (3, 2)])  13.2 us
    pallas_call x1, Pallas kernels, feed_out(): call(kernel, (rows // TILE,), [rows_of(FF), rows_of(D), rows_of(D), whole...  11.1 us
    convert_element_type x20, other arithmetic, low_sum(): return total.astype(bf16)  11.1 us
  transfers between devices with their start and end apart: 82, of which 21 were waited for; matrix products, arithmetic and copies ran while one was open for 9% of the time, Pallas kernels for 31%

profile of v2, /device:TPU:0, one launch (start us, length us, event | category | flops | bytes accessed | tf_op | source)
XLA Modules:
  0.0 292.7 jit_solution(7375048136396945058)
XLA Ops:
  0.7 1.3 convert.33
  2.1 3.0 %collective-permute-start = (bf16[96,1152]{1,0:T(8,128)(2,1)S(1)}, bf16[96,1152]{1,0:T(8,128)(2,1)S(1)}, u32[]{:S(2)}, u32[]{:S(2)}) collective-permute-start(bf16[96,1152]{1,0:T(8,128)(2,1)S(1)} %pad_maximum_fusion.5.rest_0_), channel_id=1, source_target_pairs={{0,2},{1,3},{2,0},{3,1},{4,6},{5,7},{6,4},{7,5},{8,10},{9,11},{10,... | collective-permute-start | bytes 663560 | tf_op jit(solution)/shard_map/ppermute | solution.py:646
  5.1 1.5 collective-permute-start.1
  7.4 3.2 %collective-permute-done.rest_1_ = bf16[96,1152]{1,0:T(8,128)(2,1)S(1)} collective-permute-done((bf16[96,1152]{1,0:T(8,128)(2,1)S(1)}, bf16[96,1152]{1,0:T(8,128)(2,1)S(1)}, u32[]{:S(2)}, u32[]{:S(2)}) %collective-permute-start) | collective-permute-done | bytes 221216 | tf_op jit(solution)/shard_map/ppermute | solution.py:646
  10.6 1.5 collective-permute-done.1.rest_2_
  12.0 1.5 collective-permute-start.4
  14.2 1.4 convert.36
  15.7 1.6 collective-permute-start.2
  18.4 2.5 collective-permute-start.7
  21.8 1.6 collective-permute-done.3.rest_2_.rest_10_
  25.0 1.4 collective-permute-start.17
  27.5 4.5 %collective-permute-done.12.rest_3_.rest_11_ = bf16[96,1152]{1,0:T(8,128)(2,1)} collective-permute-done((bf16[96,1152]{1,0:T(8,128)(2,1)}, bf16[96,1152]{1,0:T(8,128)(2,1)}, u32[]{:S(2)}, u32[]{:S(2)}) %collective-permute-start.12) | collective-permute-done | bytes 221216 | tf_op jit(solution)/shard_map/ppermute | solution.py:646
  32.5 1.4 collective-permute-start.20
  34.7 4.1 %qkv.2.qkv_ref = bf16[1024,1152]{1,0:T(8,128)(2,1)S(1)} custom-call(s32[1]{0:T(128)} %bitcast.s, bf16[1024,768]{1,0:T(8,128)(2,1)S(1)} %copy-done, f32[1,1152]{1,0:T(1,128)S(1)} %get-tuple-element.263.b_ref, bf16[96,1152]{1,0:T(8,128)(2,1)} %copy-done.23, bf16[96,1152]{1,0:T(8,128)(2,1)} %copy-done.59, bf16[96,1152]{1,0:T(8,128)(2,1)} %copy-done.60, ...), custom_call_target="tpu_custom_call" | custom-call | flops 1811939 | bytes 9830 | tf_op jit(solution)/shard_map/qkv/pallas_call | solution.py:157
  39.7 3.9 %qkv.3.qkv_ref = bf16[1024,1152]{1,0:T(8,128)(2,1)S(1)} custom-call(s32[1]{0:T(128)} %bitcast.s, bf16[1024,768]{1,0:T(8,128)(2,1)S(1)} %copy-done, f32[1,1152]{1,0:T(1,128)S(1)} %get-tuple-element.262.b_ref, bf16[96,1152]{1,0:T(8,128)(2,1)} %copy-done.24, bf16[96,1152]{1,0:T(8,128)(2,1)} %collective-permute-done.2.rest_1_.rest_9_, ...), custom_call_target="tpu_custom_call" | custom-call | flops 1811939 | bytes 9830 | tf_op jit(solution)/shard_map/qkv/pallas_call | solution.py:157
  43.6 5.4 %attention.2 = (bf16[1024,384]{1,0:T(8,128)(2,1)S(1)}, f32[1024,768]{1,0:T(8,128)}) custom-call(s32[8]{0:T(128)S(1)} %copy-done.13, bf16[1024,1152]{1,0:T(8,128)(2,1)S(1)} %qkv.2.qkv_ref), custom_call_target="tpu_custom_call" | custom-call | flops 4000000 | bytes 6291 | tf_op jit(solution)/shard_map/attention/pallas_call | solution.py:211
  50.4 1.6 collective-permute-start.26
  52.5 7.7 %collective-permute-done.21.rest_3_ = bf16[96,1920]{1,0:T(8,128)(2,1)S(1)} collective-permute-done((bf16[96,1920]{1,0:T(8,128)(2,1)S(1)}, bf16[96,1920]{1,0:T(8,128)(2,1)S(1)}, u32[]{:S(2)}, u32[]{:S(2)}) %collective-permute-start.21) | collective-permute-done | bytes 368672 | tf_op jit(solution)/shard_map/ppermute | solution.py:646
  61.5 1.6 collective-permute-start.31
  65.7 5.4 %attention.3 = (bf16[1024,384]{1,0:T(8,128)(2,1)S(1)}, f32[1024,768]{1,0:T(8,128)}) custom-call(s32[8]{0:T(128)S(1)} %copy-done.13, bf16[1024,1152]{1,0:T(8,128)(2,1)S(1)} %qkv.3.qkv_ref), custom_call_target="tpu_custom_call" | custom-call | flops 4000000 | bytes 6291 | tf_op jit(solution)/shard_map/attention/pallas_call | solution.py:211
  71.9 16.2 %feed_in.1 = (f32[1024,768]{1,0:T(8,128)S(1)}, f32[1024,1]{1,0:T(8,128)S(1)}, bf16[1024,768]{1,0:T(8,128)(2,1)S(1)}, bf16[1024,3072]{1,0:T(8,128)(2,1)S(1)}, bf16[1024,3072]{1,0:T(8,128)(2,1)S(1)}) custom-call(s32[1]{0:T(128)} %bitcast.s, bf16[1024,384]{1,0:T(8,128)(2,1)S(1)} %get-tuple-element.125.o0_ref, bf16[1024,384]{1,0:T(8,128)(2,1)S(1)} %get-tuple-element.133.o1_ref, ...), custom_call_target="tpu_custom_call" | custom-call | flops 6039797 | bytes 26345 | tf_op jit(solution)/shard_map/feed_in/pallas_call | solution.py:257
  88.2 2.7 copy-done.5
  91.0 1.4 collective-permute-start.33
  92.5 1.4 collective-permute-start.40
  94.4 5.9 %collective-permute-done.33.rest_3_ = bf16[192,768]{1,0:T(8,128)(2,1)S(1)} collective-permute-done((bf16[192,768]{1,0:T(8,128)(2,1)S(1)}, bf16[192,768]{1,0:T(8,128)(2,1)S(1)}, u32[]{:S(2)}, u32[]{:S(2)}) %collective-permute-start.33) | collective-permute-done | bytes 294944 | tf_op jit(solution)/shard_map/ppermute | solution.py:646
  104.1 11.1 %feed_out.1 = (bf16[1024,768]{1,0:T(8,128)(2,1)}, f32[1024,768]{1,0:T(8,128)S(1)}, bf16[1024,768]{1,0:T(8,128)(2,1)S(1)}, f32[8,768]{1,0:T(8,128)S(1)}) custom-call(s32[1]{0:T(128)} %bitcast.s, bf16[1024,3072]{1,0:T(8,128)(2,1)S(1)} %get-tuple-element.134.f_ref, f32[1024,768]{1,0:T(8,128)S(1)} %get-tuple-element.135.n1_ref, ...), custom_call_target="tpu_custom_call" | custom-call | flops 4831838 | bytes 22020 | tf_op jit(solution)/shard_map/feed_out/pallas_call | solution.py:306
  115.2 6.3 %grad_w_out.1 = (bf16[4,384,768]{2,1,0:T(8,128)(2,1)S(1)}, bf16[4,384,768]{2,1,0:T(8,128)(2,1)S(1)}) custom-call(s32[1]{0:T(128)} %bitcast.s, bf16[1024,3072]{1,0:T(8,128)(2,1)S(1)} %get-tuple-element.134.f_ref, bf16[1024,768]{1,0:T(8,128)(2,1)S(1)} %get-tuple-element.147.dz_ref), custom_call_target="tpu_custom_call" | custom-call | flops 4831838 | bytes 12582 | tf_op jit(solution)/shard_map/grad_w_out/pallas_call | solution.py:337
  121.7 8.8 %back_out.1 = (bf16[1024,3072]{1,0:T(8,128)(2,1)S(1)}, f32[1,3072]{1,0:T(1,128)S(1)}) custom-call(s32[1]{0:T(128)} %bitcast.s, bf16[1024,768]{1,0:T(8,128)(2,1)S(1)} %get-tuple-element.147.dz_ref, bf16[1024,3072]{1,0:T(8,128)(2,1)S(1)} %copy-done.6, bf16[192,768]{1,0:T(8,128)(2,1)} %copy-done.19, bf16[192,768]{1,0:T(8,128)(2,1)} %copy-done.45, ...), custom_call_target="tpu_custom_call" | custom-call | flops 4831838 | bytes 18874 | tf_op jit(solution)/shard_map/back_out/pallas_call | solution.py:375
  131.8 6.5 %grad_w_in.1 = (bf16[4,96,3072]{2,1,0:T(8,128)(2,1)S(1)}, bf16[4,96,3072]{2,1,0:T(8,128)(2,1)S(1)}) custom-call(s32[1]{0:T(128)} %bitcast.s, bf16[1024,768]{1,0:T(8,128)(2,1)S(1)} %get-tuple-element.150.h_ref, bf16[1024,3072]{1,0:T(8,128)(2,1)S(1)} %get-tuple-element.155.du_ref), custom_call_target="tpu_custom_call" | custom-call | flops 4831838 | bytes 14155 | tf_op jit(solution)/shard_map/grad_w_in/pallas_call | solution.py:471
  138.8 1.4 collective-permute-start.46
  141.0 14.3 %back_in.1 = (f32[1024,768]{1,0:T(8,128)S(1)}, bf16[1024,768]{1,0:T(8,128)(2,1)S(1)}, bf16[1024,384]{1,0:T(8,128)(2,1)S(1)}, bf16[1024,384]{1,0:T(8,128)(2,1)S(1)}, f32[8,768]{1,0:T(8,128)S(1)}) custom-call(s32[1]{0:T(128)} %bitcast.s, bf16[1024,3072]{1,0:T(8,128)(2,1)S(1)} %get-tuple-element.155.du_ref, f32[1024,768]{1,0:T(8,128)S(1)} %get-tuple-element.156.dr2_ref, ...), custom_call_target="tpu_custom_call" | custom-call | flops 6039797 | bytes 24772 | tf_op jit(solution)/shard_map/back_in/pallas_call | solution.py:423
  155.4 1.7 copy-done.7
  159.8 1.7 add_convert_fusion.4
  161.6 1.4 collective-permute-start.49
  163.8 8.6 %attention_back.2 = (bf16[1024,1152]{1,0:T(8,128)(2,1)S(1)}, f32[8,384]{1,0:T(8,128)S(1)}) custom-call(s32[8]{0:T(128)S(1)} %copy-done.13, bf16[1024,1152]{1,0:T(8,128)(2,1)S(1)} %qkv.2.qkv_ref, f32[1024,768]{1,0:T(8,128)} %get-tuple-element.143.p_ref, bf16[1024,384]{1,0:T(8,128)(2,1)S(1)} %get-tuple-element.163.do_ref), custom_call_target="tpu_custom_call" | custom-call | flops 7000000 | bytes 8650 | tf_op jit(solution)/shard_map/attention_back/pallas_call | solution.py:523
  174.1 4.7 %grad_w_mixed.1 = (bf16[4,96,1920]{2,1,0:T(8,128)(2,1)}, bf16[4,96,1920]{2,1,0:T(8,128)(2,1)S(1)}) custom-call(s32[1]{0:T(128)} %bitcast.s, bf16[1024,768]{1,0:T(8,128)(2,1)S(1)} %copy-done, bf16[1024,1152]{1,0:T(8,128)(2,1)S(1)} %get-tuple-element.169.g_ref.g0_ref, bf16[1024,384]{1,0:T(8,128)(2,1)S(1)} %get-tuple-element.125.o0_ref, ...), custom_call_target="tpu_custom_call" | custom-call | flops 3019898 | bytes 12386 | tf_op jit(solution)/shard_map/grad_w_mixed/pallas_call | solution.py:575
  180.1 3.5 %collective-permute-start.56 = (bf16[384,768]{1,0:T(8,128)(2,1)}, bf16[384,768]{1,0:T(8,128)(2,1)S(1)}, u32[]{:S(2)}, u32[]{:S(2)}) collective-permute-start(bf16[384,768]{1,0:T(8,128)(2,1)} %pad_maximum_fusion), channel_id=1, source_target_pairs={{0,8},{24,16},{1,9},{25,17},{2,10},{26,18},{3,11},{27,19},{4,12},{... | collective-permute-start | bytes 1769480 | tf_op jit(solution)/shard_map/ppermute | solution.py:723
  183.6 1.8 fusion.12
  186.0 1.3 collective-permute-start.54
  188.4 8.9 %attention_back.3 = (bf16[1024,1152]{1,0:T(8,128)(2,1)S(1)}, f32[8,384]{1,0:T(8,128)S(1)}) custom-call(s32[8]{0:T(128)S(1)} %copy-done.13, bf16[1024,1152]{1,0:T(8,128)(2,1)S(1)} %copy-done.2, f32[1024,768]{1,0:T(8,128)} %get-tuple-element.165.p_ref, bf16[1024,384]{1,0:T(8,128)(2,1)S(1)} %copy-done.12), custom_call_target="tpu_custom_call" | custom-call | flops 7000000 | bytes 8650 | tf_op jit(solution)/shard_map/attention_back/pallas_call | solution.py:523
  199.5 1.4 collective-permute-start.57
  201.8 2.2 grad_w_qkv.1
  204.2 1.9 fusion.4
  206.1 6.5 %collective-permute-start.72 = (bf16[96,3072]{1,0:T(8,128)(2,1)S(1)}, bf16[96,3072]{1,0:T(8,128)(2,1)S(1)}, u32[]{:S(2)}, u32[]{:S(2)}) collective-permute-start(bf16[96,3072]{1,0:T(8,128)(2,1)S(1)} %pad_maximum_fusion.1), channel_id=1, source_target_pairs={{0,8},{24,16},{1,9},{25,17},{2,10},{26,18},{3,11},{27,19},{4,12},{... | collective-permute-start | bytes 1769480 | tf_op jit(solution)/shard_map/ppermute | solution.py:723
  212.6 8.8 %back_qkv.1 = bf16[1024,768]{1,0:T(8,128)(2,1)} custom-call(s32[1]{0:T(128)} %bitcast.s, bf16[1024,1152]{1,0:T(8,128)(2,1)S(1)} %copy-done.4, bf16[1024,1152]{1,0:T(8,128)(2,1)S(1)} %get-tuple-element.183.g_ref.g1_ref, f32[1024,768]{1,0:T(8,128)S(1)} %copy-done.8, bf16[96,1152]{1,0:T(8,128)(2,1)} %copy-done.23, bf16[96,1152]{1,0:T(8,128)(2,1)} %copy-done.59, ...), custom_call_target="tpu_custom_call" | custom-call | flops 3623878 | bytes 12976 | tf_op jit(solution)/shard_map/back_qkv/pallas_call | solution.py:614
  222.6 1.4 collective-permute-start.59
  225.0 1.3 collective-permute-start.76
  226.3 3.1 %collective-permute-done.59 = bf16[48,1920]{1,0:T(8,128)(2,1)S(1)} collective-permute-done((bf16[48,1920]{1,0:T(8,128)(2,1)S(1)}, bf16[48,1920]{1,0:T(8,128)(2,1)S(1)}, u32[]{:S(2)}, u32[]{:S(2)}) %collective-permute-start.59) | collective-permute-done | bytes 184352 | tf_op jit(solution)/shard_map/ppermute | solution.py:646
  231.8 1.7 collective-permute-start.61
  235.9 5.9 %collective-permute-done.76 = bf16[384,768]{1,0:T(8,128)(2,1)S(1)} collective-permute-done((bf16[384,768]{1,0:T(8,128)(2,1)S(1)}, bf16[384,768]{1,0:T(8,128)(2,1)S(1)}, u32[]{:S(2)}, u32[]{:S(2)}) %collective-permute-start.76) | collective-permute-done | bytes 589856 | tf_op jit(solution)/shard_map/ppermute | solution.py:733
  241.8 2.5 add_divide_fusion
  246.3 1.4 collective-permute-start.78
  248.5 2.5 collective-permute-done.78
  251.2 1.5 collective-permute-start.69
  254.0 1.3 collective-permute-start.74
  255.3 1.5 collective-permute-done.79
  258.1 4.2 %collective-permute-start.80 = (f32[12,768]{1,0:T(8,128)S(1)}, f32[12,768]{1,0:T(8,128)S(1)}, u32[]{:S(2)}, u32[]{:S(2)}) collective-permute-start(f32[12,768]{1,0:T(8,128)S(1)} %add.357), channel_id=1, source_target_pairs={{0,8},{8,0},{16,24},{24,16},{1,9},{9,1},{17,25},{25,17},{2,10},{10... | collective-permute-start | bytes 110600 | tf_op jit(solution)/shard_map/ppermute | solution.py:939
  262.4 1.4 collective-permute-start.63
  263.9 9.4 %collective-permute-done.80 = f32[12,768]{1,0:T(8,128)S(1)} collective-permute-done((f32[12,768]{1,0:T(8,128)S(1)}, f32[12,768]{1,0:T(8,128)S(1)}, u32[]{:S(2)}, u32[]{:S(2)}) %collective-permute-start.80) | collective-permute-done | bytes 36896 | tf_op jit(solution)/shard_map/ppermute | solution.py:939
  273.3 1.3 collective-permute-start.71
  274.6 2.6 collective-permute-start.81
  277.2 5.0 %collective-permute-done.63 = bf16[96,1920]{1,0:T(8,128)(2,1)S(1)} collective-permute-done((bf16[96,1920]{1,0:T(8,128)(2,1)S(1)}, bf16[96,1920]{1,0:T(8,128)(2,1)S(1)}, u32[]{:S(2)}, u32[]{:S(2)}) %collective-permute-start.63) | collective-permute-done | bytes 368672 | tf_op jit(solution)/shard_map/ppermute | solution.py:733
  284.4 4.1 %add_divide_fusion.1 = (f32[96,3072]{1,0:T(8,128)}, f32[96,3072]{1,0:T(8,128)}, f32[96,3072]{1,0:T(8,128)}, f32[96,3072]{1,0:T(8,128)}) fusion(f32[96,3072]{1,0:T(8,128)S(1)} %copy-done.42, f32[96,3072]{1,0:T(8,128)} %param.32, bf16[96,3072]{1,0:T(8,128)(2,1)S(1)} %add_convert_fusion.1, bf16[96,3072]{1,0:T(8,128)(2,1)} %collective-permute-done.74, pred[]{:T(512)S(6)} %or.2), kind=kLoop, calls=%fused_computation.8 | loop fusion | flops 3833856 | bytes 8257537 | tf_op jit(solution)/shard_map/div | solution.py:632
  289.7 2.5 add_divide_fusion.2
  (345 shorter events, 49.0 us)
Async XLA Ops:
  2.1 8.4 %collective-permute-start = (bf16[96,1152]{1,0:T(8,128)(2,1)S(1)}, bf16[96,1152]{1,0:T(8,128)(2,1)S(1)}, u32[]{:S(2)}, u32[]{:S(2)}) collective-permute-start(bf16[96,1152]{1,0:T(8,128)(2,1)S(1)} %pad_maximum_fusion.5.rest_0_), channel_id=1, source_target_pairs={{0,2},{1,3},{2,0},{3,1},{4,6},{5,7},{6,4},{7,5},{8,10},{9,11},{10,... | collective-permute-start | bytes 663560 | tf_op jit(solution)/shard_map/ppermute | solution.py:646
  5.1 6.9 %collective-permute-start.1 = (bf16[96,1152]{1,0:T(8,128)(2,1)S(1)}, bf16[96,1152]{1,0:T(8,128)(2,1)S(1)}, u32[]{:S(2)}, u32[]{:S(2)}) collective-permute-start(bf16[96,1152]{1,0:T(8,128)(2,1)S(1)} %pad_maximum_fusion.5.rest_0_), channel_id=1, source_target_pairs={{0,4},{1,5},{2,6},{3,7},{4,0},{5,1},{6,2},{7,3},{8,12},{9,13},{10,... | collective-permute-start | bytes 663560 | tf_op jit(solution)/shard_map/ppermute | solution.py:646
  6.8 6.8 %collective-permute-start.5 = (bf16[1,1152]{1,0:T(2,128)(2,1)S(1)}, bf16[1,1152]{1,0:T(2,128)(2,1)S(1)}, u32[]{:S(2)}, u32[]{:S(2)}) collective-permute-start(bf16[1,1152]{1,0:T(2,128)(2,1)S(1)} %constant_dynamic-update-slice_fusion), channel_id=1, source_target_pairs={{0,1},{1,0},{2,3},{3,2},{4,5},{5,4},{6,7},{7,6},{8,9},{9,8},{10,11... | collective-permute-start | bytes 6920 | tf_op jit(solution)/shard_map/ppermute | solution.py:646
  6.9 17.1 %collective-permute-start.8 = (bf16[96,1152]{1,0:T(8,128)(2,1)S(1)}, bf16[96,1152]{1,0:T(8,128)(2,1)S(1)}, u32[]{:S(2)}, u32[]{:S(2)}) collective-permute-start(bf16[96,1152]{1,0:T(8,128)(2,1)S(1)} %pad_maximum_fusion.5.rest_0_), channel_id=1, source_target_pairs={{0,1},{1,0},{2,3},{3,2},{4,5},{5,4},{6,7},{7,6},{8,9},{9,8},{10,11... | collective-permute-start | bytes 663560 | tf_op jit(solution)/shard_map/ppermute | solution.py:646
  12.0 6.4 %collective-permute-start.4 = (bf16[96,1152]{1,0:T(8,128)(2,1)S(1)}, bf16[96,1152]{1,0:T(8,128)(2,1)S(1)}, u32[]{:S(2)}, u32[]{:S(2)}) collective-permute-start(bf16[96,1152]{1,0:T(8,128)(2,1)S(1)} %collective-permute-done.rest_1_), channel_id=1, source_target_pairs={{0,4},{1,5},{2,6},{3,7},{4,0},{5,1},{6,2},{7,3},{8,12},{9,13},{10,... | collective-permute-start | bytes 663560 | tf_op jit(solution)/shard_map/ppermute | solution.py:646
  17.2 6.1 %collective-permute-start.3 = (bf16[96,1152]{1,0:T(8,128)(2,1)S(1)}, bf16[96,1152]{1,0:T(8,128)(2,1)}, u32[]{:S(2)}, u32[]{:S(2)}) collective-permute-start(bf16[96,1152]{1,0:T(8,128)(2,1)S(1)} %pad_maximum_fusion.4.rest_0_.rest_8_), channel_id=1, source_target_pairs={{0,4},{1,5},{2,6},{3,7},{4,0},{5,1},{6,2},{7,3},{8,12},{9,13},{10,... | collective-permute-start | bytes 663560 | tf_op jit(solution)/shard_map/ppermute | solution.py:646
  17.8 6.4 %collective-permute-start.9 = (bf16[96,1152]{1,0:T(8,128)(2,1)S(1)}, bf16[96,1152]{1,0:T(8,128)(2,1)}, u32[]{:S(2)}, u32[]{:S(2)}) collective-permute-start(bf16[96,1152]{1,0:T(8,128)(2,1)S(1)} %collective-permute-done.rest_1_), channel_id=1, source_target_pairs={{0,1},{1,0},{2,3},{3,2},{4,5},{5,4},{6,7},{7,6},{8,9},{9,8},{10,11... | collective-permute-start | bytes 663560 | tf_op jit(solution)/shard_map/ppermute | solution.py:646
  23.4 8.6 %collective-permute-start.12 = (bf16[96,1152]{1,0:T(8,128)(2,1)}, bf16[96,1152]{1,0:T(8,128)(2,1)}, u32[]{:S(2)}, u32[]{:S(2)}) collective-permute-start(bf16[96,1152]{1,0:T(8,128)(2,1)} %collective-permute-done.3.rest_2_.rest_10_), channel_id=1, source_target_pairs={{0,2},{1,3},{2,0},{3,1},{4,6},{5,7},{6,4},{7,5},{8,10},{9,11},{10,... | collective-permute-start | bytes 663560 | tf_op jit(solution)/shard_map/ppermute | solution.py:646
  24.0 8.6 %collective-permute-start.14 = (bf16[96,1152]{1,0:T(8,128)(2,1)}, bf16[96,1152]{1,0:T(8,128)(2,1)S(1)}, u32[]{:S(2)}, u32[]{:S(2)}) collective-permute-start(bf16[96,1152]{1,0:T(8,128)(2,1)} %collective-permute-done.2.rest_1_.rest_9_), channel_id=1, source_target_pairs={{0,1},{1,0},{2,3},{3,2},{4,5},{5,4},{6,7},{7,6},{8,9},{9,8},{10,11... | collective-permute-start | bytes 663560 | tf_op jit(solution)/shard_map/ppermute | solution.py:646
  24.7 9.2 %collective-permute-start.15 = (bf16[96,1152]{1,0:T(8,128)(2,1)}, bf16[96,1152]{1,0:T(8,128)(2,1)S(1)}, u32[]{:S(2)}, u32[]{:S(2)}) collective-permute-start(bf16[96,1152]{1,0:T(8,128)(2,1)} %collective-permute-done.3.rest_2_.rest_10_), channel_id=1, source_target_pairs={{0,1},{1,0},{2,3},{3,2},{4,5},{5,4},{6,7},{7,6},{8,9},{9,8},{10,11... | collective-permute-start | bytes 663560 | tf_op jit(solution)/shard_map/ppermute | solution.py:646
  25.0 24.1 %collective-permute-start.17 = (bf16[96,1920]{1,0:T(8,128)(2,1)S(1)}, bf16[96,1920]{1,0:T(8,128)(2,1)S(1)}, u32[]{:S(2)}, u32[]{:S(2)}) collective-permute-start(bf16[96,1920]{1,0:T(8,128)(2,1)S(1)} %pad_maximum_fusion.2.rest_0_), channel_id=1, source_target_pairs={{0,2},{1,3},{2,0},{3,1},{4,6},{5,7},{6,4},{7,5},{8,10},{9,11},{10,... | collective-permute-start | bytes 1105928 | tf_op jit(solution)/shard_map/ppermute | solution.py:646
  26.4 23.2 %collective-permute-start.18 = (bf16[96,1920]{1,0:T(8,128)(2,1)S(1)}, bf16[96,1920]{1,0:T(8,128)(2,1)S(1)}, u32[]{:S(2)}, u32[]{:S(2)}) collective-permute-start(bf16[96,1920]{1,0:T(8,128)(2,1)S(1)} %pad_maximum_fusion.2.rest_0_), channel_id=1, source_target_pairs={{0,4},{1,5},{2,6},{3,7},{4,0},{5,1},{6,2},{7,3},{8,12},{9,13},{10,... | collective-permute-start | bytes 1105928 | tf_op jit(solution)/shard_map/ppermute | solution.py:646
  32.0 18.3 %collective-permute-start.19 = (bf16[96,1920]{1,0:T(8,128)(2,1)S(1)}, bf16[96,1920]{1,0:T(8,128)(2,1)S(1)}, u32[]{:S(2)}, u32[]{:S(2)}) collective-permute-start(bf16[96,1920]{1,0:T(8,128)(2,1)S(1)} %slice.396.rest_8_), channel_id=1, source_target_pairs={{0,2},{1,3},{2,0},{3,1},{4,6},{5,7},{6,4},{7,5},{8,10},{9,11},{10,... | collective-permute-start | bytes 1105928 | tf_op jit(solution)/shard_map/ppermute | solution.py:646
  32.5 17.8 %collective-permute-start.20 = (bf16[96,1920]{1,0:T(8,128)(2,1)S(1)}, bf16[96,1920]{1,0:T(8,128)(2,1)S(1)}, u32[]{:S(2)}, u32[]{:S(2)}) collective-permute-start(bf16[96,1920]{1,0:T(8,128)(2,1)S(1)} %slice.396.rest_8_), channel_id=1, source_target_pairs={{0,4},{1,5},{2,6},{3,7},{4,0},{5,1},{6,2},{7,3},{8,12},{9,13},{10,... | collective-permute-start | bytes 1105928 | tf_op jit(solution)/shard_map/ppermute | solution.py:646
  38.9 13.0 %collective-permute-start.22 = (bf16[96,1920]{1,0:T(8,128)(2,1)S(1)}, bf16[96,1920]{1,0:T(8,128)(2,1)S(1)}, u32[]{:S(2)}, u32[]{:S(2)}) collective-permute-start(bf16[96,1920]{1,0:T(8,128)(2,1)S(1)} %pad_maximum_fusion.2.rest_0_), channel_id=1, source_target_pairs={{0,1},{1,0},{2,3},{3,2},{4,5},{5,4},{6,7},{7,6},{8,9},{9,8},{10,11... | collective-permute-start | bytes 1105928 | tf_op jit(solution)/shard_map/ppermute | solution.py:646
  49.6 10.6 %collective-permute-start.21 = (bf16[96,1920]{1,0:T(8,128)(2,1)S(1)}, bf16[96,1920]{1,0:T(8,128)(2,1)S(1)}, u32[]{:S(2)}, u32[]{:S(2)}) collective-permute-start(bf16[96,1920]{1,0:T(8,128)(2,1)S(1)} %collective-permute-done.17.rest_1_), channel_id=1, source_target_pairs={{0,4},{1,5},{2,6},{3,7},{4,0},{5,1},{6,2},{7,3},{8,12},{9,13},{10,... | collective-permute-start | bytes 1105928 | tf_op jit(solution)/shard_map/ppermute | solution.py:646
  50.3 9.9 %collective-permute-start.23 = (bf16[96,1920]{1,0:T(8,128)(2,1)S(1)}, bf16[96,1920]{1,0:T(8,128)(2,1)S(1)}, u32[]{:S(2)}, u32[]{:S(2)}) collective-permute-start(bf16[96,1920]{1,0:T(8,128)(2,1)S(1)} %collective-permute-done.17.rest_1_), channel_id=1, source_target_pairs={{0,1},{1,0},{2,3},{3,2},{4,5},{5,4},{6,7},{7,6},{8,9},{9,8},{10,11... | collective-permute-start | bytes 1105928 | tf_op jit(solution)/shard_map/ppermute | solution.py:646
  50.4 11.0 %collective-permute-start.26 = (bf16[96,1920]{1,0:T(8,128)(2,1)S(1)}, bf16[96,1920]{1,0:T(8,128)(2,1)S(1)}, u32[]{:S(2)}, u32[]{:S(2)}) collective-permute-start(bf16[96,1920]{1,0:T(8,128)(2,1)S(1)} %collective-permute-done.20.rest_10_), channel_id=1, source_target_pairs={{0,2},{1,3},{2,0},{3,1},{4,6},{5,7},{6,4},{7,5},{8,10},{9,11},{10,... | collective-permute-start | bytes 1105928 | tf_op jit(solution)/shard_map/ppermute | solution.py:646
  52.0 9.6 %collective-permute-start.24 = (bf16[96,1920]{1,0:T(8,128)(2,1)S(1)}, bf16[96,1920]{1,0:T(8,128)(2,1)S(1)}, u32[]{:S(2)}, u32[]{:S(2)}) collective-permute-start(bf16[96,1920]{1,0:T(8,128)(2,1)S(1)} %collective-permute-done.18.rest_2_), channel_id=1, source_target_pairs={{0,1},{1,0},{2,3},{3,2},{4,5},{5,4},{6,7},{7,6},{8,9},{9,8},{10,11... | collective-permute-start | bytes 1105928 | tf_op jit(solution)/shard_map/ppermute | solution.py:646
  52.1 11.0 %collective-permute-start.28 = (bf16[96,1920]{1,0:T(8,128)(2,1)S(1)}, bf16[96,1920]{1,0:T(8,128)(2,1)S(1)}, u32[]{:S(2)}, u32[]{:S(2)}) collective-permute-start(bf16[96,1920]{1,0:T(8,128)(2,1)S(1)} %collective-permute-done.19.rest_9_), channel_id=1, source_target_pairs={{0,1},{1,0},{2,3},{3,2},{4,5},{5,4},{6,7},{7,6},{8,9},{9,8},{10,11... | collective-permute-start | bytes 1105928 | tf_op jit(solution)/shard_map/ppermute | solution.py:646
  61.4 9.8 %collective-permute-start.30 = (bf16[96,1920]{1,0:T(8,128)(2,1)S(1)}, bf16[96,1920]{1,0:T(8,128)(2,1)S(1)}, u32[]{:S(2)}, u32[]{:S(2)}) collective-permute-start(bf16[96,1920]{1,0:T(8,128)(2,1)S(1)} %collective-permute-done.26.rest_11_), channel_id=1, source_target_pairs={{0,1},{1,0},{2,3},{3,2},{4,5},{5,4},{6,7},{7,6},{8,9},{9,8},{10,11... | collective-permute-start | bytes 1105928 | tf_op jit(solution)/shard_map/ppermute | solution.py:646
  61.5 29.3 %collective-permute-start.31 = (bf16[192,768]{1,0:T(8,128)(2,1)S(1)}, bf16[192,768]{1,0:T(8,128)(2,1)S(1)}, u32[]{:S(2)}, u32[]{:S(2)}) collective-permute-start(bf16[192,768]{1,0:T(8,128)(2,1)S(1)} %get-tuple-element.136.rest_0_), channel_id=1, source_target_pairs={{0,2},{1,3},{2,0},{3,1},{4,6},{5,7},{6,4},{7,5},{8,10},{9,11},{10,... | collective-permute-start | bytes 884744 | tf_op jit(solution)/shard_map/ppermute | solution.py:646
  63.1 27.8 %collective-permute-start.32 = (bf16[192,768]{1,0:T(8,128)(2,1)S(1)}, bf16[192,768]{1,0:T(8,128)(2,1)S(1)}, u32[]{:S(2)}, u32[]{:S(2)}) collective-permute-start(bf16[192,768]{1,0:T(8,128)(2,1)S(1)} %get-tuple-element.136.rest_0_), channel_id=1, source_target_pairs={{0,4},{1,5},{2,6},{3,7},{4,0},{5,1},{6,2},{7,3},{8,12},{9,13},{10,... | collective-permute-start | bytes 884744 | tf_op jit(solution)/shard_map/ppermute | solution.py:646
  64.3 28.0 %collective-permute-start.38 = (bf16[192,768]{1,0:T(8,128)(2,1)S(1)}, bf16[192,768]{1,0:T(8,128)(2,1)S(1)}, u32[]{:S(2)}, u32[]{:S(2)}) collective-permute-start(bf16[192,768]{1,0:T(8,128)(2,1)S(1)} %get-tuple-element.139.rest_8_), channel_id=1, source_target_pairs={{0,2},{1,3},{2,0},{3,1},{4,6},{5,7},{6,4},{7,5},{8,10},{9,11},{10,... | collective-permute-start | bytes 884744 | tf_op jit(solution)/shard_map/ppermute | solution.py:646
  65.0 27.5 %collective-permute-start.39 = (bf16[192,768]{1,0:T(8,128)(2,1)S(1)}, bf16[192,768]{1,0:T(8,128)(2,1)S(1)}, u32[]{:S(2)}, u32[]{:S(2)}) collective-permute-start(bf16[192,768]{1,0:T(8,128)(2,1)S(1)} %get-tuple-element.139.rest_8_), channel_id=1, source_target_pairs={{0,4},{1,5},{2,6},{3,7},{4,0},{5,1},{6,2},{7,3},{8,12},{9,13},{10,... | collective-permute-start | bytes 884744 | tf_op jit(solution)/shard_map/ppermute | solution.py:646
  71.2 22.7 %collective-permute-start.34 = (bf16[192,768]{1,0:T(8,128)(2,1)S(1)}, bf16[192,768]{1,0:T(8,128)(2,1)S(1)}, u32[]{:S(2)}, u32[]{:S(2)}) collective-permute-start(bf16[192,768]{1,0:T(8,128)(2,1)S(1)} %get-tuple-element.136.rest_0_), channel_id=1, source_target_pairs={{0,1},{1,0},{2,3},{3,2},{4,5},{5,4},{6,7},{7,6},{8,9},{9,8},{10,11... | collective-permute-start | bytes 884744 | tf_op jit(solution)/shard_map/ppermute | solution.py:646
  91.0 9.4 %collective-permute-start.33 = (bf16[192,768]{1,0:T(8,128)(2,1)S(1)}, bf16[192,768]{1,0:T(8,128)(2,1)S(1)}, u32[]{:S(2)}, u32[]{:S(2)}) collective-permute-start(bf16[192,768]{1,0:T(8,128)(2,1)S(1)} %collective-permute-done.31.rest_1_), channel_id=1, source_target_pairs={{0,4},{1,5},{2,6},{3,7},{4,0},{5,1},{6,2},{7,3},{8,12},{9,13},{10,... | collective-permute-start | bytes 884744 | tf_op jit(solution)/shard_map/ppermute | solution.py:646
  92.3 8.0 %collective-permute-start.35 = (bf16[192,768]{1,0:T(8,128)(2,1)S(1)}, bf16[192,768]{1,0:T(8,128)(2,1)S(1)}, u32[]{:S(2)}, u32[]{:S(2)}) collective-permute-start(bf16[192,768]{1,0:T(8,128)(2,1)S(1)} %collective-permute-done.31.rest_1_), channel_id=1, source_target_pairs={{0,1},{1,0},{2,3},{3,2},{4,5},{5,4},{6,7},{7,6},{8,9},{9,8},{10,11... | collective-permute-start | bytes 884744 | tf_op jit(solution)/shard_map/ppermute | solution.py:646
  92.5 9.3 %collective-permute-start.40 = (bf16[192,768]{1,0:T(8,128)(2,1)S(1)}, bf16[192,768]{1,0:T(8,128)(2,1)S(1)}, u32[]{:S(2)}, u32[]{:S(2)}) collective-permute-start(bf16[192,768]{1,0:T(8,128)(2,1)S(1)} %collective-permute-done.39.rest_10_), channel_id=1, source_target_pairs={{0,2},{1,3},{2,0},{3,1},{4,6},{5,7},{6,4},{7,5},{8,10},{9,11},{10,... | collective-permute-start | bytes 884744 | tf_op jit(solution)/shard_map/ppermute | solution.py:646
  93.9 8.1 %collective-permute-start.43 = (bf16[192,768]{1,0:T(8,128)(2,1)S(1)}, bf16[192,768]{1,0:T(8,128)(2,1)S(1)}, u32[]{:S(2)}, u32[]{:S(2)}) collective-permute-start(bf16[192,768]{1,0:T(8,128)(2,1)S(1)} %collective-permute-done.39.rest_10_), channel_id=1, source_target_pairs={{0,1},{1,0},{2,3},{3,2},{4,5},{5,4},{6,7},{7,6},{8,9},{9,8},{10,11... | collective-permute-start | bytes 884744 | tf_op jit(solution)/shard_map/ppermute | solution.py:646
  94.0 7.8 %collective-permute-start.36 = (bf16[192,768]{1,0:T(8,128)(2,1)S(1)}, bf16[192,768]{1,0:T(8,128)(2,1)S(1)}, u32[]{:S(2)}, u32[]{:S(2)}) collective-permute-start(bf16[192,768]{1,0:T(8,128)(2,1)S(1)} %collective-permute-done.32.rest_2_), channel_id=1, source_target_pairs={{0,1},{1,0},{2,3},{3,2},{4,5},{5,4},{6,7},{7,6},{8,9},{9,8},{10,11... | collective-permute-start | bytes 884744 | tf_op jit(solution)/shard_map/ppermute | solution.py:646
  121.4 9.0 %collective-permute-start.45 = (bf16[4,384,768]{2,1,0:T(8,128)(2,1)S(1)}, bf16[4,384,768]{2,1,0:T(8,128)(2,1)S(1)}, u32[]{:S(2)}, u32[]{:S(2)}) collective-permute-start(bf16[4,384,768]{2,1,0:T(8,128)(2,1)S(1)} %get-tuple-element.145), channel_id=1, source_target_pairs={{0,1},{1,0},{2,3},{3,2},{4,5},{5,4},{6,7},{7,6},{8,9},{9,8},{10,11... | collective-permute-start | bytes 7077896 | tf_op jit(solution)/shard_map/ppermute | solution.py:646
  138.4 21.4 %collective-permute-start.48 = (bf16[4,96,3072]{2,1,0:T(8,128)(2,1)S(1)}, bf16[4,96,3072]{2,1,0:T(8,128)(2,1)S(1)}, u32[]{:S(2)}, u32[]{:S(2)}) collective-permute-start(bf16[4,96,3072]{2,1,0:T(8,128)(2,1)S(1)} %get-tuple-element.153), channel_id=1, source_target_pairs={{0,1},{1,0},{2,3},{3,2},{4,5},{5,4},{6,7},{7,6},{8,9},{9,8},{10,11... | collective-permute-start | bytes 7077896 | tf_op jit(solution)/shard_map/ppermute | solution.py:646
  138.8 18.3 %collective-permute-start.46 = (bf16[2,192,768]{2,1,0:T(8,128)(2,1)S(1)}, bf16[2,192,768]{2,1,0:T(8,128)(2,1)S(1)}, u32[]{:S(2)}, u32[]{:S(2)}) collective-permute-start(bf16[2,192,768]{2,1,0:T(8,128)(2,1)S(1)} %get-tuple-element.237), channel_id=1, source_target_pairs={{0,2},{1,3},{2,0},{3,1},{4,6},{5,7},{6,4},{7,5},{8,10},{9,11},{10,... | collective-permute-start | bytes 1769480 | tf_op jit(solution)/shard_map/ppermute | solution.py:646
  140.2 16.9 %collective-permute-start.47 = (bf16[2,192,768]{2,1,0:T(8,128)(2,1)S(1)}, bf16[2,192,768]{2,1,0:T(8,128)(2,1)S(1)}, u32[]{:S(2)}, u32[]{:S(2)}) collective-permute-start(bf16[2,192,768]{2,1,0:T(8,128)(2,1)S(1)} %get-tuple-element.236), channel_id=1, source_target_pairs={{0,4},{1,5},{2,6},{3,7},{4,0},{5,1},{6,2},{7,3},{8,12},{9,13},{10,... | collective-permute-start | bytes 1769480 | tf_op jit(solution)/shard_map/ppermute | solution.py:646
  158.0 14.5 %collective-permute-start.51 = (bf16[192,768]{1,0:T(8,128)(2,1)S(1)}, bf16[192,768]{1,0:T(8,128)(2,1)S(1)}, u32[]{:S(2)}, u32[]{:S(2)}) collective-permute-start(bf16[192,768]{1,0:T(8,128)(2,1)S(1)} %get-tuple-element.235), channel_id=1, source_target_pairs={{0,2},{1,3},{2,0},{3,1},{4,6},{5,7},{6,4},{7,5},{8,10},{9,11},{10,... | collective-permute-start | bytes 884744 | tf_op jit(solution)/shard_map/ppermute | solution.py:646
  158.5 14.0 %collective-permute-start.52 = (bf16[192,768]{1,0:T(8,128)(2,1)S(1)}, bf16[192,768]{1,0:T(8,128)(2,1)S(1)}, u32[]{:S(2)}, u32[]{:S(2)}) collective-permute-start(bf16[192,768]{1,0:T(8,128)(2,1)S(1)} %get-tuple-element.234), channel_id=1, source_target_pairs={{0,4},{1,5},{2,6},{3,7},{4,0},{5,1},{6,2},{7,3},{8,12},{9,13},{10,... | collective-permute-start | bytes 884744 | tf_op jit(solution)/shard_map/ppermute | solution.py:646
  161.6 22.0 %collective-permute-start.49 = (bf16[2,48,3072]{2,1,0:T(8,128)(2,1)}, bf16[2,48,3072]{2,1,0:T(8,128)(2,1)}, u32[]{:S(2)}, u32[]{:S(2)}) collective-permute-start(bf16[2,48,3072]{2,1,0:T(8,128)(2,1)} %get-tuple-element.233), channel_id=1, source_target_pairs={{0,2},{1,3},{2,0},{3,1},{4,6},{5,7},{6,4},{7,5},{8,10},{9,11},{10,... | collective-permute-start | bytes 1769480 | tf_op jit(solution)/shard_map/ppermute | solution.py:646
  163.0 20.6 %collective-permute-start.50 = (bf16[2,48,3072]{2,1,0:T(8,128)(2,1)}, bf16[2,48,3072]{2,1,0:T(8,128)(2,1)}, u32[]{:S(2)}, u32[]{:S(2)}) collective-permute-start(bf16[2,48,3072]{2,1,0:T(8,128)(2,1)} %get-tuple-element.232), channel_id=1, source_target_pairs={{0,4},{1,5},{2,6},{3,7},{4,0},{5,1},{6,2},{7,3},{8,12},{9,13},{10,... | collective-permute-start | bytes 1769480 | tf_op jit(solution)/shard_map/ppermute | solution.py:646
  178.8 19.4 %collective-permute-start.55 = (bf16[4,96,1920]{2,1,0:T(8,128)(2,1)}, bf16[4,96,1920]{2,1,0:T(8,128)(2,1)}, u32[]{:S(2)}, u32[]{:S(2)}) collective-permute-start(bf16[4,96,1920]{2,1,0:T(8,128)(2,1)} %get-tuple-element.170), channel_id=1, source_target_pairs={{0,1},{1,0},{2,3},{3,2},{4,5},{5,4},{6,7},{7,6},{8,9},{9,8},{10,11... | collective-permute-start | bytes 4423688 | tf_op jit(solution)/shard_map/ppermute | solution.py:646
  180.1 17.3 %collective-permute-start.56 = (bf16[384,768]{1,0:T(8,128)(2,1)}, bf16[384,768]{1,0:T(8,128)(2,1)S(1)}, u32[]{:S(2)}, u32[]{:S(2)}) collective-permute-start(bf16[384,768]{1,0:T(8,128)(2,1)} %pad_maximum_fusion), channel_id=1, source_target_pairs={{0,8},{24,16},{1,9},{25,17},{2,10},{26,18},{3,11},{27,19},{4,12},{... | collective-permute-start | bytes 1769480 | tf_op jit(solution)/shard_map/ppermute | solution.py:723
  185.4 18.6 %collective-permute-start.53 = (bf16[48,3072]{1,0:T(8,128)(2,1)S(1)}, bf16[48,3072]{1,0:T(8,128)(2,1)S(1)}, u32[]{:S(2)}, u32[]{:S(2)}) collective-permute-start(bf16[48,3072]{1,0:T(8,128)(2,1)S(1)} %get-tuple-element.229), channel_id=1, source_target_pairs={{0,2},{1,3},{2,0},{3,1},{4,6},{5,7},{6,4},{7,5},{8,10},{9,11},{10,... | collective-permute-start | bytes 884744 | tf_op jit(solution)/shard_map/ppermute | solution.py:646
  186.0 18.1 %collective-permute-start.54 = (bf16[48,3072]{1,0:T(8,128)(2,1)S(1)}, bf16[48,3072]{1,0:T(8,128)(2,1)S(1)}, u32[]{:S(2)}, u32[]{:S(2)}) collective-permute-start(bf16[48,3072]{1,0:T(8,128)(2,1)S(1)} %get-tuple-element.228), channel_id=1, source_target_pairs={{0,4},{1,5},{2,6},{3,7},{4,0},{5,1},{6,2},{7,3},{8,12},{9,13},{10,... | collective-permute-start | bytes 884744 | tf_op jit(solution)/shard_map/ppermute | solution.py:646
  197.5 24.0 %collective-permute-start.75 = (bf16[384,768]{1,0:T(8,128)(2,1)S(1)}, bf16[384,768]{1,0:T(8,128)(2,1)S(1)}, u32[]{:S(2)}, u32[]{:S(2)}) collective-permute-start(bf16[384,768]{1,0:T(8,128)(2,1)S(1)} %add_convert_fusion.3), channel_id=1, source_target_pairs={{8,16},{16,8},{9,17},{17,9},{10,18},{18,10},{11,19},{19,11},{12,20... | collective-permute-start | bytes 1769480 | tf_op jit(solution)/shard_map/ppermute | solution.py:728
  199.5 21.9 %collective-permute-start.57 = (bf16[2,48,1920]{2,1,0:T(8,128)(2,1)S(1)}, bf16[2,48,1920]{2,1,0:T(8,128)(2,1)S(1)}, u32[]{:S(2)}, u32[]{:S(2)}) collective-permute-start(bf16[2,48,1920]{2,1,0:T(8,128)(2,1)S(1)} %get-tuple-element.243), channel_id=1, source_target_pairs={{0,2},{1,3},{2,0},{3,1},{4,6},{5,7},{6,4},{7,5},{8,10},{9,11},{10,... | collective-permute-start | bytes 1105928 | tf_op jit(solution)/shard_map/ppermute | solution.py:646
  200.9 20.5 %collective-permute-start.58 = (bf16[2,48,1920]{2,1,0:T(8,128)(2,1)S(1)}, bf16[2,48,1920]{2,1,0:T(8,128)(2,1)S(1)}, u32[]{:S(2)}, u32[]{:S(2)}) collective-permute-start(bf16[2,48,1920]{2,1,0:T(8,128)(2,1)S(1)} %get-tuple-element.242), channel_id=1, source_target_pairs={{0,4},{1,5},{2,6},{3,7},{4,0},{5,1},{6,2},{7,3},{8,12},{9,13},{10,... | collective-permute-start | bytes 1105928 | tf_op jit(solution)/shard_map/ppermute | solution.py:646
  204.1 30.3 %collective-permute-start.64 = (bf16[4,96,1152]{2,1,0:T(8,128)(2,1)S(1)}, bf16[4,96,1152]{2,1,0:T(8,128)(2,1)S(1)}, u32[]{:S(2)}, u32[]{:S(2)}) collective-permute-start(bf16[4,96,1152]{2,1,0:T(8,128)(2,1)S(1)} %get-tuple-element.179), channel_id=1, source_target_pairs={{0,1},{1,0},{2,3},{3,2},{4,5},{5,4},{6,7},{7,6},{8,9},{9,8},{10,11... | collective-permute-start | bytes 2654216 | tf_op jit(solution)/shard_map/ppermute | solution.py:646
  206.1 27.4 %collective-permute-start.72 = (bf16[96,3072]{1,0:T(8,128)(2,1)S(1)}, bf16[96,3072]{1,0:T(8,128)(2,1)S(1)}, u32[]{:S(2)}, u32[]{:S(2)}) collective-permute-start(bf16[96,3072]{1,0:T(8,128)(2,1)S(1)} %pad_maximum_fusion.1), channel_id=1, source_target_pairs={{0,8},{24,16},{1,9},{25,17},{2,10},{26,18},{3,11},{27,19},{4,12},{... | collective-permute-start | bytes 1769480 | tf_op jit(solution)/shard_map/ppermute | solution.py:723
  222.6 6.8 %collective-permute-start.59 = (bf16[48,1920]{1,0:T(8,128)(2,1)S(1)}, bf16[48,1920]{1,0:T(8,128)(2,1)S(1)}, u32[]{:S(2)}, u32[]{:S(2)}) collective-permute-start(bf16[48,1920]{1,0:T(8,128)(2,1)S(1)} %get-tuple-element.241), channel_id=1, source_target_pairs={{0,2},{1,3},{2,0},{3,1},{4,6},{5,7},{6,4},{7,5},{8,10},{9,11},{10,... | collective-permute-start | bytes 552968 | tf_op jit(solution)/shard_map/ppermute | solution.py:646
  224.1 6.5 %collective-permute-start.60 = (bf16[48,1920]{1,0:T(8,128)(2,1)S(1)}, bf16[48,1920]{1,0:T(8,128)(2,1)S(1)}, u32[]{:S(2)}, u32[]{:S(2)}) collective-permute-start(bf16[48,1920]{1,0:T(8,128)(2,1)S(1)} %get-tuple-element.240), channel_id=1, source_target_pairs={{0,4},{1,5},{2,6},{3,7},{4,0},{5,1},{6,2},{7,3},{8,12},{9,13},{10,... | collective-permute-start | bytes 552968 | tf_op jit(solution)/shard_map/ppermute | solution.py:646
  225.0 16.8 %collective-permute-start.76 = (bf16[384,768]{1,0:T(8,128)(2,1)S(1)}, bf16[384,768]{1,0:T(8,128)(2,1)S(1)}, u32[]{:S(2)}, u32[]{:S(2)}) collective-permute-start(bf16[384,768]{1,0:T(8,128)(2,1)S(1)} %add_convert_fusion), channel_id=1, source_target_pairs={{8,0},{16,24},{9,1},{17,25},{10,2},{18,26},{11,3},{19,27},{12,4},{... | collective-permute-start | bytes 1769480 | tf_op jit(solution)/shard_map/ppermute | solution.py:733
  231.8 12.5 %collective-permute-start.61 = (bf16[96,1920]{1,0:T(8,128)(2,1)S(1)}, bf16[96,1920]{1,0:T(8,128)(2,1)S(1)}, u32[]{:S(2)}, u32[]{:S(2)}) collective-permute-start(bf16[96,1920]{1,0:T(8,128)(2,1)S(1)} %pad_maximum_fusion.3), channel_id=1, source_target_pairs={{0,8},{24,16},{1,9},{25,17},{2,10},{26,18},{3,11},{27,19},{4,12},{... | collective-permute-start | bytes 1105928 | tf_op jit(solution)/shard_map/ppermute | solution.py:723
  233.6 17.4 %collective-permute-start.73 = (bf16[96,3072]{1,0:T(8,128)(2,1)S(1)}, bf16[96,3072]{1,0:T(8,128)(2,1)S(1)}, u32[]{:S(2)}, u32[]{:S(2)}) collective-permute-start(bf16[96,3072]{1,0:T(8,128)(2,1)S(1)} %add_convert_fusion.2), channel_id=1, source_target_pairs={{8,16},{16,8},{9,17},{17,9},{10,18},{18,10},{11,19},{19,11},{12,20... | collective-permute-start | bytes 1769480 | tf_op jit(solution)/shard_map/ppermute | solution.py:728
  234.5 9.9 %collective-permute-start.65 = (bf16[2,48,1152]{2,1,0:T(8,128)(2,1)S(1)}, bf16[2,48,1152]{2,1,0:T(8,128)(2,1)S(1)}, u32[]{:S(2)}, u32[]{:S(2)}) collective-permute-start(bf16[2,48,1152]{2,1,0:T(8,128)(2,1)S(1)} %get-tuple-element.249), channel_id=1, source_target_pairs={{0,2},{1,3},{2,0},{3,1},{4,6},{5,7},{6,4},{7,5},{8,10},{9,11},{10,... | collective-permute-start | bytes 663560 | tf_op jit(solution)/shard_map/ppermute | solution.py:646
  235.2 9.1 %collective-permute-start.66 = (bf16[2,48,1152]{2,1,0:T(8,128)(2,1)S(1)}, bf16[2,48,1152]{2,1,0:T(8,128)(2,1)S(1)}, u32[]{:S(2)}, u32[]{:S(2)}) collective-permute-start(bf16[2,48,1152]{2,1,0:T(8,128)(2,1)S(1)} %get-tuple-element.248), channel_id=1, source_target_pairs={{0,4},{1,5},{2,6},{3,7},{4,0},{5,1},{6,2},{7,3},{8,12},{9,13},{10,... | collective-permute-start | bytes 663560 | tf_op jit(solution)/shard_map/ppermute | solution.py:646
  244.4 6.6 %collective-permute-start.67 = (bf16[48,1152]{1,0:T(8,128)(2,1)S(1)}, bf16[48,1152]{1,0:T(8,128)(2,1)S(1)}, u32[]{:S(2)}, u32[]{:S(2)}) collective-permute-start(bf16[48,1152]{1,0:T(8,128)(2,1)S(1)} %get-tuple-element.247), channel_id=1, source_target_pairs={{0,2},{1,3},{2,0},{3,1},{4,6},{5,7},{6,4},{7,5},{8,10},{9,11},{10,... | collective-permute-start | bytes 331784 | tf_op jit(solution)/shard_map/ppermute | solution.py:646
  247.8 9.1 %collective-permute-start.62 = (bf16[96,1920]{1,0:T(8,128)(2,1)S(1)}, bf16[96,1920]{1,0:T(8,128)(2,1)S(1)}, u32[]{:S(2)}, u32[]{:S(2)}) collective-permute-start(bf16[96,1920]{1,0:T(8,128)(2,1)S(1)} %add_convert_fusion.9), channel_id=1, source_target_pairs={{8,16},{16,8},{9,17},{17,9},{10,18},{18,10},{11,19},{19,11},{12,20... | collective-permute-start | bytes 1105928 | tf_op jit(solution)/shard_map/ppermute | solution.py:728
  251.2 6.1 %collective-permute-start.69 = (bf16[96,1152]{1,0:T(8,128)(2,1)S(1)}, bf16[96,1152]{1,0:T(8,128)(2,1)S(1)}, u32[]{:S(2)}, u32[]{:S(2)}) collective-permute-start(bf16[96,1152]{1,0:T(8,128)(2,1)S(1)} %pad_maximum_fusion.6), channel_id=1, source_target_pairs={{0,8},{24,16},{1,9},{25,17},{2,10},{26,18},{3,11},{27,19},{4,12},{... | collective-permute-start | bytes 663560 | tf_op jit(solution)/shard_map/ppermute | solution.py:723
  254.0 30.3 %collective-permute-start.74 = (bf16[96,3072]{1,0:T(8,128)(2,1)S(1)}, bf16[96,3072]{1,0:T(8,128)(2,1)}, u32[]{:S(2)}, u32[]{:S(2)}) collective-permute-start(bf16[96,3072]{1,0:T(8,128)(2,1)S(1)} %add_convert_fusion.1), channel_id=1, source_target_pairs={{8,0},{16,24},{9,1},{17,25},{10,2},{18,26},{11,3},{19,27},{12,4},{... | collective-permute-start | bytes 1769480 | tf_op jit(solution)/shard_map/ppermute | solution.py:733
  257.4 15.9 %collective-permute-start.70 = (bf16[96,1152]{1,0:T(8,128)(2,1)S(1)}, bf16[96,1152]{1,0:T(8,128)(2,1)S(1)}, u32[]{:S(2)}, u32[]{:S(2)}) collective-permute-start(bf16[96,1152]{1,0:T(8,128)(2,1)S(1)} %add_convert_fusion.17), channel_id=1, source_target_pairs={{8,16},{16,8},{9,17},{17,9},{10,18},{18,10},{11,19},{19,11},{12,20... | collective-permute-start | bytes 663560 | tf_op jit(solution)/shard_map/ppermute | solution.py:728
  258.1 15.2 %collective-permute-start.80 = (f32[12,768]{1,0:T(8,128)S(1)}, f32[12,768]{1,0:T(8,128)S(1)}, u32[]{:S(2)}, u32[]{:S(2)}) collective-permute-start(f32[12,768]{1,0:T(8,128)S(1)} %add.357), channel_id=1, source_target_pairs={{0,8},{8,0},{16,24},{24,16},{1,9},{9,1},{17,25},{25,17},{2,10},{10... | collective-permute-start | bytes 110600 | tf_op jit(solution)/shard_map/ppermute | solution.py:939
  262.4 19.8 %collective-permute-start.63 = (bf16[96,1920]{1,0:T(8,128)(2,1)S(1)}, bf16[96,1920]{1,0:T(8,128)(2,1)S(1)}, u32[]{:S(2)}, u32[]{:S(2)}) collective-permute-start(bf16[96,1920]{1,0:T(8,128)(2,1)S(1)} %add_convert_fusion.8), channel_id=1, source_target_pairs={{8,0},{16,24},{9,1},{17,25},{10,2},{18,26},{11,3},{19,27},{12,4},{... | collective-permute-start | bytes 1105928 | tf_op jit(solution)/shard_map/ppermute | solution.py:733
  273.3 15.1 %collective-permute-start.71 = (bf16[96,1152]{1,0:T(8,128)(2,1)S(1)}, bf16[96,1152]{1,0:T(8,128)(2,1)S(1)}, u32[]{:S(2)}, u32[]{:S(2)}) collective-permute-start(bf16[96,1152]{1,0:T(8,128)(2,1)S(1)} %add_convert_fusion.16), channel_id=1, source_target_pairs={{8,0},{16,24},{9,1},{17,25},{10,2},{18,26},{11,3},{19,27},{12,4},{... | collective-permute-start | bytes 663560 | tf_op jit(solution)/shard_map/ppermute | solution.py:733
  274.6 8.3 %collective-permute-start.81 = (f32[12,768]{1,0:T(8,128)S(1)}, f32[12,768]{1,0:T(8,128)S(1)}, u32[]{:S(2)}, u32[]{:S(2)}) collective-permute-start(f32[12,768]{1,0:T(8,128)S(1)} %add.358), channel_id=1, source_target_pairs={{0,16},{8,24},{16,0},{24,8},{1,17},{9,25},{17,1},{25,9},{2,18},{10... | collective-permute-start | bytes 110600 | tf_op jit(solution)/shard_map/ppermute | solution.py:942
  (92 other events, 744.6 us)

commit v3 on v2

--- a/solution.py
+++ b/solution.py
@@ -30,7 +30,7 @@
 NN = (((1,), (0,)), ((), ()))
 NT = (((1,), (1,)), ((), ()))
 TN = (((0,), (0,)), ((), ()))
-VMEM_BYTES = 24 * 1024 * 1024
+VMEM_BYTES = 20 * 1024 * 1024
 TILE = 256
 LIGHT = 1000
 
@@ -69,51 +69,43 @@
 
 
 ANY = pl.BlockSpec(memory_space=pl.ANY)
+HELD = pl.BlockSpec(memory_space=pltpu.VMEM)
+
+
+def in_vmem(array):
+    return pltpu.with_memory_space_constraint(array, pltpu.VMEM)
 
 
 def in_hbm(array):
     return pltpu.with_memory_space_constraint(array, pltpu.HBM)
 
 
-class Pieces:
-    def __init__(self, arrays, places):
+class Weight:
+    def __init__(self, arrays, shape, by_rank=False):
         self.arrays = [in_hbm(array) for array in arrays]
-        self.places = places
+        self.shape, self.by_rank = shape, by_rank
 
     def __len__(self):
         return len(self.arrays)
 
-
-def load_weight(pieces, me, refs, scratch, sem):
-    copies = []
-    for ref, place in zip(refs, pieces.places):
-        if place is None:
-            target = scratch
+    def load(self, me, refs, held, sem):
+        if len(refs) == 1:
+            copies = [pltpu.make_async_copy(refs[0], held, sem)]
         else:
-            mask, first, count = place
-            target = scratch.at[me ^ mask, pl.ds(first, count)]
-        copies.append(pltpu.make_async_copy(ref, target, sem))
-    for copy in copies:
-        copy.start()
-    for copy in copies:
-        copy.wait()
-
-
-def load_halves(halves, me, refs, scratch, sem):
-    rows = scratch.shape[1] // 2
-    copies = []
-    for number, pieces in enumerate(halves):
-        for ref, place in zip(refs[number * len(pieces) :], pieces.places):
-            at = pl.ds(number * rows, rows)
-            if place is None:
-                target = scratch.at[:, at]
-            else:
-                target = scratch.at[me ^ place[0], at]
-            copies.append(pltpu.make_async_copy(ref, target, sem))
-    for copy in copies:
-        copy.start()
-    for copy in copies:
-        copy.wait()
+            copies = []
+            for number, ref in enumerate(refs):
+                owner = me if number < 4 else me ^ 1
+                half = owner & 1
+                along = jnp.where(half == 0, 2, 4)
+                mask = (0, along, 6 - along, 6)[number % 4]
+                for core in range(2):
+                    rank = owner ^ mask ^ core
+                    target = held.at[rank, half] if self.by_rank else held.at[half, rank]
+                    copies.append(pltpu.make_async_copy(ref.at[core], target, sem))
+        for copy in copies:
+            copy.start()
+        for copy in copies:
+            copy.wait()
 
 
 def lane_sum(value):
@@ -145,23 +137,27 @@
     width = 3 * PART
 
     def kernel(s, x_ref, b_ref, *rest):
-        refs, (out_ref, w_ref, sem) = rest[:count], rest[count:]
+        refs, (out0_ref, out1_ref, w_ref, sem) = rest[:count], rest[count:]
 
         @pl.when(pl.program_id(0) == 0)
         def _():
-            load_weight(weight, s[0], refs, w_ref, sem)
-
-        w = w_ref[...].reshape(D, width)
-        out_ref[...] = (dot(x_ref[...], w, NN) + b_ref[...]).astype(bf16)
-
-    return call(
-        kernel,
-        (rows // 512,),
-        [rows_of(D, 512), whole((1, width))] + [ANY] * count,
-        rows_of(width, 512),
-        jax.ShapeDtypeStruct((rows, width), bf16),
-        [pltpu.VMEM((RANKS, SHARD, width), bf16), pltpu.SemaphoreType.DMA],
-        flops=2 * rows * D * width,
+            weight.load(s[0], refs, w_ref, sem)
+
+        for h, out_ref in enumerate((out0_ref, out1_ref)):
+            w = w_ref[h].reshape(D, width)
+            out_ref[...] = (dot(x_ref[...], w, NN) + b_ref[h : h + 1]).astype(bf16)
+
+    return call(
+        kernel,
+        (rows // TILE,),
+        [rows_of(D), whole((2, width))] + [ANY] * count,
+        [rows_of(width), rows_of(width)],
+        [
+            jax.ShapeDtypeStruct((rows, width), bf16),
+            jax.ShapeDtypeStruct((rows, width), bf16),
+        ],
+        [pltpu.VMEM(weight.shape, bf16), pltpu.SemaphoreType.DMA],
+        flops=2 * rows * D * width * 2,
         bytes_accessed=2 * (rows * D * 4 + 3 * D * D),
         name="qkv",
     )(me, tokens, bias, *weight.arrays)
@@ -222,21 +218,18 @@
 
 def feed_in(me, attended, tokens, weight, vectors, in_bias):
     rows = tokens.shape[0]
-    count = len(weight[0])
-    total = 2 * count
-    tile = 384
+    count = len(weight)
     width = (D + FF) // 2
 
     def kernel(s, o0_ref, o1_ref, x_ref, v_ref, b_ref, *rest):
-        refs = rest[:total]
-        n1_ref, inv_ref, hb_ref, f_ref, sl_ref, w0_ref, w1_ref, sem = rest[total:]
+        refs = rest[:count]
+        n1_ref, inv_ref, hb_ref, f_ref, sl_ref, w_ref, sem = rest[count:]
 
         @pl.when(pl.program_id(0) == 0)
         def _():
-            load_weight(weight[0], s[0], refs[:count], w0_ref, sem)
-            load_weight(weight[1], s[0], refs[count:], w1_ref, sem)
-
-        w_proj = w0_ref[:, :, :D].reshape(D, D)
+            weight.load(s[0], refs, w_ref, sem)
+
+        w_proj = w_ref[0, :, :, :D].reshape(D, D)
         branch = (
             dot(o0_ref[...], w_proj[:PART], NN) + dot(o1_ref[...], w_proj[PART:], NN) + v_ref[2:3, :]
         )
@@ -246,7 +239,7 @@
         low = (normed * v_ref[3:4, :] + v_ref[4:5, :]).astype(bf16)
         hb_ref[...] = low
         for j, lead, end in IN_TILES:
-            w = (w0_ref, w1_ref)[j][:, :, lead:end].reshape(D, end - lead)
+            w = w_ref[j, :, :, lead:end].reshape(D, end - lead)
             start = j * width + lead - D
             lanes = slice(start, start + end - lead)
             pre_act = dot(low, w, NN) + b_ref[:, lanes]
@@ -257,20 +250,21 @@
     return call(
         kernel,
         (rows // TILE,),
-        [rows_of(PART), rows_of(PART), rows_of(D), whole((8, D)), whole((1, FF))] + [ANY] * total,
-        [rows_of(D), rows_of(1), rows_of(D), rows_of(FF), rows_of(FF)],
+        [rows_of(PART), rows_of(PART), rows_of(D), whole((8, D)), whole((1, FF))] + [ANY] * count,
+        [rows_of(D), rows_of(1), rows_of(D), rows_of(FF), rows_of(FF), HELD],
         [
-            jax.ShapeDtypeStruct((rows, D), f32),
-            jax.ShapeDtypeStruct((rows, 1), f32),
+            pltpu.HBM((rows, D), f32),
+            pltpu.HBM((rows, 1), f32),
             jax.ShapeDtypeStruct((rows, D), bf16),
-            jax.ShapeDtypeStruct((rows, FF), bf16),
-            jax.ShapeDtypeStruct((rows, FF), bf16),
+            pltpu.VMEM((rows, FF), bf16),
+            pltpu.VMEM((rows, FF), bf16),
+            pltpu.VMEM(weight.shape, bf16),
         ],
-        [pltpu.VMEM((RANKS, SHARD, width), bf16)] * 2 + [pltpu.SemaphoreType.DMA],
+        [pltpu.SemaphoreType.DMA],
         flops=2 * rows * D * (D + FF),
         bytes_accessed=rows * (D * 10 + FF * 4) + 2 * D * (D + FF),
         name="feed_in",
-    )(me, *attended, tokens, vectors, in_bias, *weight[0].arrays, *weight[1].arrays)
+    )(me, *attended, tokens, vectors, in_bias, *weight.arrays)
 
 
 IN_TILES = ((0, 768, 1280), (0, 1280, 1920), (1, 0, 512), (1, 512, 1024), (1, 1024, 1536), (1, 1536, 1920))
@@ -278,16 +272,15 @@
 
 def feed_out(me, activated, normed_one, cotangent, weight, vectors):
     rows = activated.shape[0]
-    count = len(weight[0])
-    total = 2 * count
+    count = len(weight)
 
     def kernel(s, f_ref, n1_ref, g_ref, v_ref, *rest):
-        refs = rest[:total]
-        y_ref, dr_ref, dz_ref, sums_ref, w_ref, sem = rest[total:]
+        refs = rest[:count]
+        y_ref, dr_ref, dz_ref, sums_ref, w_ref, sem = rest[count:]
 
         @pl.when(pl.program_id(0) == 0)
         def _():
-            load_halves(weight, s[0], refs, w_ref, sem)
+            weight.load(s[0], refs, w_ref, sem)
             sums_ref[...] = jnp.zeros_like(sums_ref)
 
         branch = dot(f_ref[...], w_ref[...].reshape(FF, D), NN) + v_ref[5:6, :]
@@ -306,19 +299,20 @@
     return call(
         kernel,
         (rows // TILE,),
-        [rows_of(FF), rows_of(D), rows_of(D), whole((8, D))] + [ANY] * total,
-        [rows_of(D), rows_of(D), rows_of(D), whole((8, D))],
+        [rows_of(FF), rows_of(D), rows_of(D), whole((8, D))] + [ANY] * count,
+        [rows_of(D), rows_of(D), rows_of(D), whole((8, D)), HELD],
         [
             jax.ShapeDtypeStruct((rows, D), bf16),
-            jax.ShapeDtypeStruct((rows, D), f32),
+            pltpu.HBM((rows, D), f32),
             jax.ShapeDtypeStruct((rows, D), bf16),
             jax.ShapeDtypeStruct((8, D), f32),
+            pltpu.VMEM(weight.shape, bf16),
         ],
-        [pltpu.VMEM((RANKS, SHARD_FF, D), bf16), pltpu.SemaphoreType.DMA],
+        [pltpu.SemaphoreType.DMA],
         flops=2 * rows * D * FF,
         bytes_accessed=rows * (D * 14 + FF * 2) + 2 * D * FF,
         name="feed_out",
-    )(me, activated, normed_one, cotangent, vectors, *weight[0].arrays, *weight[1].arrays)
+    )(me, in_vmem(activated), in_hbm(normed_one), cotangent, vectors, *weight.arrays)
 
 
 def grad_w_out(me, activated, grad_ffn):
@@ -332,7 +326,7 @@
         m_ref[0] = jnp.where(even, low, high)
         t_ref[0] = jnp.where(even, high, low)
 
-    shape = jax.ShapeDtypeStruct((half, SHARD_FF, D), bf16)
+    shape = pltpu.HBM((half, SHARD_FF, D), bf16)
     out = pl.BlockSpec((1, SHARD_FF, D), lambda i, s: (i, 0, 0))
     return call(
         kernel,
@@ -346,21 +340,15 @@
         flops=2 * rows * D * FF,
         bytes_accessed=rows * (D * 2 + FF * 2) + 2 * D * FF,
         name="grad_w_out",
-    )(me, activated, grad_ffn)
+    )(me, in_vmem(activated), grad_ffn)
 
 
 def back_out(me, grad_ffn, slope, weight):
     rows = grad_ffn.shape[0]
-    count = len(weight[0])
-    total = 2 * count
-
-    def kernel(s, dz_ref, sl_ref, *rest):
-        refs = rest[:total]
-        du_ref, sums_ref, w_ref, sem = rest[total:]
-
+
+    def kernel(s, dz_ref, sl_ref, w_ref, du_ref, sums_ref):
         @pl.when(pl.program_id(0) == 0)
         def _():
-            load_halves(weight, s[0], refs, w_ref, sem)
             sums_ref[...] = jnp.zeros_like(sums_ref)
 
         dz = dz_ref[...]
@@ -375,36 +363,30 @@
     return call(
         kernel,
         (rows // TILE,),
-        [rows_of(D), rows_of(FF)] + [ANY] * total,
+        [rows_of(D), rows_of(FF), HELD],
         [rows_of(FF), whole((1, FF))],
         [jax.ShapeDtypeStruct((rows, FF), bf16), jax.ShapeDtypeStruct((1, FF), f32)],
-        [pltpu.VMEM((RANKS, SHARD_FF, D), bf16), pltpu.SemaphoreType.DMA],
         flops=2 * rows * D * FF,
         bytes_accessed=rows * (D * 2 + FF * 4) + 2 * D * FF,
         name="back_out",
-    )(me, grad_ffn, slope, *weight[0].arrays, *weight[1].arrays)
+    )(me, grad_ffn, in_vmem(slope), in_vmem(weight))
 
 
 def back_in(me, grad_pre, grad_res_two, normed_one, inv_one, weight, vectors):
     rows = grad_pre.shape[0]
-    count = len(weight[0])
-    total = 2 * count
     width = (D + FF) // 2
 
-    def kernel(s, du_ref, dr2_ref, n1_ref, inv_ref, v_ref, *rest):
-        refs = rest[:total]
-        dr1_ref, da_ref, do0_ref, do1_ref, sums_ref, w0_ref, w1_ref, sem = rest[total:]
-
+    def kernel(
+        s, du_ref, dr2_ref, n1_ref, inv_ref, v_ref, w_ref, dr1_ref, da_ref, do0_ref, do1_ref, sums_ref
+    ):
         @pl.when(pl.program_id(0) == 0)
         def _():
-            load_weight(weight[0], s[0], refs[:count], w0_ref, sem)
-            load_weight(weight[1], s[0], refs[count:], w1_ref, sem)
             sums_ref[...] = jnp.zeros_like(sums_ref)
 
         cut = width - D
         grad_hidden = (
-            dot(du_ref[:, :cut], w0_ref[:, :, D:].reshape(D, cut), NT)
-            + dot(du_ref[:, cut:], w1_ref[...].reshape(D, width), NT)
+            dot(du_ref[:, :cut], w_ref[0, :, :, D:].reshape(D, cut), NT)
+            + dot(du_ref[:, cut:], w_ref[1].reshape(D, width), NT)
             + dr2_ref[...]
         )
         normed = n1_ref[...]
@@ -415,7 +397,7 @@
         low = grad_res.astype(bf16)
         da_ref[...] = low
         sums_ref[0:1, :] += jnp.sum(low.astype(f32), axis=0, keepdims=True)
-        w_proj = w0_ref[:, :, :D].reshape(D, D)
+        w_proj = w_ref[0, :, :, :D].reshape(D, D)
         grad_attended = dot(low, w_proj, NT).astype(bf16)
         do0_ref[...] = grad_attended[:, :PART]
         do1_ref[...] = grad_attended[:, PART:]
@@ -423,28 +405,26 @@
     return call(
         kernel,
         (rows // TILE,),
-        [rows_of(FF), rows_of(D), rows_of(D), rows_of(1), whole((8, D))] + [ANY] * total,
+        [rows_of(FF), rows_of(D), rows_of(D), rows_of(1), whole((8, D))] + [HELD],
         [rows_of(D), rows_of(D), rows_of(PART), rows_of(PART), whole((8, D))],
         [
-            jax.ShapeDtypeStruct((rows, D), f32),
+            pltpu.HBM((rows, D), f32),
             jax.ShapeDtypeStruct((rows, D), bf16),
             jax.ShapeDtypeStruct((rows, PART), bf16),
             jax.ShapeDtypeStruct((rows, PART), bf16),
             jax.ShapeDtypeStruct((8, D), f32),
         ],
-        [pltpu.VMEM((RANKS, SHARD, width), bf16)] * 2 + [pltpu.SemaphoreType.DMA],
         flops=2 * rows * D * (D + FF),
         bytes_accessed=rows * (D * 16 + FF * 2) + 2 * D * (D + FF),
         name="back_in",
     )(
         me,
         grad_pre,
-        grad_res_two,
-        normed_one,
-        inv_one,
+        in_hbm(grad_res_two),
+        in_hbm(normed_one),
+        in_hbm(inv_one),
         vectors,
-        *weight[0].arrays,
-        *weight[1].arrays,
+        in_vmem(weight),
     )
 
 
@@ -455,8 +435,8 @@
     for k in range(RANKS // 2):
         low = block[2 * k * SHARD : (2 * k + 1) * SHARD]
         high = block[(2 * k + 1) * SHARD : (2 * k + 2) * SHARD]
-        m_ref[chip ^ k, :, lanes] = jnp.where(even, low, high)
-        t_ref[chip ^ k, :, lanes] = jnp.where(even, high, low)
+        m_ref[chip ^ k, :SHARD, lanes] = jnp.where(even, low, high)
+        t_ref[chip ^ k, :SHARD, lanes] = jnp.where(even, high, low)
 
 
 def grad_w_in(me, hidden_low, grad_pre):
@@ -466,7 +446,7 @@
     def kernel(s, h_ref, du_ref, t_ref, m_ref):
         store_by_rank(s, dot(h_ref[...], du_ref[...], TN).astype(bf16), t_ref, m_ref)
 
-    shape = jax.ShapeDtypeStruct((half, SHARD, FF), bf16)
+    shape = pltpu.HBM((half, SHARD, FF), bf16)
     out = pl.BlockSpec((half, SHARD, D), lambda i, s: (0, 0, i))
     return call(
         kernel,
@@ -532,26 +512,62 @@
     )(lengths, qkv, in_hbm(weights), grad_attended)
 
 
-def grad_w_qkv(me, tokens, grad_mixed):
+EXTRA = 16
+IN_AT = 128
+
+
+def grad_w_qkv(me, tokens, grad_mixed, sums_qkv, sums_one, sums_two, sums_in):
     rows = tokens.shape[0]
     half = RANKS // 2
     width = 3 * PART
 
-    def kernel(s, x_ref, g_ref, t_ref, m_ref):
+    def kernel(s, x_ref, g_ref, q0_ref, q1_ref, one_ref, two_ref, in_ref, t_ref, m_ref):
         store_by_rank(s, dot(x_ref[...], g_ref[...], TN).astype(bf16), t_ref, m_ref)
-
-    shape = jax.ShapeDtypeStruct((half, SHARD, width), bf16)
-    out = whole((half, SHARD, width))
+        vectors = jnp.concatenate(
+            [
+                jnp.concatenate([q0_ref[0:2], q1_ref[0:2]], axis=1),
+                one_ref[0:3],
+                two_ref[0:3],
+            ],
+            axis=0,
+        )
+        even = (s[0] & 1) == 0
+        chip = s[0] >> 1
+        for k in range(half):
+            blocks = []
+            for rank in (2 * k, 2 * k + 1):
+                vec = vectors[:, rank * SHARD : (rank + 1) * SHARD]
+                vec = jnp.concatenate([vec, jnp.zeros((8, IN_AT - SHARD), f32)], axis=1)
+                bias = in_ref[:, rank * SHARD_FF : (rank + 1) * SHARD_FF]
+                bias = jnp.concatenate([bias, jnp.zeros((7, SHARD_FF), f32)], axis=0)
+                block = jnp.concatenate([vec, bias], axis=1)
+                blocks.append(jnp.concatenate([block, jnp.zeros_like(block)], axis=0).astype(bf16))
+            end = IN_AT + SHARD_FF
+            m_ref[chip ^ k, SHARD:, :end] = jnp.where(even, blocks[0], blocks[1])
+            t_ref[chip ^ k, SHARD:, :end] = jnp.where(even, blocks[1], blocks[0])
+            m_ref[chip ^ k, SHARD:, end:] = jnp.zeros((EXTRA, width - end), bf16)
+            t_ref[chip ^ k, SHARD:, end:] = jnp.zeros((EXTRA, width - end), bf16)
+
+    shape = pltpu.HBM((half, SHARD + EXTRA, width), bf16)
+    out = whole((half, SHARD + EXTRA, width))
     return call(
         kernel,
         (1,),
-        [whole((rows, D)), whole((rows, width))],
+        [
+            whole((rows, D)),
+            whole((rows, width)),
+            whole((8, PART)),
+            whole((8, PART)),
+            whole((8, D)),
+            whole((8, D)),
+            whole((1, FF)),
+        ],
         [out, out],
         [shape, shape],
         flops=2 * rows * D * width,
         bytes_accessed=rows * (D * 8) + 2 * D * width,
         name="grad_w_qkv",
-    )(me, tokens, grad_mixed)
+    )(me, tokens, grad_mixed, *sums_qkv, sums_one, sums_two, sums_in)
 
 
 def grad_w_mixed(me, tokens, grad_mixed, attended, grad_branch):
@@ -570,7 +586,7 @@
         )
         store_by_rank(s, proj, t_ref, m_ref, width)
 
-    shape = jax.ShapeDtypeStruct((half, SHARD, width + D), bf16)
+    shape = pltpu.HBM((half, SHARD, width + D), bf16)
     out = whole((half, SHARD, width + D))
     return call(
         kernel,
@@ -592,36 +608,33 @@
 
 def back_qkv(me, grad_mixed, grad_res_one, weight):
     rows = grad_res_one.shape[0]
-    count = len(weight[0])
-    total = 2 * count
+    count = len(weight)
     width = 3 * PART
 
     def kernel(s, g0_ref, g1_ref, dr_ref, *rest):
-        refs = rest[:total]
-        out_ref, w0_ref, w1_ref, sem = rest[total:]
+        refs, (out_ref, w_ref, sem) = rest[:count], rest[count:]
 
         @pl.when(pl.program_id(0) == 0)
         def _():
-            load_weight(weight[0], s[0], refs[:count], w0_ref, sem)
-            load_weight(weight[1], s[0], refs[count:], w1_ref, sem)
+            weight.load(s[0], refs, w_ref, sem)
 
         out_ref[...] = (
-            dot(g0_ref[...], w0_ref[...].reshape(D, width), NT)
-            + dot(g1_ref[...], w1_ref[...].reshape(D, width), NT)
+            dot(g0_ref[...], w_ref[0].reshape(D, width), NT)
+            + dot(g1_ref[...], w_ref[1].reshape(D, width), NT)
             + dr_ref[...]
         ).astype(bf16)
 
     return call(
         kernel,
         (rows // TILE,),
-        [rows_of(width), rows_of(width), rows_of(D)] + [ANY] * total,
+        [rows_of(width), rows_of(width), rows_of(D)] + [ANY] * count,
         rows_of(D),
         jax.ShapeDtypeStruct((rows, D), bf16),
-        [pltpu.VMEM((RANKS, SHARD, width), bf16)] * 2 + [pltpu.SemaphoreType.DMA],
+        [pltpu.VMEM(weight.shape, bf16), pltpu.SemaphoreType.DMA],
         flops=2 * rows * D * 3 * D,
         bytes_accessed=rows * D * 12 + 2 * D * 3 * D,
         name="back_qkv",
-    )(me, *grad_mixed, grad_res_one, *weight[0].arrays, *weight[1].arrays)
+    )(me, *grad_mixed, in_hbm(grad_res_one), *weight.arrays)
 
 
 def adamw_math(moment, square, gradient):
@@ -650,33 +663,41 @@
     return lax.optimization_barrier((value,) + others)[0]
 
 
+def split_swap(value, even_bit, odd_bit):
+    return lax.ppermute(
+        value, "fsdp", [(i, i ^ (odd_bit if i & 1 else even_bit)) for i in range(RANKS)]
+    )
+
+
 class Gather:
-    def __init__(self, shard, turn):
-        self.shard, self.turn = shard, turn
+    def __init__(self, halves, core):
+        first = core == 0
+        keep = jnp.where(first, halves[0], halves[1]).astype(bf16)
+        send = jnp.where(first, halves[1], halves[0]).astype(bf16)
+        self.pair = jnp.stack([keep, swap(send, 1)])
 
     def start(self, *others):
-        self.shard = after(self.shard, *others) if others else self.shard
-        self.x = swap(self.shard, 2)
-        self.y = swap(self.shard, 4)
-        return self
+        if others:
+            self.pair = after(self.pair, *others)
+        self.one = split_swap(self.pair, 2, 4)
+        self.two = split_swap(self.pair, 4, 2)
+
+    def direct(self, *others):
+        self.start(*others)
+        self.far = swap(self.pair, 6)
+
+    def cross(self, *others):
+        self.other = [swap(after(piece, *others), 1) for piece in (self.pair, self.one, self.two)]
 
     def forward(self, *others):
-        self.x, self.y = lax.optimization_barrier((self.x, self.y) + others)[:2]
-        self.far = swap(self.x if self.turn == 4 else self.y, self.turn)
-        return self
-
-    def cross(self):
-        self.mine = [self.shard, self.x, self.y, self.far]
-        self.other = [swap(piece, 1) for piece in self.mine]
-        return self
-
-    def pieces(self):
-        rows = self.shard.shape[0]
-        masks = (0, 2, 4, 6)
-        return Pieces(
-            self.mine + self.other,
-            [(m, 0, rows) for m in masks] + [(m ^ 1, 0, rows) for m in masks],
-        )
+        self.one, self.two = lax.optimization_barrier((self.one, self.two) + others)[:2]
+        self.far = split_swap(self.one, 4, 2)
+        self.other = [swap(piece, 1) for piece in (self.pair, self.one, self.two)]
+
+    def finish(self, *others):
+        self.far = after(self.far, *others)
+        self.other.append(swap(self.far, 1))
+        return [self.pair, self.one, self.two, self.far] + self.other
 
 
 def low_sum(*values):
@@ -720,8 +741,10 @@
             ],
             axis=0,
         )
+        return (self.owned,)
+
+    def line(self):
         self.near = lax.ppermute(self.owned, "rep", [(0, 1), (3, 2)])
-        return (self.owned,)
 
     def four(self, *others):
         self.near = low_sum(self.owned, after(self.near, *others))
@@ -732,6 +755,13 @@
         self.total = low_sum(self.near, after(self.across, *others))
         self.back = lax.ppermute(self.total, "rep", [(1, 0), (2, 3)])
         return (self.total,)
+
+    def all_copies(self):
+        near, across, far = [
+            lax.ppermute(self.owned, "rep", [(i, i ^ bit) for i in range(4)]).astype(f32)
+            for bit in (1, 2, 3)
+        ]
+        return (self.owned.astype(f32) + near) + (across + far)
 
     def result(self, rep_index):
         inner = (rep_index == 1) | (rep_index == 2)
@@ -775,111 +805,82 @@
     rep_index = lax.axis_index("rep")
     part = D // fsdp
     cut = (FF - D) // 2
-    low_a = [jnp.concatenate(by_head_half(w_attn, h), axis=1).astype(bf16) for h in range(2)]
-    low_b = [
-        jnp.concatenate([w_attn[:, 3 * D :], w_in[:, :cut]], axis=1).astype(bf16),
-        w_in[:, cut:].astype(bf16),
-    ]
     middle = w_out.shape[0] // 2
-    low_c = [w_out[:middle].astype(bf16), w_out[middle:].astype(bf16)]
+    halves_a = [jnp.concatenate(by_head_half(w_attn, h), axis=1) for h in range(2)]
+    halves_b = [jnp.concatenate([w_attn[:, 3 * D :], w_in[:, :cut]], axis=1), w_in[:, cut:]]
+    halves_c = [w_out[:middle], w_out[middle:]]
+    shape_a = (2, RANKS, SHARD, 3 * PART)
+    shape_b = (2, RANKS, SHARD, (D + FF) // 2)
+    shape_c = (RANKS, 2, SHARD_FF // 2, D)
     small = jnp.concatenate([vecs.reshape(1, -1), b_in.reshape(1, -1)], axis=1).astype(bf16)
     if direct:
         me = position.reshape(1)
-        a = [Gather(low, turn) for low, turn in zip(low_a, (4, 2))]
-        b = [Gather(low, turn) for low, turn in zip(low_b, (4, 2))]
-        c = [Gather(low, turn) for low, turn in zip(low_c, (4, 2))]
-        a[0].start()
-        small_all = gather_small(small, position, 0, a[0].x, a[0].y)
-        a[0].forward()
-        a[1].start(a[0].x, a[0].y)
-        small_all = gather_small(small_all, position, 1, a[0].far)
-        a[0].cross()
-        small_all = gather_small(small_all, position, 2, a[1].x, a[1].y)
-        a[1].forward(a[0].far)
-        for g in b:
-            g.start(a[1].x, a[1].y)
-        a[1].cross()
-        pieces_a = [g.pieces() for g in a]
+        core = position & 1
+        a = Gather(halves_a, core)
+        b = Gather(halves_b, core)
+        c = Gather(halves_c, core)
+        small_all = gather_small(small, position, 0)
+        a.start(small_all)
+        small_all = gather_small(small_all, position, 1)
+        a.forward(small_all)
+        small_all = gather_small(small_all, position, 2, a.one, a.two)
+        b.start(a.one, a.two)
+        weight_a = Weight(a.finish(), shape_a)
     else:
         me = jnp.zeros((1,), jnp.int32)
 
-        def gather(shard):
-            full = lax.all_gather(shard, "fsdp", axis=0, tiled=True)
-            return Pieces([full.reshape(RANKS, -1, full.shape[1])], [None])
-
-        def gather_rows(shards):
-            full = lax.all_gather(jnp.concatenate(shards, axis=0), "fsdp", axis=0, tiled=True)
-            full = full.reshape(RANKS, 2, -1, full.shape[1])
-            return [Pieces([full[:, h]], [None]) for h in range(2)]
-
-        pieces_a = [gather(low) for low in low_a]
-        pieces_b = [gather(low) for low in low_b]
-        pieces_c = gather_rows(low_c)
+        def gather(halves, shape):
+            halves = [
+                lax.all_gather(half.astype(bf16), "fsdp", axis=0, tiled=True) for half in halves
+            ]
+            return Weight([jnp.stack(halves).reshape(shape)], shape)
+
+        weight_a = gather(halves_a, shape_a)
+        weight_b = gather(halves_b, shape_b)
+        full_c = lax.all_gather(w_out.astype(bf16), "fsdp", axis=0, tiled=True)
+        weight_c = Weight([full_c.reshape(shape_c)], shape_c, by_rank=True)
         small_all = lax.all_gather(small, "fsdp", axis=0, tiled=True)
+
+    def ordered(value, *others):
+        return after(value, *others) if direct else value
+
     small_all = small_all.astype(f32)
     vectors = small_all[:, : 8 * part].reshape(fsdp, 8, part).transpose(1, 0, 2).reshape(8, D)
     in_bias = small_all[:, 8 * part :].reshape(1, FF)
-    bias = [
-        jnp.concatenate(
-            [
-                vectors[0:1, h * PART : (h + 1) * PART],
-                jnp.zeros((1, PART), f32),
-                vectors[1:2, h * PART : (h + 1) * PART],
-            ],
-            axis=1,
-        )
-        for h in range(2)
-    ]
-
-    x = after(tokens, a[1].x, a[1].y) if direct else tokens
-    qkv = [project_qkv(me, x, pieces_a[0], bias[0])]
-    x = after(tokens, qkv[0])
-    qkv.append(project_qkv(me, x, pieces_a[1], bias[1]))
+    bias = jnp.stack([vectors[0], jnp.zeros((D,), f32), vectors[1]]).reshape(3, 2, PART)
+    bias = bias.transpose(1, 0, 2).reshape(2, 3 * PART)
+
+    qkv = project_qkv(me, tokens, weight_a, bias)
     attended, weights = [None, None], [None, None]
-    attended[0], weights[0] = attention(lengths, after(qkv[0], qkv[1]))
+    attended[0], weights[0] = attention(lengths, qkv[0])
+    second = qkv[1]
     if direct:
-        for g in b:
-            g.forward(attended[0])
-        for g in c:
-            g.start(b[0].x, b[0].y, b[1].x, b[1].y)
-        for g in b:
-            g.cross()
-        pieces_b = [g.pieces() for g in b]
-        second = after(qkv[1], attended[0], b[0].x, b[0].y, b[1].x, b[1].y)
-    else:
-        second = qkv[1]
+        b.forward(attended[0])
+        c.direct(b.one, b.two)
+        second = after(second, attended[0], b.one, b.two)
     attended[1], weights[1] = attention(lengths, second)
-    normed_one, inv_one, hidden_low, activated, slope = feed_in(
-        me, attended, tokens, pieces_b, vectors, in_bias
-    )
     if direct:
-        for g in c:
-            g.forward(activated)
-            g.cross()
-        pieces_c = [g.pieces() for g in c]
-    output, grad_res_two, grad_ffn, sums_two = feed_out(
-        me, activated, normed_one, cotangent, pieces_c, vectors
-    )
-
-    def ordered(value, *others):
-        return after(value, *others) if direct else value
+        weight_b = Weight(b.finish(attended[1]), shape_b)
+    normed_one, inv_one, hidden_low, activated, slope, held_b = feed_in(
+        me, attended, tokens, weight_b, vectors, in_bias
+    )
+    if direct:
+        c.cross(activated)
+        weight_c = Weight(c.finish(), shape_c, by_rank=True)
+    output, grad_res_two, grad_ffn, sums_two, held_c = feed_out(
+        me, activated, normed_one, cotangent, weight_c, vectors
+    )
+    held_c = held_c.reshape(RANKS, SHARD_FF, D)
 
     parts_out = grad_w_out(me, activated, grad_ffn)
-    grad_pre, sums_in = back_out(me, ordered(grad_ffn, *parts_out), slope, pieces_c)
+    grad_pre, sums_in = back_out(me, ordered(grad_ffn, *parts_out), slope, held_c)
+    sent = ()
     if direct:
         r_out = Scatter(parts_out)
         sent = r_out.one(grad_pre)
-    else:
-        sent = ()
     parts_in = grad_w_in(me, hidden_low, ordered(grad_pre, *sent))
     grad_res_one, grad_branch, *grad_attended, sums_one = back_in(
-        me,
-        ordered(grad_pre, *parts_in),
-        grad_res_two,
-        normed_one,
-        inv_one,
-        pieces_b,
-        vectors,
+        me, ordered(grad_pre, *parts_in), grad_res_two, normed_one, inv_one, held_b, vectors
     )
     if direct:
         r_in = Scatter(parts_in)
@@ -889,6 +890,7 @@
     )
     if direct:
         sent = r_out.three(mixed0)
+        r_out.line()
     parts_mix = grad_w_mixed(me, tokens, ordered(mixed0, *sent), attended, grad_branch)
     if direct:
         r_mix = Scatter(parts_mix)
@@ -896,55 +898,38 @@
     mixed1, sums_q1 = attention_back(
         lengths, qkv[1], weights[1], ordered(grad_attended[1], *sent, *parts_mix)
     )
-    if direct:
-        sent = r_mix.one(mixed1) + r_out.four(mixed1)
-    parts_qkv = grad_w_qkv(me, tokens, ordered(mixed1, *sent))
-    local_vecs = jnp.concatenate(
-        [
-            jnp.concatenate([sums_q0[0:2], sums_q1[0:2]], axis=1),
-            sums_one[0:3],
-            sums_two[0:3],
-            sums_in.reshape(FF // D, D),
-        ],
-        axis=0,
-    )
+    parts_qkv = grad_w_qkv(me, tokens, mixed1, (sums_q0, sums_q1), sums_one, sums_two, sums_in)
+    sent = ()
     if direct:
         r_qkv = Scatter(parts_qkv)
         sent = r_in.three(*parts_qkv)
+        r_in.line()
+        sent = r_mix.one(*sent)
+        sent = r_out.four(*sent)
+        sent = r_qkv.one(*sent)
     grad_tokens = back_qkv(
-        me,
-        (mixed0, ordered(mixed1, *sent, *parts_qkv)),
-        grad_res_one,
-        pieces_a,
+        me, (mixed0, ordered(mixed1, *sent, *parts_qkv)), grad_res_one, weight_a
     )
     if direct:
-        r_qkv.one(grad_tokens)
-        r_mix.two(grad_tokens)
-        r_out.five(grad_tokens)
-        r_in.four(grad_tokens)
-        local_vecs = after(local_vecs, r_qkv.send_x)
-        local_vecs = local_vecs + swap(local_vecs, 1)
-        r_mix.three()
-        sent = r_qkv.two()
-        local_vecs = after(local_vecs, *sent)
-        local_vecs = local_vecs + swap(local_vecs, 2)
-        r_in.five()
-        r_mix.four()
-        sent = r_qkv.three()
-        local_vecs = after(local_vecs, *sent)
-        local_vecs = local_vecs + swap(local_vecs, 4)
-        r_mix.five()
-        sent = r_qkv.four()
-        local_vecs = after(local_vecs, *sent)
-        local_vecs = local_vecs + lax.ppermute(local_vecs, "rep", [(i, i ^ 1) for i in range(4)])
-        sent = r_qkv.five()
-        local_vecs = after(local_vecs, *sent)
-        local_vecs = local_vecs + lax.ppermute(local_vecs, "rep", [(i, i ^ 2) for i in range(4)])
-        sum_out, sum_in, sum_mix, sum_qkv = [
-            r.result(rep_index) for r in (r_out, r_in, r_mix, r_qkv)
-        ]
+        sent = r_mix.two(grad_tokens)
+        sent = r_qkv.two(*sent)
+        sent = r_in.four(*sent)
+        sent = r_out.five(*sent)
+        sent = r_mix.three(*sent)
+        r_mix.line()
+        sent = r_qkv.three(*sent)
+        r_qkv.line()
+        sent = r_in.five(*sent)
+        sent = r_mix.four(*sent)
+        sent = r_qkv.four(*sent)
+        sent = r_mix.five(*sent)
+        sent = r_qkv.five(*sent)
+        sum_qkv = r_qkv.result(rep_index)
+        sum_out, sum_in, sum_mix = [r.result(rep_index) for r in (r_out, r_in, r_mix)]
+        sum_vecs = sum_qkv[SHARD : SHARD + 8, :part]
+        sum_bin = sum_qkv[SHARD, IN_AT : IN_AT + FF // fsdp]
+        sum_qkv = sum_qkv[:SHARD]
     else:
-        local_vecs = lax.psum(local_vecs, ("fsdp", "rep"))
 
         def reduce(theirs, mine):
             full = jnp.stack([mine, theirs], axis=1)
@@ -952,18 +937,22 @@
             owned = lax.psum_scatter(full, "fsdp", scatter_dimension=0, tiled=True)
             return lax.psum(owned, "rep")
 
-        sum_out, sum_in, sum_mix, sum_qkv = [
-            reduce(*parts) for parts in (parts_out, parts_in, parts_mix, parts_qkv)
-        ]
-    sum_vecs = lax.dynamic_slice(local_vecs, (0, position * part), (8, part))
-    sum_bin = lax.dynamic_slice(local_vecs[8:].reshape(FF), (position * (FF // fsdp),), (FF // fsdp,))
+        sum_out, sum_in, sum_mix = [reduce(*parts) for parts in (parts_out, parts_in, parts_mix)]
+        sum_qkv = reduce(*[parts[:, :SHARD] for parts in parts_qkv])
+        extra = jnp.stack([parts_qkv[1][:, SHARD:], parts_qkv[0][:, SHARD:]], axis=1)
+        extra = extra.reshape(RANKS, EXTRA, 3 * PART).astype(f32)
+        extra = lax.psum(extra[:, :8], ("fsdp", "rep"))
+        all_vecs = extra[:, :, :SHARD].transpose(1, 0, 2).reshape(8, D)
+        all_bin = extra[:, 0, IN_AT : IN_AT + SHARD_FF].reshape(FF)
+        sum_vecs = lax.dynamic_slice(all_vecs, (0, position * part), (8, part))
+        sum_bin = lax.dynamic_slice(all_bin, (position * (FF // fsdp),), (FF // fsdp,))
 
     grad_out, step_out, mom_out, sq_out = adamw(m_out, v_out, sum_out)
     grad_in, step_in, mom_in, sq_in = adamw(m_in, v_in, sum_in)
     columns = []
     for k in range(3):
-        columns += [sum_mix[:, k * PART : (k + 1) * PART], sum_qkv[:, k * PART : (k + 1) * PART]]
-    sum_attn = jnp.concatenate(columns + [sum_mix[:, 3 * PART :]], axis=1)
+        columns += [sum_mix[:, k * PART : (k + 1) * PART].astype(f32), sum_qkv[:, k * PART : (k + 1) * PART].astype(f32)]
+    sum_attn = jnp.concatenate(columns + [sum_mix[:, 3 * PART :].astype(f32)], axis=1)
     grad_attn, step_attn, mom_attn, sq_attn = adamw(m_attn, v_attn, sum_attn)
     grad_bin, step_bin, mom_bin, sq_bin = adamw(m_bin, v_bin, sum_bin)
     grad_vecs, step_vecs, mom_vecs, sq_vecs = adamw(m_vecs, v_vecs, sum_vecs)

time: 296 us -> 265 us (0.90)
  starting transfers between devices: 77.6 us -> 56.2 us
  waiting for transfers between devices: 57.2 us -> 52.5 us
    ppermute x68 -> x39, starting transfers between devices: 49.6 us -> 26.3 us  [swap(): return lax.ppermute(value, 'fsdp', flip(bit))]
    ppermute x68 -> x39, waiting for transfers between devices: 36.4 us -> 18.6 us  [swap(): return lax.ppermute(value, 'fsdp', flip(bit))]
    ppermute x6 -> x12, waiting for transfers between devices: 9.88 us -> 20 us  [the longest x8 14.5 us: split_swap(): lax.ppermute(value, 'fsdp', [(i, i ^ (odd_bit if i & 1 else even_bit)) fo...]
    another operation x5 -> x7, other arithmetic: 2.81 us -> 8.52 us  [the longest x5 7.15 us: __init__(): self.pair = jnp.stack([keep, swap(send, 1)])]
    unnamed x157 -> x104, local copies, waits for them, and re-layouts: 11 us -> 5.99 us
    ppermute x4, waiting for transfers between devices: 10.9 us -> 13.9 us  [five(): self.back = lax.ppermute(self.total, 'rep', [(1, 0), (2, 3)])]
    pallas_call x4 -> x3, Pallas kernels: 19.1 us -> 16.6 us  [the longest x1 6.89 us: project_qkv(): call(kernel, (rows // TILE,), [rows_of(D), whole((2, width))] + [ANY] * c...]
    ppermute x6 -> x12, starting transfers between devices: 20 us -> 21.5 us  [the longest x4 12 us: line(): self.near = lax.ppermute(self.owned, 'rep', [(0, 1), (3, 2)])]
  transfers between devices with their start and end apart: 82 -> 59, of which waited for: 21 -> 16; matrix products, arithmetic and copies ran while one was open for 9% -> 11% of each run, Pallas kernels for 31% -> 33%
where the time goes in v3:
time: 265 us; the launch traced here: 264 us
  Pallas kernels  115 us (43%)
  starting transfers between devices  56.2 us (21%)
  waiting for transfers between devices  52.5 us (20%)
  other arithmetic  29.2 us (11%)
  local copies, waits for them, and re-layouts  9.88 us (4%)
    ppermute x39, starting transfers between devices, swap(): return lax.ppermute(value, 'fsdp', flip(bit))  26.3 us
    ppermute x39, waiting for transfers between devices, swap(): return lax.ppermute(value, 'fsdp', flip(bit))  18.6 us
    pallas_call x2, Pallas kernels, attention_back(): call(kernel, (rows // (GROUP * SEQ),), [rows_of(3 * PART, GROUP * SEQ), r...  17.4 us
    pallas_call x1, Pallas kernels, feed_in(): call(kernel, (rows // TILE,), [rows_of(PART), rows_of(PART), rows_of(D),...  16.1 us
    ppermute x8, waiting for transfers between devices, split_swap(): lax.ppermute(value, 'fsdp', [(i, i ^ (odd_bit if i & 1 else even_bit)) fo...  14.5 us
    ppermute x4, waiting for transfers between devices, five(): self.back = lax.ppermute(self.total, 'rep', [(1, 0), (2, 3)])  13.9 us
    pallas_call x1, Pallas kernels, feed_out(): call(kernel, (rows // TILE,), [rows_of(FF), rows_of(D), rows_of(D), whole...  12.6 us
    pallas_call x1, Pallas kernels, back_in(): call(kernel, (rows // TILE,), [rows_of(FF), rows_of(D), rows_of(D), rows_...  12.4 us
  transfers between devices with their start and end apart: 59, of which 16 were waited for; matrix products, arithmetic and copies ran while one was open for 11% of the time, Pallas kernels for 33%

profile of v3, /device:TPU:0, one launch (start us, length us, event | category | flops | bytes accessed | tf_op | source)
XLA Modules:
  0.0 264.3 jit_solution(2275574763342109603)
XLA Ops:
  2.7 1.3 slice_bitcast_fusion.3
  4.3 1.0 slice.279
  5.2 1.0 slice.280
  6.4 3.0 %collective-permute-start.5 = (bf16[2,96,1152]{2,1,0:T(8,128)(2,1)S(1)}, bf16[2,96,1152]{2,1,0:T(8,128)(2,1)S(1)}, u32[]{:S(2)}, u32[]{:S(2)}) collective-permute-start(bf16[2,96,1152]{2,1,0:T(8,128)(2,1)S(1)} %pad_maximum_fusion.5.rest_0_), channel_id=1, source_target_pairs={{0,4},{1,3},{2,6},{3,1},{4,0},{5,7},{6,2},{7,5},{8,12},{9,11},{10,... | collective-permute-start | bytes 1327112 | tf_op jit(solution)/shard_map/ppermute | solution.py:667
  9.4 1.5 collective-permute-start.4
  10.9 2.0 fusion.9
  13.4 6.4 %collective-permute-done.1 = bf16[2,1152]{1,0:T(2,128)(2,1)S(1)} collective-permute-done((bf16[2,1152]{1,0:T(2,128)(2,1)S(1)}, bf16[2,1152]{1,0:T(2,128)(2,1)S(1)}, u32[]{:S(2)}, u32[]{:S(2)}) %collective-permute-start.1) | collective-permute-done | bytes 4640 | tf_op jit(solution)/shard_map/ppermute | solution.py:659
  19.9 1.8 collective-permute-start.2
  23.0 2.2 pad_maximum_fusion.1.rest_0_
  25.2 1.3 collective-permute-start.9
  27.0 1.3 collective-permute-start.12
  28.3 2.1 fusion.12
  33.9 6.9 %qkv.1 = (bf16[1024,1152]{1,0:T(8,128)(2,1)S(1)}, bf16[1024,1152]{1,0:T(8,128)(2,1)S(1)}) custom-call(s32[1]{0:T(128)} %bitcast.s, bf16[1024,768]{1,0:T(8,128)(2,1)S(1)} %copy-done, f32[2,1152]{1,0:T(2,128)S(1)} %bitcast.81, bf16[2,96,1152]{2,1,0:T(8,128)(2,1)} %copy-done.11, bf16[2,96,1152]{2,1,0:T(8,128)(2,1)} %copy-done.19, ...), custom_call_target="tpu_custom_call" | custom-call | flops 3623878 | bytes 9830 | tf_op jit(solution)/shard_map/qkv/pallas_call | solution.py:150
  40.9 5.5 %attention.2 = (bf16[1024,384]{1,0:T(8,128)(2,1)S(1)}, f32[1024,768]{1,0:T(8,128)}) custom-call(s32[8]{0:T(128)S(1)} %copy-done.10, bf16[1024,1152]{1,0:T(8,128)(2,1)S(1)} %get-tuple-element.110.qkv_ref), custom_call_target="tpu_custom_call" | custom-call | flops 4000000 | bytes 6291 | tf_op jit(solution)/shard_map/attention/pallas_call | solution.py:207
  46.3 1.5 copy-done.5
  50.3 1.6 collective-permute-start.22
  52.4 5.4 %attention.3 = (bf16[1024,384]{1,0:T(8,128)(2,1)S(1)}, f32[1024,768]{1,0:T(8,128)}) custom-call(s32[8]{0:T(128)S(1)} %copy-done.10, bf16[1024,1152]{1,0:T(8,128)(2,1)S(1)} %get-tuple-element.116.qkv_ref), custom_call_target="tpu_custom_call" | custom-call | flops 4000000 | bytes 6291 | tf_op jit(solution)/shard_map/attention/pallas_call | solution.py:207
  57.9 14.4 %collective-permute-done.14.rest_3_ = bf16[2,96,1920]{2,1,0:T(8,128)(2,1)} collective-permute-done((bf16[2,96,1920]{2,1,0:T(8,128)(2,1)}, bf16[2,96,1920]{2,1,0:T(8,128)(2,1)}, u32[]{:S(2)}, u32[]{:S(2)}) %collective-permute-start.14) | collective-permute-done | bytes 737312 | tf_op jit(solution)/shard_map/ppermute | solution.py:667
  72.4 1.8 collective-permute-start.20
  75.2 16.1 %feed_in.1 = (f32[1024,768]{1,0:T(8,128)}, f32[1024,1]{1,0:T(8,128)}, bf16[1024,768]{1,0:T(8,128)(2,1)S(1)}, bf16[1024,3072]{1,0:T(8,128)(2,1)S(1)}, bf16[1024,3...) custom-call(s32[1]{0:T(128)} %bitcast.s, bf16[1024,384]{1,0:T(8,128)(2,1)S(1)} %get-tuple-element.111.o0_ref, ...), custom_call_target="tpu_custom_call" | custom-call | flops 6039797 | bytes 26345 | tf_op jit(solution)/shard_map/feed_in/pallas_call | solution.py:250
  92.1 1.6 collective-permute-done.23.rest_4_
  96.2 12.6 %feed_out.1 = (bf16[1024,768]{1,0:T(8,128)(2,1)}, f32[1024,768]{1,0:T(8,128)}, bf16[1024,768]{1,0:T(8,128)(2,1)S(1)}, f32[8,768]{1,0:T(8,128)S(1)}, bf16[8,2,192,768]{3,2,1,0:T(8,128)(2,1)S(1)}) custom-call(s32[1]{0:T(128)} %bitcast.s, bf16[1024,3072]{1,0:T(8,128)(2,1)S(1)} %get-tuple-element.119.f_ref, f32[1024,768]{1,0:T(8,128)} %get-tuple-element.120.n1_ref, ...), custom_call_target="tpu_custom_call" | custom-call | flops 4831838 | bytes 22020 | tf_op jit(solution)/shard_map/feed_out/pallas_call | solution.py:299
  108.8 7.3 %grad_w_out.1 = (bf16[4,384,768]{2,1,0:T(8,128)(2,1)}, bf16[4,384,768]{2,1,0:T(8,128)(2,1)}) custom-call(s32[1]{0:T(128)} %bitcast.s, bf16[1024,3072]{1,0:T(8,128)(2,1)S(1)} %get-tuple-element.119.f_ref, bf16[1024,768]{1,0:T(8,128)(2,1)S(1)} %get-tuple-element.130.dz_ref), custom_call_target="tpu_custom_call" | custom-call | flops 4831838 | bytes 12582 | tf_op jit(solution)/shard_map/grad_w_out/pallas_call | solution.py:331
  116.2 6.2 %back_out.1 = (bf16[1024,3072]{1,0:T(8,128)(2,1)S(1)}, f32[1,3072]{1,0:T(1,128)S(1)}) custom-call(s32[1]{0:T(128)} %bitcast.s, bf16[1024,768]{1,0:T(8,128)(2,1)S(1)} %get-tuple-element.130.dz_ref, bf16[1024,3072]{1,0:T(8,128)(2,1)S(1)} %get-tuple-element.131.sl_ref, bf16[8,384,768]{2,1,0:T(8,128)(2,1)S(1)} %bitcast.79), custom_call_target="tpu_custom_call" | custom-call | flops 4831838 | bytes 18874 | tf_op jit(solution)/shard_map/back_out/pallas_call | solution.py:363
  122.7 7.5 %grad_w_in.1 = (bf16[4,96,3072]{2,1,0:T(8,128)(2,1)}, bf16[4,96,3072]{2,1,0:T(8,128)(2,1)}) custom-call(s32[1]{0:T(128)} %bitcast.s, bf16[1024,768]{1,0:T(8,128)(2,1)S(1)} %get-tuple-element.134.h_ref, bf16[1024,3072]{1,0:T(8,128)(2,1)S(1)} %get-tuple-element.139.du_ref), custom_call_target="tpu_custom_call" | custom-call | flops 4831838 | bytes 14155 | tf_op jit(solution)/shard_map/grad_w_in/pallas_call | solution.py:451
  130.5 1.2 collective-permute-start.29
  132.6 12.4 %back_in.1 = (f32[1024,768]{1,0:T(8,128)}, bf16[1024,768]{1,0:T(8,128)(2,1)S(1)}, bf16[1024,384]{1,0:T(8,128)(2,1)S(1)}, bf16[1024,384]{1,0:T(8,128)(2,1)S(1)}, f32[8,768]{1,0:T(8,128)S(1)}) custom-call(s32[1]{0:T(128)} %bitcast.s, bf16[1024,3072]{1,0:T(8,128)(2,1)S(1)} %get-tuple-element.139.du_ref, f32[1024,768]{1,0:T(8,128)} %get-tuple-element.140.dr2_ref, ...), custom_call_target="tpu_custom_call" | custom-call | flops 6039797 | bytes 24772 | tf_op jit(solution)/shard_map/back_in/pallas_call | solution.py:405
  145.0 0.9 collective-permute-done.29
  145.9 1.2 collective-permute-done.28
  148.0 1.3 collective-permute-start.33
  149.7 1.0 collective-permute-start.32
  150.7 1.3 collective-permute-start.31
  151.9 8.6 %attention_back.2 = (bf16[1024,1152]{1,0:T(8,128)(2,1)S(1)}, f32[8,384]{1,0:T(8,128)S(1)}) custom-call(s32[8]{0:T(128)S(1)} %copy-done.10, bf16[1024,1152]{1,0:T(8,128)(2,1)S(1)} %copy-done.6, f32[1024,768]{1,0:T(8,128)} %get-tuple-element.126.p_ref, bf16[1024,384]{1,0:T(8,128)(2,1)S(1)} %get-tuple-element.148.do_ref), custom_call_target="tpu_custom_call" | custom-call | flops 7000000 | bytes 8650 | tf_op jit(solution)/shard_map/attention_back/pallas_call | solution.py:503
  160.6 1.8 fusion.6
  163.3 5.2 %grad_w_mixed.1 = (bf16[4,96,1920]{2,1,0:T(8,128)(2,1)}, bf16[4,96,1920]{2,1,0:T(8,128)(2,1)}) custom-call(s32[1]{0:T(128)} %bitcast.s, bf16[1024,768]{1,0:T(8,128)(2,1)S(1)} %copy-done, bf16[1024,1152]{1,0:T(8,128)(2,1)S(1)} %get-tuple-element.154.g_ref.g0_ref, bf16[1024,384]{1,0:T(8,128)(2,1)S(1)} %get-tuple-element.111.o0_ref, ...), custom_call_target="tpu_custom_call" | custom-call | flops 3019898 | bytes 12386 | tf_op jit(solution)/shard_map/grad_w_mixed/pallas_call | solution.py:591
  168.5 1.0 fusion.16
  169.7 1.3 collective-permute-start.39
  171.7 3.5 %collective-permute-start.36 = (bf16[384,768]{1,0:T(8,128)(2,1)}, bf16[384,768]{1,0:T(8,128)(2,1)S(1)}, u32[]{:S(2)}, u32[]{:S(2)}) collective-permute-start(bf16[384,768]{1,0:T(8,128)(2,1)} %pad_maximum_fusion.3), channel_id=1, source_target_pairs={{0,8},{24,16},{1,9},{25,17},{2,10},{26,18},{3,11},{27,19},{4,12},{... | collective-permute-start | bytes 1769480 | tf_op jit(solution)/shard_map/ppermute | solution.py:747
  175.3 1.7 copy-done.4
  176.9 8.8 %attention_back.3 = (bf16[1024,1152]{1,0:T(8,128)(2,1)S(1)}, f32[8,384]{1,0:T(8,128)S(1)}) custom-call(s32[8]{0:T(128)S(1)} %copy-done.10, bf16[1024,1152]{1,0:T(8,128)(2,1)S(1)} %copy-done.4, f32[1024,768]{1,0:T(8,128)} %get-tuple-element.150.p_ref, bf16[1024,384]{1,0:T(8,128)(2,1)S(1)} %copy-done.9), custom_call_target="tpu_custom_call" | custom-call | flops 7000000 | bytes 8650 | tf_op jit(solution)/shard_map/attention_back/pallas_call | solution.py:503
  185.8 3.6 %grad_w_qkv.1 = (bf16[4,112,1152]{2,1,0:T(8,128)(2,1)}, bf16[4,112,1152]{2,1,0:T(8,128)(2,1)}) custom-call(s32[1]{0:T(128)} %bitcast.s, bf16[1024,768]{1,0:T(8,128)(2,1)S(1)} %copy-done, bf16[1024,1152]{1,0:T(8,128)(2,1)S(1)} %get-tuple-element.173.g_ref.g1_ref, f32[8,384]{1,0:T(8,128)S(1)} %get-tuple-element.161.q0_ref, ...), custom_call_target="tpu_custom_call" | custom-call | flops 1811939 | bytes 8060 | tf_op jit(solution)/shard_map/grad_w_qkv/pallas_call | solution.py:553
  189.4 1.9 fusion.4
  191.3 1.5 collective-permute-start.45
  192.8 1.4 add_convert_fusion.10
  195.1 1.2 collective-permute-start.40
  197.4 1.4 collective-permute-start.47
  198.7 8.8 %back_qkv.1 = bf16[1024,768]{1,0:T(8,128)(2,1)} custom-call(s32[1]{0:T(128)} %bitcast.s, bf16[1024,1152]{1,0:T(8,128)(2,1)S(1)} %copy-done.2, bf16[1024,1152]{1,0:T(8,128)(2,1)S(1)} %get-tuple-element.173.g_ref.g1_ref, f32[1024,768]{1,0:T(8,128)} %get-tuple-element.174.dr_ref, bf16[2,96,1152]{2,1,0:T(8,128)(2,1)} %copy-done.11, ...), custom_call_target="tpu_custom_call" | custom-call | flops 3623878 | bytes 12976 | tf_op jit(solution)/shard_map/back_qkv/pallas_call | solution.py:627
  208.4 1.2 fusion.20
  210.8 1.3 collective-permute-start.42
  212.0 4.7 %collective-permute-done.46 = bf16[2,56,1152]{2,1,0:T(8,128)(2,1)S(1)} collective-permute-done((bf16[2,56,1152]{2,1,0:T(8,128)(2,1)S(1)}, bf16[2,56,1152]{2,1,0:T(8,128)(2,1)S(1)}, u32[]{:S(2)}, u32[]{:S(2)}) %collective-permute-start.46) | collective-permute-done | bytes 258080 | tf_op jit(solution)/shard_map/ppermute | solution.py:659
  219.5 1.3 collective-permute-start.58
  220.8 1.2 fusion.11
  222.1 5.7 %collective-permute-start.48 = (bf16[96,1920]{1,0:T(8,128)(2,1)S(1)}, bf16[96,1920]{1,0:T(8,128)(2,1)S(1)}, u32[]{:S(2)}, u32[]{:S(2)}) collective-permute-start(bf16[96,1920]{1,0:T(8,128)(2,1)S(1)} %pad_maximum_fusion.6), channel_id=1, source_target_pairs={{0,8},{24,16},{1,9},{25,17},{2,10},{26,18},{3,11},{27,19},{4,12},{... | collective-permute-start | bytes 1105928 | tf_op jit(solution)/shard_map/ppermute | solution.py:747
  228.0 1.3 collective-permute-start.53
  229.5 1.4 collective-permute-start.57
  231.0 3.6 %collective-permute-done.48 = bf16[96,1920]{1,0:T(8,128)(2,1)S(1)} collective-permute-done((bf16[96,1920]{1,0:T(8,128)(2,1)S(1)}, bf16[96,1920]{1,0:T(8,128)(2,1)S(1)}, u32[]{:S(2)}, u32[]{:S(2)}) %collective-permute-start.48) | collective-permute-done | bytes 368672 | tf_op jit(solution)/shard_map/ppermute | solution.py:747
  235.3 2.0 collective-permute-done.53
  238.1 2.5 add_divide_fusion
  240.7 1.4 collective-permute-start.54
  242.2 1.4 collective-permute-start.56
  243.7 6.3 %collective-permute-done.57 = bf16[96,3072]{1,0:T(8,128)(2,1)S(1)} collective-permute-done((bf16[96,3072]{1,0:T(8,128)(2,1)S(1)}, bf16[96,3072]{1,0:T(8,128)(2,1)S(1)}, u32[]{:S(2)}, u32[]{:S(2)}) %collective-permute-start.57) | collective-permute-done | bytes 589856 | tf_op jit(solution)/shard_map/ppermute | solution.py:756
  250.0 2.5 add_divide_fusion.1
  252.5 7.6 %collective-permute-done.56 = bf16[112,1152]{1,0:T(8,128)(2,1)S(1)} collective-permute-done((bf16[112,1152]{1,0:T(8,128)(2,1)S(1)}, bf16[112,1152]{1,0:T(8,128)(2,1)S(1)}, u32[]{:S(2)}, u32[]{:S(2)}) %collective-permute-start.56) | collective-permute-done | bytes 258080 | tf_op jit(solution)/shard_map/ppermute | solution.py:756
  261.8 2.5 add_divide_fusion.2
  (231 shorter events, 30.7 us)
Async XLA Ops:
  2.1 4.2 %collective-permute-start = (bf16[1,1152]{1,0:T(2,128)(2,1)S(1)}, bf16[1,1152]{1,0:T(2,128)(2,1)S(1)}, u32[]{:S(2)}, u32[]{:S(2)}) collective-permute-start(bf16[1,1152]{1,0:T(2,128)(2,1)S(1)} %constant_dynamic-update-slice_fusion), channel_id=1, source_target_pairs={{0,1},{1,0},{2,3},{3,2},{4,5},{5,4},{6,7},{7,6},{8,9},{9,8},{10,11... | collective-permute-start | bytes 6920 | tf_op jit(solution)/shard_map/ppermute | solution.py:659
  4.1 2.3 collective-permute-start.3
  6.4 18.8 %copy-start.11 = (bf16[2,96,1152]{2,1,0:T(8,128)(2,1)}, bf16[2,96,1152]{2,1,0:T(8,128)(2,1)S(1)}, u32[]{:S(2)}) copy-start(bf16[2,96,1152]{2,1,0:T(8,128)(2,1)S(1)} %pad_maximum_fusion.5.rest_0_) | copy-start | bytes 1327108
  6.4 15.3 %collective-permute-start.5 = (bf16[2,96,1152]{2,1,0:T(8,128)(2,1)S(1)}, bf16[2,96,1152]{2,1,0:T(8,128)(2,1)S(1)}, u32[]{:S(2)}, u32[]{:S(2)}) collective-permute-start(bf16[2,96,1152]{2,1,0:T(8,128)(2,1)S(1)} %pad_maximum_fusion.5.rest_0_), channel_id=1, source_target_pairs={{0,4},{1,3},{2,6},{3,1},{4,0},{5,7},{6,2},{7,5},{8,12},{9,11},{10,... | collective-permute-start | bytes 1327112 | tf_op jit(solution)/shard_map/ppermute | solution.py:667
  9.4 12.3 %collective-permute-start.4 = (bf16[2,96,1152]{2,1,0:T(8,128)(2,1)S(1)}, bf16[2,96,1152]{2,1,0:T(8,128)(2,1)S(1)}, u32[]{:S(2)}, u32[]{:S(2)}) collective-permute-start(bf16[2,96,1152]{2,1,0:T(8,128)(2,1)S(1)} %pad_maximum_fusion.5.rest_0_), channel_id=1, source_target_pairs={{0,2},{1,5},{2,0},{3,7},{4,6},{5,1},{6,4},{7,3},{8,10},{9,13},{10,... | collective-permute-start | bytes 1327112 | tf_op jit(solution)/shard_map/ppermute | solution.py:667
  12.9 9.4 %collective-permute-start.11 = (bf16[96,1920]{1,0:T(8,128)(2,1)S(1)}, bf16[96,1920]{1,0:T(8,128)(2,1)S(1)}, u32[]{:S(2)}, u32[]{:S(2)}) collective-permute-start(bf16[96,1920]{1,0:T(8,128)(2,1)S(1)} %get-tuple-element.236), channel_id=1, source_target_pairs={{0,1},{1,0},{2,3},{3,2},{4,5},{5,4},{6,7},{7,6},{8,9},{9,8},{10,11... | collective-permute-start | bytes 1105928 | tf_op jit(solution)/shard_map/ppermute | solution.py:659
  12.9 7.0 %collective-permute-start.1 = (bf16[2,1152]{1,0:T(2,128)(2,1)S(1)}, bf16[2,1152]{1,0:T(2,128)(2,1)S(1)}, u32[]{:S(2)}, u32[]{:S(2)}) collective-permute-start(bf16[2,1152]{1,0:T(2,128)(2,1)S(1)} %broadcast_select_fusion.2), channel_id=1, source_target_pairs={{0,2},{1,3},{2,0},{3,1},{4,6},{5,7},{6,4},{7,5},{8,10},{9,11},{10,... | collective-permute-start | bytes 13832 | tf_op jit(solution)/shard_map/ppermute | solution.py:659
  19.9 7.1 %collective-permute-start.2 = (bf16[4,1152]{1,0:T(4,128)(2,1)S(1)}, bf16[4,1152]{1,0:T(4,128)(2,1)S(1)}, u32[]{:S(2)}, u32[]{:S(2)}) collective-permute-start(bf16[4,1152]{1,0:T(4,128)(2,1)S(1)} %maximum_select_fusion.3), channel_id=1, source_target_pairs={{0,4},{1,5},{2,6},{3,7},{4,0},{5,1},{6,2},{7,3},{8,12},{9,13},{10,... | collective-permute-start | bytes 27656 | tf_op jit(solution)/shard_map/ppermute | solution.py:659
  21.7 8.8 %collective-permute-start.7 = (bf16[2,96,1152]{2,1,0:T(8,128)(2,1)S(1)}, bf16[2,96,1152]{2,1,0:T(8,128)(2,1)S(1)}, u32[]{:S(2)}, u32[]{:S(2)}) collective-permute-start(bf16[2,96,1152]{2,1,0:T(8,128)(2,1)S(1)} %pad_maximum_fusion.5.rest_0_), channel_id=1, source_target_pairs={{0,1},{1,0},{2,3},{3,2},{4,5},{5,4},{6,7},{7,6},{8,9},{9,8},{10,11... | collective-permute-start | bytes 1327112 | tf_op jit(solution)/shard_map/ppermute | solution.py:659
  21.8 8.8 %collective-permute-start.6 = (bf16[2,96,1152]{2,1,0:T(8,128)(2,1)S(1)}, bf16[2,96,1152]{2,1,0:T(8,128)(2,1)}, u32[]{:S(2)}, u32[]{:S(2)}) collective-permute-start(bf16[2,96,1152]{2,1,0:T(8,128)(2,1)S(1)} %collective-permute-done.4.rest_1_), channel_id=1, source_target_pairs={{0,4},{1,3},{2,6},{3,1},{4,0},{5,7},{6,2},{7,5},{8,12},{9,11},{10,... | collective-permute-start | bytes 1327112 | tf_op jit(solution)/shard_map/ppermute | solution.py:667
  25.2 6.2 %collective-permute-start.9 = (bf16[2,96,1152]{2,1,0:T(8,128)(2,1)S(1)}, bf16[2,96,1152]{2,1,0:T(8,128)(2,1)}, u32[]{:S(2)}, u32[]{:S(2)}) collective-permute-start(bf16[2,96,1152]{2,1,0:T(8,128)(2,1)S(1)} %collective-permute-done.5.rest_2_), channel_id=1, source_target_pairs={{0,1},{1,0},{2,3},{3,2},{4,5},{5,4},{6,7},{7,6},{8,9},{9,8},{10,11... | collective-permute-start | bytes 1327112 | tf_op jit(solution)/shard_map/ppermute | solution.py:659
  26.5 21.4 %collective-permute-start.13 = (bf16[2,96,1920]{2,1,0:T(8,128)(2,1)}, bf16[2,96,1920]{2,1,0:T(8,128)(2,1)}, u32[]{:S(2)}, u32[]{:S(2)}) collective-permute-start(bf16[2,96,1920]{2,1,0:T(8,128)(2,1)} %pad_maximum_fusion.1.rest_0_), channel_id=1, source_target_pairs={{0,4},{1,3},{2,6},{3,1},{4,0},{5,7},{6,2},{7,5},{8,12},{9,11},{10,... | collective-permute-start | bytes 2211848 | tf_op jit(solution)/shard_map/ppermute | solution.py:667
  27.0 20.9 %collective-permute-start.12 = (bf16[2,96,1920]{2,1,0:T(8,128)(2,1)}, bf16[2,96,1920]{2,1,0:T(8,128)(2,1)}, u32[]{:S(2)}, u32[]{:S(2)}) collective-permute-start(bf16[2,96,1920]{2,1,0:T(8,128)(2,1)} %pad_maximum_fusion.1.rest_0_), channel_id=1, source_target_pairs={{0,2},{1,5},{2,0},{3,7},{4,6},{5,1},{6,4},{7,3},{8,10},{9,13},{10,... | collective-permute-start | bytes 2211848 | tf_op jit(solution)/shard_map/ppermute | solution.py:667
  30.5 1.9 collective-permute-start.8
  30.6 2.6 collective-permute-start.10
  31.4 18.1 %collective-permute-start.19 = (bf16[192,768]{1,0:T(8,128)(2,1)}, bf16[192,768]{1,0:T(8,128)(2,1)S(1)}, u32[]{:S(2)}, u32[]{:S(2)}) collective-permute-start(bf16[192,768]{1,0:T(8,128)(2,1)} %get-tuple-element.238), channel_id=1, source_target_pairs={{0,1},{1,0},{2,3},{3,2},{4,5},{5,4},{6,7},{7,6},{8,9},{9,8},{10,11... | collective-permute-start | bytes 884744 | tf_op jit(solution)/shard_map/ppermute | solution.py:659
  47.8 24.4 %collective-permute-start.14 = (bf16[2,96,1920]{2,1,0:T(8,128)(2,1)}, bf16[2,96,1920]{2,1,0:T(8,128)(2,1)}, u32[]{:S(2)}, u32[]{:S(2)}) collective-permute-start(bf16[2,96,1920]{2,1,0:T(8,128)(2,1)} %collective-permute-done.12.rest_1_), channel_id=1, source_target_pairs={{0,4},{1,3},{2,6},{3,1},{4,0},{5,7},{6,2},{7,5},{8,12},{9,11},{10,... | collective-permute-start | bytes 2211848 | tf_op jit(solution)/shard_map/ppermute | solution.py:667
  48.5 23.7 %collective-permute-start.15 = (bf16[2,96,1920]{2,1,0:T(8,128)(2,1)}, bf16[2,96,1920]{2,1,0:T(8,128)(2,1)S(1)}, u32[]{:S(2)}, u32[]{:S(2)}) collective-permute-start(bf16[2,96,1920]{2,1,0:T(8,128)(2,1)} %pad_maximum_fusion.1.rest_0_), channel_id=1, source_target_pairs={{0,1},{1,0},{2,3},{3,2},{4,5},{5,4},{6,7},{7,6},{8,9},{9,8},{10,11... | collective-permute-start | bytes 2211848 | tf_op jit(solution)/shard_map/ppermute | solution.py:659
  50.3 22.0 %collective-permute-start.22 = (bf16[2,192,768]{2,1,0:T(8,128)(2,1)}, bf16[2,192,768]{2,1,0:T(8,128)(2,1)S(1)}, u32[]{:S(2)}, u32[]{:S(2)}) collective-permute-start(bf16[2,192,768]{2,1,0:T(8,128)(2,1)} %pad_maximum_fusion.2.rest_0_), channel_id=1, source_target_pairs={{0,6},{1,7},{2,4},{3,5},{4,2},{5,3},{6,0},{7,1},{8,14},{9,15},{10,... | collective-permute-start | bytes 1769480 | tf_op jit(solution)/shard_map/ppermute | solution.py:659
  51.9 22.4 %collective-permute-start.17 = (bf16[2,96,1920]{2,1,0:T(8,128)(2,1)}, bf16[2,96,1920]{2,1,0:T(8,128)(2,1)}, u32[]{:S(2)}, u32[]{:S(2)}) collective-permute-start(bf16[2,96,1920]{2,1,0:T(8,128)(2,1)} %collective-permute-done.13.rest_2_), channel_id=1, source_target_pairs={{0,1},{1,0},{2,3},{3,2},{4,5},{5,4},{6,7},{7,6},{8,9},{9,8},{10,11... | collective-permute-start | bytes 2211848 | tf_op jit(solution)/shard_map/ppermute | solution.py:659
  52.1 23.1 %collective-permute-start.16 = (bf16[2,96,1920]{2,1,0:T(8,128)(2,1)}, bf16[2,96,1920]{2,1,0:T(8,128)(2,1)}, u32[]{:S(2)}, u32[]{:S(2)}) collective-permute-start(bf16[2,96,1920]{2,1,0:T(8,128)(2,1)} %collective-permute-done.12.rest_1_), channel_id=1, source_target_pairs={{0,1},{1,0},{2,3},{3,2},{4,5},{5,4},{6,7},{7,6},{8,9},{9,8},{10,11... | collective-permute-start | bytes 2211848 | tf_op jit(solution)/shard_map/ppermute | solution.py:659
  72.2 3.0 %collective-permute-start.18 = (bf16[2,96,1920]{2,1,0:T(8,128)(2,1)}, bf16[2,96,1920]{2,1,0:T(8,128)(2,1)}, u32[]{:S(2)}, u32[]{:S(2)}) collective-permute-start(bf16[2,96,1920]{2,1,0:T(8,128)(2,1)} %collective-permute-done.14.rest_3_), channel_id=1, source_target_pairs={{0,1},{1,0},{2,3},{3,2},{4,5},{5,4},{6,7},{7,6},{8,9},{9,8},{10,11... | collective-permute-start | bytes 2211848 | tf_op jit(solution)/shard_map/ppermute | solution.py:659
  72.3 19.1 %collective-permute-start.21 = (bf16[2,192,768]{2,1,0:T(8,128)(2,1)}, bf16[2,192,768]{2,1,0:T(8,128)(2,1)}, u32[]{:S(2)}, u32[]{:S(2)}) collective-permute-start(bf16[2,192,768]{2,1,0:T(8,128)(2,1)} %pad_maximum_fusion.2.rest_0_), channel_id=1, source_target_pairs={{0,4},{1,3},{2,6},{3,1},{4,0},{5,7},{6,2},{7,5},{8,12},{9,11},{10,... | collective-permute-start | bytes 1769480 | tf_op jit(solution)/shard_map/ppermute | solution.py:667
  72.4 19.0 %collective-permute-start.20 = (bf16[2,192,768]{2,1,0:T(8,128)(2,1)}, bf16[2,192,768]{2,1,0:T(8,128)(2,1)}, u32[]{:S(2)}, u32[]{:S(2)}) collective-permute-start(bf16[2,192,768]{2,1,0:T(8,128)(2,1)} %pad_maximum_fusion.2.rest_0_), channel_id=1, source_target_pairs={{0,2},{1,5},{2,0},{3,7},{4,6},{5,1},{6,4},{7,3},{8,10},{9,13},{10,... | collective-permute-start | bytes 1769480 | tf_op jit(solution)/shard_map/ppermute | solution.py:667
  74.3 17.7 %collective-permute-start.26 = (bf16[2,192,768]{2,1,0:T(8,128)(2,1)}, bf16[2,192,768]{2,1,0:T(8,128)(2,1)S(1)}, u32[]{:S(2)}, u32[]{:S(2)}) collective-permute-start(bf16[2,192,768]{2,1,0:T(8,128)(2,1)} %copy-done.36), channel_id=1, source_target_pairs={{0,1},{1,0},{2,3},{3,2},{4,5},{5,4},{6,7},{7,6},{8,9},{9,8},{10,11... | collective-permute-start | bytes 1769480 | tf_op jit(solution)/shard_map/ppermute | solution.py:659
  75.2 21.0 %copy-start.7 = (bf16[1024,768]{1,0:T(8,128)(2,1)S(1)}, bf16[1024,768]{1,0:T(8,128)(2,1)}, u32[]{:S(2)}) copy-start(bf16[1024,768]{1,0:T(8,128)(2,1)} %g_ref.1) | copy-start | bytes 4718596
  91.4 2.3 collective-permute-start.23
  91.5 3.0 %collective-permute-start.24 = (bf16[2,192,768]{2,1,0:T(8,128)(2,1)}, bf16[2,192,768]{2,1,0:T(8,128)(2,1)S(1)}, u32[]{:S(2)}, u32[]{:S(2)}) collective-permute-start(bf16[2,192,768]{2,1,0:T(8,128)(2,1)} %collective-permute-done.20.rest_1_), channel_id=1, source_target_pairs={{0,1},{1,0},{2,3},{3,2},{4,5},{5,4},{6,7},{7,6},{8,9},{9,8},{10,11... | collective-permute-start | bytes 1769480 | tf_op jit(solution)/shard_map/ppermute | solution.py:659
  92.0 3.4 %collective-permute-start.25 = (bf16[2,192,768]{2,1,0:T(8,128)(2,1)}, bf16[2,192,768]{2,1,0:T(8,128)(2,1)S(1)}, u32[]{:S(2)}, u32[]{:S(2)}) collective-permute-start(bf16[2,192,768]{2,1,0:T(8,128)(2,1)} %collective-permute-done.21.rest_2_), channel_id=1, source_target_pairs={{0,1},{1,0},{2,3},{3,2},{4,5},{5,4},{6,7},{7,6},{8,9},{9,8},{10,11... | collective-permute-start | bytes 1769480 | tf_op jit(solution)/shard_map/ppermute | solution.py:659
  116.0 6.3 %collective-permute-start.27 = (bf16[4,384,768]{2,1,0:T(8,128)(2,1)}, bf16[4,384,768]{2,1,0:T(8,128)(2,1)S(1)}, u32[]{:S(2)}, u32[]{:S(2)}) collective-permute-start(bf16[4,384,768]{2,1,0:T(8,128)(2,1)} %get-tuple-element.128), channel_id=1, source_target_pairs={{0,1},{1,0},{2,3},{3,2},{4,5},{5,4},{6,7},{7,6},{8,9},{9,8},{10,11... | collective-permute-start | bytes 7077896 | tf_op jit(solution)/shard_map/ppermute | solution.py:659
  122.4 24.7 %copy-start.17 = (bf16[4,384,768]{2,1,0:T(8,128)(2,1)}, bf16[4,384,768]{2,1,0:T(8,128)(2,1)S(1)}, u32[]{:S(2)}) copy-start(bf16[4,384,768]{2,1,0:T(8,128)(2,1)S(1)} %collective-permute-done.27) | copy-start | bytes 7077892
  130.2 19.1 %collective-permute-start.30 = (bf16[4,96,3072]{2,1,0:T(8,128)(2,1)}, bf16[4,96,3072]{2,1,0:T(8,128)(2,1)S(1)}, u32[]{:S(2)}, u32[]{:S(2)}) collective-permute-start(bf16[4,96,3072]{2,1,0:T(8,128)(2,1)} %get-tuple-element.137), channel_id=1, source_target_pairs={{0,1},{1,0},{2,3},{3,2},{4,5},{5,4},{6,7},{7,6},{8,9},{9,8},{10,11... | collective-permute-start | bytes 7077896 | tf_op jit(solution)/shard_map/ppermute | solution.py:659
  130.5 15.4 %collective-permute-start.29 = (bf16[2,192,768]{2,1,0:T(8,128)(2,1)S(1)}, bf16[2,192,768]{2,1,0:T(8,128)(2,1)S(1)}, u32[]{:S(2)}, u32[]{:S(2)}) collective-permute-start(bf16[2,192,768]{2,1,0:T(8,128)(2,1)S(1)} %get-tuple-element.221), channel_id=1, source_target_pairs={{0,4},{1,5},{2,6},{3,7},{4,0},{5,1},{6,2},{7,3},{8,12},{9,13},{10,... | collective-permute-start | bytes 1769480 | tf_op jit(solution)/shard_map/ppermute | solution.py:659
  131.8 15.3 %collective-permute-start.28 = (bf16[2,192,768]{2,1,0:T(8,128)(2,1)S(1)}, bf16[2,192,768]{2,1,0:T(8,128)(2,1)S(1)}, u32[]{:S(2)}, u32[]{:S(2)}) collective-permute-start(bf16[2,192,768]{2,1,0:T(8,128)(2,1)S(1)} %get-tuple-element.222), channel_id=1, source_target_pairs={{0,2},{1,3},{2,0},{3,1},{4,6},{5,7},{6,4},{7,5},{8,10},{9,11},{10,... | collective-permute-start | bytes 1769480 | tf_op jit(solution)/shard_map/ppermute | solution.py:659
  147.3 13.2 %collective-permute-start.34 = (bf16[192,768]{1,0:T(8,128)(2,1)S(1)}, bf16[192,768]{1,0:T(8,128)(2,1)S(1)}, u32[]{:S(2)}, u32[]{:S(2)}) collective-permute-start(bf16[192,768]{1,0:T(8,128)(2,1)S(1)} %get-tuple-element.219), channel_id=1, source_target_pairs={{0,4},{1,5},{2,6},{3,7},{4,0},{5,1},{6,2},{7,3},{8,12},{9,13},{10,... | collective-permute-start | bytes 884744 | tf_op jit(solution)/shard_map/ppermute | solution.py:659
  148.0 12.6 %collective-permute-start.33 = (bf16[192,768]{1,0:T(8,128)(2,1)S(1)}, bf16[192,768]{1,0:T(8,128)(2,1)S(1)}, u32[]{:S(2)}, u32[]{:S(2)}) collective-permute-start(bf16[192,768]{1,0:T(8,128)(2,1)S(1)} %get-tuple-element.220), channel_id=1, source_target_pairs={{0,2},{1,3},{2,0},{3,1},{4,6},{5,7},{6,4},{7,5},{8,10},{9,11},{10,... | collective-permute-start | bytes 884744 | tf_op jit(solution)/shard_map/ppermute | solution.py:659
  149.2 19.3 %copy-start.15 = (bf16[4,96,3072]{2,1,0:T(8,128)(2,1)}, bf16[4,96,3072]{2,1,0:T(8,128)(2,1)S(1)}, u32[]{:S(2)}) copy-start(bf16[4,96,3072]{2,1,0:T(8,128)(2,1)S(1)} %collective-permute-done.30) | copy-start | bytes 7077892
  149.7 18.8 %collective-permute-start.32 = (bf16[2,48,3072]{2,1,0:T(8,128)(2,1)S(1)}, bf16[2,48,3072]{2,1,0:T(8,128)(2,1)S(1)}, u32[]{:S(2)}, u32[]{:S(2)}) collective-permute-start(bf16[2,48,3072]{2,1,0:T(8,128)(2,1)S(1)} %get-tuple-element.217), channel_id=1, source_target_pairs={{0,4},{1,5},{2,6},{3,7},{4,0},{5,1},{6,2},{7,3},{8,12},{9,13},{10,... | collective-permute-start | bytes 1769480 | tf_op jit(solution)/shard_map/ppermute | solution.py:659
  150.7 17.8 %collective-permute-start.31 = (bf16[2,48,3072]{2,1,0:T(8,128)(2,1)S(1)}, bf16[2,48,3072]{2,1,0:T(8,128)(2,1)S(1)}, u32[]{:S(2)}, u32[]{:S(2)}) collective-permute-start(bf16[2,48,3072]{2,1,0:T(8,128)(2,1)S(1)} %get-tuple-element.218), channel_id=1, source_target_pairs={{0,2},{1,3},{2,0},{3,1},{4,6},{5,7},{6,4},{7,5},{8,10},{9,11},{10,... | collective-permute-start | bytes 1769480 | tf_op jit(solution)/shard_map/ppermute | solution.py:659
  168.5 24.3 %collective-permute-start.37 = (bf16[4,96,1920]{2,1,0:T(8,128)(2,1)}, bf16[4,96,1920]{2,1,0:T(8,128)(2,1)}, u32[]{:S(2)}, u32[]{:S(2)}) collective-permute-start(bf16[4,96,1920]{2,1,0:T(8,128)(2,1)} %get-tuple-element.155), channel_id=1, source_target_pairs={{0,1},{1,0},{2,3},{3,2},{4,5},{5,4},{6,7},{7,6},{8,9},{9,8},{10,11... | collective-permute-start | bytes 4423688 | tf_op jit(solution)/shard_map/ppermute | solution.py:659
  169.7 19.7 %collective-permute-start.39 = (bf16[48,3072]{1,0:T(8,128)(2,1)}, bf16[48,3072]{1,0:T(8,128)(2,1)}, u32[]{:S(2)}, u32[]{:S(2)}) collective-permute-start(bf16[48,3072]{1,0:T(8,128)(2,1)} %get-tuple-element.213), channel_id=1, source_target_pairs={{0,4},{1,5},{2,6},{3,7},{4,0},{5,1},{6,2},{7,3},{8,12},{9,13},{10,... | collective-permute-start | bytes 884744 | tf_op jit(solution)/shard_map/ppermute | solution.py:659
  171.0 18.4 %collective-permute-start.38 = (bf16[48,3072]{1,0:T(8,128)(2,1)}, bf16[48,3072]{1,0:T(8,128)(2,1)}, u32[]{:S(2)}, u32[]{:S(2)}) collective-permute-start(bf16[48,3072]{1,0:T(8,128)(2,1)} %get-tuple-element.214), channel_id=1, source_target_pairs={{0,2},{1,3},{2,0},{3,1},{4,6},{5,7},{6,4},{7,5},{8,10},{9,11},{10,... | collective-permute-start | bytes 884744 | tf_op jit(solution)/shard_map/ppermute | solution.py:659
  171.7 24.5 %collective-permute-start.36 = (bf16[384,768]{1,0:T(8,128)(2,1)}, bf16[384,768]{1,0:T(8,128)(2,1)S(1)}, u32[]{:S(2)}, u32[]{:S(2)}) collective-permute-start(bf16[384,768]{1,0:T(8,128)(2,1)} %pad_maximum_fusion.3), channel_id=1, source_target_pairs={{0,8},{24,16},{1,9},{25,17},{2,10},{26,18},{3,11},{27,19},{4,12},{... | collective-permute-start | bytes 1769480 | tf_op jit(solution)/shard_map/ppermute | solution.py:747
  189.4 7.9 %collective-permute-start.35 = (bf16[4,112,1152]{2,1,0:T(8,128)(2,1)}, bf16[4,112,1152]{2,1,0:T(8,128)(2,1)S(1)}, u32[]{:S(2)}, u32[]{:S(2)}) collective-permute-start(bf16[4,112,1152]{2,1,0:T(8,128)(2,1)} %get-tuple-element.167), channel_id=1, source_target_pairs={{0,1},{1,0},{2,3},{3,2},{4,5},{5,4},{6,7},{7,6},{8,9},{9,8},{10,11... | collective-permute-start | bytes 3096584 | tf_op jit(solution)/shard_map/ppermute | solution.py:659
  191.3 26.3 %collective-permute-start.45 = (bf16[96,3072]{1,0:T(8,128)(2,1)S(1)}, bf16[96,3072]{1,0:T(8,128)(2,1)S(1)}, u32[]{:S(2)}, u32[]{:S(2)}) collective-permute-start(bf16[96,3072]{1,0:T(8,128)(2,1)S(1)} %pad_maximum_fusion.4), channel_id=1, source_target_pairs={{0,8},{24,16},{1,9},{25,17},{2,10},{26,18},{3,11},{27,19},{4,12},{... | collective-permute-start | bytes 1769480 | tf_op jit(solution)/shard_map/ppermute | solution.py:747
  194.2 13.3 %collective-permute-start.41 = (bf16[2,48,1920]{2,1,0:T(8,128)(2,1)S(1)}, bf16[2,48,1920]{2,1,0:T(8,128)(2,1)S(1)}, u32[]{:S(2)}, u32[]{:S(2)}) collective-permute-start(bf16[2,48,1920]{2,1,0:T(8,128)(2,1)S(1)} %get-tuple-element.227), channel_id=1, source_target_pairs={{0,4},{1,5},{2,6},{3,7},{4,0},{5,1},{6,2},{7,3},{8,12},{9,13},{10,... | collective-permute-start | bytes 1105928 | tf_op jit(solution)/shard_map/ppermute | solution.py:659
  195.1 13.3 %collective-permute-start.40 = (bf16[2,48,1920]{2,1,0:T(8,128)(2,1)S(1)}, bf16[2,48,1920]{2,1,0:T(8,128)(2,1)S(1)}, u32[]{:S(2)}, u32[]{:S(2)}) collective-permute-start(bf16[2,48,1920]{2,1,0:T(8,128)(2,1)S(1)} %get-tuple-element.228), channel_id=1, source_target_pairs={{0,2},{1,3},{2,0},{3,1},{4,6},{5,7},{6,4},{7,5},{8,10},{9,11},{10,... | collective-permute-start | bytes 1105928 | tf_op jit(solution)/shard_map/ppermute | solution.py:659
  196.4 22.3 %collective-permute-start.44 = (bf16[384,768]{1,0:T(8,128)(2,1)S(1)}, bf16[384,768]{1,0:T(8,128)(2,1)S(1)}, u32[]{:S(2)}, u32[]{:S(2)}) collective-permute-start(bf16[384,768]{1,0:T(8,128)(2,1)S(1)} %add_convert_fusion.3), channel_id=1, source_target_pairs={{8,16},{16,8},{9,17},{17,9},{10,18},{18,10},{11,19},{19,11},{12,20... | collective-permute-start | bytes 1769480 | tf_op jit(solution)/shard_map/ppermute | solution.py:751
  197.4 13.4 %collective-permute-start.47 = (bf16[2,56,1152]{2,1,0:T(8,128)(2,1)S(1)}, bf16[2,56,1152]{2,1,0:T(8,128)(2,1)S(1)}, u32[]{:S(2)}, u32[]{:S(2)}) collective-permute-start(bf16[2,56,1152]{2,1,0:T(8,128)(2,1)S(1)} %get-tuple-element.233), channel_id=1, source_target_pairs={{0,4},{1,5},{2,6},{3,7},{4,0},{5,1},{6,2},{7,3},{8,12},{9,13},{10,... | collective-permute-start | bytes 774152 | tf_op jit(solution)/shard_map/ppermute | solution.py:659
  207.5 9.2 %collective-permute-start.46 = (bf16[2,56,1152]{2,1,0:T(8,128)(2,1)S(1)}, bf16[2,56,1152]{2,1,0:T(8,128)(2,1)S(1)}, u32[]{:S(2)}, u32[]{:S(2)}) collective-permute-start(bf16[2,56,1152]{2,1,0:T(8,128)(2,1)S(1)} %get-tuple-element.234), channel_id=1, source_target_pairs={{0,2},{1,3},{2,0},{3,1},{4,6},{5,7},{6,4},{7,5},{8,10},{9,11},{10,... | collective-permute-start | bytes 774152 | tf_op jit(solution)/shard_map/ppermute | solution.py:659
  209.5 10.0 %collective-permute-start.43 = (bf16[48,1920]{1,0:T(8,128)(2,1)S(1)}, bf16[48,1920]{1,0:T(8,128)(2,1)S(1)}, u32[]{:S(2)}, u32[]{:S(2)}) collective-permute-start(bf16[48,1920]{1,0:T(8,128)(2,1)S(1)} %get-tuple-element.225), channel_id=1, source_target_pairs={{0,4},{1,5},{2,6},{3,7},{4,0},{5,1},{6,2},{7,3},{8,12},{9,13},{10,... | collective-permute-start | bytes 552968 | tf_op jit(solution)/shard_map/ppermute | solution.py:659
  210.8 10.1 %collective-permute-start.42 = (bf16[48,1920]{1,0:T(8,128)(2,1)S(1)}, bf16[48,1920]{1,0:T(8,128)(2,1)S(1)}, u32[]{:S(2)}, u32[]{:S(2)}) collective-permute-start(bf16[48,1920]{1,0:T(8,128)(2,1)S(1)} %get-tuple-element.226), channel_id=1, source_target_pairs={{0,2},{1,3},{2,0},{3,1},{4,6},{5,7},{6,4},{7,5},{8,10},{9,11},{10,... | collective-permute-start | bytes 552968 | tf_op jit(solution)/shard_map/ppermute | solution.py:659
  216.8 11.0 %collective-permute-start.51 = (bf16[56,1152]{1,0:T(8,128)(2,1)S(1)}, bf16[56,1152]{1,0:T(8,128)(2,1)S(1)}, u32[]{:S(2)}, u32[]{:S(2)}) collective-permute-start(bf16[56,1152]{1,0:T(8,128)(2,1)S(1)} %get-tuple-element.231), channel_id=1, source_target_pairs={{0,4},{1,5},{2,6},{3,7},{4,0},{5,1},{6,2},{7,3},{8,12},{9,13},{10,... | collective-permute-start | bytes 387080 | tf_op jit(solution)/shard_map/ppermute | solution.py:659
  217.6 10.2 %collective-permute-start.50 = (bf16[56,1152]{1,0:T(8,128)(2,1)S(1)}, bf16[56,1152]{1,0:T(8,128)(2,1)S(1)}, u32[]{:S(2)}, u32[]{:S(2)}) collective-permute-start(bf16[56,1152]{1,0:T(8,128)(2,1)S(1)} %get-tuple-element.232), channel_id=1, source_target_pairs={{0,2},{1,3},{2,0},{3,1},{4,6},{5,7},{6,4},{7,5},{8,10},{9,11},{10,... | collective-permute-start | bytes 387080 | tf_op jit(solution)/shard_map/ppermute | solution.py:659
  218.7 10.7 %collective-permute-start.49 = (bf16[96,3072]{1,0:T(8,128)(2,1)S(1)}, bf16[96,3072]{1,0:T(8,128)(2,1)S(1)}, u32[]{:S(2)}, u32[]{:S(2)}) collective-permute-start(bf16[96,3072]{1,0:T(8,128)(2,1)S(1)} %add_convert_fusion.2), channel_id=1, source_target_pairs={{8,16},{16,8},{9,17},{17,9},{10,18},{18,10},{11,19},{19,11},{12,20... | collective-permute-start | bytes 1769480 | tf_op jit(solution)/shard_map/ppermute | solution.py:751
  219.5 18.5 %collective-permute-start.58 = (bf16[384,768]{1,0:T(8,128)(2,1)S(1)}, bf16[384,768]{1,0:T(8,128)(2,1)S(1)}, u32[]{:S(2)}, u32[]{:S(2)}) collective-permute-start(bf16[384,768]{1,0:T(8,128)(2,1)S(1)} %add_convert_fusion.1), channel_id=1, source_target_pairs={{8,0},{16,24},{9,1},{17,25},{10,2},{18,26},{11,3},{19,27},{12,4},{... | collective-permute-start | bytes 1769480 | tf_op jit(solution)/shard_map/ppermute | solution.py:756
  222.1 12.5 %collective-permute-start.48 = (bf16[96,1920]{1,0:T(8,128)(2,1)S(1)}, bf16[96,1920]{1,0:T(8,128)(2,1)S(1)}, u32[]{:S(2)}, u32[]{:S(2)}) collective-permute-start(bf16[96,1920]{1,0:T(8,128)(2,1)S(1)} %pad_maximum_fusion.6), channel_id=1, source_target_pairs={{0,8},{24,16},{1,9},{25,17},{2,10},{26,18},{3,11},{27,19},{4,12},{... | collective-permute-start | bytes 1105928 | tf_op jit(solution)/shard_map/ppermute | solution.py:747
  228.0 9.3 %collective-permute-start.53 = (bf16[112,1152]{1,0:T(8,128)(2,1)S(1)}, bf16[112,1152]{1,0:T(8,128)(2,1)S(1)}, u32[]{:S(2)}, u32[]{:S(2)}) collective-permute-start(bf16[112,1152]{1,0:T(8,128)(2,1)S(1)} %pad_maximum_fusion.7), channel_id=1, source_target_pairs={{0,8},{24,16},{1,9},{25,17},{2,10},{26,18},{3,11},{27,19},{4,12},{... | collective-permute-start | bytes 774152 | tf_op jit(solution)/shard_map/ppermute | solution.py:747
  229.5 20.4 %collective-permute-start.57 = (bf16[96,3072]{1,0:T(8,128)(2,1)S(1)}, bf16[96,3072]{1,0:T(8,128)(2,1)S(1)}, u32[]{:S(2)}, u32[]{:S(2)}) collective-permute-start(bf16[96,3072]{1,0:T(8,128)(2,1)S(1)} %add_convert_fusion), channel_id=1, source_target_pairs={{8,0},{16,24},{9,1},{17,25},{10,2},{18,26},{11,3},{19,27},{12,4},{... | collective-permute-start | bytes 1769480 | tf_op jit(solution)/shard_map/ppermute | solution.py:756
  234.7 5.9 %collective-permute-start.52 = (bf16[96,1920]{1,0:T(8,128)(2,1)S(1)}, bf16[96,1920]{1,0:T(8,128)(2,1)S(1)}, u32[]{:S(2)}, u32[]{:S(2)}) collective-permute-start(bf16[96,1920]{1,0:T(8,128)(2,1)S(1)} %add_convert_fusion.9), channel_id=1, source_target_pairs={{8,16},{16,8},{9,17},{17,9},{10,18},{18,10},{11,19},{19,11},{12,20... | collective-permute-start | bytes 1105928 | tf_op jit(solution)/shard_map/ppermute | solution.py:751
  237.4 4.7 %collective-permute-start.55 = (bf16[112,1152]{1,0:T(8,128)(2,1)S(1)}, bf16[112,1152]{1,0:T(8,128)(2,1)S(1)}, u32[]{:S(2)}, u32[]{:S(2)}) collective-permute-start(bf16[112,1152]{1,0:T(8,128)(2,1)S(1)} %add_convert_fusion.17), channel_id=1, source_target_pairs={{8,16},{16,8},{9,17},{17,9},{10,18},{18,10},{11,19},{19,11},{12,20... | collective-permute-start | bytes 774152 | tf_op jit(solution)/shard_map/ppermute | solution.py:751
  240.7 20.8 %collective-permute-start.54 = (bf16[96,1920]{1,0:T(8,128)(2,1)S(1)}, bf16[96,1920]{1,0:T(8,128)(2,1)S(1)}, u32[]{:S(2)}, u32[]{:S(2)}) collective-permute-start(bf16[96,1920]{1,0:T(8,128)(2,1)S(1)} %add_convert_fusion.8), channel_id=1, source_target_pairs={{8,0},{16,24},{9,1},{17,25},{10,2},{18,26},{11,3},{19,27},{12,4},{... | collective-permute-start | bytes 1105928 | tf_op jit(solution)/shard_map/ppermute | solution.py:756
  242.2 18.6 %copy-start.43 = (f32[8,96]{1,0:T(8,128)S(1)}, f32[8,96]{1,0:T(8,128)}, u32[]{:S(2)}) copy-start(f32[8,96]{1,0:T(8,128)} %param.30) | copy-start | bytes 9220
  242.2 17.9 %collective-permute-start.56 = (bf16[112,1152]{1,0:T(8,128)(2,1)S(1)}, bf16[112,1152]{1,0:T(8,128)(2,1)S(1)}, u32[]{:S(2)}, u32[]{:S(2)}) collective-permute-start(bf16[112,1152]{1,0:T(8,128)(2,1)S(1)} %add_convert_fusion.16), channel_id=1, source_target_pairs={{8,0},{16,24},{9,1},{17,25},{10,2},{18,26},{11,3},{19,27},{12,4},{... | collective-permute-start | bytes 774152 | tf_op jit(solution)/shard_map/ppermute | solution.py:756
  (42 other events, 228.6 us)

commit v4 on v3

--- a/solution.py
+++ b/solution.py
@@ -30,7 +30,7 @@
 NN = (((1,), (0,)), ((), ()))
 NT = (((1,), (1,)), ((), ()))
 TN = (((0,), (0,)), ((), ()))
-VMEM_BYTES = 20 * 1024 * 1024
+VMEM_BYTES = 17 * 1024 * 1024
 TILE = 256
 LIGHT = 1000
 
@@ -39,7 +39,7 @@
     return lax.dot_general(left, right, dims, preferred_element_type=f32)
 
 
-def call(kernel, grid, in_specs, out_specs, out_shape, scratch=(), flops=0, bytes_accessed=0, name=None):
+def call(kernel, grid, in_specs, out_specs, out_shape, scratch=(), flops=0, bytes_accessed=0, name=None, aliases=None):
     return pl.pallas_call(
         kernel,
         grid_spec=pltpu.PrefetchScalarGridSpec(
@@ -50,6 +50,7 @@
             scratch_shapes=list(scratch),
         ),
         out_shape=out_shape,
+        input_output_aliases=aliases or {},
         compiler_params=pltpu.CompilerParams(
             vmem_limit_bytes=VMEM_BYTES, dimension_semantics=("arbitrary",) * len(grid)
         ),
@@ -60,8 +61,8 @@
     )
 
 
-def rows_of(width, tile=TILE):
-    return pl.BlockSpec((tile, width), lambda i, s: (i, 0))
+def rows_of(width, tile=TILE, first=0):
+    return pl.BlockSpec((tile, width), lambda i, s: (i + first, 0))
 
 
 def whole(shape):
@@ -81,9 +82,9 @@
 
 
 class Weight:
-    def __init__(self, arrays, shape, by_rank=False):
+    def __init__(self, arrays):
         self.arrays = [in_hbm(array) for array in arrays]
-        self.shape, self.by_rank = shape, by_rank
+        self.shape = (RANKS,) + self.arrays[0].shape[-2:]
 
     def __len__(self):
         return len(self.arrays)
@@ -95,13 +96,9 @@
             copies = []
             for number, ref in enumerate(refs):
                 owner = me if number < 4 else me ^ 1
-                half = owner & 1
-                along = jnp.where(half == 0, 2, 4)
-                mask = (0, along, 6 - along, 6)[number % 4]
-                for core in range(2):
-                    rank = owner ^ mask ^ core
-                    target = held.at[rank, half] if self.by_rank else held.at[half, rank]
-                    copies.append(pltpu.make_async_copy(ref.at[core], target, sem))
+                first = jnp.where((owner & 1) == 0, 2, 4)
+                rank = owner ^ (0, first, 6 - first, 6)[number % 4]
+                copies.append(pltpu.make_async_copy(ref, held.at[rank], sem))
         for copy in copies:
             copy.start()
         for copy in copies:
@@ -143,18 +140,20 @@
         def _():
             weight.load(s[0], refs, w_ref, sem)
 
+        rounded = (dot(x_ref[...], w_ref[...].reshape(D, 2 * width), NN) + b_ref[...]).astype(bf16)
         for h, out_ref in enumerate((out0_ref, out1_ref)):
-            w = w_ref[h].reshape(D, width)
-            out_ref[...] = (dot(x_ref[...], w, NN) + b_ref[h : h + 1]).astype(bf16)
+            lead = h * width
+            out_ref[:, :PART] = rounded[:, lead : lead + PART] * HDIM ** (-0.5)
+            out_ref[:, PART:] = rounded[:, lead + PART : lead + width]
 
     return call(
         kernel,
         (rows // TILE,),
-        [rows_of(D), whole((2, width))] + [ANY] * count,
+        [rows_of(D), whole((1, 2 * width))] + [ANY] * count,
         [rows_of(width), rows_of(width)],
         [
-            jax.ShapeDtypeStruct((rows, width), bf16),
-            jax.ShapeDtypeStruct((rows, width), bf16),
+            pltpu.HBM((rows, width), bf16),
+            pltpu.HBM((rows, width), bf16),
         ],
         [pltpu.VMEM(weight.shape, bf16), pltpu.SemaphoreType.DMA],
         flops=2 * rows * D * width * 2,
@@ -178,7 +177,6 @@
 
 def attention(lengths, qkv):
     rows = qkv.shape[0]
-    scale = HDIM ** (-0.5)
     wide = 2 * HDIM
 
     def kernel(s, qkv_ref, out_ref, p_ref):
@@ -192,13 +190,13 @@
                 q = qkv_ref[at, lanes]
                 k = qkv_ref[at, PART + h * wide : PART + (h + 1) * wide]
                 v = qkv_ref[at, 2 * PART + h * wide : 2 * PART + (h + 1) * wide]
-                scores = dot(q, stack_heads(k, first), NT) * scale
+                scores = dot(q, stack_heads(k, first), NT)
                 halves = []
                 for part in range(2):
                     one = jnp.where(valid, scores[:, part * SEQ : (part + 1) * SEQ], masked_score)
                     top = jnp.max(one, axis=-1, keepdims=True)
                     raised = jnp.exp(one - top)
-                    halves.append(raised / lane_sum(raised))
+                    halves.append(raised * (1.0 / lane_sum(raised)))
                 weights = jnp.concatenate(halves, axis=1)
                 p_ref[at, h * 2 * SEQ : (h + 1) * 2 * SEQ] = weights
                 out_ref[at, lanes] = dot(weights.astype(bf16), stack_heads(v, first), NN).astype(bf16)
@@ -209,65 +207,72 @@
         (rows // (GROUP * SEQ),),
         [rows_of(3 * PART, GROUP * SEQ)],
         [rows_of(PART, GROUP * SEQ), rows_of(width, GROUP * SEQ)],
-        [jax.ShapeDtypeStruct((rows, PART), bf16), pltpu.HBM((rows, width), f32)],
+        [pltpu.VMEM((rows, PART), bf16), pltpu.HBM((rows, width), f32)],
         flops=4e9,
         bytes_accessed=rows * (PART * 8 + width * 4),
         name="attention",
-    )(lengths, qkv)
-
-
-def feed_in(me, attended, tokens, weight, vectors, in_bias):
+    )(lengths, in_hbm(qkv))
+
+
+def project(me, attended, tokens, weight, vectors):
     rows = tokens.shape[0]
     count = len(weight)
-    width = (D + FF) // 2
-
-    def kernel(s, o0_ref, o1_ref, x_ref, v_ref, b_ref, *rest):
-        refs = rest[:count]
-        n1_ref, inv_ref, hb_ref, f_ref, sl_ref, w_ref, sem = rest[count:]
+
+    def kernel(s, o0_ref, o1_ref, x_ref, v_ref, *rest):
+        refs, (n1_ref, inv_ref, hb_ref, w_ref, sem) = rest[:count], rest[count:]
 
         @pl.when(pl.program_id(0) == 0)
         def _():
             weight.load(s[0], refs, w_ref, sem)
 
-        w_proj = w_ref[0, :, :, :D].reshape(D, D)
-        branch = (
-            dot(o0_ref[...], w_proj[:PART], NN) + dot(o1_ref[...], w_proj[PART:], NN) + v_ref[2:3, :]
-        )
+        both = jnp.concatenate([o0_ref[...], o1_ref[...]], axis=1)
+        branch = dot(both, w_ref[:, :, :D].reshape(D, D), NN) + v_ref[2:3, :]
         normed, inv_std = normalize(x_ref[...].astype(f32) + branch)
         n1_ref[...] = normed
         inv_ref[...] = inv_std
-        low = (normed * v_ref[3:4, :] + v_ref[4:5, :]).astype(bf16)
-        hb_ref[...] = low
-        for j, lead, end in IN_TILES:
-            w = w_ref[j, :, :, lead:end].reshape(D, end - lead)
-            start = j * width + lead - D
-            lanes = slice(start, start + end - lead)
-            pre_act = dot(low, w, NN) + b_ref[:, lanes]
-            act, slope = gelu_and_slope(pre_act)
-            f_ref[:, lanes] = act.astype(bf16)
-            sl_ref[:, lanes] = slope.astype(bf16)
+        hb_ref[...] = (normed * v_ref[3:4, :] + v_ref[4:5, :]).astype(bf16)
 
     return call(
         kernel,
         (rows // TILE,),
-        [rows_of(PART), rows_of(PART), rows_of(D), whole((8, D)), whole((1, FF))] + [ANY] * count,
-        [rows_of(D), rows_of(1), rows_of(D), rows_of(FF), rows_of(FF), HELD],
+        [rows_of(PART), rows_of(PART), rows_of(D), whole((8, D))] + [ANY] * count,
+        [rows_of(D), rows_of(1), rows_of(D), HELD],
         [
             pltpu.HBM((rows, D), f32),
             pltpu.HBM((rows, 1), f32),
-            jax.ShapeDtypeStruct((rows, D), bf16),
-            pltpu.VMEM((rows, FF), bf16),
-            pltpu.VMEM((rows, FF), bf16),
+            pltpu.VMEM((rows, D), bf16),
             pltpu.VMEM(weight.shape, bf16),
         ],
         [pltpu.SemaphoreType.DMA],
-        flops=2 * rows * D * (D + FF),
-        bytes_accessed=rows * (D * 10 + FF * 4) + 2 * D * (D + FF),
-        name="feed_in",
-    )(me, *attended, tokens, vectors, in_bias, *weight.arrays)
-
-
-IN_TILES = ((0, 768, 1280), (0, 1280, 1920), (1, 0, 512), (1, 512, 1024), (1, 1024, 1536), (1, 1536, 1920))
+        flops=2 * rows * D * D,
+        bytes_accessed=rows * D * 10 + 2 * D * (D + FF),
+        name="project",
+    )(me, *[in_vmem(half) for half in attended], tokens, vectors, *weight.arrays)
+
+
+def expand(me, hidden_low, weight, in_bias):
+    rows = hidden_low.shape[0]
+    tile = 512
+
+    def kernel(s, h_ref, b_ref, w_ref, f_ref, sl_ref):
+        low = h_ref[...]
+        for j in range(FF // tile):
+            lanes = slice(j * tile, (j + 1) * tile)
+            w = w_ref[:, :, D + j * tile : D + (j + 1) * tile].reshape(D, tile)
+            act, slope = gelu_and_slope(dot(low, w, NN) + b_ref[:, lanes])
+            f_ref[:, lanes] = act.astype(bf16)
+            sl_ref[:, lanes] = slope.astype(bf16)
+
+    return call(
+        kernel,
+        (rows // TILE,),
+        [rows_of(D), whole((1, FF)), HELD],
+        [rows_of(FF), rows_of(FF)],
+        [pltpu.VMEM((rows, FF), bf16), pltpu.VMEM((rows, FF), bf16)],
+        flops=2 * rows * D * FF,
+        bytes_accessed=rows * (D * 2 + FF * 4) + 2 * D * FF,
+        name="expand",
+    )(me, in_vmem(hidden_low), in_bias, in_vmem(weight))
 
 
 def feed_out(me, activated, normed_one, cotangent, weight, vectors):
@@ -315,6 +320,10 @@
     )(me, in_vmem(activated), in_hbm(normed_one), cotangent, vectors, *weight.arrays)
 
 
+def slot(chip, core):
+    return jnp.where(core == 0, chip, (chip & 1) * 2 + (chip >> 1))
+
+
 def grad_w_out(me, activated, grad_ffn):
     rows = activated.shape[0]
     half = RANKS // 2
@@ -327,7 +336,10 @@
         t_ref[0] = jnp.where(even, high, low)
 
     shape = pltpu.HBM((half, SHARD_FF, D), bf16)
-    out = pl.BlockSpec((1, SHARD_FF, D), lambda i, s: (i, 0, 0))
+
+    def out(flip):
+        return pl.BlockSpec((1, SHARD_FF, D), lambda i, s: (slot(i, (s[0] & 1) ^ flip), 0, 0))
+
     return call(
         kernel,
         (half,),
@@ -335,7 +347,7 @@
             pl.BlockSpec((rows, 2 * SHARD_FF), lambda i, s: (0, (s[0] >> 1) ^ i)),
             whole((rows, D)),
         ],
-        [out, out],
+        [out(1), out(0)],
         [shape, shape],
         flops=2 * rows * D * FF,
         bytes_accessed=rows * (D * 2 + FF * 2) + 2 * D * FF,
@@ -365,7 +377,7 @@
         (rows // TILE,),
         [rows_of(D), rows_of(FF), HELD],
         [rows_of(FF), whole((1, FF))],
-        [jax.ShapeDtypeStruct((rows, FF), bf16), jax.ShapeDtypeStruct((1, FF), f32)],
+        [pltpu.VMEM((rows, FF), bf16), jax.ShapeDtypeStruct((1, FF), f32)],
         flops=2 * rows * D * FF,
         bytes_accessed=rows * (D * 2 + FF * 4) + 2 * D * FF,
         name="back_out",
@@ -374,7 +386,6 @@
 
 def back_in(me, grad_pre, grad_res_two, normed_one, inv_one, weight, vectors):
     rows = grad_pre.shape[0]
-    width = (D + FF) // 2
 
     def kernel(
         s, du_ref, dr2_ref, n1_ref, inv_ref, v_ref, w_ref, dr1_ref, da_ref, do0_ref, do1_ref, sums_ref
@@ -383,12 +394,8 @@
         def _():
             sums_ref[...] = jnp.zeros_like(sums_ref)
 
-        cut = width - D
-        grad_hidden = (
-            dot(du_ref[:, :cut], w_ref[0, :, :, D:].reshape(D, cut), NT)
-            + dot(du_ref[:, cut:], w_ref[1].reshape(D, width), NT)
-            + dr2_ref[...]
-        )
+        w_in = w_ref[:, :, D:].reshape(D, FF)
+        grad_hidden = dot(du_ref[...], w_in, NT) + dr2_ref[...]
         normed = n1_ref[...]
         sums_ref[1:2, :] += jnp.sum(grad_hidden * normed, axis=0, keepdims=True)
         sums_ref[2:3, :] += jnp.sum(grad_hidden, axis=0, keepdims=True)
@@ -397,7 +404,7 @@
         low = grad_res.astype(bf16)
         da_ref[...] = low
         sums_ref[0:1, :] += jnp.sum(low.astype(f32), axis=0, keepdims=True)
-        w_proj = w_ref[0, :, :, :D].reshape(D, D)
+        w_proj = w_ref[:, :, :D].reshape(D, D)
         grad_attended = dot(low, w_proj, NT).astype(bf16)
         do0_ref[...] = grad_attended[:, :PART]
         do1_ref[...] = grad_attended[:, PART:]
@@ -409,9 +416,9 @@
         [rows_of(D), rows_of(D), rows_of(PART), rows_of(PART), whole((8, D))],
         [
             pltpu.HBM((rows, D), f32),
-            jax.ShapeDtypeStruct((rows, D), bf16),
-            jax.ShapeDtypeStruct((rows, PART), bf16),
-            jax.ShapeDtypeStruct((rows, PART), bf16),
+            pltpu.VMEM((rows, D), bf16),
+            pltpu.VMEM((rows, PART), bf16),
+            pltpu.VMEM((rows, PART), bf16),
             jax.ShapeDtypeStruct((8, D), f32),
         ],
         flops=2 * rows * D * (D + FF),
@@ -419,7 +426,7 @@
         name="back_in",
     )(
         me,
-        grad_pre,
+        in_vmem(grad_pre),
         in_hbm(grad_res_two),
         in_hbm(normed_one),
         in_hbm(inv_one),
@@ -429,14 +436,14 @@
 
 
 def store_by_rank(s, block, t_ref, m_ref, first=0):
-    even = (s[0] & 1) == 0
-    chip = s[0] >> 1
+    core = s[0] & 1
     lanes = slice(first, first + block.shape[1])
     for k in range(RANKS // 2):
         low = block[2 * k * SHARD : (2 * k + 1) * SHARD]
         high = block[(2 * k + 1) * SHARD : (2 * k + 2) * SHARD]
-        m_ref[chip ^ k, :SHARD, lanes] = jnp.where(even, low, high)
-        t_ref[chip ^ k, :SHARD, lanes] = jnp.where(even, high, low)
+        away = (s[0] >> 1) ^ k
+        m_ref[slot(away, core), :SHARD, lanes] = jnp.where(core == 0, low, high)
+        t_ref[slot(away, 1 - core), :SHARD, lanes] = jnp.where(core == 0, high, low)
 
 
 def grad_w_in(me, hidden_low, grad_pre):
@@ -457,7 +464,7 @@
         flops=2 * rows * D * FF,
         bytes_accessed=rows * (D * 4 + FF * 2) + 2 * D * FF,
         name="grad_w_in",
-    )(me, hidden_low, grad_pre)
+    )(me, in_vmem(hidden_low), in_vmem(grad_pre))
 
 
 def attention_back(lengths, qkv, weights, grad_attended):
@@ -493,7 +500,7 @@
                 grad_v = jnp.where(first, grad_v[:SEQ], grad_v[SEQ:]).astype(bf16)
                 grad_q = (dot(grad_s, stack_heads(k, first), NN) * scale).astype(bf16)
                 grad_k = dot(grad_s, q, TN)
-                grad_k = (jnp.where(first, grad_k[:SEQ], grad_k[SEQ:]) * scale).astype(bf16)
+                grad_k = jnp.where(first, grad_k[:SEQ], grad_k[SEQ:]).astype(bf16)
                 out_ref[at, lanes] = grad_q
                 out_ref[at, k_lanes] = grad_k
                 out_ref[at, v_lanes] = grad_v
@@ -505,11 +512,11 @@
         (rows // (GROUP * SEQ),),
         [rows_of(3 * PART, GROUP * SEQ), rows_of(width, GROUP * SEQ), rows_of(PART, GROUP * SEQ)],
         [rows_of(3 * PART, GROUP * SEQ), whole((8, PART))],
-        [jax.ShapeDtypeStruct((rows, 3 * PART), bf16), jax.ShapeDtypeStruct((8, PART), f32)],
+        [pltpu.VMEM((rows, 3 * PART), bf16), jax.ShapeDtypeStruct((8, PART), f32)],
         flops=7e9,
         bytes_accessed=rows * (PART * 14 + width * 4),
         name="attention_back",
-    )(lengths, qkv, in_hbm(weights), grad_attended)
+    )(lengths, in_hbm(qkv), in_hbm(weights), in_vmem(grad_attended))
 
 
 EXTRA = 16
@@ -531,8 +538,9 @@
             ],
             axis=0,
         )
-        even = (s[0] & 1) == 0
-        chip = s[0] >> 1
+        core = s[0] & 1
+        end = IN_AT + SHARD_FF
+        rest = jnp.zeros((EXTRA, width - end), bf16)
         for k in range(half):
             blocks = []
             for rank in (2 * k, 2 * k + 1):
@@ -542,11 +550,13 @@
                 bias = jnp.concatenate([bias, jnp.zeros((7, SHARD_FF), f32)], axis=0)
                 block = jnp.concatenate([vec, bias], axis=1)
                 blocks.append(jnp.concatenate([block, jnp.zeros_like(block)], axis=0).astype(bf16))
-            end = IN_AT + SHARD_FF
-            m_ref[chip ^ k, SHARD:, :end] = jnp.where(even, blocks[0], blocks[1])
-            t_ref[chip ^ k, SHARD:, :end] = jnp.where(even, blocks[1], blocks[0])
-            m_ref[chip ^ k, SHARD:, end:] = jnp.zeros((EXTRA, width - end), bf16)
-            t_ref[chip ^ k, SHARD:, end:] = jnp.zeros((EXTRA, width - end), bf16)
+            away = (s[0] >> 1) ^ k
+            for ref, here, block in (
+                (m_ref, core, jnp.where(core == 0, blocks[0], blocks[1])),
+                (t_ref, 1 - core, jnp.where(core == 0, blocks[1], blocks[0])),
+            ):
+                ref[slot(away, here), SHARD:, :end] = block
+                ref[slot(away, here), SHARD:, end:] = rest
 
     shape = pltpu.HBM((half, SHARD + EXTRA, width), bf16)
     out = whole((half, SHARD + EXTRA, width))
@@ -555,7 +565,7 @@
         (1,),
         [
             whole((rows, D)),
-            whole((rows, width)),
+            HELD,
             whole((8, PART)),
             whole((8, PART)),
             whole((8, D)),
@@ -567,7 +577,7 @@
         flops=2 * rows * D * width,
         bytes_accessed=rows * (D * 8) + 2 * D * width,
         name="grad_w_qkv",
-    )(me, tokens, grad_mixed, *sums_qkv, sums_one, sums_two, sums_in)
+    )(me, tokens, in_vmem(grad_mixed), *sums_qkv, sums_one, sums_two, sums_in)
 
 
 def grad_w_mixed(me, tokens, grad_mixed, attended, grad_branch):
@@ -577,13 +587,8 @@
 
     def kernel(s, x_ref, g_ref, o0_ref, o1_ref, da_ref, t_ref, m_ref):
         store_by_rank(s, dot(x_ref[...], g_ref[...], TN).astype(bf16), t_ref, m_ref)
-        proj = jnp.concatenate(
-            [
-                dot(o0_ref[...], da_ref[...], TN).astype(bf16),
-                dot(o1_ref[...], da_ref[...], TN).astype(bf16),
-            ],
-            axis=0,
-        )
+        both = jnp.concatenate([o0_ref[...], o1_ref[...]], axis=1)
+        proj = dot(both, da_ref[...], TN).astype(bf16)
         store_by_rank(s, proj, t_ref, m_ref, width)
 
     shape = pltpu.HBM((half, SHARD, width + D), bf16)
@@ -593,48 +598,67 @@
         (1,),
         [
             whole((rows, D)),
-            whole((rows, width)),
-            whole((rows, PART)),
-            whole((rows, PART)),
-            whole((rows, D)),
+            HELD,
+            HELD,
+            HELD,
+            HELD,
         ],
         [out, out],
         [shape, shape],
         flops=2 * rows * D * (width + D),
         bytes_accessed=rows * (D * 12) + 2 * D * (width + D),
         name="grad_w_mixed",
-    )(me, tokens, grad_mixed, *attended, grad_branch)
-
-
-def back_qkv(me, grad_mixed, grad_res_one, weight):
+    )(
+        me,
+        tokens,
+        in_vmem(grad_mixed),
+        *[in_vmem(half) for half in attended],
+        in_vmem(grad_branch),
+    )
+
+
+def back_qkv(me, grad_mixed, grad_res_one, weight, before=None):
     rows = grad_res_one.shape[0]
-    count = len(weight)
+    steps = rows // TILE // 2
     width = 3 * PART
 
-    def kernel(s, g0_ref, g1_ref, dr_ref, *rest):
-        refs, (out_ref, w_ref, sem) = rest[:count], rest[count:]
+    def compute(g0_ref, g1_ref, dr_ref, w_ref, out_ref):
+        both = jnp.concatenate([g0_ref[...], g1_ref[...]], axis=1)
+        w = w_ref[...].reshape(D, 2 * width)
+        out_ref[...] = (dot(both, w, NT) + dr_ref[...]).astype(bf16)
+
+    def kernel_one(s, g0_ref, g1_ref, dr_ref, *rest):
+        refs, (out_ref, w_ref, sem) = rest[: len(weight)], rest[len(weight) :]
 
         @pl.when(pl.program_id(0) == 0)
         def _():
             weight.load(s[0], refs, w_ref, sem)
 
-        out_ref[...] = (
-            dot(g0_ref[...], w_ref[0].reshape(D, width), NT)
-            + dot(g1_ref[...], w_ref[1].reshape(D, width), NT)
-            + dr_ref[...]
-        ).astype(bf16)
-
-    return call(
-        kernel,
-        (rows // TILE,),
-        [rows_of(width), rows_of(width), rows_of(D)] + [ANY] * count,
-        rows_of(D),
-        jax.ShapeDtypeStruct((rows, D), bf16),
-        [pltpu.VMEM(weight.shape, bf16), pltpu.SemaphoreType.DMA],
-        flops=2 * rows * D * 3 * D,
-        bytes_accessed=rows * D * 12 + 2 * D * 3 * D,
-        name="back_qkv",
-    )(me, *grad_mixed, in_hbm(grad_res_one), *weight.arrays)
+        compute(g0_ref, g1_ref, dr_ref, w_ref, out_ref)
+
+    def kernel_two(s, g0_ref, g1_ref, dr_ref, w_ref, before_ref, out_ref):
+        compute(g0_ref, g1_ref, dr_ref, w_ref, out_ref)
+
+    def at(width):
+        return rows_of(width, TILE, steps if before is not None else 0)
+
+    operands = (me, *[in_vmem(half) for half in grad_mixed], in_hbm(grad_res_one))
+    blocks = [at(width), at(width), at(D)]
+    out = pltpu.HBM((rows, D), bf16)
+    cost = dict(flops=rows * D * 3 * D, bytes_accessed=rows * D * 6 + 2 * D * 3 * D, name="back_qkv")
+    if before is None:
+        return call(
+            kernel_one,
+            (steps,),
+            blocks + [ANY] * len(weight),
+            [at(D), HELD],
+            [out, pltpu.VMEM(weight.shape, bf16)],
+            [pltpu.SemaphoreType.DMA],
+            **cost,
+        )(*operands, *weight.arrays)
+    return call(
+        kernel_two, (steps,), blocks + [HELD, ANY], at(D), out, aliases={5: 0}, **cost
+    )(*operands, in_vmem(weight), in_hbm(before))
 
 
 def adamw_math(moment, square, gradient):
@@ -670,34 +694,24 @@
 
 
 class Gather:
-    def __init__(self, halves, core):
-        first = core == 0
-        keep = jnp.where(first, halves[0], halves[1]).astype(bf16)
-        send = jnp.where(first, halves[1], halves[0]).astype(bf16)
-        self.pair = jnp.stack([keep, swap(send, 1)])
+    def __init__(self, shard):
+        self.shard = shard
 
     def start(self, *others):
         if others:
-            self.pair = after(self.pair, *others)
-        self.one = split_swap(self.pair, 2, 4)
-        self.two = split_swap(self.pair, 4, 2)
-
-    def direct(self, *others):
-        self.start(*others)
-        self.far = swap(self.pair, 6)
-
-    def cross(self, *others):
-        self.other = [swap(after(piece, *others), 1) for piece in (self.pair, self.one, self.two)]
+            self.shard = after(self.shard, *others)
+        self.one = split_swap(self.shard, 2, 4)
+        self.two = split_swap(self.shard, 4, 2)
 
     def forward(self, *others):
         self.one, self.two = lax.optimization_barrier((self.one, self.two) + others)[:2]
         self.far = split_swap(self.one, 4, 2)
-        self.other = [swap(piece, 1) for piece in (self.pair, self.one, self.two)]
+        self.other = [swap(piece, 1) for piece in (self.shard, self.one, self.two)]
 
     def finish(self, *others):
         self.far = after(self.far, *others)
         self.other.append(swap(self.far, 1))
-        return [self.pair, self.one, self.two, self.far] + self.other
+        return Weight([self.shard, self.one, self.two, self.far] + self.other)
 
 
 def low_sum(*values):
@@ -710,37 +724,23 @@
 class Scatter:
     def __init__(self, parts):
         self.theirs, self.mine = parts
-        self.half = self.mine.shape[1] // 2
         self.got = swap(self.theirs, 1)
 
     def one(self, *others):
-        half, mine = self.half, self.mine
         self.got = after(self.got, *others)
-        self.send_x = low_sum(mine[1::2, :half], self.got[1::2, :half])
-        self.send_y = low_sum(mine[2:, half:], self.got[2:, half:])
-        self.got_x = swap(self.send_x, 2)
-        self.got_y = swap(self.send_y, 4)
-        return self.send_x, self.send_y
+        send = low_sum(self.mine[1::2], self.got[1::2])
+        self.near_got = split_swap(send, 2, 4)
+        return (send,)
 
     def two(self, *others):
-        half, mine, got = self.half, self.mine, self.got
-        self.got_x, self.got_y = lax.optimization_barrier((self.got_x, self.got_y) + others)[:2]
-        send_y = low_sum(mine[2, :half], got[2, :half], self.got_x[1])
-        send_x = low_sum(mine[1, half:], got[1, half:], self.got_y[1])
-        self.last_y = swap(send_y, 4)
-        self.last_x = swap(send_x, 2)
-        return send_x, send_y
+        self.near_got = after(self.near_got, *others)
+        send = low_sum(self.mine[2], self.got[2], self.near_got[1])
+        self.last = split_swap(send, 4, 2)
+        return (send,)
 
     def three(self, *others):
-        half, mine, got = self.half, self.mine, self.got
-        self.last_x, self.last_y = lax.optimization_barrier((self.last_x, self.last_y) + others)[:2]
-        self.owned = jnp.concatenate(
-            [
-                low_sum(mine[0, :half], got[0, :half], self.got_x[0], self.last_y),
-                low_sum(mine[0, half:], got[0, half:], self.got_y[0], self.last_x),
-            ],
-            axis=0,
-        )
+        last = after(self.last, *others)
+        self.owned = low_sum(self.mine[0], self.got[0], self.near_got[0], last)
         return (self.owned,)
 
     def line(self):
@@ -756,22 +756,16 @@
         self.back = lax.ppermute(self.total, "rep", [(1, 0), (2, 3)])
         return (self.total,)
 
-    def all_copies(self):
-        near, across, far = [
-            lax.ppermute(self.owned, "rep", [(i, i ^ bit) for i in range(4)]).astype(f32)
-            for bit in (1, 2, 3)
-        ]
-        return (self.owned.astype(f32) + near) + (across + far)
-
     def result(self, rep_index):
         inner = (rep_index == 1) | (rep_index == 2)
         return jnp.where(inner, self.total, self.back)
 
 
-def gather_small(value, me, position, *others):
-    got = after(swap(value, 1 << position), *others)
-    low_first = ((me >> position) & 1) == 0
-    return jnp.where(low_first, jnp.concatenate([value, got]), jnp.concatenate([got, value]))
+def by_rank(pairs, position):
+    stacked = jnp.stack(pairs)
+    stacked = jnp.where((position & 2) == 0, stacked, stacked[jnp.array([1, 0, 3, 2])])
+    stacked = jnp.where((position & 4) == 0, stacked, stacked[jnp.array([2, 3, 0, 1])])
+    return stacked.reshape(RANKS, -1)
 
 
 def by_head_half(value, half):
@@ -804,41 +798,37 @@
     position = lax.axis_index("fsdp")
     rep_index = lax.axis_index("rep")
     part = D // fsdp
-    cut = (FF - D) // 2
-    middle = w_out.shape[0] // 2
-    halves_a = [jnp.concatenate(by_head_half(w_attn, h), axis=1) for h in range(2)]
-    halves_b = [jnp.concatenate([w_attn[:, 3 * D :], w_in[:, :cut]], axis=1), w_in[:, cut:]]
-    halves_c = [w_out[:middle], w_out[middle:]]
-    shape_a = (2, RANKS, SHARD, 3 * PART)
-    shape_b = (2, RANKS, SHARD, (D + FF) // 2)
-    shape_c = (RANKS, 2, SHARD_FF // 2, D)
-    small = jnp.concatenate([vecs.reshape(1, -1), b_in.reshape(1, -1)], axis=1).astype(bf16)
+    heads_a = [jnp.concatenate(by_head_half(w_attn, h), axis=1) for h in range(2)]
+    low_a = jnp.concatenate(heads_a, axis=1).astype(bf16)
     if direct:
         me = position.reshape(1)
-        core = position & 1
-        a = Gather(halves_a, core)
-        b = Gather(halves_b, core)
-        c = Gather(halves_c, core)
-        small_all = gather_small(small, position, 0)
-        a.start(small_all)
-        small_all = gather_small(small_all, position, 1)
-        a.forward(small_all)
-        small_all = gather_small(small_all, position, 2, a.one, a.two)
-        b.start(a.one, a.two)
-        weight_a = Weight(a.finish(), shape_a)
+        a = Gather(low_a)
+        a.start()
+        wait = lambda value: after(value, low_a)
     else:
         me = jnp.zeros((1,), jnp.int32)
-
-        def gather(halves, shape):
-            halves = [
-                lax.all_gather(half.astype(bf16), "fsdp", axis=0, tiled=True) for half in halves
-            ]
-            return Weight([jnp.stack(halves).reshape(shape)], shape)
-
-        weight_a = gather(halves_a, shape_a)
-        weight_b = gather(halves_b, shape_b)
-        full_c = lax.all_gather(w_out.astype(bf16), "fsdp", axis=0, tiled=True)
-        weight_c = Weight([full_c.reshape(shape_c)], shape_c, by_rank=True)
+        wait = lambda value: value
+    low_b = jnp.concatenate([wait(w_attn)[:, 3 * D :], w_in], axis=1).astype(bf16)
+    low_c = wait(w_out).astype(bf16)
+    small = jnp.concatenate([wait(vecs).reshape(1, -1), b_in.reshape(1, -1)], axis=1).astype(bf16)
+    if direct:
+        b = Gather(low_b)
+        c = Gather(low_c)
+        got = swap(small, 1)
+        first = (position & 1) == 0
+        pair = jnp.concatenate([jnp.where(first, small, got), jnp.where(first, got, small)])
+        pairs = [pair] + [swap(pair, bit) for bit in (2, 4, 6)]
+        a.forward(*pairs)
+        b.start(a.one, a.two, *pairs)
+        small_all = by_rank(pairs, position)
+        weight_a = a.finish()
+    else:
+
+        def gather(low):
+            full = lax.all_gather(low, "fsdp", axis=0, tiled=True)
+            return Weight([full.reshape(RANKS, -1, full.shape[1])])
+
+        weight_a, weight_b, weight_c = gather(low_a), gather(low_b), gather(low_c)
         small_all = lax.all_gather(small, "fsdp", axis=0, tiled=True)
 
     def ordered(value, *others):
@@ -848,29 +838,31 @@
     vectors = small_all[:, : 8 * part].reshape(fsdp, 8, part).transpose(1, 0, 2).reshape(8, D)
     in_bias = small_all[:, 8 * part :].reshape(1, FF)
     bias = jnp.stack([vectors[0], jnp.zeros((D,), f32), vectors[1]]).reshape(3, 2, PART)
-    bias = bias.transpose(1, 0, 2).reshape(2, 3 * PART)
+    bias = bias.transpose(1, 0, 2).reshape(1, 6 * PART)
 
     qkv = project_qkv(me, tokens, weight_a, bias)
     attended, weights = [None, None], [None, None]
-    attended[0], weights[0] = attention(lengths, qkv[0])
-    second = qkv[1]
-    if direct:
-        b.forward(attended[0])
-        c.direct(b.one, b.two)
-        second = after(second, attended[0], b.one, b.two)
+    first, second = qkv
+    if direct:
+        b.forward(*qkv)
+        first = after(first, b.one, b.two)
+    attended[0], weights[0] = attention(lengths, first)
+    if direct:
+        c.start(attended[0], *b.other)
+        second = after(second, attended[0], *b.other)
+        weight_b = b.finish(attended[0])
     attended[1], weights[1] = attention(lengths, second)
-    if direct:
-        weight_b = Weight(b.finish(attended[1]), shape_b)
-    normed_one, inv_one, hidden_low, activated, slope, held_b = feed_in(
-        me, attended, tokens, weight_b, vectors, in_bias
-    )
-    if direct:
-        c.cross(activated)
-        weight_c = Weight(c.finish(), shape_c, by_rank=True)
+    normed_one, inv_one, hidden_low, held_b = project(me, attended, tokens, weight_b, vectors)
+    inner = hidden_low
+    if direct:
+        c.forward(hidden_low)
+        inner = after(hidden_low, c.one, c.two)
+    activated, slope = expand(me, inner, held_b, in_bias)
+    if direct:
+        weight_c = c.finish(activated)
     output, grad_res_two, grad_ffn, sums_two, held_c = feed_out(
         me, activated, normed_one, cotangent, weight_c, vectors
     )
-    held_c = held_c.reshape(RANKS, SHARD_FF, D)
 
     parts_out = grad_w_out(me, activated, grad_ffn)
     grad_pre, sums_in = back_out(me, ordered(grad_ffn, *parts_out), slope, held_c)
@@ -882,21 +874,22 @@
     grad_res_one, grad_branch, *grad_attended, sums_one = back_in(
         me, ordered(grad_pre, *parts_in), grad_res_two, normed_one, inv_one, held_b, vectors
     )
+    sent = ()
     if direct:
         r_in = Scatter(parts_in)
         sent = r_out.two(grad_branch) + r_in.one(grad_branch)
     mixed0, sums_q0 = attention_back(
         lengths, qkv[0], weights[0], ordered(grad_attended[0], *sent)
     )
-    if direct:
-        sent = r_out.three(mixed0)
+    parts_mix = grad_w_mixed(me, tokens, mixed0, attended, grad_branch)
+    sent = parts_mix
+    if direct:
+        r_mix = Scatter(parts_mix)
+        sent = r_out.three(*parts_mix)
         r_out.line()
-    parts_mix = grad_w_mixed(me, tokens, ordered(mixed0, *sent), attended, grad_branch)
-    if direct:
-        r_mix = Scatter(parts_mix)
-        sent = r_in.two(*parts_mix)
+        sent = r_in.two(*sent)
     mixed1, sums_q1 = attention_back(
-        lengths, qkv[1], weights[1], ordered(grad_attended[1], *sent, *parts_mix)
+        lengths, qkv[1], weights[1], ordered(grad_attended[1], *sent)
     )
     parts_qkv = grad_w_qkv(me, tokens, mixed1, (sums_q0, sums_q1), sums_one, sums_two, sums_in)
     sent = ()
@@ -905,25 +898,30 @@
         sent = r_in.three(*parts_qkv)
         r_in.line()
         sent = r_mix.one(*sent)
+        sent = r_qkv.one(*sent)
         sent = r_out.four(*sent)
-        sent = r_qkv.one(*sent)
-    grad_tokens = back_qkv(
+    half_tokens, held_a = back_qkv(
         me, (mixed0, ordered(mixed1, *sent, *parts_qkv)), grad_res_one, weight_a
     )
-    if direct:
-        sent = r_mix.two(grad_tokens)
+    sent = ()
+    if direct:
+        sent = r_mix.two(half_tokens)
         sent = r_qkv.two(*sent)
         sent = r_in.four(*sent)
-        sent = r_out.five(*sent)
+    grad_tokens = back_qkv(
+        me, (mixed0, ordered(mixed1, *sent)), grad_res_one, held_a, half_tokens
+    )
+    if direct:
+        sent = r_qkv.three(grad_tokens)
+        r_qkv.line()
         sent = r_mix.three(*sent)
         r_mix.line()
-        sent = r_qkv.three(*sent)
-        r_qkv.line()
+        sent = r_out.five(*sent)
         sent = r_in.five(*sent)
+        sent = r_qkv.four(*sent)
         sent = r_mix.four(*sent)
-        sent = r_qkv.four(*sent)
+        sent = r_qkv.five(*sent)
         sent = r_mix.five(*sent)
-        sent = r_qkv.five(*sent)
         sum_qkv = r_qkv.result(rep_index)
         sum_out, sum_in, sum_mix = [r.result(rep_index) for r in (r_out, r_in, r_mix)]
         sum_vecs = sum_qkv[SHARD : SHARD + 8, :part]
@@ -932,14 +930,15 @@
     else:
 
         def reduce(theirs, mine):
-            full = jnp.stack([mine, theirs], axis=1)
+            full = jnp.stack([mine, theirs[jnp.array([0, 2, 1, 3])]], axis=1)
             full = full.reshape(-1, full.shape[-1])
             owned = lax.psum_scatter(full, "fsdp", scatter_dimension=0, tiled=True)
             return lax.psum(owned, "rep")
 
         sum_out, sum_in, sum_mix = [reduce(*parts) for parts in (parts_out, parts_in, parts_mix)]
         sum_qkv = reduce(*[parts[:, :SHARD] for parts in parts_qkv])
-        extra = jnp.stack([parts_qkv[1][:, SHARD:], parts_qkv[0][:, SHARD:]], axis=1)
+        theirs, mine = [parts[:, SHARD:] for parts in parts_qkv]
+        extra = jnp.stack([mine, theirs[jnp.array([0, 2, 1, 3])]], axis=1)
         extra = extra.reshape(RANKS, EXTRA, 3 * PART).astype(f32)
         extra = lax.psum(extra[:, :8], ("fsdp", "rep"))
         all_vecs = extra[:, :, :SHARD].transpose(1, 0, 2).reshape(8, D)

time: 265 us -> 256 us (0.966)
  starting transfers between devices: 56.2 us -> 44.8 us
  other arithmetic: 29.2 us -> 20.7 us
  waiting for transfers between devices: 52.5 us -> 61 us
  Pallas kernels: 115 us -> 119 us
    ppermute x39 -> x20, starting transfers between devices: 26.3 us -> 6.62 us  [swap(): return lax.ppermute(value, 'fsdp', flip(bit))]
    ppermute x8 -> x17, waiting for transfers between devices: 14.5 us -> 27.6 us  [split_swap(): lax.ppermute(value, 'fsdp', [(i, i ^ (odd_bit if i & 1 else even_bit)) fo...]
    ppermute x39 -> x20, waiting for transfers between devices: 18.6 us -> 6.88 us  [swap(): return lax.ppermute(value, 'fsdp', flip(bit))]
    ppermute x8 -> x17, starting transfers between devices: 9.45 us -> 20.3 us  [split_swap(): lax.ppermute(value, 'fsdp', [(i, i ^ (odd_bit if i & 1 else even_bit)) fo...]
    ppermute x4, waiting for transfers between devices: 13.9 us -> 22 us  [five(): self.back = lax.ppermute(self.total, 'rep', [(1, 0), (2, 3)])]
    another operation x7 -> x6, other arithmetic: 8.52 us -> 1.55 us  [the longest x5 7.15 us: __init__(): self.pair = jnp.stack([keep, swap(send, 1)])]
    pallas_call x5 -> x7, Pallas kernels: 40.6 us -> 42 us  [the longest x1 8.88 us: expand(): call(kernel, (rows // TILE,), [rows_of(D), whole((1, FF)), HELD], [rows_o...]
  transfers between devices with their start and end apart: 59 -> 49, of which waited for: 16 -> 20; matrix products, arithmetic and copies ran while one was open for 11% -> 8% of each run, Pallas kernels for 33% -> 36%
where the time goes in v4:
time: 256 us; the launch traced here: 255 us
  Pallas kernels  119 us (46%)
  waiting for transfers between devices  61 us (24%)
  starting transfers between devices  44.8 us (18%)
  other arithmetic  20.7 us (8%)
  local copies, waits for them, and re-layouts  7.58 us (3%)
    ppermute x17, waiting for transfers between devices, split_swap(): lax.ppermute(value, 'fsdp', [(i, i ^ (odd_bit if i & 1 else even_bit)) fo...  27.6 us
    ppermute x4, waiting for transfers between devices, five(): self.back = lax.ppermute(self.total, 'rep', [(1, 0), (2, 3)])  22 us
    ppermute x17, starting transfers between devices, split_swap(): lax.ppermute(value, 'fsdp', [(i, i ^ (odd_bit if i & 1 else even_bit)) fo...  20.3 us
    pallas_call x2, Pallas kernels, attention_back(): call(kernel, (rows // (GROUP * SEQ),), [rows_of(3 * PART, GROUP * SEQ), r...  17.6 us
    pallas_call x2, Pallas kernels, attention(): call(kernel, (rows // (GROUP * SEQ),), [rows_of(3 * PART, GROUP * SEQ)],...  13.5 us
    pallas_call x1, Pallas kernels, feed_out(): call(kernel, (rows // TILE,), [rows_of(FF), rows_of(D), rows_of(D), whole...  12.7 us
    pallas_call x1, Pallas kernels, back_in(): call(kernel, (rows // TILE,), [rows_of(FF), rows_of(D), rows_of(D), rows_...  12.2 us
    ppermute x4, starting transfers between devices, line(): self.near = lax.ppermute(self.owned, 'rep', [(0, 1), (3, 2)])  9.66 us
  transfers between devices with their start and end apart: 49, of which 20 were waited for; matrix products, arithmetic and copies ran while one was open for 8% of the time, Pallas kernels for 36%

profile of v4, /device:TPU:0, one launch (start us, length us, event | category | flops | bytes accessed | tf_op | source)
XLA Modules:
  0.0 254.9 jit_solution(14653866390216200425)
XLA Ops:
  0.7 1.4 convert.32
  2.3 3.0 %collective-permute-start.5 = (bf16[96,2304]{1,0:T(8,128)(2,1)S(1)}, bf16[96,2304]{1,0:T(8,128)(2,1)}, u32[]{:S(2)}, u32[]{:S(2)}) collective-permute-start(bf16[96,2304]{1,0:T(8,128)(2,1)S(1)} %slice_dynamic-update-slice_fusion.7.rest_0_), channel_id=1, source_target_pairs={{0,4},{1,3},{2,6},{3,1},{4,0},{5,7},{6,2},{7,5},{8,12},{9,11},{10,... | collective-permute-start | bytes 1327112 | tf_op jit(solution)/shard_map/ppermute | solution.py:691
  5.3 1.5 collective-permute-start.4
  7.0 1.0 slice.298
  8.9 1.9 collective-permute-start.2
  10.9 1.5 collective-permute-start.1
  12.4 4.4 %collective-permute-done.3 = bf16[2,1152]{1,0:T(2,128)(2,1)S(1)} collective-permute-done((bf16[2,1152]{1,0:T(2,128)(2,1)S(1)}, bf16[2,1152]{1,0:T(2,128)(2,1)S(1)}, u32[]{:S(2)}, u32[]{:S(2)}) %collective-permute-start.3) | collective-permute-done | bytes 4640 | tf_op jit(solution)/shard_map/ppermute | solution.py:683
  17.5 1.7 collective-permute-start.6
  20.8 5.4 %collective-permute-done.6.rest_3_ = bf16[96,2304]{1,0:T(8,128)(2,1)} collective-permute-done((bf16[96,2304]{1,0:T(8,128)(2,1)}, bf16[96,2304]{1,0:T(8,128)(2,1)}, u32[]{:S(2)}, u32[]{:S(2)}) %collective-permute-start.6) | collective-permute-done | bytes 442400 | tf_op jit(solution)/shard_map/ppermute | solution.py:691
  26.2 1.5 collective-permute-start.11
  30.4 7.3 %qkv.1 = (bf16[1024,1152]{1,0:T(8,128)(2,1)}, bf16[1024,1152]{1,0:T(8,128)(2,1)}) custom-call(s32[1]{0:T(128)} %bitcast.s, bf16[1024,768]{1,0:T(8,128)(2,1)S(1)} %copy-done, f32[1,2304]{1,0:T(1,128)S(1)} %reshape.165.b_ref, bf16[96,2304]{1,0:T(8,128)(2,1)} %copy-done.9, bf16[96,2304]{1,0:T(8,128)(2,1)} %collective-permute-done.4.rest_1_, ...), custom_call_target="tpu_custom_call" | custom-call | flops 3623878 | bytes 9830 | tf_op jit(solution)/shard_map/qkv/pallas_call | solution.py:149
  37.7 1.8 collective-permute-done.12.rest_2_
  39.5 1.9 collective-permute-done.11.rest_1_
  41.5 1.3 collective-permute-start.16
  43.5 6.7 %attention.2 = (bf16[1024,384]{1,0:T(8,128)(2,1)S(1)}, f32[1024,768]{1,0:T(8,128)}) custom-call(s32[8]{0:T(128)S(1)} %copy-done.4, bf16[1024,1152]{1,0:T(8,128)(2,1)} %get-tuple-element.112.qkv_ref), custom_call_target="tpu_custom_call" | custom-call | flops 4000000 | bytes 6291 | tf_op jit(solution)/shard_map/attention/pallas_call | solution.py:205
  50.2 3.0 %collective-permute-done.16.rest_3_ = bf16[96,3840]{1,0:T(8,128)(2,1)} collective-permute-done((bf16[96,3840]{1,0:T(8,128)(2,1)}, bf16[96,3840]{1,0:T(8,128)(2,1)}, u32[]{:S(2)}, u32[]{:S(2)}) %collective-permute-start.16) | collective-permute-done | bytes 737312 | tf_op jit(solution)/shard_map/ppermute | solution.py:691
  53.3 0.9 convert_element_type.296.rest_0_
  54.2 1.3 collective-permute-start.19
  56.5 6.7 %attention.3 = (bf16[1024,384]{1,0:T(8,128)(2,1)S(1)}, f32[1024,768]{1,0:T(8,128)}) custom-call(s32[8]{0:T(128)S(1)} %copy-done.4, bf16[1024,1152]{1,0:T(8,128)(2,1)} %get-tuple-element.114.qkv_ref), custom_call_target="tpu_custom_call" | custom-call | flops 4000000 | bytes 6291 | tf_op jit(solution)/shard_map/attention/pallas_call | solution.py:205
  63.2 6.7 %project.1 = (f32[1024,768]{1,0:T(8,128)}, f32[1024,1]{1,0:T(8,128)}, bf16[1024,768]{1,0:T(8,128)(2,1)S(1)}, bf16[8,96,3840]{2,1,0:T(8,128)(2,1)S(1)}) custom-call(s32[1]{0:T(128)} %bitcast.s, bf16[1024,384]{1,0:T(8,128)(2,1)S(1)} %get-tuple-element.113.o0_ref, bf16[1024,384]{1,0:T(8,128)(2,1)S(1)} %get-tuple-element.115.o1_ref, ...), custom_call_target="tpu_custom_call" | custom-call | flops 1207959 | bytes 13762 | tf_op jit(solution)/shard_map/project/pallas_call | solution.py:235
  70.3 1.6 collective-permute-start.20
  73.2 8.9 %expand.1 = (bf16[1024,3072]{1,0:T(8,128)(2,1)S(1)}, bf16[1024,3072]{1,0:T(8,128)(2,1)S(1)}) custom-call(s32[1]{0:T(128)} %bitcast.s, bf16[1024,768]{1,0:T(8,128)(2,1)S(1)} %get-tuple-element.122.h_ref, f32[1,3072]{1,0:T(1,128)S(1)} %bitcast.38, bf16[8,96,3840]{2,1,0:T(8,128)(2,1)S(1)} %get-tuple-element.123.w_ref), custom_call_target="tpu_custom_call" | custom-call | flops 4831838 | bytes 18874 | tf_op jit(solution)/shard_map/expand/pallas_call | solution.py:266
  82.7 1.6 collective-permute-done.24.rest_7_
  85.1 12.7 %feed_out.1 = (bf16[1024,768]{1,0:T(8,128)(2,1)}, f32[1024,768]{1,0:T(8,128)}, bf16[1024,768]{1,0:T(8,128)(2,1)S(1)}, f32[8,768]{1,0:T(8,128)S(1)}, bf16[8,384,768]{2,1,0:T(8,128)(2,1)S(1)}) custom-call(s32[1]{0:T(128)} %bitcast.s, bf16[1024,3072]{1,0:T(8,128)(2,1)S(1)} %get-tuple-element.124.f_ref, f32[1024,768]{1,0:T(8,128)} %get-tuple-element.125.n1_ref, ...), custom_call_target="tpu_custom_call" | custom-call | flops 4831838 | bytes 22020 | tf_op jit(solution)/shard_map/feed_out/pallas_call | solution.py:304
  97.9 7.4 %grad_w_out.1 = (bf16[4,384,768]{2,1,0:T(8,128)(2,1)}, bf16[4,384,768]{2,1,0:T(8,128)(2,1)}) custom-call(s32[1]{0:T(128)} %bitcast.s, bf16[1024,3072]{1,0:T(8,128)(2,1)S(1)} %get-tuple-element.124.f_ref, bf16[1024,768]{1,0:T(8,128)(2,1)S(1)} %get-tuple-element.132.dz_ref), custom_call_target="tpu_custom_call" | custom-call | flops 4831838 | bytes 12582 | tf_op jit(solution)/shard_map/grad_w_out/pallas_call | solution.py:343
  105.7 6.3 %back_out.1 = (bf16[1024,3072]{1,0:T(8,128)(2,1)S(1)}, f32[1,3072]{1,0:T(1,128)S(1)}) custom-call(s32[1]{0:T(128)} %bitcast.s, bf16[1024,768]{1,0:T(8,128)(2,1)S(1)} %get-tuple-element.132.dz_ref, bf16[1024,3072]{1,0:T(8,128)(2,1)S(1)} %get-tuple-element.133.sl_ref, bf16[8,384,768]{2,1,0:T(8,128)(2,1)S(1)} %get-tuple-element.134.w_ref), custom_call_target="tpu_custom_call" | custom-call | flops 4831838 | bytes 18874 | tf_op jit(solution)/shard_map/back_out/pallas_call | solution.py:375
  112.3 7.5 %grad_w_in.1 = (bf16[4,96,3072]{2,1,0:T(8,128)(2,1)}, bf16[4,96,3072]{2,1,0:T(8,128)(2,1)}) custom-call(s32[1]{0:T(128)} %bitcast.s, bf16[1024,768]{1,0:T(8,128)(2,1)S(1)} %get-tuple-element.122.h_ref, bf16[1024,3072]{1,0:T(8,128)(2,1)S(1)} %get-tuple-element.140.du_ref), custom_call_target="tpu_custom_call" | custom-call | flops 4831838 | bytes 14155 | tf_op jit(solution)/shard_map/grad_w_in/pallas_call | solution.py:458
  120.5 12.2 %back_in.1 = (f32[1024,768]{1,0:T(8,128)}, bf16[1024,768]{1,0:T(8,128)(2,1)S(1)}, bf16[1024,384]{1,0:T(8,128)(2,1)S(1)}, bf16[1024,384]{1,0:T(8,128)(2,1)S(1)}, f32[8,768]{1,0:T(8,128)S(1)}) custom-call(s32[1]{0:T(128)} %bitcast.s, bf16[1024,3072]{1,0:T(8,128)(2,1)S(1)} %get-tuple-element.140.du_ref, f32[1024,768]{1,0:T(8,128)} %get-tuple-element.141.dr2_ref, ...), custom_call_target="tpu_custom_call" | custom-call | flops 6039797 | bytes 24772 | tf_op jit(solution)/shard_map/back_in/pallas_call | solution.py:412
  133.2 1.6 collective-permute-start.28
  134.7 1.5 collective-permute-done.26
  137.0 8.8 %attention_back.2 = (bf16[1024,1152]{1,0:T(8,128)(2,1)S(1)}, f32[8,384]{1,0:T(8,128)S(1)}) custom-call(s32[8]{0:T(128)S(1)} %copy-done.4, bf16[1024,1152]{1,0:T(8,128)(2,1)} %get-tuple-element.112.qkv_ref, f32[1024,768]{1,0:T(8,128)} %get-tuple-element.128.p_ref, bf16[1024,384]{1,0:T(8,128)(2,1)S(1)} %get-tuple-element.147.do_ref), custom_call_target="tpu_custom_call" | custom-call | flops 7000000 | bytes 8650 | tf_op jit(solution)/shard_map/attention_back/pallas_call | solution.py:510
  145.8 5.2 %grad_w_mixed.1 = (bf16[4,96,1920]{2,1,0:T(8,128)(2,1)}, bf16[4,96,1920]{2,1,0:T(8,128)(2,1)}) custom-call(s32[1]{0:T(128)} %bitcast.s, bf16[1024,768]{1,0:T(8,128)(2,1)S(1)} %copy-done, bf16[1024,1152]{1,0:T(8,128)(2,1)S(1)} %get-tuple-element.148.g_ref.g0_ref, bf16[1024,384]{1,0:T(8,128)(2,1)S(1)} %get-tuple-element.113.o0_ref, ...), custom_call_target="tpu_custom_call" | custom-call | flops 3019898 | bytes 12386 | tf_op jit(solution)/shard_map/grad_w_mixed/pallas_call | solution.py:596
  151.0 1.8 collective-permute-done.29
  153.1 2.6 %collective-permute-done.28 = bf16[2,96,3072]{2,1,0:T(8,128)(2,1)S(1)} collective-permute-done((bf16[2,96,3072]{2,1,0:T(8,128)(2,1)S(1)}, bf16[2,96,3072]{2,1,0:T(8,128)(2,1)S(1)}, u32[]{:S(2)}, u32[]{:S(2)}) %collective-permute-start.28) | collective-permute-done | bytes 1179680 | tf_op jit(solution)/shard_map/ppermute | solution.py:691
  155.7 1.2 fusion.7
  157.0 1.6 collective-permute-start.30
  158.5 3.6 %collective-permute-start.36 = (bf16[384,768]{1,0:T(8,128)(2,1)S(1)}, bf16[384,768]{1,0:T(8,128)(2,1)S(1)}, u32[]{:S(2)}, u32[]{:S(2)}) collective-permute-start(bf16[384,768]{1,0:T(8,128)(2,1)S(1)} %fusion.4), channel_id=1, source_target_pairs={{0,8},{24,16},{1,9},{25,17},{2,10},{26,18},{3,11},{27,19},{4,12},{... | collective-permute-start | bytes 1769480 | tf_op jit(solution)/shard_map/ppermute | solution.py:747
  162.2 8.8 %attention_back.3 = (bf16[1024,1152]{1,0:T(8,128)(2,1)S(1)}, f32[8,384]{1,0:T(8,128)S(1)}) custom-call(s32[8]{0:T(128)S(1)} %copy-done.4, bf16[1024,1152]{1,0:T(8,128)(2,1)} %get-tuple-element.114.qkv_ref, f32[1024,768]{1,0:T(8,128)} %get-tuple-element.149.p_ref, bf16[1024,384]{1,0:T(8,128)(2,1)S(1)} %get-tuple-element.155.do_ref), custom_call_target="tpu_custom_call" | custom-call | flops 7000000 | bytes 8650 | tf_op jit(solution)/shard_map/attention_back/pallas_call | solution.py:510
  171.0 3.6 %grad_w_qkv.1 = (bf16[4,112,1152]{2,1,0:T(8,128)(2,1)}, bf16[4,112,1152]{2,1,0:T(8,128)(2,1)}) custom-call(s32[1]{0:T(128)} %bitcast.s, bf16[1024,768]{1,0:T(8,128)(2,1)S(1)} %copy-done, bf16[1024,1152]{1,0:T(8,128)(2,1)S(1)} %get-tuple-element.174.g_ref.g1_ref, f32[8,384]{1,0:T(8,128)S(1)} %get-tuple-element.157.q0_ref, ...), custom_call_target="tpu_custom_call" | custom-call | flops 1811939 | bytes 8060 | tf_op jit(solution)/shard_map/grad_w_qkv/pallas_call | solution.py:563
  174.6 1.9 fusion.3
  176.5 1.7 collective-permute-start.31
  178.2 1.3 add_convert_fusion.2
  180.1 1.7 collective-permute-start.34
  182.7 6.2 %back_qkv.2 = (bf16[1024,768]{1,0:T(8,128)(2,1)}, bf16[8,96,2304]{2,1,0:T(8,128)(2,1)S(1)}) custom-call(s32[1]{0:T(128)} %bitcast.s, bf16[1024,1152]{1,0:T(8,128)(2,1)S(1)} %copy-done.2, bf16[1024,1152]{1,0:T(8,128)(2,1)S(1)} %get-tuple-element.174.g_ref.g1_ref, f32[1024,768]{1,0:T(8,128)} %get-tuple-element.169.dr_ref, bf16[96,2304]{1,0:T(8,128)(2,1)} %copy-done.9, ...), custom_call_target="tpu_custom_call" | custom-call | flops 1811939 | bytes 8257 | tf_op jit(solution)/shard_map/back_qkv/pallas_call | solution.py:650
  188.9 2.2 collective-permute-done.35
  191.1 1.1 fusion.9
  192.6 6.0 %collective-permute-done.34 = bf16[2,112,1152]{2,1,0:T(8,128)(2,1)S(1)} collective-permute-done((bf16[2,112,1152]{2,1,0:T(8,128)(2,1)S(1)}, bf16[2,112,1152]{2,1,0:T(8,128)(2,1)S(1)}, u32[]{:S(2)}, u32[]{:S(2)}) %collective-permute-start.34) | collective-permute-done | bytes 516128 | tf_op jit(solution)/shard_map/ppermute | solution.py:691
  200.0 4.1 %back_qkv.3 = bf16[1024,768]{1,0:T(8,128)(2,1)} custom-call(s32[1]{0:T(128)} %bitcast.s, bf16[1024,1152]{1,0:T(8,128)(2,1)S(1)} %copy-done.2, bf16[1024,1152]{1,0:T(8,128)(2,1)S(1)} %get-tuple-element.174.g_ref.g1_ref, f32[1024,768]{1,0:T(8,128)} %get-tuple-element.169.dr_ref, ...), custom_call_target="tpu_custom_call", output_to_operand_aliasing={{}: (5, {})} | custom-call | flops 1811939 | bytes 8257 | tf_op jit(solution)/shard_map/back_qkv/pallas_call | solution.py:659
  204.1 1.0 collective-permute-done.38
  205.3 3.1 %collective-permute-start.40 = (bf16[112,1152]{1,0:T(8,128)(2,1)S(1)}, bf16[112,1152]{1,0:T(8,128)(2,1)S(1)}, u32[]{:S(2)}, u32[]{:S(2)}) collective-permute-start(bf16[112,1152]{1,0:T(8,128)(2,1)S(1)} %fusion.8), channel_id=1, source_target_pairs={{0,8},{24,16},{1,9},{25,17},{2,10},{26,18},{3,11},{27,19},{4,12},{... | collective-permute-start | bytes 774152 | tf_op jit(solution)/shard_map/ppermute | solution.py:747
  208.3 1.2 fusion.5
  209.5 1.3 collective-permute-start.39
  211.0 1.3 collective-permute-start.48
  212.5 1.4 collective-permute-start.47
  213.9 1.1 collective-permute-done.40
  215.7 3.4 %collective-permute-done.39 = bf16[96,1920]{1,0:T(8,128)(2,1)S(1)} collective-permute-done((bf16[96,1920]{1,0:T(8,128)(2,1)S(1)}, bf16[96,1920]{1,0:T(8,128)(2,1)S(1)}, u32[]{:S(2)}, u32[]{:S(2)}) %collective-permute-start.39) | collective-permute-done | bytes 368672 | tf_op jit(solution)/shard_map/ppermute | solution.py:747
  220.0 1.3 collective-permute-start.46
  221.3 7.8 %collective-permute-done.48 = bf16[384,768]{1,0:T(8,128)(2,1)S(1)} collective-permute-done((bf16[384,768]{1,0:T(8,128)(2,1)S(1)}, bf16[384,768]{1,0:T(8,128)(2,1)S(1)}, u32[]{:S(2)}, u32[]{:S(2)}) %collective-permute-start.48) | collective-permute-done | bytes 589856 | tf_op jit(solution)/shard_map/ppermute | solution.py:756
  229.2 2.5 add_divide_fusion
  231.8 1.4 collective-permute-start.45
  233.2 14.1 %collective-permute-done.46 = bf16[112,1152]{1,0:T(8,128)(2,1)S(1)} collective-permute-done((bf16[112,1152]{1,0:T(8,128)(2,1)S(1)}, bf16[112,1152]{1,0:T(8,128)(2,1)S(1)}, u32[]{:S(2)}, u32[]{:S(2)}) %collective-permute-start.46) | collective-permute-done | bytes 258080 | tf_op jit(solution)/shard_map/ppermute | solution.py:756
  248.6 2.5 add_divide_fusion.1
  251.4 1.0 copy-done.21
  252.4 2.5 add_divide_fusion.2
  (213 shorter events, 20.7 us)
Async XLA Ops:
  2.2 14.5 %copy-start.9 = (bf16[96,2304]{1,0:T(8,128)(2,1)}, bf16[96,2304]{1,0:T(8,128)(2,1)S(1)}, u32[]{:S(2)}) copy-start(bf16[96,2304]{1,0:T(8,128)(2,1)S(1)} %slice_dynamic-update-slice_fusion.7.rest_0_) | copy-start | bytes 1327108
  2.3 15.2 %collective-permute-start.5 = (bf16[96,2304]{1,0:T(8,128)(2,1)S(1)}, bf16[96,2304]{1,0:T(8,128)(2,1)}, u32[]{:S(2)}, u32[]{:S(2)}) collective-permute-start(bf16[96,2304]{1,0:T(8,128)(2,1)S(1)} %slice_dynamic-update-slice_fusion.7.rest_0_), channel_id=1, source_target_pairs={{0,4},{1,3},{2,6},{3,1},{4,0},{5,7},{6,2},{7,5},{8,12},{9,11},{10,... | collective-permute-start | bytes 1327112 | tf_op jit(solution)/shard_map/ppermute | solution.py:691
  5.3 12.2 %collective-permute-start.4 = (bf16[96,2304]{1,0:T(8,128)(2,1)S(1)}, bf16[96,2304]{1,0:T(8,128)(2,1)}, u32[]{:S(2)}, u32[]{:S(2)}) collective-permute-start(bf16[96,2304]{1,0:T(8,128)(2,1)S(1)} %slice_dynamic-update-slice_fusion.7.rest_0_), channel_id=1, source_target_pairs={{0,2},{1,5},{2,0},{3,7},{4,6},{5,1},{6,4},{7,3},{8,10},{9,13},{10,... | collective-permute-start | bytes 1327112 | tf_op jit(solution)/shard_map/ppermute | solution.py:691
  6.9 1.8 collective-permute-start
  8.1 22.3 %copy-start = (bf16[1024,768]{1,0:T(8,128)(2,1)S(1)}, bf16[1024,768]{1,0:T(8,128)(2,1)}, u32[]{:S(2)}) copy-start(bf16[1024,768]{1,0:T(8,128)(2,1)} %x_ref.7) | copy-start | bytes 4718596
  8.7 34.1 %copy-start.5 = (bf16[96,3840]{1,0:T(8,128)(2,1)}, bf16[96,3840]{1,0:T(8,128)(2,1)S(1)}, u32[]{:S(2)}) copy-start(bf16[96,3840]{1,0:T(8,128)(2,1)S(1)} %pad_maximum_fusion.rest_0_) | copy-start | bytes 2211844
  8.8 8.0 %collective-permute-start.3 = (bf16[2,1152]{1,0:T(2,128)(2,1)S(1)}, bf16[2,1152]{1,0:T(2,128)(2,1)S(1)}, u32[]{:S(2)}, u32[]{:S(2)}) collective-permute-start(bf16[2,1152]{1,0:T(2,128)(2,1)S(1)} %pad_maximum_fusion.2), channel_id=1, source_target_pairs={{0,6},{1,7},{2,4},{3,5},{4,2},{5,3},{6,0},{7,1},{8,14},{9,15},{10,... | collective-permute-start | bytes 13832 | tf_op jit(solution)/shard_map/ppermute | solution.py:683
  8.9 7.9 %collective-permute-start.2 = (bf16[2,1152]{1,0:T(2,128)(2,1)S(1)}, bf16[2,1152]{1,0:T(2,128)(2,1)S(1)}, u32[]{:S(2)}, u32[]{:S(2)}) collective-permute-start(bf16[2,1152]{1,0:T(2,128)(2,1)S(1)} %pad_maximum_fusion.2), channel_id=1, source_target_pairs={{0,4},{1,5},{2,6},{3,7},{4,0},{5,1},{6,2},{7,3},{8,12},{9,13},{10,... | collective-permute-start | bytes 13832 | tf_op jit(solution)/shard_map/ppermute | solution.py:683
  10.9 5.9 %collective-permute-start.1 = (bf16[2,1152]{1,0:T(2,128)(2,1)S(1)}, bf16[2,1152]{1,0:T(2,128)(2,1)S(1)}, u32[]{:S(2)}, u32[]{:S(2)}) collective-permute-start(bf16[2,1152]{1,0:T(2,128)(2,1)S(1)} %pad_maximum_fusion.2), channel_id=1, source_target_pairs={{0,2},{1,3},{2,0},{3,1},{4,6},{5,7},{6,4},{7,5},{8,10},{9,11},{10,... | collective-permute-start | bytes 13832 | tf_op jit(solution)/shard_map/ppermute | solution.py:683
  16.8 10.9 %collective-permute-start.7 = (bf16[96,2304]{1,0:T(8,128)(2,1)S(1)}, bf16[96,2304]{1,0:T(8,128)(2,1)S(1)}, u32[]{:S(2)}, u32[]{:S(2)}) collective-permute-start(bf16[96,2304]{1,0:T(8,128)(2,1)S(1)} %slice_dynamic-update-slice_fusion.7.rest_0_), channel_id=1, source_target_pairs={{0,1},{1,0},{2,3},{3,2},{4,5},{5,4},{6,7},{7,6},{8,9},{9,8},{10,11... | collective-permute-start | bytes 1327112 | tf_op jit(solution)/shard_map/ppermute | solution.py:683
  17.5 8.7 %collective-permute-start.6 = (bf16[96,2304]{1,0:T(8,128)(2,1)}, bf16[96,2304]{1,0:T(8,128)(2,1)}, u32[]{:S(2)}, u32[]{:S(2)}) collective-permute-start(bf16[96,2304]{1,0:T(8,128)(2,1)} %collective-permute-done.4.rest_1_), channel_id=1, source_target_pairs={{0,4},{1,3},{2,6},{3,1},{4,0},{5,7},{6,2},{7,5},{8,12},{9,11},{10,... | collective-permute-start | bytes 1327112 | tf_op jit(solution)/shard_map/ppermute | solution.py:691
  19.8 9.0 %collective-permute-start.8 = (bf16[96,2304]{1,0:T(8,128)(2,1)}, bf16[96,2304]{1,0:T(8,128)(2,1)}, u32[]{:S(2)}, u32[]{:S(2)}) collective-permute-start(bf16[96,2304]{1,0:T(8,128)(2,1)} %collective-permute-done.4.rest_1_), channel_id=1, source_target_pairs={{0,1},{1,0},{2,3},{3,2},{4,5},{5,4},{6,7},{7,6},{8,9},{9,8},{10,11... | collective-permute-start | bytes 1327112 | tf_op jit(solution)/shard_map/ppermute | solution.py:683
  19.9 8.9 %collective-permute-start.9 = (bf16[96,2304]{1,0:T(8,128)(2,1)}, bf16[96,2304]{1,0:T(8,128)(2,1)}, u32[]{:S(2)}, u32[]{:S(2)}) collective-permute-start(bf16[96,2304]{1,0:T(8,128)(2,1)} %collective-permute-done.5.rest_2_), channel_id=1, source_target_pairs={{0,1},{1,0},{2,3},{3,2},{4,5},{5,4},{6,7},{7,6},{8,9},{9,8},{10,11... | collective-permute-start | bytes 1327112 | tf_op jit(solution)/shard_map/ppermute | solution.py:683
  20.4 19.1 %collective-permute-start.12 = (bf16[96,3840]{1,0:T(8,128)(2,1)S(1)}, bf16[96,3840]{1,0:T(8,128)(2,1)}, u32[]{:S(2)}, u32[]{:S(2)}) collective-permute-start(bf16[96,3840]{1,0:T(8,128)(2,1)S(1)} %pad_maximum_fusion.rest_0_), channel_id=1, source_target_pairs={{0,4},{1,3},{2,6},{3,1},{4,0},{5,7},{6,2},{7,5},{8,12},{9,11},{10,... | collective-permute-start | bytes 2211848 | tf_op jit(solution)/shard_map/ppermute | solution.py:691
  26.2 15.3 %collective-permute-start.11 = (bf16[96,3840]{1,0:T(8,128)(2,1)S(1)}, bf16[96,3840]{1,0:T(8,128)(2,1)}, u32[]{:S(2)}, u32[]{:S(2)}) collective-permute-start(bf16[96,3840]{1,0:T(8,128)(2,1)S(1)} %pad_maximum_fusion.rest_0_), channel_id=1, source_target_pairs={{0,2},{1,5},{2,0},{3,7},{4,6},{5,1},{6,4},{7,3},{8,10},{9,13},{10,... | collective-permute-start | bytes 2211848 | tf_op jit(solution)/shard_map/ppermute | solution.py:691
  27.6 2.0 collective-permute-start.10
  28.5 14.8 %copy-start.33 = (f32[8,8,96]{2,1,0:T(8,128)}, f32[8,8,96]{2,1,0:T(8,128)S(1)}, u32[]{:S(2)}) copy-start(f32[8,8,96]{2,1,0:T(8,128)S(1)} %reshape.164) | copy-start | bytes 73732
  30.4 13.1 %copy-start.4 = (s32[8]{0:T(128)S(1)}, s32[8]{0:T(128)}, u32[]{:S(2)}) copy-start(s32[8]{0:T(128)} %s.7) | copy-start | bytes 100
  41.5 11.8 %collective-permute-start.16 = (bf16[96,3840]{1,0:T(8,128)(2,1)}, bf16[96,3840]{1,0:T(8,128)(2,1)}, u32[]{:S(2)}, u32[]{:S(2)}) collective-permute-start(bf16[96,3840]{1,0:T(8,128)(2,1)} %collective-permute-done.11.rest_1_), channel_id=1, source_target_pairs={{0,4},{1,3},{2,6},{3,1},{4,0},{5,7},{6,2},{7,5},{8,12},{9,11},{10,... | collective-permute-start | bytes 2211848 | tf_op jit(solution)/shard_map/ppermute | solution.py:691
  42.8 11.4 %collective-permute-start.13 = (bf16[96,3840]{1,0:T(8,128)(2,1)S(1)}, bf16[96,3840]{1,0:T(8,128)(2,1)S(1)}, u32[]{:S(2)}, u32[]{:S(2)}) collective-permute-start(bf16[96,3840]{1,0:T(8,128)(2,1)S(1)} %pad_maximum_fusion.rest_0_), channel_id=1, source_target_pairs={{0,1},{1,0},{2,3},{3,2},{4,5},{5,4},{6,7},{7,6},{8,9},{9,8},{10,11... | collective-permute-start | bytes 2211848 | tf_op jit(solution)/shard_map/ppermute | solution.py:683
  43.0 11.2 %collective-permute-start.15 = (bf16[96,3840]{1,0:T(8,128)(2,1)}, bf16[96,3840]{1,0:T(8,128)(2,1)S(1)}, u32[]{:S(2)}, u32[]{:S(2)}) collective-permute-start(bf16[96,3840]{1,0:T(8,128)(2,1)} %collective-permute-done.12.rest_2_), channel_id=1, source_target_pairs={{0,1},{1,0},{2,3},{3,2},{4,5},{5,4},{6,7},{7,6},{8,9},{9,8},{10,11... | collective-permute-start | bytes 2211848 | tf_op jit(solution)/shard_map/ppermute | solution.py:683
  43.3 10.9 %collective-permute-start.14 = (bf16[96,3840]{1,0:T(8,128)(2,1)}, bf16[96,3840]{1,0:T(8,128)(2,1)S(1)}, u32[]{:S(2)}, u32[]{:S(2)}) collective-permute-start(bf16[96,3840]{1,0:T(8,128)(2,1)} %collective-permute-done.11.rest_1_), channel_id=1, source_target_pairs={{0,1},{1,0},{2,3},{3,2},{4,5},{5,4},{6,7},{7,6},{8,9},{9,8},{10,11... | collective-permute-start | bytes 2211848 | tf_op jit(solution)/shard_map/ppermute | solution.py:683
  53.3 9.9 %collective-permute-start.17 = (bf16[96,3840]{1,0:T(8,128)(2,1)}, bf16[96,3840]{1,0:T(8,128)(2,1)}, u32[]{:S(2)}, u32[]{:S(2)}) collective-permute-start(bf16[96,3840]{1,0:T(8,128)(2,1)} %collective-permute-done.16.rest_3_), channel_id=1, source_target_pairs={{0,1},{1,0},{2,3},{3,2},{4,5},{5,4},{6,7},{7,6},{8,9},{9,8},{10,11... | collective-permute-start | bytes 2211848 | tf_op jit(solution)/shard_map/ppermute | solution.py:683
  54.2 15.8 %collective-permute-start.19 = (bf16[384,768]{1,0:T(8,128)(2,1)}, bf16[384,768]{1,0:T(8,128)(2,1)S(1)}, u32[]{:S(2)}, u32[]{:S(2)}) collective-permute-start(bf16[384,768]{1,0:T(8,128)(2,1)} %convert_element_type.296.rest_0_), channel_id=1, source_target_pairs={{0,4},{1,3},{2,6},{3,1},{4,0},{5,7},{6,2},{7,5},{8,12},{9,11},{10,... | collective-permute-start | bytes 1769480 | tf_op jit(solution)/shard_map/ppermute | solution.py:691
  55.5 14.8 %collective-permute-start.18 = (bf16[384,768]{1,0:T(8,128)(2,1)}, bf16[384,768]{1,0:T(8,128)(2,1)}, u32[]{:S(2)}, u32[]{:S(2)}) collective-permute-start(bf16[384,768]{1,0:T(8,128)(2,1)} %convert_element_type.296.rest_0_), channel_id=1, source_target_pairs={{0,2},{1,5},{2,0},{3,7},{4,6},{5,1},{6,4},{7,3},{8,10},{9,13},{10,... | collective-permute-start | bytes 1769480 | tf_op jit(solution)/shard_map/ppermute | solution.py:691
  70.3 11.8 %collective-permute-start.20 = (bf16[384,768]{1,0:T(8,128)(2,1)}, bf16[384,768]{1,0:T(8,128)(2,1)S(1)}, u32[]{:S(2)}, u32[]{:S(2)}) collective-permute-start(bf16[384,768]{1,0:T(8,128)(2,1)} %collective-permute-done.18.rest_1_), channel_id=1, source_target_pairs={{0,4},{1,3},{2,6},{3,1},{4,0},{5,7},{6,2},{7,5},{8,12},{9,11},{10,... | collective-permute-start | bytes 1769480 | tf_op jit(solution)/shard_map/ppermute | solution.py:691
  72.6 10.1 %collective-permute-start.21 = (bf16[384,768]{1,0:T(8,128)(2,1)}, bf16[384,768]{1,0:T(8,128)(2,1)S(1)}, u32[]{:S(2)}, u32[]{:S(2)}) collective-permute-start(bf16[384,768]{1,0:T(8,128)(2,1)} %convert_element_type.296.rest_0_), channel_id=1, source_target_pairs={{0,1},{1,0},{2,3},{3,2},{4,5},{5,4},{6,7},{7,6},{8,9},{9,8},{10,11... | collective-permute-start | bytes 1769480 | tf_op jit(solution)/shard_map/ppermute | solution.py:683
  72.7 10.0 %collective-permute-start.23 = (bf16[384,768]{1,0:T(8,128)(2,1)S(1)}, bf16[384,768]{1,0:T(8,128)(2,1)S(1)}, u32[]{:S(2)}, u32[]{:S(2)}) collective-permute-start(bf16[384,768]{1,0:T(8,128)(2,1)S(1)} %collective-permute-done.19.rest_2_), channel_id=1, source_target_pairs={{0,1},{1,0},{2,3},{3,2},{4,5},{5,4},{6,7},{7,6},{8,9},{9,8},{10,11... | collective-permute-start | bytes 1769480 | tf_op jit(solution)/shard_map/ppermute | solution.py:683
  73.2 9.5 %collective-permute-start.22 = (bf16[384,768]{1,0:T(8,128)(2,1)}, bf16[384,768]{1,0:T(8,128)(2,1)S(1)}, u32[]{:S(2)}, u32[]{:S(2)}) collective-permute-start(bf16[384,768]{1,0:T(8,128)(2,1)} %collective-permute-done.18.rest_1_), channel_id=1, source_target_pairs={{0,1},{1,0},{2,3},{3,2},{4,5},{5,4},{6,7},{7,6},{8,9},{9,8},{10,11... | collective-permute-start | bytes 1769480 | tf_op jit(solution)/shard_map/ppermute | solution.py:683
  82.2 2.1 collective-permute-start.24
  105.3 6.7 %collective-permute-start.25 = (bf16[4,384,768]{2,1,0:T(8,128)(2,1)}, bf16[4,384,768]{2,1,0:T(8,128)(2,1)S(1)}, u32[]{:S(2)}, u32[]{:S(2)}) collective-permute-start(bf16[4,384,768]{2,1,0:T(8,128)(2,1)} %get-tuple-element.130), channel_id=1, source_target_pairs={{0,1},{1,0},{2,3},{3,2},{4,5},{5,4},{6,7},{7,6},{8,9},{9,8},{10,11... | collective-permute-start | bytes 7077896 | tf_op jit(solution)/shard_map/ppermute | solution.py:683
  119.8 12.9 %collective-permute-start.27 = (bf16[4,96,3072]{2,1,0:T(8,128)(2,1)}, bf16[4,96,3072]{2,1,0:T(8,128)(2,1)S(1)}, u32[]{:S(2)}, u32[]{:S(2)}) collective-permute-start(bf16[4,96,3072]{2,1,0:T(8,128)(2,1)} %get-tuple-element.138), channel_id=1, source_target_pairs={{0,1},{1,0},{2,3},{3,2},{4,5},{5,4},{6,7},{7,6},{8,9},{9,8},{10,11... | collective-permute-start | bytes 7077896 | tf_op jit(solution)/shard_map/ppermute | solution.py:683
  120.0 16.2 %collective-permute-start.26 = (bf16[2,384,768]{2,1,0:T(8,128)(2,1)S(1)}, bf16[2,384,768]{2,1,0:T(8,128)(2,1)S(1)}, u32[]{:S(2)}, u32[]{:S(2)}) collective-permute-start(bf16[2,384,768]{2,1,0:T(8,128)(2,1)S(1)} %add_convert_fusion.1), channel_id=1, source_target_pairs={{0,2},{1,5},{2,0},{3,7},{4,6},{5,1},{6,4},{7,3},{8,10},{9,13},{10,... | collective-permute-start | bytes 3538952 | tf_op jit(solution)/shard_map/ppermute | solution.py:691
  120.5 12.2 %copy-start.6 = (bf16[4,96,3072]{2,1,0:T(8,128)(2,1)S(1)}, bf16[4,96,3072]{2,1,0:T(8,128)(2,1)}, u32[]{:S(2)}) copy-start(bf16[4,96,3072]{2,1,0:T(8,128)(2,1)} %get-tuple-element.139) | copy-start | bytes 7077892
  132.7 23.0 %copy-start.7 = (bf16[4,96,3072]{2,1,0:T(8,128)(2,1)}, bf16[4,96,3072]{2,1,0:T(8,128)(2,1)S(1)}, u32[]{:S(2)}) copy-start(bf16[4,96,3072]{2,1,0:T(8,128)(2,1)S(1)} %collective-permute-done.27) | copy-start | bytes 7077892
  133.2 22.6 %collective-permute-start.28 = (bf16[2,96,3072]{2,1,0:T(8,128)(2,1)S(1)}, bf16[2,96,3072]{2,1,0:T(8,128)(2,1)S(1)}, u32[]{:S(2)}, u32[]{:S(2)}) collective-permute-start(bf16[2,96,3072]{2,1,0:T(8,128)(2,1)S(1)} %add_convert_fusion), channel_id=1, source_target_pairs={{0,2},{1,5},{2,0},{3,7},{4,6},{5,1},{6,4},{7,3},{8,10},{9,13},{10,... | collective-permute-start | bytes 3538952 | tf_op jit(solution)/shard_map/ppermute | solution.py:691
  136.4 16.3 %collective-permute-start.29 = (bf16[384,768]{1,0:T(8,128)(2,1)S(1)}, bf16[384,768]{1,0:T(8,128)(2,1)S(1)}, u32[]{:S(2)}, u32[]{:S(2)}) collective-permute-start(bf16[384,768]{1,0:T(8,128)(2,1)S(1)} %fusion.6), channel_id=1, source_target_pairs={{0,4},{1,3},{2,6},{3,1},{4,0},{5,7},{6,2},{7,5},{8,12},{9,11},{10,... | collective-permute-start | bytes 1769480 | tf_op jit(solution)/shard_map/ppermute | solution.py:691
  151.0 27.2 %collective-permute-start.33 = (bf16[4,96,1920]{2,1,0:T(8,128)(2,1)}, bf16[4,96,1920]{2,1,0:T(8,128)(2,1)}, u32[]{:S(2)}, u32[]{:S(2)}) collective-permute-start(bf16[4,96,1920]{2,1,0:T(8,128)(2,1)} %get-tuple-element.151), channel_id=1, source_target_pairs={{0,1},{1,0},{2,3},{3,2},{4,5},{5,4},{6,7},{7,6},{8,9},{9,8},{10,11... | collective-permute-start | bytes 4423688 | tf_op jit(solution)/shard_map/ppermute | solution.py:683
  157.0 17.6 %collective-permute-start.30 = (bf16[96,3072]{1,0:T(8,128)(2,1)}, bf16[96,3072]{1,0:T(8,128)(2,1)}, u32[]{:S(2)}, u32[]{:S(2)}) collective-permute-start(bf16[96,3072]{1,0:T(8,128)(2,1)} %fusion.7), channel_id=1, source_target_pairs={{0,4},{1,3},{2,6},{3,1},{4,0},{5,7},{6,2},{7,5},{8,12},{9,11},{10,... | collective-permute-start | bytes 1769480 | tf_op jit(solution)/shard_map/ppermute | solution.py:691
  158.5 23.3 %collective-permute-start.36 = (bf16[384,768]{1,0:T(8,128)(2,1)S(1)}, bf16[384,768]{1,0:T(8,128)(2,1)S(1)}, u32[]{:S(2)}, u32[]{:S(2)}) collective-permute-start(bf16[384,768]{1,0:T(8,128)(2,1)S(1)} %fusion.4), channel_id=1, source_target_pairs={{0,8},{24,16},{1,9},{25,17},{2,10},{26,18},{3,11},{27,19},{4,12},{... | collective-permute-start | bytes 1769480 | tf_op jit(solution)/shard_map/ppermute | solution.py:747
  174.6 5.4 %collective-permute-start.32 = (bf16[4,112,1152]{2,1,0:T(8,128)(2,1)}, bf16[4,112,1152]{2,1,0:T(8,128)(2,1)S(1)}, u32[]{:S(2)}, u32[]{:S(2)}) collective-permute-start(bf16[4,112,1152]{2,1,0:T(8,128)(2,1)} %get-tuple-element.162), channel_id=1, source_target_pairs={{0,1},{1,0},{2,3},{3,2},{4,5},{5,4},{6,7},{7,6},{8,9},{9,8},{10,11... | collective-permute-start | bytes 3096584 | tf_op jit(solution)/shard_map/ppermute | solution.py:683
  176.5 22.6 %collective-permute-start.31 = (bf16[96,3072]{1,0:T(8,128)(2,1)S(1)}, bf16[96,3072]{1,0:T(8,128)(2,1)S(1)}, u32[]{:S(2)}, u32[]{:S(2)}) collective-permute-start(bf16[96,3072]{1,0:T(8,128)(2,1)S(1)} %fusion.3), channel_id=1, source_target_pairs={{0,8},{24,16},{1,9},{25,17},{2,10},{26,18},{3,11},{27,19},{4,12},{... | collective-permute-start | bytes 1769480 | tf_op jit(solution)/shard_map/ppermute | solution.py:747
  179.5 11.5 %collective-permute-start.35 = (bf16[2,96,1920]{2,1,0:T(8,128)(2,1)S(1)}, bf16[2,96,1920]{2,1,0:T(8,128)(2,1)S(1)}, u32[]{:S(2)}, u32[]{:S(2)}) collective-permute-start(bf16[2,96,1920]{2,1,0:T(8,128)(2,1)S(1)} %add_convert_fusion.2), channel_id=1, source_target_pairs={{0,2},{1,5},{2,0},{3,7},{4,6},{5,1},{6,4},{7,3},{8,10},{9,13},{10,... | collective-permute-start | bytes 2211848 | tf_op jit(solution)/shard_map/ppermute | solution.py:691
  180.1 18.5 %collective-permute-start.34 = (bf16[2,112,1152]{2,1,0:T(8,128)(2,1)S(1)}, bf16[2,112,1152]{2,1,0:T(8,128)(2,1)S(1)}, u32[]{:S(2)}, u32[]{:S(2)}) collective-permute-start(bf16[2,112,1152]{2,1,0:T(8,128)(2,1)S(1)} %add_convert_fusion.9), channel_id=1, source_target_pairs={{0,2},{1,5},{2,0},{3,7},{4,6},{5,1},{6,4},{7,3},{8,10},{9,13},{10,... | collective-permute-start | bytes 1548296 | tf_op jit(solution)/shard_map/ppermute | solution.py:691
  182.0 28.9 %collective-permute-start.42 = (bf16[384,768]{1,0:T(8,128)(2,1)S(1)}, bf16[384,768]{1,0:T(8,128)(2,1)S(1)}, u32[]{:S(2)}, u32[]{:S(2)}) collective-permute-start(bf16[384,768]{1,0:T(8,128)(2,1)S(1)} %add_convert_fusion.6), channel_id=1, source_target_pairs={{8,16},{16,8},{9,17},{17,9},{10,18},{18,10},{11,19},{19,11},{12,20... | collective-permute-start | bytes 1769480 | tf_op jit(solution)/shard_map/ppermute | solution.py:751
  192.2 16.1 %collective-permute-start.37 = (bf16[96,1920]{1,0:T(8,128)(2,1)S(1)}, bf16[96,1920]{1,0:T(8,128)(2,1)S(1)}, u32[]{:S(2)}, u32[]{:S(2)}) collective-permute-start(bf16[96,1920]{1,0:T(8,128)(2,1)S(1)} %fusion.9), channel_id=1, source_target_pairs={{0,4},{1,3},{2,6},{3,1},{4,0},{5,7},{6,2},{7,5},{8,12},{9,11},{10,... | collective-permute-start | bytes 1105928 | tf_op jit(solution)/shard_map/ppermute | solution.py:691
  198.7 6.4 %collective-permute-start.38 = (bf16[112,1152]{1,0:T(8,128)(2,1)S(1)}, bf16[112,1152]{1,0:T(8,128)(2,1)S(1)}, u32[]{:S(2)}, u32[]{:S(2)}) collective-permute-start(bf16[112,1152]{1,0:T(8,128)(2,1)S(1)} %fusion.10), channel_id=1, source_target_pairs={{0,4},{1,3},{2,6},{3,1},{4,0},{5,7},{6,2},{7,5},{8,12},{9,11},{10,... | collective-permute-start | bytes 774152 | tf_op jit(solution)/shard_map/ppermute | solution.py:691
  199.3 13.0 %collective-permute-start.41 = (bf16[96,3072]{1,0:T(8,128)(2,1)S(1)}, bf16[96,3072]{1,0:T(8,128)(2,1)S(1)}, u32[]{:S(2)}, u32[]{:S(2)}) collective-permute-start(bf16[96,3072]{1,0:T(8,128)(2,1)S(1)} %add_convert_fusion.5), channel_id=1, source_target_pairs={{8,16},{16,8},{9,17},{17,9},{10,18},{18,10},{11,19},{19,11},{12,20... | collective-permute-start | bytes 1769480 | tf_op jit(solution)/shard_map/ppermute | solution.py:751
  205.3 9.7 %collective-permute-start.40 = (bf16[112,1152]{1,0:T(8,128)(2,1)S(1)}, bf16[112,1152]{1,0:T(8,128)(2,1)S(1)}, u32[]{:S(2)}, u32[]{:S(2)}) collective-permute-start(bf16[112,1152]{1,0:T(8,128)(2,1)S(1)} %fusion.8), channel_id=1, source_target_pairs={{0,8},{24,16},{1,9},{25,17},{2,10},{26,18},{3,11},{27,19},{4,12},{... | collective-permute-start | bytes 774152 | tf_op jit(solution)/shard_map/ppermute | solution.py:747
  209.5 9.6 %collective-permute-start.39 = (bf16[96,1920]{1,0:T(8,128)(2,1)S(1)}, bf16[96,1920]{1,0:T(8,128)(2,1)S(1)}, u32[]{:S(2)}, u32[]{:S(2)}) collective-permute-start(bf16[96,1920]{1,0:T(8,128)(2,1)S(1)} %fusion.5), channel_id=1, source_target_pairs={{0,8},{24,16},{1,9},{25,17},{2,10},{26,18},{3,11},{27,19},{4,12},{... | collective-permute-start | bytes 1105928 | tf_op jit(solution)/shard_map/ppermute | solution.py:747
  211.0 18.2 %collective-permute-start.48 = (bf16[384,768]{1,0:T(8,128)(2,1)S(1)}, bf16[384,768]{1,0:T(8,128)(2,1)S(1)}, u32[]{:S(2)}, u32[]{:S(2)}) collective-permute-start(bf16[384,768]{1,0:T(8,128)(2,1)S(1)} %add_convert_fusion.4), channel_id=1, source_target_pairs={{8,0},{16,24},{9,1},{17,25},{10,2},{18,26},{11,3},{19,27},{12,4},{... | collective-permute-start | bytes 1769480 | tf_op jit(solution)/shard_map/ppermute | solution.py:756
  212.5 16.7 %copy-start.15 = (f32[384,768]{1,0:T(8,128)S(1)}, f32[384,768]{1,0:T(8,128)}, u32[]{:S(2)}) copy-start(f32[384,768]{1,0:T(8,128)} %param.30) | copy-start | bytes 3538948
  212.5 16.7 %copy-start.16 = (f32[384,768]{1,0:T(8,128)S(1)}, f32[384,768]{1,0:T(8,128)}, u32[]{:S(2)}) copy-start(f32[384,768]{1,0:T(8,128)} %param.35) | copy-start | bytes 3538948
  212.5 36.1 %collective-permute-start.47 = (bf16[96,3072]{1,0:T(8,128)(2,1)S(1)}, bf16[96,3072]{1,0:T(8,128)(2,1)S(1)}, u32[]{:S(2)}, u32[]{:S(2)}) collective-permute-start(bf16[96,3072]{1,0:T(8,128)(2,1)S(1)} %add_convert_fusion.3), channel_id=1, source_target_pairs={{8,0},{16,24},{9,1},{17,25},{10,2},{18,26},{11,3},{19,27},{12,4},{... | collective-permute-start | bytes 1769480 | tf_op jit(solution)/shard_map/ppermute | solution.py:756
  215.0 4.9 %collective-permute-start.44 = (bf16[112,1152]{1,0:T(8,128)(2,1)S(1)}, bf16[112,1152]{1,0:T(8,128)(2,1)S(1)}, u32[]{:S(2)}, u32[]{:S(2)}) collective-permute-start(bf16[112,1152]{1,0:T(8,128)(2,1)S(1)} %add_convert_fusion.14), channel_id=1, source_target_pairs={{8,16},{16,8},{9,17},{17,9},{10,18},{18,10},{11,19},{19,11},{12,20... | collective-permute-start | bytes 774152 | tf_op jit(solution)/shard_map/ppermute | solution.py:751
  219.2 12.4 %collective-permute-start.43 = (bf16[96,1920]{1,0:T(8,128)(2,1)S(1)}, bf16[96,1920]{1,0:T(8,128)(2,1)S(1)}, u32[]{:S(2)}, u32[]{:S(2)}) collective-permute-start(bf16[96,1920]{1,0:T(8,128)(2,1)S(1)} %add_convert_fusion.11), channel_id=1, source_target_pairs={{8,16},{16,8},{9,17},{17,9},{10,18},{18,10},{11,19},{19,11},{12,20... | collective-permute-start | bytes 1105928 | tf_op jit(solution)/shard_map/ppermute | solution.py:751
  220.0 27.3 %collective-permute-start.46 = (bf16[112,1152]{1,0:T(8,128)(2,1)S(1)}, bf16[112,1152]{1,0:T(8,128)(2,1)S(1)}, u32[]{:S(2)}, u32[]{:S(2)}) collective-permute-start(bf16[112,1152]{1,0:T(8,128)(2,1)S(1)} %add_convert_fusion.13), channel_id=1, source_target_pairs={{8,0},{16,24},{9,1},{17,25},{10,2},{18,26},{11,3},{19,27},{12,4},{... | collective-permute-start | bytes 774152 | tf_op jit(solution)/shard_map/ppermute | solution.py:756
  229.2 19.4 %copy-start.18 = (f32[96,3072]{1,0:T(8,128)S(1)}, f32[96,3072]{1,0:T(8,128)}, u32[]{:S(2)}) copy-start(f32[96,3072]{1,0:T(8,128)} %param.34) | copy-start | bytes 3538948
  231.6 15.7 %copy-start.41 = (f32[384]{0:T(512)S(1)}, f32[384]{0:T(512)}, u32[]{:S(2)}) copy-start(f32[384]{0:T(512)} %param.31) | copy-start | bytes 4612
  231.6 15.7 %copy-start.42 = (f32[384]{0:T(512)S(1)}, f32[384]{0:T(512)}, u32[]{:S(2)}) copy-start(f32[384]{0:T(512)} %param.36) | copy-start | bytes 4612
  231.6 16.3 %copy-start.38 = (f32[8,96]{1,0:T(8,128)S(1)}, f32[8,96]{1,0:T(8,128)}, u32[]{:S(2)}) copy-start(f32[8,96]{1,0:T(8,128)} %param.32) | copy-start | bytes 9220
  231.6 16.3 %copy-start.39 = (f32[8,96]{1,0:T(8,128)S(1)}, f32[8,96]{1,0:T(8,128)}, u32[]{:S(2)}) copy-start(f32[8,96]{1,0:T(8,128)} %param.37) | copy-start | bytes 9220
  231.6 16.9 %copy-start.17 = (f32[96,3072]{1,0:T(8,128)S(1)}, f32[96,3072]{1,0:T(8,128)}, u32[]{:S(2)}) copy-start(f32[96,3072]{1,0:T(8,128)} %param.29) | copy-start | bytes 3538948
  231.8 19.4 %collective-permute-start.45 = (bf16[96,1920]{1,0:T(8,128)(2,1)S(1)}, bf16[96,1920]{1,0:T(8,128)(2,1)S(1)}, u32[]{:S(2)}, u32[]{:S(2)}) collective-permute-start(bf16[96,1920]{1,0:T(8,128)(2,1)S(1)} %add_convert_fusion.10), channel_id=1, source_target_pairs={{8,0},{16,24},{9,1},{17,25},{10,2},{18,26},{11,3},{19,27},{12,4},{... | collective-permute-start | bytes 1105928 | tf_op jit(solution)/shard_map/ppermute | solution.py:756
  (30 other events, 115.6 us)

commit v5 on v4

--- a/solution.py
+++ b/solution.py
@@ -172,34 +172,63 @@
     return jnp.concatenate([jnp.where(first, value, zero), jnp.where(first, zero, value)], axis=0)
 
 
-GROUP = 2
+GROUP = 4
+
+
+def by_stages(units, stages):
+    for stage in stages:
+        for unit in units:
+            stage(unit)
+
+
+def staggered(units, stages):
+    for start in range(len(units) + len(stages) - 1):
+        for number in reversed(range(len(stages))):
+            if 0 <= start - number < len(units):
+                stages[number](units[start - number])
+
+
+def place(unit, part=0):
+    lead = part * PART + unit[1] * 2 * HDIM
+    return slice(unit[0] * SEQ, (unit[0] + 1) * SEQ), slice(lead, lead + 2 * HDIM)
+
+
+def weight_place(unit):
+    return slice(unit[0] * SEQ, (unit[0] + 1) * SEQ), slice(unit[1] * 2 * SEQ, (unit[1] + 1) * 2 * SEQ)
+
+
+UNITS = [(pair, heads) for pair in range(GROUP) for heads in range(PART // (2 * HDIM))]
 
 
 def attention(lengths, qkv):
     rows = qkv.shape[0]
-    wide = 2 * HDIM
 
     def kernel(s, qkv_ref, out_ref, p_ref):
         first = head_masks()
-        for g in range(GROUP):
-            at = slice(g * SEQ, (g + 1) * SEQ)
-            length = s[pl.program_id(0) * GROUP + g]
-            valid = lax.broadcasted_iota(jnp.int32, (SEQ, SEQ), 1) < length
-            for h in range(PART // wide):
-                lanes = slice(h * wide, (h + 1) * wide)
-                q = qkv_ref[at, lanes]
-                k = qkv_ref[at, PART + h * wide : PART + (h + 1) * wide]
-                v = qkv_ref[at, 2 * PART + h * wide : 2 * PART + (h + 1) * wide]
-                scores = dot(q, stack_heads(k, first), NT)
-                halves = []
-                for part in range(2):
-                    one = jnp.where(valid, scores[:, part * SEQ : (part + 1) * SEQ], masked_score)
-                    top = jnp.max(one, axis=-1, keepdims=True)
-                    raised = jnp.exp(one - top)
-                    halves.append(raised * (1.0 / lane_sum(raised)))
-                weights = jnp.concatenate(halves, axis=1)
-                p_ref[at, h * 2 * SEQ : (h + 1) * 2 * SEQ] = weights
-                out_ref[at, lanes] = dot(weights.astype(bf16), stack_heads(v, first), NN).astype(bf16)
+        key = lax.broadcasted_iota(jnp.int32, (SEQ, SEQ), 1)
+        valid = [key < s[pl.program_id(0) * GROUP + pair] for pair in range(GROUP)]
+        scores, low = {}, {}
+
+        def score(unit):
+            keys = stack_heads(qkv_ref[place(unit, 1)], first)
+            scores[unit] = dot(qkv_ref[place(unit)], keys, NT)
+
+        def soften(unit):
+            halves = []
+            for part in range(2):
+                one = scores[unit][:, part * SEQ : (part + 1) * SEQ]
+                one = jnp.where(valid[unit[0]], one, masked_score)
+                raised = jnp.exp(one - jnp.max(one, axis=-1, keepdims=True))
+                halves.append(raised * (1.0 / lane_sum(raised)))
+            weights = jnp.concatenate(halves, axis=1)
+            p_ref[weight_place(unit)] = weights
+            low[unit] = weights.astype(bf16)
+
+        def attend(unit):
+            values = stack_heads(qkv_ref[place(unit, 2)], first)
+            out_ref[place(unit)] = dot(low[unit], values, NN).astype(bf16)
+
+        staggered(UNITS, (score, soften, attend))
 
     width = HEADS * SEQ // 2
     return call(
@@ -238,7 +267,7 @@
         [rows_of(PART), rows_of(PART), rows_of(D), whole((8, D))] + [ANY] * count,
         [rows_of(D), rows_of(1), rows_of(D), HELD],
         [
-            pltpu.HBM((rows, D), f32),
+            pltpu.VMEM((rows, D), f32),
             pltpu.HBM((rows, 1), f32),
             pltpu.VMEM((rows, D), bf16),
             pltpu.VMEM(weight.shape, bf16),
@@ -308,7 +337,7 @@
         [rows_of(D), rows_of(D), rows_of(D), whole((8, D)), HELD],
         [
             jax.ShapeDtypeStruct((rows, D), bf16),
-            pltpu.HBM((rows, D), f32),
+            pltpu.VMEM((rows, D), f32),
             jax.ShapeDtypeStruct((rows, D), bf16),
             jax.ShapeDtypeStruct((8, D), f32),
             pltpu.VMEM(weight.shape, bf16),
@@ -317,7 +346,7 @@
         flops=2 * rows * D * FF,
         bytes_accessed=rows * (D * 14 + FF * 2) + 2 * D * FF,
         name="feed_out",
-    )(me, in_vmem(activated), in_hbm(normed_one), cotangent, vectors, *weight.arrays)
+    )(me, in_vmem(activated), in_vmem(normed_one), cotangent, vectors, *weight.arrays)
 
 
 def slot(chip, core):
@@ -427,8 +456,8 @@
     )(
         me,
         in_vmem(grad_pre),
-        in_hbm(grad_res_two),
-        in_hbm(normed_one),
+        in_vmem(grad_res_two),
+        in_vmem(normed_one),
         in_hbm(inv_one),
         vectors,
         in_vmem(weight),
@@ -470,7 +499,6 @@
 def attention_back(lengths, qkv, weights, grad_attended):
     rows = qkv.shape[0]
     scale = HDIM ** (-0.5)
-    wide = 2 * HDIM
     width = HEADS * SEQ // 2
 
     def kernel(s, qkv_ref, p_ref, do_ref, out_ref, sums_ref):
@@ -479,33 +507,44 @@
             sums_ref[...] = jnp.zeros_like(sums_ref)
 
         first = head_masks()
-        for g in range(GROUP):
-            at = slice(g * SEQ, (g + 1) * SEQ)
-            for h in range(PART // wide):
-                lanes = slice(h * wide, (h + 1) * wide)
-                k_lanes = slice(PART + h * wide, PART + (h + 1) * wide)
-                v_lanes = slice(2 * PART + h * wide, 2 * PART + (h + 1) * wide)
-                q, k, v = qkv_ref[at, lanes], qkv_ref[at, k_lanes], qkv_ref[at, v_lanes]
-                grad_out = do_ref[at, lanes]
-                p = p_ref[at, h * 2 * SEQ : (h + 1) * 2 * SEQ]
-                grad_p = dot(grad_out, stack_heads(v, first), NT)
-                both = grad_p * p
-                halves = []
-                for part in range(2):
-                    cut = slice(part * SEQ, (part + 1) * SEQ)
-                    inner = grad_p[:, cut] - lane_sum(both[:, cut])
-                    halves.append((p[:, cut] * inner).astype(bf16))
-                grad_s = jnp.concatenate(halves, axis=1)
-                grad_v = dot(p.astype(bf16), grad_out, TN)
-                grad_v = jnp.where(first, grad_v[:SEQ], grad_v[SEQ:]).astype(bf16)
-                grad_q = (dot(grad_s, stack_heads(k, first), NN) * scale).astype(bf16)
-                grad_k = dot(grad_s, q, TN)
-                grad_k = jnp.where(first, grad_k[:SEQ], grad_k[SEQ:]).astype(bf16)
-                out_ref[at, lanes] = grad_q
-                out_ref[at, k_lanes] = grad_k
-                out_ref[at, v_lanes] = grad_v
-                sums_ref[0:1, lanes] += jnp.sum(grad_q.astype(f32), axis=0, keepdims=True)
-                sums_ref[1:2, lanes] += jnp.sum(grad_v.astype(f32), axis=0, keepdims=True)
+        grad_p, grad_s, grad_q, grad_k, grad_v = {}, {}, {}, {}, {}
+
+        def back_weights(unit):
+            values = stack_heads(qkv_ref[place(unit, 2)], first)
+            grad_p[unit] = dot(do_ref[place(unit)], values, NT)
+
+        def back_values(unit):
+            both = dot(p_ref[weight_place(unit)].astype(bf16), do_ref[place(unit)], TN)
+            grad_v[unit] = jnp.where(first, both[:SEQ], both[SEQ:]).astype(bf16)
+
+        def back_softmax(unit):
+            p = p_ref[weight_place(unit)]
+            product = grad_p[unit] * p
+            halves = []
+            for part in range(2):
+                cut = slice(part * SEQ, (part + 1) * SEQ)
+                inner = grad_p[unit][:, cut] - lane_sum(product[:, cut])
+                halves.append((p[:, cut] * inner).astype(bf16))
+            grad_s[unit] = jnp.concatenate(halves, axis=1)
+
+        def back_queries(unit):
+            keys = stack_heads(qkv_ref[place(unit, 1)], first)
+            grad_q[unit] = (dot(grad_s[unit], keys, NN) * scale).astype(bf16)
+
+        def back_keys(unit):
+            both = dot(grad_s[unit], qkv_ref[place(unit)], TN)
+            grad_k[unit] = jnp.where(first, both[:SEQ], both[SEQ:]).astype(bf16)
+
+        def store(unit):
+            out_ref[place(unit)] = grad_q[unit]
+            out_ref[place(unit, 1)] = grad_k[unit]
+            out_ref[place(unit, 2)] = grad_v[unit]
+            lanes = place(unit)[1]
+            sums_ref[0:1, lanes] += jnp.sum(grad_q[unit].astype(f32), axis=0, keepdims=True)
+            sums_ref[1:2, lanes] += jnp.sum(grad_v[unit].astype(f32), axis=0, keepdims=True)
+
+        stages = (back_weights, back_values, back_softmax, back_queries, back_keys, store)
+        by_stages(UNITS, stages)
 
     return call(
         kernel,

time: 256 us -> 250 us (0.977)
  Pallas kernels: 119 us -> 108 us
  waiting for transfers between devices: 61 us -> 67.2 us
    pallas_call x2, Pallas kernels: 17.6 us -> 9.88 us  [attention_back(): call(kernel, (rows // (GROUP * SEQ),), [rows_of(3 * PART, GROUP * SEQ), r...]
    ppermute x17, waiting for transfers between devices: 27.6 us -> 33.9 us  [split_swap(): lax.ppermute(value, 'fsdp', [(i, i ^ (odd_bit if i & 1 else even_bit)) fo...]
  transfers between devices with their start and end apart: 49 -> 49, of which waited for: 20 -> 20; matrix products, arithmetic and copies ran while one was open for 8% -> 8% of each run, Pallas kernels for 36% -> 33%
where the time goes in v5:
time: 250 us
  Pallas kernels  108 us (43%)
  waiting for transfers between devices  67.2 us (27%)
  starting transfers between devices  44.6 us (18%)
  other arithmetic  20.8 us (8%)
  local copies, waits for them, and re-layouts  7.58 us (3%)
    ppermute x17, waiting for transfers between devices, split_swap(): lax.ppermute(value, 'fsdp', [(i, i ^ (odd_bit if i & 1 else even_bit)) fo...  33.9 us
    ppermute x4, waiting for transfers between devices, five(): self.back = lax.ppermute(self.total, 'rep', [(1, 0), (2, 3)])  22 us
    ppermute x17, starting transfers between devices, split_swap(): lax.ppermute(value, 'fsdp', [(i, i ^ (odd_bit if i & 1 else even_bit)) fo...  20.3 us
    pallas_call x1, Pallas kernels, back_in(): call(kernel, (rows // TILE,), [rows_of(FF), rows_of(D), rows_of(D), rows_...  12.4 us
    pallas_call x2, Pallas kernels, attention(): call(kernel, (rows // (GROUP * SEQ),), [rows_of(3 * PART, GROUP * SEQ)],...  11.4 us
    pallas_call x1, Pallas kernels, feed_out(): call(kernel, (rows // TILE,), [rows_of(FF), rows_of(D), rows_of(D), whole...  11.2 us
    pallas_call x2, Pallas kernels, attention_back(): call(kernel, (rows // (GROUP * SEQ),), [rows_of(3 * PART, GROUP * SEQ), r...  9.88 us
    ppermute x4, starting transfers between devices, line(): self.near = lax.ppermute(self.owned, 'rep', [(0, 1), (3, 2)])  9.44 us
  transfers between devices with their start and end apart: 49, of which 20 were waited for; matrix products, arithmetic and copies ran while one was open for 8% of the time, Pallas kernels for 33%

profile of v5, /device:TPU:0, one launch (start us, length us, event | category | flops | bytes accessed | tf_op | source)
XLA Modules:
  0.0 249.6 jit_solution(8396215427310201646)
XLA Ops:
  0.7 1.4 convert.32
  2.3 3.0 %collective-permute-start.5 = (bf16[96,2304]{1,0:T(8,128)(2,1)S(1)}, bf16[96,2304]{1,0:T(8,128)(2,1)}, u32[]{:S(2)}, u32[]{:S(2)}) collective-permute-start(bf16[96,2304]{1,0:T(8,128)(2,1)S(1)} %slice_dynamic-update-slice_fusion.7.rest_0_), channel_id=1, source_target_pairs={{0,4},{1,3},{2,6},{3,1},{4,0},{5,7},{6,2},{7,5},{8,12},{9,11},{10,... | collective-permute-start | bytes 1327112 | tf_op jit(solution)/shard_map/ppermute | solution.py:730
  5.3 1.5 collective-permute-start.4
  7.0 1.0 slice.298
  8.9 1.9 collective-permute-start.2
  10.9 1.5 collective-permute-start.1
  12.4 4.4 %collective-permute-done.3 = bf16[2,1152]{1,0:T(2,128)(2,1)S(1)} collective-permute-done((bf16[2,1152]{1,0:T(2,128)(2,1)S(1)}, bf16[2,1152]{1,0:T(2,128)(2,1)S(1)}, u32[]{:S(2)}, u32[]{:S(2)}) %collective-permute-start.3) | collective-permute-done | bytes 4640 | tf_op jit(solution)/shard_map/ppermute | solution.py:722
  17.5 1.7 collective-permute-start.6
  20.8 5.4 %collective-permute-done.6.rest_3_ = bf16[96,2304]{1,0:T(8,128)(2,1)} collective-permute-done((bf16[96,2304]{1,0:T(8,128)(2,1)}, bf16[96,2304]{1,0:T(8,128)(2,1)}, u32[]{:S(2)}, u32[]{:S(2)}) %collective-permute-start.6) | collective-permute-done | bytes 442400 | tf_op jit(solution)/shard_map/ppermute | solution.py:730
  26.2 1.5 collective-permute-start.11
  30.4 7.3 %qkv.1 = (bf16[1024,1152]{1,0:T(8,128)(2,1)}, bf16[1024,1152]{1,0:T(8,128)(2,1)}) custom-call(s32[1]{0:T(128)} %bitcast.s, bf16[1024,768]{1,0:T(8,128)(2,1)S(1)} %copy-done, f32[1,2304]{1,0:T(1,128)S(1)} %reshape.165.b_ref, bf16[96,2304]{1,0:T(8,128)(2,1)} %copy-done.9, bf16[96,2304]{1,0:T(8,128)(2,1)} %collective-permute-done.4.rest_1_, ...), custom_call_target="tpu_custom_call" | custom-call | flops 3623878 | bytes 9830 | tf_op jit(solution)/shard_map/qkv/pallas_call | solution.py:149
  37.8 1.8 collective-permute-done.12.rest_2_
  39.5 1.9 collective-permute-done.11.rest_1_
  41.5 1.3 collective-permute-start.16
  43.5 5.7 %attention.2 = (bf16[1024,384]{1,0:T(8,128)(2,1)S(1)}, f32[1024,768]{1,0:T(8,128)}) custom-call(s32[8]{0:T(128)S(1)} %copy-done.4, bf16[1024,1152]{1,0:T(8,128)(2,1)} %get-tuple-element.112.qkv_ref), custom_call_target="tpu_custom_call" | custom-call | flops 4000000 | bytes 6291 | tf_op jit(solution)/shard_map/attention/pallas_call | solution.py:234
  49.2 4.0 %collective-permute-done.16.rest_3_ = bf16[96,3840]{1,0:T(8,128)(2,1)} collective-permute-done((bf16[96,3840]{1,0:T(8,128)(2,1)}, bf16[96,3840]{1,0:T(8,128)(2,1)}, u32[]{:S(2)}, u32[]{:S(2)}) %collective-permute-start.16) | collective-permute-done | bytes 737312 | tf_op jit(solution)/shard_map/ppermute | solution.py:730
  54.2 1.3 collective-permute-start.19
  56.5 5.7 %attention.3 = (bf16[1024,384]{1,0:T(8,128)(2,1)S(1)}, f32[1024,768]{1,0:T(8,128)}) custom-call(s32[8]{0:T(128)S(1)} %copy-done.4, bf16[1024,1152]{1,0:T(8,128)(2,1)} %get-tuple-element.114.qkv_ref), custom_call_target="tpu_custom_call" | custom-call | flops 4000000 | bytes 6291 | tf_op jit(solution)/shard_map/attention/pallas_call | solution.py:234
  62.2 6.3 %project.1 = (f32[1024,768]{1,0:T(8,128)S(1)}, f32[1024,1]{1,0:T(8,128)}, bf16[1024,768]{1,0:T(8,128)(2,1)S(1)}, bf16[8,96,3840]{2,1,0:T(8,128)(2,1)S(1)}) custom-call(s32[1]{0:T(128)} %bitcast.s, bf16[1024,384]{1,0:T(8,128)(2,1)S(1)} %get-tuple-element.113.o0_ref, bf16[1024,384]{1,0:T(8,128)(2,1)S(1)} %get-tuple-element.115.o1_ref, ...), custom_call_target="tpu_custom_call" | custom-call | flops 1207959 | bytes 13762 | tf_op jit(solution)/shard_map/project/pallas_call | solution.py:264
  68.5 1.5 collective-permute-done.19.rest_2_
  70.3 1.6 collective-permute-start.20
  73.2 8.8 %expand.1 = (bf16[1024,3072]{1,0:T(8,128)(2,1)S(1)}, bf16[1024,3072]{1,0:T(8,128)(2,1)S(1)}) custom-call(s32[1]{0:T(128)} %bitcast.s, bf16[1024,768]{1,0:T(8,128)(2,1)S(1)} %get-tuple-element.122.h_ref, f32[1,3072]{1,0:T(1,128)S(1)} %bitcast.38, bf16[8,96,3840]{2,1,0:T(8,128)(2,1)S(1)} %get-tuple-element.123.w_ref), custom_call_target="tpu_custom_call" | custom-call | flops 4831838 | bytes 18874 | tf_op jit(solution)/shard_map/expand/pallas_call | solution.py:295
  82.6 1.6 collective-permute-done.24.rest_7_
  85.0 11.2 %feed_out.1 = (bf16[1024,768]{1,0:T(8,128)(2,1)}, f32[1024,768]{1,0:T(8,128)S(1)}, bf16[1024,768]{1,0:T(8,128)(2,1)S(1)}, f32[8,768]{1,0:T(8,128)S(1)}, bf16[8,384,768]{2,1,0:T(8,128)(2,1)S(1)}) custom-call(s32[1]{0:T(128)} %bitcast.s, bf16[1024,3072]{1,0:T(8,128)(2,1)S(1)} %get-tuple-element.124.f_ref, f32[1024,768]{1,0:T(8,128)S(1)} %get-tuple-element.125.n1_ref, ...), custom_call_target="tpu_custom_call" | custom-call | flops 4831838 | bytes 22020 | tf_op jit(solution)/shard_map/feed_out/pallas_call | solution.py:333
  96.3 7.4 %grad_w_out.1 = (bf16[4,384,768]{2,1,0:T(8,128)(2,1)}, bf16[4,384,768]{2,1,0:T(8,128)(2,1)}) custom-call(s32[1]{0:T(128)} %bitcast.s, bf16[1024,3072]{1,0:T(8,128)(2,1)S(1)} %get-tuple-element.124.f_ref, bf16[1024,768]{1,0:T(8,128)(2,1)S(1)} %get-tuple-element.132.dz_ref), custom_call_target="tpu_custom_call" | custom-call | flops 4831838 | bytes 12582 | tf_op jit(solution)/shard_map/grad_w_out/pallas_call | solution.py:372
  104.0 6.4 %back_out.1 = (bf16[1024,3072]{1,0:T(8,128)(2,1)S(1)}, f32[1,3072]{1,0:T(1,128)S(1)}) custom-call(s32[1]{0:T(128)} %bitcast.s, bf16[1024,768]{1,0:T(8,128)(2,1)S(1)} %get-tuple-element.132.dz_ref, bf16[1024,3072]{1,0:T(8,128)(2,1)S(1)} %get-tuple-element.133.sl_ref, bf16[8,384,768]{2,1,0:T(8,128)(2,1)S(1)} %get-tuple-element.134.w_ref), custom_call_target="tpu_custom_call" | custom-call | flops 4831838 | bytes 18874 | tf_op jit(solution)/shard_map/back_out/pallas_call | solution.py:404
  110.7 7.5 %grad_w_in.1 = (bf16[4,96,3072]{2,1,0:T(8,128)(2,1)}, bf16[4,96,3072]{2,1,0:T(8,128)(2,1)}) custom-call(s32[1]{0:T(128)} %bitcast.s, bf16[1024,768]{1,0:T(8,128)(2,1)S(1)} %get-tuple-element.122.h_ref, bf16[1024,3072]{1,0:T(8,128)(2,1)S(1)} %get-tuple-element.140.du_ref), custom_call_target="tpu_custom_call" | custom-call | flops 4831838 | bytes 14155 | tf_op jit(solution)/shard_map/grad_w_in/pallas_call | solution.py:487
  118.9 12.4 %back_in.1 = (f32[1024,768]{1,0:T(8,128)}, bf16[1024,768]{1,0:T(8,128)(2,1)S(1)}, bf16[1024,384]{1,0:T(8,128)(2,1)S(1)}, bf16[1024,384]{1,0:T(8,128)(2,1)S(1)}, f32[8,768]{1,0:T(8,128)S(1)}) custom-call(s32[1]{0:T(128)} %bitcast.s, bf16[1024,3072]{1,0:T(8,128)(2,1)S(1)} %get-tuple-element.140.du_ref, f32[1024,768]{1,0:T(8,128)S(1)} %get-tuple-element.141.dr2_ref, ...), custom_call_target="tpu_custom_call" | custom-call | flops 6039797 | bytes 24772 | tf_op jit(solution)/shard_map/back_in/pallas_call | solution.py:441
  131.8 1.5 collective-permute-start.28
  133.3 1.2 collective-permute-done.26
  135.4 4.8 %attention_back.2 = (bf16[1024,1152]{1,0:T(8,128)(2,1)S(1)}, f32[8,384]{1,0:T(8,128)S(1)}) custom-call(s32[8]{0:T(128)S(1)} %copy-done.4, bf16[1024,1152]{1,0:T(8,128)(2,1)} %get-tuple-element.112.qkv_ref, f32[1024,768]{1,0:T(8,128)} %get-tuple-element.128.p_ref, bf16[1024,384]{1,0:T(8,128)(2,1)S(1)} %get-tuple-element.147.do_ref), custom_call_target="tpu_custom_call" | custom-call | flops 7000000 | bytes 8650 | tf_op jit(solution)/shard_map/attention_back/pallas_call | solution.py:549
  140.2 5.2 %grad_w_mixed.1 = (bf16[4,96,1920]{2,1,0:T(8,128)(2,1)}, bf16[4,96,1920]{2,1,0:T(8,128)(2,1)}) custom-call(s32[1]{0:T(128)} %bitcast.s, bf16[1024,768]{1,0:T(8,128)(2,1)S(1)} %copy-done, bf16[1024,1152]{1,0:T(8,128)(2,1)S(1)} %get-tuple-element.148.g_ref.g0_ref, bf16[1024,384]{1,0:T(8,128)(2,1)S(1)} %get-tuple-element.113.o0_ref, ...), custom_call_target="tpu_custom_call" | custom-call | flops 3019898 | bytes 12386 | tf_op jit(solution)/shard_map/grad_w_mixed/pallas_call | solution.py:635
  145.4 5.7 %collective-permute-done.29 = bf16[384,768]{1,0:T(8,128)(2,1)S(1)} collective-permute-done((bf16[384,768]{1,0:T(8,128)(2,1)S(1)}, bf16[384,768]{1,0:T(8,128)(2,1)S(1)}, u32[]{:S(2)}, u32[]{:S(2)}) %collective-permute-start.29) | collective-permute-done | bytes 589856 | tf_op jit(solution)/shard_map/ppermute | solution.py:730
  151.5 2.9 %collective-permute-done.28 = bf16[2,96,3072]{2,1,0:T(8,128)(2,1)S(1)} collective-permute-done((bf16[2,96,3072]{2,1,0:T(8,128)(2,1)S(1)}, bf16[2,96,3072]{2,1,0:T(8,128)(2,1)S(1)}, u32[]{:S(2)}, u32[]{:S(2)}) %collective-permute-start.28) | collective-permute-done | bytes 1179680 | tf_op jit(solution)/shard_map/ppermute | solution.py:730
  154.4 1.2 fusion.7
  155.6 1.6 collective-permute-start.30
  157.2 3.6 %collective-permute-start.36 = (bf16[384,768]{1,0:T(8,128)(2,1)S(1)}, bf16[384,768]{1,0:T(8,128)(2,1)S(1)}, u32[]{:S(2)}, u32[]{:S(2)}) collective-permute-start(bf16[384,768]{1,0:T(8,128)(2,1)S(1)} %fusion.4), channel_id=1, source_target_pairs={{0,8},{24,16},{1,9},{25,17},{2,10},{26,18},{3,11},{27,19},{4,12},{... | collective-permute-start | bytes 1769480 | tf_op jit(solution)/shard_map/ppermute | solution.py:786
  160.8 5.1 %attention_back.3 = (bf16[1024,1152]{1,0:T(8,128)(2,1)S(1)}, f32[8,384]{1,0:T(8,128)S(1)}) custom-call(s32[8]{0:T(128)S(1)} %copy-done.4, bf16[1024,1152]{1,0:T(8,128)(2,1)} %get-tuple-element.114.qkv_ref, f32[1024,768]{1,0:T(8,128)} %get-tuple-element.149.p_ref, bf16[1024,384]{1,0:T(8,128)(2,1)S(1)} %get-tuple-element.155.do_ref), custom_call_target="tpu_custom_call" | custom-call | flops 7000000 | bytes 8650 | tf_op jit(solution)/shard_map/attention_back/pallas_call | solution.py:549
  165.8 3.6 %grad_w_qkv.1 = (bf16[4,112,1152]{2,1,0:T(8,128)(2,1)}, bf16[4,112,1152]{2,1,0:T(8,128)(2,1)}) custom-call(s32[1]{0:T(128)} %bitcast.s, bf16[1024,768]{1,0:T(8,128)(2,1)S(1)} %copy-done, bf16[1024,1152]{1,0:T(8,128)(2,1)S(1)} %get-tuple-element.174.g_ref.g1_ref, f32[8,384]{1,0:T(8,128)S(1)} %get-tuple-element.157.q0_ref, ...), custom_call_target="tpu_custom_call" | custom-call | flops 1811939 | bytes 8060 | tf_op jit(solution)/shard_map/grad_w_qkv/pallas_call | solution.py:602
  169.4 1.9 fusion.3
  171.4 1.5 collective-permute-start.31
  172.8 1.3 add_convert_fusion.2
  174.8 1.7 collective-permute-start.34
  177.3 6.2 %back_qkv.2 = (bf16[1024,768]{1,0:T(8,128)(2,1)}, bf16[8,96,2304]{2,1,0:T(8,128)(2,1)S(1)}) custom-call(s32[1]{0:T(128)} %bitcast.s, bf16[1024,1152]{1,0:T(8,128)(2,1)S(1)} %copy-done.2, bf16[1024,1152]{1,0:T(8,128)(2,1)S(1)} %get-tuple-element.174.g_ref.g1_ref, f32[1024,768]{1,0:T(8,128)} %get-tuple-element.169.dr_ref, bf16[96,2304]{1,0:T(8,128)(2,1)} %copy-done.9, ...), custom_call_target="tpu_custom_call" | custom-call | flops 1811939 | bytes 8257 | tf_op jit(solution)/shard_map/back_qkv/pallas_call | solution.py:689
  183.5 2.2 collective-permute-done.35
  185.7 1.1 fusion.9
  187.3 6.0 %collective-permute-done.34 = bf16[2,112,1152]{2,1,0:T(8,128)(2,1)S(1)} collective-permute-done((bf16[2,112,1152]{2,1,0:T(8,128)(2,1)S(1)}, bf16[2,112,1152]{2,1,0:T(8,128)(2,1)S(1)}, u32[]{:S(2)}, u32[]{:S(2)}) %collective-permute-start.34) | collective-permute-done | bytes 516128 | tf_op jit(solution)/shard_map/ppermute | solution.py:730
  194.7 4.1 %back_qkv.3 = bf16[1024,768]{1,0:T(8,128)(2,1)} custom-call(s32[1]{0:T(128)} %bitcast.s, bf16[1024,1152]{1,0:T(8,128)(2,1)S(1)} %copy-done.2, bf16[1024,1152]{1,0:T(8,128)(2,1)S(1)} %get-tuple-element.174.g_ref.g1_ref, f32[1024,768]{1,0:T(8,128)} %get-tuple-element.169.dr_ref, ...), custom_call_target="tpu_custom_call", output_to_operand_aliasing={{}: (5, {})} | custom-call | flops 1811939 | bytes 8257 | tf_op jit(solution)/shard_map/back_qkv/pallas_call | solution.py:698
  198.8 0.9 collective-permute-done.38
  199.9 3.1 %collective-permute-start.40 = (bf16[112,1152]{1,0:T(8,128)(2,1)S(1)}, bf16[112,1152]{1,0:T(8,128)(2,1)S(1)}, u32[]{:S(2)}, u32[]{:S(2)}) collective-permute-start(bf16[112,1152]{1,0:T(8,128)(2,1)S(1)} %fusion.8), channel_id=1, source_target_pairs={{0,8},{24,16},{1,9},{25,17},{2,10},{26,18},{3,11},{27,19},{4,12},{... | collective-permute-start | bytes 774152 | tf_op jit(solution)/shard_map/ppermute | solution.py:786
  203.0 1.2 fusion.5
  204.2 1.3 collective-permute-start.39
  205.6 1.3 collective-permute-start.48
  207.1 1.4 collective-permute-start.47
  208.6 1.1 collective-permute-done.40
  210.4 3.4 %collective-permute-done.39 = bf16[96,1920]{1,0:T(8,128)(2,1)S(1)} collective-permute-done((bf16[96,1920]{1,0:T(8,128)(2,1)S(1)}, bf16[96,1920]{1,0:T(8,128)(2,1)S(1)}, u32[]{:S(2)}, u32[]{:S(2)}) %collective-permute-start.39) | collective-permute-done | bytes 368672 | tf_op jit(solution)/shard_map/ppermute | solution.py:786
  214.7 1.3 collective-permute-start.46
  216.0 7.8 %collective-permute-done.48 = bf16[384,768]{1,0:T(8,128)(2,1)S(1)} collective-permute-done((bf16[384,768]{1,0:T(8,128)(2,1)S(1)}, bf16[384,768]{1,0:T(8,128)(2,1)S(1)}, u32[]{:S(2)}, u32[]{:S(2)}) %collective-permute-start.48) | collective-permute-done | bytes 589856 | tf_op jit(solution)/shard_map/ppermute | solution.py:795
  223.8 2.5 add_divide_fusion
  226.4 1.4 collective-permute-start.45
  227.9 14.1 %collective-permute-done.46 = bf16[112,1152]{1,0:T(8,128)(2,1)S(1)} collective-permute-done((bf16[112,1152]{1,0:T(8,128)(2,1)S(1)}, bf16[112,1152]{1,0:T(8,128)(2,1)S(1)}, u32[]{:S(2)}, u32[]{:S(2)}) %collective-permute-start.46) | collective-permute-done | bytes 258080 | tf_op jit(solution)/shard_map/ppermute | solution.py:795
  243.3 2.5 %add_divide_fusion.1 = (f32[96,3072]{1,0:T(8,128)}, f32[96,3072]{1,0:T(8,128)}, f32[96,3072]{1,0:T(8,128)}, f32[96,3072]{1,0:T(8,128)}) fusion(f32[96,3072]{1,0:T(8,128)S(1)} %copy-done.17, f32[96,3072]{1,0:T(8,128)S(1)} %copy-done.18, bf16[96,3072]{1,0:T(8,128)(2,1)S(1)} %add_convert_fusion.3, bf16[96,3072]{1,0:T(8,128)(2,1)S(1)} %collective-permute-done.47, ...), kind=kLoop, calls=%fused_computation.17 | loop fusion | flops 3833856 | bytes 8257537 | tf_op jit(solution)/shard_map/div | solution.py:708
  246.1 1.0 copy-done.21
  247.1 2.5 %add_divide_fusion.2 = (f32[96,3072]{1,0:T(8,128)}, f32[96,3072]{1,0:T(8,128)}, f32[96,3072]{1,0:T(8,128)}, f32[96,3072]{1,0:T(8,128)}) fusion(f32[96,3072]{1,0:T(8,128)S(1)} %copy-done.21, f32[96,3072]{1,0:T(8,128)S(1)} %copy-done.22, bf16[96,3072]{1,0:T(8,128)(2,1)S(1)} %slice_dynamic-update-slice_fusion), kind=kLoop, calls=%fused_computation.19 | loop fusion | flops 3538944 | bytes 7667712 | tf_op jit(solution)/shard_map/div | solution.py:708
  (213 shorter events, 21.6 us)
Async XLA Ops:
  2.2 14.5 %copy-start.9 = (bf16[96,2304]{1,0:T(8,128)(2,1)}, bf16[96,2304]{1,0:T(8,128)(2,1)S(1)}, u32[]{:S(2)}) copy-start(bf16[96,2304]{1,0:T(8,128)(2,1)S(1)} %slice_dynamic-update-slice_fusion.7.rest_0_) | copy-start | bytes 1327108
  2.3 15.2 %collective-permute-start.5 = (bf16[96,2304]{1,0:T(8,128)(2,1)S(1)}, bf16[96,2304]{1,0:T(8,128)(2,1)}, u32[]{:S(2)}, u32[]{:S(2)}) collective-permute-start(bf16[96,2304]{1,0:T(8,128)(2,1)S(1)} %slice_dynamic-update-slice_fusion.7.rest_0_), channel_id=1, source_target_pairs={{0,4},{1,3},{2,6},{3,1},{4,0},{5,7},{6,2},{7,5},{8,12},{9,11},{10,... | collective-permute-start | bytes 1327112 | tf_op jit(solution)/shard_map/ppermute | solution.py:730
  5.3 12.2 %collective-permute-start.4 = (bf16[96,2304]{1,0:T(8,128)(2,1)S(1)}, bf16[96,2304]{1,0:T(8,128)(2,1)}, u32[]{:S(2)}, u32[]{:S(2)}) collective-permute-start(bf16[96,2304]{1,0:T(8,128)(2,1)S(1)} %slice_dynamic-update-slice_fusion.7.rest_0_), channel_id=1, source_target_pairs={{0,2},{1,5},{2,0},{3,7},{4,6},{5,1},{6,4},{7,3},{8,10},{9,13},{10,... | collective-permute-start | bytes 1327112 | tf_op jit(solution)/shard_map/ppermute | solution.py:730
  6.9 1.8 collective-permute-start
  8.1 22.3 %copy-start = (bf16[1024,768]{1,0:T(8,128)(2,1)S(1)}, bf16[1024,768]{1,0:T(8,128)(2,1)}, u32[]{:S(2)}) copy-start(bf16[1024,768]{1,0:T(8,128)(2,1)} %x_ref.7) | copy-start | bytes 4718596
  8.7 34.1 %copy-start.5 = (bf16[96,3840]{1,0:T(8,128)(2,1)}, bf16[96,3840]{1,0:T(8,128)(2,1)S(1)}, u32[]{:S(2)}) copy-start(bf16[96,3840]{1,0:T(8,128)(2,1)S(1)} %pad_maximum_fusion.rest_0_) | copy-start | bytes 2211844
  8.8 8.0 %collective-permute-start.3 = (bf16[2,1152]{1,0:T(2,128)(2,1)S(1)}, bf16[2,1152]{1,0:T(2,128)(2,1)S(1)}, u32[]{:S(2)}, u32[]{:S(2)}) collective-permute-start(bf16[2,1152]{1,0:T(2,128)(2,1)S(1)} %pad_maximum_fusion.2), channel_id=1, source_target_pairs={{0,6},{1,7},{2,4},{3,5},{4,2},{5,3},{6,0},{7,1},{8,14},{9,15},{10,... | collective-permute-start | bytes 13832 | tf_op jit(solution)/shard_map/ppermute | solution.py:722
  8.9 7.9 %collective-permute-start.2 = (bf16[2,1152]{1,0:T(2,128)(2,1)S(1)}, bf16[2,1152]{1,0:T(2,128)(2,1)S(1)}, u32[]{:S(2)}, u32[]{:S(2)}) collective-permute-start(bf16[2,1152]{1,0:T(2,128)(2,1)S(1)} %pad_maximum_fusion.2), channel_id=1, source_target_pairs={{0,4},{1,5},{2,6},{3,7},{4,0},{5,1},{6,2},{7,3},{8,12},{9,13},{10,... | collective-permute-start | bytes 13832 | tf_op jit(solution)/shard_map/ppermute | solution.py:722
  10.9 5.9 %collective-permute-start.1 = (bf16[2,1152]{1,0:T(2,128)(2,1)S(1)}, bf16[2,1152]{1,0:T(2,128)(2,1)S(1)}, u32[]{:S(2)}, u32[]{:S(2)}) collective-permute-start(bf16[2,1152]{1,0:T(2,128)(2,1)S(1)} %pad_maximum_fusion.2), channel_id=1, source_target_pairs={{0,2},{1,3},{2,0},{3,1},{4,6},{5,7},{6,4},{7,5},{8,10},{9,11},{10,... | collective-permute-start | bytes 13832 | tf_op jit(solution)/shard_map/ppermute | solution.py:722
  16.8 10.9 %collective-permute-start.7 = (bf16[96,2304]{1,0:T(8,128)(2,1)S(1)}, bf16[96,2304]{1,0:T(8,128)(2,1)S(1)}, u32[]{:S(2)}, u32[]{:S(2)}) collective-permute-start(bf16[96,2304]{1,0:T(8,128)(2,1)S(1)} %slice_dynamic-update-slice_fusion.7.rest_0_), channel_id=1, source_target_pairs={{0,1},{1,0},{2,3},{3,2},{4,5},{5,4},{6,7},{7,6},{8,9},{9,8},{10,11... | collective-permute-start | bytes 1327112 | tf_op jit(solution)/shard_map/ppermute | solution.py:722
  17.5 8.7 %collective-permute-start.6 = (bf16[96,2304]{1,0:T(8,128)(2,1)}, bf16[96,2304]{1,0:T(8,128)(2,1)}, u32[]{:S(2)}, u32[]{:S(2)}) collective-permute-start(bf16[96,2304]{1,0:T(8,128)(2,1)} %collective-permute-done.4.rest_1_), channel_id=1, source_target_pairs={{0,4},{1,3},{2,6},{3,1},{4,0},{5,7},{6,2},{7,5},{8,12},{9,11},{10,... | collective-permute-start | bytes 1327112 | tf_op jit(solution)/shard_map/ppermute | solution.py:730
  19.8 9.0 %collective-permute-start.8 = (bf16[96,2304]{1,0:T(8,128)(2,1)}, bf16[96,2304]{1,0:T(8,128)(2,1)}, u32[]{:S(2)}, u32[]{:S(2)}) collective-permute-start(bf16[96,2304]{1,0:T(8,128)(2,1)} %collective-permute-done.4.rest_1_), channel_id=1, source_target_pairs={{0,1},{1,0},{2,3},{3,2},{4,5},{5,4},{6,7},{7,6},{8,9},{9,8},{10,11... | collective-permute-start | bytes 1327112 | tf_op jit(solution)/shard_map/ppermute | solution.py:722
  19.9 8.9 %collective-permute-start.9 = (bf16[96,2304]{1,0:T(8,128)(2,1)}, bf16[96,2304]{1,0:T(8,128)(2,1)}, u32[]{:S(2)}, u32[]{:S(2)}) collective-permute-start(bf16[96,2304]{1,0:T(8,128)(2,1)} %collective-permute-done.5.rest_2_), channel_id=1, source_target_pairs={{0,1},{1,0},{2,3},{3,2},{4,5},{5,4},{6,7},{7,6},{8,9},{9,8},{10,11... | collective-permute-start | bytes 1327112 | tf_op jit(solution)/shard_map/ppermute | solution.py:722
  20.4 19.1 %collective-permute-start.12 = (bf16[96,3840]{1,0:T(8,128)(2,1)S(1)}, bf16[96,3840]{1,0:T(8,128)(2,1)}, u32[]{:S(2)}, u32[]{:S(2)}) collective-permute-start(bf16[96,3840]{1,0:T(8,128)(2,1)S(1)} %pad_maximum_fusion.rest_0_), channel_id=1, source_target_pairs={{0,4},{1,3},{2,6},{3,1},{4,0},{5,7},{6,2},{7,5},{8,12},{9,11},{10,... | collective-permute-start | bytes 2211848 | tf_op jit(solution)/shard_map/ppermute | solution.py:730
  26.2 15.3 %collective-permute-start.11 = (bf16[96,3840]{1,0:T(8,128)(2,1)S(1)}, bf16[96,3840]{1,0:T(8,128)(2,1)}, u32[]{:S(2)}, u32[]{:S(2)}) collective-permute-start(bf16[96,3840]{1,0:T(8,128)(2,1)S(1)} %pad_maximum_fusion.rest_0_), channel_id=1, source_target_pairs={{0,2},{1,5},{2,0},{3,7},{4,6},{5,1},{6,4},{7,3},{8,10},{9,13},{10,... | collective-permute-start | bytes 2211848 | tf_op jit(solution)/shard_map/ppermute | solution.py:730
  27.6 2.0 collective-permute-start.10
  28.5 14.8 %copy-start.33 = (f32[8,8,96]{2,1,0:T(8,128)}, f32[8,8,96]{2,1,0:T(8,128)S(1)}, u32[]{:S(2)}) copy-start(f32[8,8,96]{2,1,0:T(8,128)S(1)} %reshape.164) | copy-start | bytes 73732
  30.4 13.1 %copy-start.4 = (s32[8]{0:T(128)S(1)}, s32[8]{0:T(128)}, u32[]{:S(2)}) copy-start(s32[8]{0:T(128)} %s.7) | copy-start | bytes 100
  41.5 11.8 %collective-permute-start.16 = (bf16[96,3840]{1,0:T(8,128)(2,1)}, bf16[96,3840]{1,0:T(8,128)(2,1)}, u32[]{:S(2)}, u32[]{:S(2)}) collective-permute-start(bf16[96,3840]{1,0:T(8,128)(2,1)} %collective-permute-done.11.rest_1_), channel_id=1, source_target_pairs={{0,4},{1,3},{2,6},{3,1},{4,0},{5,7},{6,2},{7,5},{8,12},{9,11},{10,... | collective-permute-start | bytes 2211848 | tf_op jit(solution)/shard_map/ppermute | solution.py:730
  42.8 11.4 %collective-permute-start.13 = (bf16[96,3840]{1,0:T(8,128)(2,1)S(1)}, bf16[96,3840]{1,0:T(8,128)(2,1)S(1)}, u32[]{:S(2)}, u32[]{:S(2)}) collective-permute-start(bf16[96,3840]{1,0:T(8,128)(2,1)S(1)} %pad_maximum_fusion.rest_0_), channel_id=1, source_target_pairs={{0,1},{1,0},{2,3},{3,2},{4,5},{5,4},{6,7},{7,6},{8,9},{9,8},{10,11... | collective-permute-start | bytes 2211848 | tf_op jit(solution)/shard_map/ppermute | solution.py:722
  43.0 11.2 %collective-permute-start.15 = (bf16[96,3840]{1,0:T(8,128)(2,1)}, bf16[96,3840]{1,0:T(8,128)(2,1)S(1)}, u32[]{:S(2)}, u32[]{:S(2)}) collective-permute-start(bf16[96,3840]{1,0:T(8,128)(2,1)} %collective-permute-done.12.rest_2_), channel_id=1, source_target_pairs={{0,1},{1,0},{2,3},{3,2},{4,5},{5,4},{6,7},{7,6},{8,9},{9,8},{10,11... | collective-permute-start | bytes 2211848 | tf_op jit(solution)/shard_map/ppermute | solution.py:722
  43.3 10.9 %collective-permute-start.14 = (bf16[96,3840]{1,0:T(8,128)(2,1)}, bf16[96,3840]{1,0:T(8,128)(2,1)S(1)}, u32[]{:S(2)}, u32[]{:S(2)}) collective-permute-start(bf16[96,3840]{1,0:T(8,128)(2,1)} %collective-permute-done.11.rest_1_), channel_id=1, source_target_pairs={{0,1},{1,0},{2,3},{3,2},{4,5},{5,4},{6,7},{7,6},{8,9},{9,8},{10,11... | collective-permute-start | bytes 2211848 | tf_op jit(solution)/shard_map/ppermute | solution.py:722
  53.3 8.9 %collective-permute-start.17 = (bf16[96,3840]{1,0:T(8,128)(2,1)}, bf16[96,3840]{1,0:T(8,128)(2,1)}, u32[]{:S(2)}, u32[]{:S(2)}) collective-permute-start(bf16[96,3840]{1,0:T(8,128)(2,1)} %collective-permute-done.16.rest_3_), channel_id=1, source_target_pairs={{0,1},{1,0},{2,3},{3,2},{4,5},{5,4},{6,7},{7,6},{8,9},{9,8},{10,11... | collective-permute-start | bytes 2211848 | tf_op jit(solution)/shard_map/ppermute | solution.py:722
  54.2 15.8 %collective-permute-start.19 = (bf16[384,768]{1,0:T(8,128)(2,1)}, bf16[384,768]{1,0:T(8,128)(2,1)S(1)}, u32[]{:S(2)}, u32[]{:S(2)}) collective-permute-start(bf16[384,768]{1,0:T(8,128)(2,1)} %convert_element_type.296.rest_0_), channel_id=1, source_target_pairs={{0,4},{1,3},{2,6},{3,1},{4,0},{5,7},{6,2},{7,5},{8,12},{9,11},{10,... | collective-permute-start | bytes 1769480 | tf_op jit(solution)/shard_map/ppermute | solution.py:730
  55.5 14.8 %collective-permute-start.18 = (bf16[384,768]{1,0:T(8,128)(2,1)}, bf16[384,768]{1,0:T(8,128)(2,1)}, u32[]{:S(2)}, u32[]{:S(2)}) collective-permute-start(bf16[384,768]{1,0:T(8,128)(2,1)} %convert_element_type.296.rest_0_), channel_id=1, source_target_pairs={{0,2},{1,5},{2,0},{3,7},{4,6},{5,1},{6,4},{7,3},{8,10},{9,13},{10,... | collective-permute-start | bytes 1769480 | tf_op jit(solution)/shard_map/ppermute | solution.py:730
  70.3 11.8 %collective-permute-start.20 = (bf16[384,768]{1,0:T(8,128)(2,1)}, bf16[384,768]{1,0:T(8,128)(2,1)S(1)}, u32[]{:S(2)}, u32[]{:S(2)}) collective-permute-start(bf16[384,768]{1,0:T(8,128)(2,1)} %collective-permute-done.18.rest_1_), channel_id=1, source_target_pairs={{0,4},{1,3},{2,6},{3,1},{4,0},{5,7},{6,2},{7,5},{8,12},{9,11},{10,... | collective-permute-start | bytes 1769480 | tf_op jit(solution)/shard_map/ppermute | solution.py:730
  72.6 10.0 %collective-permute-start.21 = (bf16[384,768]{1,0:T(8,128)(2,1)}, bf16[384,768]{1,0:T(8,128)(2,1)S(1)}, u32[]{:S(2)}, u32[]{:S(2)}) collective-permute-start(bf16[384,768]{1,0:T(8,128)(2,1)} %convert_element_type.296.rest_0_), channel_id=1, source_target_pairs={{0,1},{1,0},{2,3},{3,2},{4,5},{5,4},{6,7},{7,6},{8,9},{9,8},{10,11... | collective-permute-start | bytes 1769480 | tf_op jit(solution)/shard_map/ppermute | solution.py:722
  72.7 9.9 %collective-permute-start.23 = (bf16[384,768]{1,0:T(8,128)(2,1)S(1)}, bf16[384,768]{1,0:T(8,128)(2,1)S(1)}, u32[]{:S(2)}, u32[]{:S(2)}) collective-permute-start(bf16[384,768]{1,0:T(8,128)(2,1)S(1)} %collective-permute-done.19.rest_2_), channel_id=1, source_target_pairs={{0,1},{1,0},{2,3},{3,2},{4,5},{5,4},{6,7},{7,6},{8,9},{9,8},{10,11... | collective-permute-start | bytes 1769480 | tf_op jit(solution)/shard_map/ppermute | solution.py:722
  73.2 9.4 %collective-permute-start.22 = (bf16[384,768]{1,0:T(8,128)(2,1)}, bf16[384,768]{1,0:T(8,128)(2,1)S(1)}, u32[]{:S(2)}, u32[]{:S(2)}) collective-permute-start(bf16[384,768]{1,0:T(8,128)(2,1)} %collective-permute-done.18.rest_1_), channel_id=1, source_target_pairs={{0,1},{1,0},{2,3},{3,2},{4,5},{5,4},{6,7},{7,6},{8,9},{9,8},{10,11... | collective-permute-start | bytes 1769480 | tf_op jit(solution)/shard_map/ppermute | solution.py:722
  82.1 2.1 collective-permute-start.24
  103.7 6.7 %collective-permute-start.25 = (bf16[4,384,768]{2,1,0:T(8,128)(2,1)}, bf16[4,384,768]{2,1,0:T(8,128)(2,1)S(1)}, u32[]{:S(2)}, u32[]{:S(2)}) collective-permute-start(bf16[4,384,768]{2,1,0:T(8,128)(2,1)} %get-tuple-element.130), channel_id=1, source_target_pairs={{0,1},{1,0},{2,3},{3,2},{4,5},{5,4},{6,7},{7,6},{8,9},{9,8},{10,11... | collective-permute-start | bytes 7077896 | tf_op jit(solution)/shard_map/ppermute | solution.py:722
  118.2 13.2 %collective-permute-start.27 = (bf16[4,96,3072]{2,1,0:T(8,128)(2,1)}, bf16[4,96,3072]{2,1,0:T(8,128)(2,1)S(1)}, u32[]{:S(2)}, u32[]{:S(2)}) collective-permute-start(bf16[4,96,3072]{2,1,0:T(8,128)(2,1)} %get-tuple-element.138), channel_id=1, source_target_pairs={{0,1},{1,0},{2,3},{3,2},{4,5},{5,4},{6,7},{7,6},{8,9},{9,8},{10,11... | collective-permute-start | bytes 7077896 | tf_op jit(solution)/shard_map/ppermute | solution.py:722
  118.4 16.2 %collective-permute-start.26 = (bf16[2,384,768]{2,1,0:T(8,128)(2,1)S(1)}, bf16[2,384,768]{2,1,0:T(8,128)(2,1)S(1)}, u32[]{:S(2)}, u32[]{:S(2)}) collective-permute-start(bf16[2,384,768]{2,1,0:T(8,128)(2,1)S(1)} %add_convert_fusion.1), channel_id=1, source_target_pairs={{0,2},{1,5},{2,0},{3,7},{4,6},{5,1},{6,4},{7,3},{8,10},{9,13},{10,... | collective-permute-start | bytes 3538952 | tf_op jit(solution)/shard_map/ppermute | solution.py:730
  118.9 12.5 %copy-start.6 = (bf16[4,96,3072]{2,1,0:T(8,128)(2,1)S(1)}, bf16[4,96,3072]{2,1,0:T(8,128)(2,1)}, u32[]{:S(2)}) copy-start(bf16[4,96,3072]{2,1,0:T(8,128)(2,1)} %get-tuple-element.139) | copy-start | bytes 7077892
  131.4 23.0 %copy-start.7 = (bf16[4,96,3072]{2,1,0:T(8,128)(2,1)}, bf16[4,96,3072]{2,1,0:T(8,128)(2,1)S(1)}, u32[]{:S(2)}) copy-start(bf16[4,96,3072]{2,1,0:T(8,128)(2,1)S(1)} %collective-permute-done.27) | copy-start | bytes 7077892
  131.8 22.6 %collective-permute-start.28 = (bf16[2,96,3072]{2,1,0:T(8,128)(2,1)S(1)}, bf16[2,96,3072]{2,1,0:T(8,128)(2,1)S(1)}, u32[]{:S(2)}, u32[]{:S(2)}) collective-permute-start(bf16[2,96,3072]{2,1,0:T(8,128)(2,1)S(1)} %add_convert_fusion), channel_id=1, source_target_pairs={{0,2},{1,5},{2,0},{3,7},{4,6},{5,1},{6,4},{7,3},{8,10},{9,13},{10,... | collective-permute-start | bytes 3538952 | tf_op jit(solution)/shard_map/ppermute | solution.py:730
  134.8 16.3 %collective-permute-start.29 = (bf16[384,768]{1,0:T(8,128)(2,1)S(1)}, bf16[384,768]{1,0:T(8,128)(2,1)S(1)}, u32[]{:S(2)}, u32[]{:S(2)}) collective-permute-start(bf16[384,768]{1,0:T(8,128)(2,1)S(1)} %fusion.6), channel_id=1, source_target_pairs={{0,4},{1,3},{2,6},{3,1},{4,0},{5,7},{6,2},{7,5},{8,12},{9,11},{10,... | collective-permute-start | bytes 1769480 | tf_op jit(solution)/shard_map/ppermute | solution.py:730
  145.4 27.4 %collective-permute-start.33 = (bf16[4,96,1920]{2,1,0:T(8,128)(2,1)}, bf16[4,96,1920]{2,1,0:T(8,128)(2,1)}, u32[]{:S(2)}, u32[]{:S(2)}) collective-permute-start(bf16[4,96,1920]{2,1,0:T(8,128)(2,1)} %get-tuple-element.151), channel_id=1, source_target_pairs={{0,1},{1,0},{2,3},{3,2},{4,5},{5,4},{6,7},{7,6},{8,9},{9,8},{10,11... | collective-permute-start | bytes 4423688 | tf_op jit(solution)/shard_map/ppermute | solution.py:722
  155.6 13.8 %collective-permute-start.30 = (bf16[96,3072]{1,0:T(8,128)(2,1)}, bf16[96,3072]{1,0:T(8,128)(2,1)}, u32[]{:S(2)}, u32[]{:S(2)}) collective-permute-start(bf16[96,3072]{1,0:T(8,128)(2,1)} %fusion.7), channel_id=1, source_target_pairs={{0,4},{1,3},{2,6},{3,1},{4,0},{5,7},{6,2},{7,5},{8,12},{9,11},{10,... | collective-permute-start | bytes 1769480 | tf_op jit(solution)/shard_map/ppermute | solution.py:730
  157.2 19.3 %collective-permute-start.36 = (bf16[384,768]{1,0:T(8,128)(2,1)S(1)}, bf16[384,768]{1,0:T(8,128)(2,1)S(1)}, u32[]{:S(2)}, u32[]{:S(2)}) collective-permute-start(bf16[384,768]{1,0:T(8,128)(2,1)S(1)} %fusion.4), channel_id=1, source_target_pairs={{0,8},{24,16},{1,9},{25,17},{2,10},{26,18},{3,11},{27,19},{4,12},{... | collective-permute-start | bytes 1769480 | tf_op jit(solution)/shard_map/ppermute | solution.py:786
  169.4 5.2 %collective-permute-start.32 = (bf16[4,112,1152]{2,1,0:T(8,128)(2,1)}, bf16[4,112,1152]{2,1,0:T(8,128)(2,1)S(1)}, u32[]{:S(2)}, u32[]{:S(2)}) collective-permute-start(bf16[4,112,1152]{2,1,0:T(8,128)(2,1)} %get-tuple-element.162), channel_id=1, source_target_pairs={{0,1},{1,0},{2,3},{3,2},{4,5},{5,4},{6,7},{7,6},{8,9},{9,8},{10,11... | collective-permute-start | bytes 3096584 | tf_op jit(solution)/shard_map/ppermute | solution.py:722
  171.4 22.5 %collective-permute-start.31 = (bf16[96,3072]{1,0:T(8,128)(2,1)S(1)}, bf16[96,3072]{1,0:T(8,128)(2,1)S(1)}, u32[]{:S(2)}, u32[]{:S(2)}) collective-permute-start(bf16[96,3072]{1,0:T(8,128)(2,1)S(1)} %fusion.3), channel_id=1, source_target_pairs={{0,8},{24,16},{1,9},{25,17},{2,10},{26,18},{3,11},{27,19},{4,12},{... | collective-permute-start | bytes 1769480 | tf_op jit(solution)/shard_map/ppermute | solution.py:786
  174.2 11.5 %collective-permute-start.35 = (bf16[2,96,1920]{2,1,0:T(8,128)(2,1)S(1)}, bf16[2,96,1920]{2,1,0:T(8,128)(2,1)S(1)}, u32[]{:S(2)}, u32[]{:S(2)}) collective-permute-start(bf16[2,96,1920]{2,1,0:T(8,128)(2,1)S(1)} %add_convert_fusion.2), channel_id=1, source_target_pairs={{0,2},{1,5},{2,0},{3,7},{4,6},{5,1},{6,4},{7,3},{8,10},{9,13},{10,... | collective-permute-start | bytes 2211848 | tf_op jit(solution)/shard_map/ppermute | solution.py:730
  174.8 18.5 %collective-permute-start.34 = (bf16[2,112,1152]{2,1,0:T(8,128)(2,1)S(1)}, bf16[2,112,1152]{2,1,0:T(8,128)(2,1)S(1)}, u32[]{:S(2)}, u32[]{:S(2)}) collective-permute-start(bf16[2,112,1152]{2,1,0:T(8,128)(2,1)S(1)} %add_convert_fusion.9), channel_id=1, source_target_pairs={{0,2},{1,5},{2,0},{3,7},{4,6},{5,1},{6,4},{7,3},{8,10},{9,13},{10,... | collective-permute-start | bytes 1548296 | tf_op jit(solution)/shard_map/ppermute | solution.py:730
  176.6 28.9 %collective-permute-start.42 = (bf16[384,768]{1,0:T(8,128)(2,1)S(1)}, bf16[384,768]{1,0:T(8,128)(2,1)S(1)}, u32[]{:S(2)}, u32[]{:S(2)}) collective-permute-start(bf16[384,768]{1,0:T(8,128)(2,1)S(1)} %add_convert_fusion.6), channel_id=1, source_target_pairs={{8,16},{16,8},{9,17},{17,9},{10,18},{18,10},{11,19},{19,11},{12,20... | collective-permute-start | bytes 1769480 | tf_op jit(solution)/shard_map/ppermute | solution.py:790
  186.8 16.2 %collective-permute-start.37 = (bf16[96,1920]{1,0:T(8,128)(2,1)S(1)}, bf16[96,1920]{1,0:T(8,128)(2,1)S(1)}, u32[]{:S(2)}, u32[]{:S(2)}) collective-permute-start(bf16[96,1920]{1,0:T(8,128)(2,1)S(1)} %fusion.9), channel_id=1, source_target_pairs={{0,4},{1,3},{2,6},{3,1},{4,0},{5,7},{6,2},{7,5},{8,12},{9,11},{10,... | collective-permute-start | bytes 1105928 | tf_op jit(solution)/shard_map/ppermute | solution.py:730
  193.4 6.4 %collective-permute-start.38 = (bf16[112,1152]{1,0:T(8,128)(2,1)S(1)}, bf16[112,1152]{1,0:T(8,128)(2,1)S(1)}, u32[]{:S(2)}, u32[]{:S(2)}) collective-permute-start(bf16[112,1152]{1,0:T(8,128)(2,1)S(1)} %fusion.10), channel_id=1, source_target_pairs={{0,4},{1,3},{2,6},{3,1},{4,0},{5,7},{6,2},{7,5},{8,12},{9,11},{10,... | collective-permute-start | bytes 774152 | tf_op jit(solution)/shard_map/ppermute | solution.py:730
  194.0 13.0 %collective-permute-start.41 = (bf16[96,3072]{1,0:T(8,128)(2,1)S(1)}, bf16[96,3072]{1,0:T(8,128)(2,1)S(1)}, u32[]{:S(2)}, u32[]{:S(2)}) collective-permute-start(bf16[96,3072]{1,0:T(8,128)(2,1)S(1)} %add_convert_fusion.5), channel_id=1, source_target_pairs={{8,16},{16,8},{9,17},{17,9},{10,18},{18,10},{11,19},{19,11},{12,20... | collective-permute-start | bytes 1769480 | tf_op jit(solution)/shard_map/ppermute | solution.py:790
  199.9 9.7 %collective-permute-start.40 = (bf16[112,1152]{1,0:T(8,128)(2,1)S(1)}, bf16[112,1152]{1,0:T(8,128)(2,1)S(1)}, u32[]{:S(2)}, u32[]{:S(2)}) collective-permute-start(bf16[112,1152]{1,0:T(8,128)(2,1)S(1)} %fusion.8), channel_id=1, source_target_pairs={{0,8},{24,16},{1,9},{25,17},{2,10},{26,18},{3,11},{27,19},{4,12},{... | collective-permute-start | bytes 774152 | tf_op jit(solution)/shard_map/ppermute | solution.py:786
  204.2 9.6 %collective-permute-start.39 = (bf16[96,1920]{1,0:T(8,128)(2,1)S(1)}, bf16[96,1920]{1,0:T(8,128)(2,1)S(1)}, u32[]{:S(2)}, u32[]{:S(2)}) collective-permute-start(bf16[96,1920]{1,0:T(8,128)(2,1)S(1)} %fusion.5), channel_id=1, source_target_pairs={{0,8},{24,16},{1,9},{25,17},{2,10},{26,18},{3,11},{27,19},{4,12},{... | collective-permute-start | bytes 1105928 | tf_op jit(solution)/shard_map/ppermute | solution.py:786
  205.6 18.2 %collective-permute-start.48 = (bf16[384,768]{1,0:T(8,128)(2,1)S(1)}, bf16[384,768]{1,0:T(8,128)(2,1)S(1)}, u32[]{:S(2)}, u32[]{:S(2)}) collective-permute-start(bf16[384,768]{1,0:T(8,128)(2,1)S(1)} %add_convert_fusion.4), channel_id=1, source_target_pairs={{8,0},{16,24},{9,1},{17,25},{10,2},{18,26},{11,3},{19,27},{12,4},{... | collective-permute-start | bytes 1769480 | tf_op jit(solution)/shard_map/ppermute | solution.py:795
  207.1 16.7 %copy-start.15 = (f32[384,768]{1,0:T(8,128)S(1)}, f32[384,768]{1,0:T(8,128)}, u32[]{:S(2)}) copy-start(f32[384,768]{1,0:T(8,128)} %param.30) | copy-start | bytes 3538948
  207.1 16.7 %copy-start.16 = (f32[384,768]{1,0:T(8,128)S(1)}, f32[384,768]{1,0:T(8,128)}, u32[]{:S(2)}) copy-start(f32[384,768]{1,0:T(8,128)} %param.35) | copy-start | bytes 3538948
  207.1 36.1 %collective-permute-start.47 = (bf16[96,3072]{1,0:T(8,128)(2,1)S(1)}, bf16[96,3072]{1,0:T(8,128)(2,1)S(1)}, u32[]{:S(2)}, u32[]{:S(2)}) collective-permute-start(bf16[96,3072]{1,0:T(8,128)(2,1)S(1)} %add_convert_fusion.3), channel_id=1, source_target_pairs={{8,0},{16,24},{9,1},{17,25},{10,2},{18,26},{11,3},{19,27},{12,4},{... | collective-permute-start | bytes 1769480 | tf_op jit(solution)/shard_map/ppermute | solution.py:795
  209.7 4.9 %collective-permute-start.44 = (bf16[112,1152]{1,0:T(8,128)(2,1)S(1)}, bf16[112,1152]{1,0:T(8,128)(2,1)S(1)}, u32[]{:S(2)}, u32[]{:S(2)}) collective-permute-start(bf16[112,1152]{1,0:T(8,128)(2,1)S(1)} %add_convert_fusion.14), channel_id=1, source_target_pairs={{8,16},{16,8},{9,17},{17,9},{10,18},{18,10},{11,19},{19,11},{12,20... | collective-permute-start | bytes 774152 | tf_op jit(solution)/shard_map/ppermute | solution.py:790
  213.9 12.4 %collective-permute-start.43 = (bf16[96,1920]{1,0:T(8,128)(2,1)S(1)}, bf16[96,1920]{1,0:T(8,128)(2,1)S(1)}, u32[]{:S(2)}, u32[]{:S(2)}) collective-permute-start(bf16[96,1920]{1,0:T(8,128)(2,1)S(1)} %add_convert_fusion.11), channel_id=1, source_target_pairs={{8,16},{16,8},{9,17},{17,9},{10,18},{18,10},{11,19},{19,11},{12,20... | collective-permute-start | bytes 1105928 | tf_op jit(solution)/shard_map/ppermute | solution.py:790
  214.7 27.3 %collective-permute-start.46 = (bf16[112,1152]{1,0:T(8,128)(2,1)S(1)}, bf16[112,1152]{1,0:T(8,128)(2,1)S(1)}, u32[]{:S(2)}, u32[]{:S(2)}) collective-permute-start(bf16[112,1152]{1,0:T(8,128)(2,1)S(1)} %add_convert_fusion.13), channel_id=1, source_target_pairs={{8,0},{16,24},{9,1},{17,25},{10,2},{18,26},{11,3},{19,27},{12,4},{... | collective-permute-start | bytes 774152 | tf_op jit(solution)/shard_map/ppermute | solution.py:795
  223.8 19.4 %copy-start.18 = (f32[96,3072]{1,0:T(8,128)S(1)}, f32[96,3072]{1,0:T(8,128)}, u32[]{:S(2)}) copy-start(f32[96,3072]{1,0:T(8,128)} %param.34) | copy-start | bytes 3538948
  226.3 15.7 %copy-start.41 = (f32[384]{0:T(512)S(1)}, f32[384]{0:T(512)}, u32[]{:S(2)}) copy-start(f32[384]{0:T(512)} %param.31) | copy-start | bytes 4612
  226.3 15.7 %copy-start.42 = (f32[384]{0:T(512)S(1)}, f32[384]{0:T(512)}, u32[]{:S(2)}) copy-start(f32[384]{0:T(512)} %param.36) | copy-start | bytes 4612
  226.3 16.3 %copy-start.38 = (f32[8,96]{1,0:T(8,128)S(1)}, f32[8,96]{1,0:T(8,128)}, u32[]{:S(2)}) copy-start(f32[8,96]{1,0:T(8,128)} %param.32) | copy-start | bytes 9220
  226.3 16.3 %copy-start.39 = (f32[8,96]{1,0:T(8,128)S(1)}, f32[8,96]{1,0:T(8,128)}, u32[]{:S(2)}) copy-start(f32[8,96]{1,0:T(8,128)} %param.37) | copy-start | bytes 9220
  226.3 16.9 %copy-start.17 = (f32[96,3072]{1,0:T(8,128)S(1)}, f32[96,3072]{1,0:T(8,128)}, u32[]{:S(2)}) copy-start(f32[96,3072]{1,0:T(8,128)} %param.29) | copy-start | bytes 3538948
  226.4 19.4 %collective-permute-start.45 = (bf16[96,1920]{1,0:T(8,128)(2,1)S(1)}, bf16[96,1920]{1,0:T(8,128)(2,1)S(1)}, u32[]{:S(2)}, u32[]{:S(2)}) collective-permute-start(bf16[96,1920]{1,0:T(8,128)(2,1)S(1)} %add_convert_fusion.10), channel_id=1, source_target_pairs={{8,0},{16,24},{9,1},{17,25},{10,2},{18,26},{11,3},{19,27},{12,4},{... | collective-permute-start | bytes 1105928 | tf_op jit(solution)/shard_map/ppermute | solution.py:795
  (30 other events, 116.1 us)

commit v6 on v5

--- a/solution.py
+++ b/solution.py
@@ -764,6 +764,7 @@
     def __init__(self, parts):
         self.theirs, self.mine = parts
         self.got = swap(self.theirs, 1)
+        self.by_pairs = False
 
     def one(self, *others):
         self.got = after(self.got, *others)
@@ -785,9 +786,16 @@
     def line(self):
         self.near = lax.ppermute(self.owned, "rep", [(0, 1), (3, 2)])
 
+    def pairs(self):
+        self.near = lax.ppermute(self.owned, "rep", [(i, i ^ 1) for i in range(4)])
+        self.by_pairs = True
+
     def four(self, *others):
         self.near = low_sum(self.owned, after(self.near, *others))
-        self.across = lax.ppermute(self.near, "rep", [(1, 2), (2, 1)])
+        if self.by_pairs:
+            self.across = lax.ppermute(self.near, "rep", [(i, i ^ 2) for i in range(4)])
+        else:
+            self.across = lax.ppermute(self.near, "rep", [(1, 2), (2, 1)])
         return (self.near,)
 
     def five(self, *others):
@@ -796,6 +804,8 @@
         return (self.total,)
 
     def result(self, rep_index):
+        if self.by_pairs:
+            return self.near.astype(f32) + self.across.astype(f32)
         inner = (rep_index == 1) | (rep_index == 2)
         return jnp.where(inner, self.total, self.back)
 
@@ -925,7 +935,7 @@
     if direct:
         r_mix = Scatter(parts_mix)
         sent = r_out.three(*parts_mix)
-        r_out.line()
+        r_out.pairs()
         sent = r_in.two(*sent)
     mixed1, sums_q1 = attention_back(
         lengths, qkv[1], weights[1], ordered(grad_attended[1], *sent)
@@ -955,7 +965,7 @@
         r_qkv.line()
         sent = r_mix.three(*sent)
         r_mix.line()
-        sent = r_out.five(*sent)
+        r_out.across = after(r_out.across, *sent)
         sent = r_in.five(*sent)
         sent = r_qkv.four(*sent)
         sent = r_mix.four(*sent)

time: 250 us -> 248 us (level)
    ppermute x0 -> x2, starting transfers between devices: none -> 3.29 us  [the longest x1 1.65 us: pairs(): self.near = lax.ppermute(self.owned, 'rep', [(i, i ^ 1) for i in range(4)])]
    ppermute x4 -> x3, starting transfers between devices: 9.44 us -> 7.44 us  [line(): self.near = lax.ppermute(self.owned, 'rep', [(0, 1), (3, 2)])]
    ppermute x4 -> x3, starting transfers between devices: 5.43 us -> 3.88 us  [five(): self.back = lax.ppermute(self.total, 'rep', [(1, 0), (2, 3)])]
    ppermute x4 -> x3, waiting for transfers between devices: 22 us -> 23.2 us  [five(): self.back = lax.ppermute(self.total, 'rep', [(1, 0), (2, 3)])]
    convert_element_type x20 -> x19, other arithmetic: 9.25 us -> 9.1 us  [low_sum(): return total.astype(bf16)]
  transfers between devices with their start and end apart: 49 -> 48, of which waited for: 20 -> 18; matrix products, arithmetic and copies ran while one was open for 8% -> 8% of each run, Pallas kernels for 33% -> 33%
where the time goes in v6:
time: 248 us
  Pallas kernels  108 us (44%)
  waiting for transfers between devices  65.2 us (26%)
  starting transfers between devices  45.9 us (19%)
  other arithmetic  20.6 us (8%)
  local copies, waits for them, and re-layouts  6.61 us (3%)
    ppermute x17, waiting for transfers between devices, split_swap(): lax.ppermute(value, 'fsdp', [(i, i ^ (odd_bit if i & 1 else even_bit)) fo...  31.5 us
    ppermute x3, waiting for transfers between devices, five(): self.back = lax.ppermute(self.total, 'rep', [(1, 0), (2, 3)])  23.2 us
    ppermute x17, starting transfers between devices, split_swap(): lax.ppermute(value, 'fsdp', [(i, i ^ (odd_bit if i & 1 else even_bit)) fo...  22.5 us
    pallas_call x1, Pallas kernels, back_in(): call(kernel, (rows // TILE,), [rows_of(FF), rows_of(D), rows_of(D), rows_...  12.4 us
    pallas_call x2, Pallas kernels, attention(): call(kernel, (rows // (GROUP * SEQ),), [rows_of(3 * PART, GROUP * SEQ)],...  11.4 us
    pallas_call x1, Pallas kernels, feed_out(): call(kernel, (rows // TILE,), [rows_of(FF), rows_of(D), rows_of(D), whole...  11.2 us
    pallas_call x2, Pallas kernels, attention_back(): call(kernel, (rows // (GROUP * SEQ),), [rows_of(3 * PART, GROUP * SEQ), r...  9.88 us
    convert_element_type x19, other arithmetic, low_sum(): return total.astype(bf16)  9.1 us
  transfers between devices with their start and end apart: 48, of which 18 were waited for; matrix products, arithmetic and copies ran while one was open for 8% of the time, Pallas kernels for 33%

profile of v6, /device:TPU:0, one launch (start us, length us, event | category | flops | bytes accessed | tf_op | source)
XLA Modules:
  0.0 247.8 jit_solution(3424612554166183507)
XLA Ops:
  0.7 1.4 convert.32
  2.3 3.0 %collective-permute-start.5 = (bf16[96,2304]{1,0:T(8,128)(2,1)S(1)}, bf16[96,2304]{1,0:T(8,128)(2,1)}, u32[]{:S(2)}, u32[]{:S(2)}) collective-permute-start(bf16[96,2304]{1,0:T(8,128)(2,1)S(1)} %slice_dynamic-update-slice_fusion.7.rest_0_), channel_id=1, source_target_pairs={{0,4},{1,3},{2,6},{3,1},{4,0},{5,7},{6,2},{7,5},{8,12},{9,11},{10,... | collective-permute-start | bytes 1327112 | tf_op jit(solution)/shard_map/ppermute | solution.py:730
  5.3 1.5 collective-permute-start.4
  7.0 1.0 slice.298
  8.9 1.9 collective-permute-start.2
  10.9 1.5 collective-permute-start.1
  12.4 4.4 %collective-permute-done.3 = bf16[2,1152]{1,0:T(2,128)(2,1)S(1)} collective-permute-done((bf16[2,1152]{1,0:T(2,128)(2,1)S(1)}, bf16[2,1152]{1,0:T(2,128)(2,1)S(1)}, u32[]{:S(2)}, u32[]{:S(2)}) %collective-permute-start.3) | collective-permute-done | bytes 4640 | tf_op jit(solution)/shard_map/ppermute | solution.py:722
  17.5 1.7 collective-permute-start.6
  20.8 5.4 %collective-permute-done.6.rest_3_ = bf16[96,2304]{1,0:T(8,128)(2,1)} collective-permute-done((bf16[96,2304]{1,0:T(8,128)(2,1)}, bf16[96,2304]{1,0:T(8,128)(2,1)}, u32[]{:S(2)}, u32[]{:S(2)}) %collective-permute-start.6) | collective-permute-done | bytes 442400 | tf_op jit(solution)/shard_map/ppermute | solution.py:730
  26.2 1.5 collective-permute-start.11
  30.4 7.3 %qkv.1 = (bf16[1024,1152]{1,0:T(8,128)(2,1)}, bf16[1024,1152]{1,0:T(8,128)(2,1)}) custom-call(s32[1]{0:T(128)} %bitcast.s, bf16[1024,768]{1,0:T(8,128)(2,1)S(1)} %copy-done, f32[1,2304]{1,0:T(1,128)S(1)} %reshape.165.b_ref, bf16[96,2304]{1,0:T(8,128)(2,1)} %copy-done.9, bf16[96,2304]{1,0:T(8,128)(2,1)} %collective-permute-done.4.rest_1_, ...), custom_call_target="tpu_custom_call" | custom-call | flops 3623878 | bytes 9830 | tf_op jit(solution)/shard_map/qkv/pallas_call | solution.py:149
  37.8 1.8 collective-permute-done.12.rest_2_
  39.5 1.9 collective-permute-done.11.rest_1_
  41.5 1.3 collective-permute-start.16
  43.5 5.7 %attention.2 = (bf16[1024,384]{1,0:T(8,128)(2,1)S(1)}, f32[1024,768]{1,0:T(8,128)}) custom-call(s32[8]{0:T(128)S(1)} %copy-done.4, bf16[1024,1152]{1,0:T(8,128)(2,1)} %get-tuple-element.112.qkv_ref), custom_call_target="tpu_custom_call" | custom-call | flops 4000000 | bytes 6291 | tf_op jit(solution)/shard_map/attention/pallas_call | solution.py:234
  49.2 4.0 %collective-permute-done.16.rest_3_ = bf16[96,3840]{1,0:T(8,128)(2,1)} collective-permute-done((bf16[96,3840]{1,0:T(8,128)(2,1)}, bf16[96,3840]{1,0:T(8,128)(2,1)}, u32[]{:S(2)}, u32[]{:S(2)}) %collective-permute-start.16) | collective-permute-done | bytes 737312 | tf_op jit(solution)/shard_map/ppermute | solution.py:730
  54.2 1.3 collective-permute-start.19
  56.5 5.7 %attention.3 = (bf16[1024,384]{1,0:T(8,128)(2,1)S(1)}, f32[1024,768]{1,0:T(8,128)}) custom-call(s32[8]{0:T(128)S(1)} %copy-done.4, bf16[1024,1152]{1,0:T(8,128)(2,1)} %get-tuple-element.114.qkv_ref), custom_call_target="tpu_custom_call" | custom-call | flops 4000000 | bytes 6291 | tf_op jit(solution)/shard_map/attention/pallas_call | solution.py:234
  62.2 6.3 %project.1 = (f32[1024,768]{1,0:T(8,128)S(1)}, f32[1024,1]{1,0:T(8,128)}, bf16[1024,768]{1,0:T(8,128)(2,1)S(1)}, bf16[8,96,3840]{2,1,0:T(8,128)(2,1)S(1)}) custom-call(s32[1]{0:T(128)} %bitcast.s, bf16[1024,384]{1,0:T(8,128)(2,1)S(1)} %get-tuple-element.113.o0_ref, bf16[1024,384]{1,0:T(8,128)(2,1)S(1)} %get-tuple-element.115.o1_ref, ...), custom_call_target="tpu_custom_call" | custom-call | flops 1207959 | bytes 13762 | tf_op jit(solution)/shard_map/project/pallas_call | solution.py:264
  68.5 1.5 collective-permute-done.19.rest_2_
  70.3 1.6 collective-permute-start.20
  73.2 8.8 %expand.1 = (bf16[1024,3072]{1,0:T(8,128)(2,1)S(1)}, bf16[1024,3072]{1,0:T(8,128)(2,1)S(1)}) custom-call(s32[1]{0:T(128)} %bitcast.s, bf16[1024,768]{1,0:T(8,128)(2,1)S(1)} %get-tuple-element.122.h_ref, f32[1,3072]{1,0:T(1,128)S(1)} %bitcast.38, bf16[8,96,3840]{2,1,0:T(8,128)(2,1)S(1)} %get-tuple-element.123.w_ref), custom_call_target="tpu_custom_call" | custom-call | flops 4831838 | bytes 18874 | tf_op jit(solution)/shard_map/expand/pallas_call | solution.py:295
  82.6 1.6 collective-permute-done.24.rest_7_
  85.0 11.2 %feed_out.1 = (bf16[1024,768]{1,0:T(8,128)(2,1)}, f32[1024,768]{1,0:T(8,128)S(1)}, bf16[1024,768]{1,0:T(8,128)(2,1)S(1)}, f32[8,768]{1,0:T(8,128)S(1)}, bf16[8,384,768]{2,1,0:T(8,128)(2,1)S(1)}) custom-call(s32[1]{0:T(128)} %bitcast.s, bf16[1024,3072]{1,0:T(8,128)(2,1)S(1)} %get-tuple-element.124.f_ref, f32[1024,768]{1,0:T(8,128)S(1)} %get-tuple-element.125.n1_ref, ...), custom_call_target="tpu_custom_call" | custom-call | flops 4831838 | bytes 22020 | tf_op jit(solution)/shard_map/feed_out/pallas_call | solution.py:333
  96.3 7.4 %grad_w_out.1 = (bf16[4,384,768]{2,1,0:T(8,128)(2,1)}, bf16[4,384,768]{2,1,0:T(8,128)(2,1)}) custom-call(s32[1]{0:T(128)} %bitcast.s, bf16[1024,3072]{1,0:T(8,128)(2,1)S(1)} %get-tuple-element.124.f_ref, bf16[1024,768]{1,0:T(8,128)(2,1)S(1)} %get-tuple-element.132.dz_ref), custom_call_target="tpu_custom_call" | custom-call | flops 4831838 | bytes 12582 | tf_op jit(solution)/shard_map/grad_w_out/pallas_call | solution.py:372
  104.0 6.4 %back_out.1 = (bf16[1024,3072]{1,0:T(8,128)(2,1)S(1)}, f32[1,3072]{1,0:T(1,128)S(1)}) custom-call(s32[1]{0:T(128)} %bitcast.s, bf16[1024,768]{1,0:T(8,128)(2,1)S(1)} %get-tuple-element.132.dz_ref, bf16[1024,3072]{1,0:T(8,128)(2,1)S(1)} %get-tuple-element.133.sl_ref, bf16[8,384,768]{2,1,0:T(8,128)(2,1)S(1)} %get-tuple-element.134.w_ref), custom_call_target="tpu_custom_call" | custom-call | flops 4831838 | bytes 18874 | tf_op jit(solution)/shard_map/back_out/pallas_call | solution.py:404
  110.7 7.5 %grad_w_in.1 = (bf16[4,96,3072]{2,1,0:T(8,128)(2,1)}, bf16[4,96,3072]{2,1,0:T(8,128)(2,1)}) custom-call(s32[1]{0:T(128)} %bitcast.s, bf16[1024,768]{1,0:T(8,128)(2,1)S(1)} %get-tuple-element.122.h_ref, bf16[1024,3072]{1,0:T(8,128)(2,1)S(1)} %get-tuple-element.140.du_ref), custom_call_target="tpu_custom_call" | custom-call | flops 4831838 | bytes 14155 | tf_op jit(solution)/shard_map/grad_w_in/pallas_call | solution.py:487
  118.9 12.4 %back_in.1 = (f32[1024,768]{1,0:T(8,128)}, bf16[1024,768]{1,0:T(8,128)(2,1)S(1)}, bf16[1024,384]{1,0:T(8,128)(2,1)S(1)}, bf16[1024,384]{1,0:T(8,128)(2,1)S(1)}, f32[8,768]{1,0:T(8,128)S(1)}) custom-call(s32[1]{0:T(128)} %bitcast.s, bf16[1024,3072]{1,0:T(8,128)(2,1)S(1)} %get-tuple-element.140.du_ref, f32[1024,768]{1,0:T(8,128)S(1)} %get-tuple-element.141.dr2_ref, ...), custom_call_target="tpu_custom_call" | custom-call | flops 6039797 | bytes 24772 | tf_op jit(solution)/shard_map/back_in/pallas_call | solution.py:441
  131.8 1.5 collective-permute-start.28
  133.3 1.3 collective-permute-done.26
  135.3 4.8 %attention_back.2 = (bf16[1024,1152]{1,0:T(8,128)(2,1)S(1)}, f32[8,384]{1,0:T(8,128)S(1)}) custom-call(s32[8]{0:T(128)S(1)} %copy-done.4, bf16[1024,1152]{1,0:T(8,128)(2,1)} %get-tuple-element.112.qkv_ref, f32[1024,768]{1,0:T(8,128)} %get-tuple-element.128.p_ref, bf16[1024,384]{1,0:T(8,128)(2,1)S(1)} %get-tuple-element.147.do_ref), custom_call_target="tpu_custom_call" | custom-call | flops 7000000 | bytes 8650 | tf_op jit(solution)/shard_map/attention_back/pallas_call | solution.py:549
  140.2 5.2 %grad_w_mixed.1 = (bf16[4,96,1920]{2,1,0:T(8,128)(2,1)}, bf16[4,96,1920]{2,1,0:T(8,128)(2,1)}) custom-call(s32[1]{0:T(128)} %bitcast.s, bf16[1024,768]{1,0:T(8,128)(2,1)S(1)} %copy-done, bf16[1024,1152]{1,0:T(8,128)(2,1)S(1)} %get-tuple-element.148.g_ref.g0_ref, bf16[1024,384]{1,0:T(8,128)(2,1)S(1)} %get-tuple-element.113.o0_ref, ...), custom_call_target="tpu_custom_call" | custom-call | flops 3019898 | bytes 12386 | tf_op jit(solution)/shard_map/grad_w_mixed/pallas_call | solution.py:635
  145.4 5.7 %collective-permute-done.29 = bf16[384,768]{1,0:T(8,128)(2,1)S(1)} collective-permute-done((bf16[384,768]{1,0:T(8,128)(2,1)S(1)}, bf16[384,768]{1,0:T(8,128)(2,1)S(1)}, u32[]{:S(2)}, u32[]{:S(2)}) %collective-permute-start.29) | collective-permute-done | bytes 589856 | tf_op jit(solution)/shard_map/ppermute | solution.py:730
  151.5 2.9 %collective-permute-done.28 = bf16[2,96,3072]{2,1,0:T(8,128)(2,1)S(1)} collective-permute-done((bf16[2,96,3072]{2,1,0:T(8,128)(2,1)S(1)}, bf16[2,96,3072]{2,1,0:T(8,128)(2,1)S(1)}, u32[]{:S(2)}, u32[]{:S(2)}) %collective-permute-start.28) | collective-permute-done | bytes 1179680 | tf_op jit(solution)/shard_map/ppermute | solution.py:730
  154.3 1.2 fusion.7
  155.6 1.6 collective-permute-start.30
  157.1 1.7 collective-permute-start.36
  158.8 5.0 %attention_back.3 = (bf16[1024,1152]{1,0:T(8,128)(2,1)S(1)}, f32[8,384]{1,0:T(8,128)S(1)}) custom-call(s32[8]{0:T(128)S(1)} %copy-done.4, bf16[1024,1152]{1,0:T(8,128)(2,1)} %get-tuple-element.114.qkv_ref, f32[1024,768]{1,0:T(8,128)} %get-tuple-element.149.p_ref, bf16[1024,384]{1,0:T(8,128)(2,1)S(1)} %get-tuple-element.155.do_ref), custom_call_target="tpu_custom_call" | custom-call | flops 7000000 | bytes 8650 | tf_op jit(solution)/shard_map/attention_back/pallas_call | solution.py:549
  163.8 3.6 %grad_w_qkv.1 = (bf16[4,112,1152]{2,1,0:T(8,128)(2,1)}, bf16[4,112,1152]{2,1,0:T(8,128)(2,1)}) custom-call(s32[1]{0:T(128)} %bitcast.s, bf16[1024,768]{1,0:T(8,128)(2,1)S(1)} %copy-done, bf16[1024,1152]{1,0:T(8,128)(2,1)S(1)} %get-tuple-element.174.g_ref.g1_ref, f32[8,384]{1,0:T(8,128)S(1)} %get-tuple-element.157.q0_ref, ...), custom_call_target="tpu_custom_call" | custom-call | flops 1811939 | bytes 8060 | tf_op jit(solution)/shard_map/grad_w_qkv/pallas_call | solution.py:602
  167.4 1.9 fusion.3
  169.3 2.5 collective-permute-start.31
  171.8 1.3 add_convert_fusion.2
  173.1 1.1 collective-permute-start.35
  174.3 1.1 collective-permute-start.34
  175.6 1.6 collective-permute-start.47
  177.2 6.2 %back_qkv.2 = (bf16[1024,768]{1,0:T(8,128)(2,1)}, bf16[8,96,2304]{2,1,0:T(8,128)(2,1)S(1)}) custom-call(s32[1]{0:T(128)} %bitcast.s, bf16[1024,1152]{1,0:T(8,128)(2,1)S(1)} %copy-done.2, bf16[1024,1152]{1,0:T(8,128)(2,1)S(1)} %get-tuple-element.174.g_ref.g1_ref, f32[1024,768]{1,0:T(8,128)} %get-tuple-element.169.dr_ref, bf16[96,2304]{1,0:T(8,128)(2,1)} %copy-done.9, ...), custom_call_target="tpu_custom_call" | custom-call | flops 1811939 | bytes 8257 | tf_op jit(solution)/shard_map/back_qkv/pallas_call | solution.py:689
  183.4 1.3 collective-permute-done.35
  184.7 1.1 fusion.9
  185.8 1.2 collective-permute-start.37
  187.0 5.5 %collective-permute-done.34 = bf16[2,112,1152]{2,1,0:T(8,128)(2,1)S(1)} collective-permute-done((bf16[2,112,1152]{2,1,0:T(8,128)(2,1)S(1)}, bf16[2,112,1152]{2,1,0:T(8,128)(2,1)S(1)}, u32[]{:S(2)}, u32[]{:S(2)}) %collective-permute-start.34) | collective-permute-done | bytes 516128 | tf_op jit(solution)/shard_map/ppermute | solution.py:730
  192.6 1.9 collective-permute-start.38
  195.4 4.2 %back_qkv.3 = bf16[1024,768]{1,0:T(8,128)(2,1)} custom-call(s32[1]{0:T(128)} %bitcast.s, bf16[1024,1152]{1,0:T(8,128)(2,1)S(1)} %copy-done.2, bf16[1024,1152]{1,0:T(8,128)(2,1)S(1)} %get-tuple-element.174.g_ref.g1_ref, f32[1024,768]{1,0:T(8,128)} %get-tuple-element.169.dr_ref, ...), custom_call_target="tpu_custom_call", output_to_operand_aliasing={{}: (5, {})} | custom-call | flops 1811939 | bytes 8257 | tf_op jit(solution)/shard_map/back_qkv/pallas_call | solution.py:698
  199.7 3.7 %collective-permute-start.40 = (bf16[112,1152]{1,0:T(8,128)(2,1)S(1)}, bf16[112,1152]{1,0:T(8,128)(2,1)S(1)}, u32[]{:S(2)}, u32[]{:S(2)}) collective-permute-start(bf16[112,1152]{1,0:T(8,128)(2,1)S(1)} %fusion.8), channel_id=1, source_target_pairs={{0,8},{24,16},{1,9},{25,17},{2,10},{26,18},{3,11},{27,19},{4,12},{... | collective-permute-start | bytes 774152 | tf_op jit(solution)/shard_map/ppermute | solution.py:787
  203.4 1.2 fusion.5
  204.6 1.3 collective-permute-start.39
  205.9 2.5 add_divide_fusion
  208.5 1.3 collective-permute-start.46
  210.8 3.4 %collective-permute-done.39 = bf16[96,1920]{1,0:T(8,128)(2,1)S(1)} collective-permute-done((bf16[96,1920]{1,0:T(8,128)(2,1)S(1)}, bf16[96,1920]{1,0:T(8,128)(2,1)S(1)}, u32[]{:S(2)}, u32[]{:S(2)}) %collective-permute-start.39) | collective-permute-done | bytes 368672 | tf_op jit(solution)/shard_map/ppermute | solution.py:787
  215.3 1.3 collective-permute-start.45
  216.7 1.3 collective-permute-start.44
  218.0 18.8 %collective-permute-done.45 = bf16[112,1152]{1,0:T(8,128)(2,1)S(1)} collective-permute-done((bf16[112,1152]{1,0:T(8,128)(2,1)S(1)}, bf16[112,1152]{1,0:T(8,128)(2,1)S(1)}, u32[]{:S(2)}, u32[]{:S(2)}) %collective-permute-start.45) | collective-permute-done | bytes 258080 | tf_op jit(solution)/shard_map/ppermute | solution.py:803
  238.1 2.5 %add_divide_fusion.1 = (f32[96,3072]{1,0:T(8,128)}, f32[96,3072]{1,0:T(8,128)}, f32[96,3072]{1,0:T(8,128)}, f32[96,3072]{1,0:T(8,128)}) fusion(f32[96,3072]{1,0:T(8,128)S(1)} %copy-done.17, f32[96,3072]{1,0:T(8,128)S(1)} %copy-done.18, bf16[96,3072]{1,0:T(8,128)(2,1)S(1)} %add_convert_fusion.3, bf16[96,3072]{1,0:T(8,128)(2,1)S(1)} %collective-permute-done.46, ...), kind=kLoop, calls=%fused_computation.17 | loop fusion | flops 3833856 | bytes 8257537 | tf_op jit(solution)/shard_map/div | solution.py:708
  240.7 4.4 %collective-permute-done.44 = bf16[96,1920]{1,0:T(8,128)(2,1)S(1)} collective-permute-done((bf16[96,1920]{1,0:T(8,128)(2,1)S(1)}, bf16[96,1920]{1,0:T(8,128)(2,1)S(1)}, u32[]{:S(2)}, u32[]{:S(2)}) %collective-permute-start.44) | collective-permute-done | bytes 368672 | tf_op jit(solution)/shard_map/ppermute | solution.py:803
  245.3 2.5 %add_divide_fusion.2 = (f32[96,3072]{1,0:T(8,128)}, f32[96,3072]{1,0:T(8,128)}, f32[96,3072]{1,0:T(8,128)}, f32[96,3072]{1,0:T(8,128)}) fusion(f32[96,3072]{1,0:T(8,128)S(1)} %copy-done.21, f32[96,3072]{1,0:T(8,128)S(1)} %copy-done.22, bf16[96,3072]{1,0:T(8,128)(2,1)S(1)} %slice_dynamic-update-slice_fusion), kind=kLoop, calls=%fused_computation.19 | loop fusion | flops 3538944 | bytes 7667712 | tf_op jit(solution)/shard_map/div | solution.py:708
  (210 shorter events, 19.7 us)
Async XLA Ops:
  2.2 14.5 %copy-start.9 = (bf16[96,2304]{1,0:T(8,128)(2,1)}, bf16[96,2304]{1,0:T(8,128)(2,1)S(1)}, u32[]{:S(2)}) copy-start(bf16[96,2304]{1,0:T(8,128)(2,1)S(1)} %slice_dynamic-update-slice_fusion.7.rest_0_) | copy-start | bytes 1327108
  2.3 15.2 %collective-permute-start.5 = (bf16[96,2304]{1,0:T(8,128)(2,1)S(1)}, bf16[96,2304]{1,0:T(8,128)(2,1)}, u32[]{:S(2)}, u32[]{:S(2)}) collective-permute-start(bf16[96,2304]{1,0:T(8,128)(2,1)S(1)} %slice_dynamic-update-slice_fusion.7.rest_0_), channel_id=1, source_target_pairs={{0,4},{1,3},{2,6},{3,1},{4,0},{5,7},{6,2},{7,5},{8,12},{9,11},{10,... | collective-permute-start | bytes 1327112 | tf_op jit(solution)/shard_map/ppermute | solution.py:730
  5.3 12.2 %collective-permute-start.4 = (bf16[96,2304]{1,0:T(8,128)(2,1)S(1)}, bf16[96,2304]{1,0:T(8,128)(2,1)}, u32[]{:S(2)}, u32[]{:S(2)}) collective-permute-start(bf16[96,2304]{1,0:T(8,128)(2,1)S(1)} %slice_dynamic-update-slice_fusion.7.rest_0_), channel_id=1, source_target_pairs={{0,2},{1,5},{2,0},{3,7},{4,6},{5,1},{6,4},{7,3},{8,10},{9,13},{10,... | collective-permute-start | bytes 1327112 | tf_op jit(solution)/shard_map/ppermute | solution.py:730
  6.9 1.8 collective-permute-start
  8.1 22.3 %copy-start = (bf16[1024,768]{1,0:T(8,128)(2,1)S(1)}, bf16[1024,768]{1,0:T(8,128)(2,1)}, u32[]{:S(2)}) copy-start(bf16[1024,768]{1,0:T(8,128)(2,1)} %x_ref.7) | copy-start | bytes 4718596
  8.7 34.1 %copy-start.5 = (bf16[96,3840]{1,0:T(8,128)(2,1)}, bf16[96,3840]{1,0:T(8,128)(2,1)S(1)}, u32[]{:S(2)}) copy-start(bf16[96,3840]{1,0:T(8,128)(2,1)S(1)} %pad_maximum_fusion.rest_0_) | copy-start | bytes 2211844
  8.8 8.0 %collective-permute-start.3 = (bf16[2,1152]{1,0:T(2,128)(2,1)S(1)}, bf16[2,1152]{1,0:T(2,128)(2,1)S(1)}, u32[]{:S(2)}, u32[]{:S(2)}) collective-permute-start(bf16[2,1152]{1,0:T(2,128)(2,1)S(1)} %pad_maximum_fusion.2), channel_id=1, source_target_pairs={{0,6},{1,7},{2,4},{3,5},{4,2},{5,3},{6,0},{7,1},{8,14},{9,15},{10,... | collective-permute-start | bytes 13832 | tf_op jit(solution)/shard_map/ppermute | solution.py:722
  8.9 7.9 %collective-permute-start.2 = (bf16[2,1152]{1,0:T(2,128)(2,1)S(1)}, bf16[2,1152]{1,0:T(2,128)(2,1)S(1)}, u32[]{:S(2)}, u32[]{:S(2)}) collective-permute-start(bf16[2,1152]{1,0:T(2,128)(2,1)S(1)} %pad_maximum_fusion.2), channel_id=1, source_target_pairs={{0,4},{1,5},{2,6},{3,7},{4,0},{5,1},{6,2},{7,3},{8,12},{9,13},{10,... | collective-permute-start | bytes 13832 | tf_op jit(solution)/shard_map/ppermute | solution.py:722
  10.9 5.9 %collective-permute-start.1 = (bf16[2,1152]{1,0:T(2,128)(2,1)S(1)}, bf16[2,1152]{1,0:T(2,128)(2,1)S(1)}, u32[]{:S(2)}, u32[]{:S(2)}) collective-permute-start(bf16[2,1152]{1,0:T(2,128)(2,1)S(1)} %pad_maximum_fusion.2), channel_id=1, source_target_pairs={{0,2},{1,3},{2,0},{3,1},{4,6},{5,7},{6,4},{7,5},{8,10},{9,11},{10,... | collective-permute-start | bytes 13832 | tf_op jit(solution)/shard_map/ppermute | solution.py:722
  16.8 10.9 %collective-permute-start.7 = (bf16[96,2304]{1,0:T(8,128)(2,1)S(1)}, bf16[96,2304]{1,0:T(8,128)(2,1)S(1)}, u32[]{:S(2)}, u32[]{:S(2)}) collective-permute-start(bf16[96,2304]{1,0:T(8,128)(2,1)S(1)} %slice_dynamic-update-slice_fusion.7.rest_0_), channel_id=1, source_target_pairs={{0,1},{1,0},{2,3},{3,2},{4,5},{5,4},{6,7},{7,6},{8,9},{9,8},{10,11... | collective-permute-start | bytes 1327112 | tf_op jit(solution)/shard_map/ppermute | solution.py:722
  17.5 8.7 %collective-permute-start.6 = (bf16[96,2304]{1,0:T(8,128)(2,1)}, bf16[96,2304]{1,0:T(8,128)(2,1)}, u32[]{:S(2)}, u32[]{:S(2)}) collective-permute-start(bf16[96,2304]{1,0:T(8,128)(2,1)} %collective-permute-done.4.rest_1_), channel_id=1, source_target_pairs={{0,4},{1,3},{2,6},{3,1},{4,0},{5,7},{6,2},{7,5},{8,12},{9,11},{10,... | collective-permute-start | bytes 1327112 | tf_op jit(solution)/shard_map/ppermute | solution.py:730
  19.8 9.0 %collective-permute-start.8 = (bf16[96,2304]{1,0:T(8,128)(2,1)}, bf16[96,2304]{1,0:T(8,128)(2,1)}, u32[]{:S(2)}, u32[]{:S(2)}) collective-permute-start(bf16[96,2304]{1,0:T(8,128)(2,1)} %collective-permute-done.4.rest_1_), channel_id=1, source_target_pairs={{0,1},{1,0},{2,3},{3,2},{4,5},{5,4},{6,7},{7,6},{8,9},{9,8},{10,11... | collective-permute-start | bytes 1327112 | tf_op jit(solution)/shard_map/ppermute | solution.py:722
  19.9 8.9 %collective-permute-start.9 = (bf16[96,2304]{1,0:T(8,128)(2,1)}, bf16[96,2304]{1,0:T(8,128)(2,1)}, u32[]{:S(2)}, u32[]{:S(2)}) collective-permute-start(bf16[96,2304]{1,0:T(8,128)(2,1)} %collective-permute-done.5.rest_2_), channel_id=1, source_target_pairs={{0,1},{1,0},{2,3},{3,2},{4,5},{5,4},{6,7},{7,6},{8,9},{9,8},{10,11... | collective-permute-start | bytes 1327112 | tf_op jit(solution)/shard_map/ppermute | solution.py:722
  20.4 19.1 %collective-permute-start.12 = (bf16[96,3840]{1,0:T(8,128)(2,1)S(1)}, bf16[96,3840]{1,0:T(8,128)(2,1)}, u32[]{:S(2)}, u32[]{:S(2)}) collective-permute-start(bf16[96,3840]{1,0:T(8,128)(2,1)S(1)} %pad_maximum_fusion.rest_0_), channel_id=1, source_target_pairs={{0,4},{1,3},{2,6},{3,1},{4,0},{5,7},{6,2},{7,5},{8,12},{9,11},{10,... | collective-permute-start | bytes 2211848 | tf_op jit(solution)/shard_map/ppermute | solution.py:730
  26.2 15.3 %collective-permute-start.11 = (bf16[96,3840]{1,0:T(8,128)(2,1)S(1)}, bf16[96,3840]{1,0:T(8,128)(2,1)}, u32[]{:S(2)}, u32[]{:S(2)}) collective-permute-start(bf16[96,3840]{1,0:T(8,128)(2,1)S(1)} %pad_maximum_fusion.rest_0_), channel_id=1, source_target_pairs={{0,2},{1,5},{2,0},{3,7},{4,6},{5,1},{6,4},{7,3},{8,10},{9,13},{10,... | collective-permute-start | bytes 2211848 | tf_op jit(solution)/shard_map/ppermute | solution.py:730
  27.6 2.0 collective-permute-start.10
  28.5 14.8 %copy-start.33 = (f32[8,8,96]{2,1,0:T(8,128)}, f32[8,8,96]{2,1,0:T(8,128)S(1)}, u32[]{:S(2)}) copy-start(f32[8,8,96]{2,1,0:T(8,128)S(1)} %reshape.164) | copy-start | bytes 73732
  30.4 13.1 %copy-start.4 = (s32[8]{0:T(128)S(1)}, s32[8]{0:T(128)}, u32[]{:S(2)}) copy-start(s32[8]{0:T(128)} %s.7) | copy-start | bytes 100
  41.5 11.8 %copy-start.14 = (f32[384,768]{1,0:T(8,128)S(1)}, f32[384,768]{1,0:T(8,128)}, u32[]{:S(2)}) copy-start(f32[384,768]{1,0:T(8,128)} %param.25) | copy-start | bytes 3538948
  41.5 11.8 %collective-permute-start.16 = (bf16[96,3840]{1,0:T(8,128)(2,1)}, bf16[96,3840]{1,0:T(8,128)(2,1)}, u32[]{:S(2)}, u32[]{:S(2)}) collective-permute-start(bf16[96,3840]{1,0:T(8,128)(2,1)} %collective-permute-done.11.rest_1_), channel_id=1, source_target_pairs={{0,4},{1,3},{2,6},{3,1},{4,0},{5,7},{6,2},{7,5},{8,12},{9,11},{10,... | collective-permute-start | bytes 2211848 | tf_op jit(solution)/shard_map/ppermute | solution.py:730
  42.8 11.4 %collective-permute-start.13 = (bf16[96,3840]{1,0:T(8,128)(2,1)S(1)}, bf16[96,3840]{1,0:T(8,128)(2,1)S(1)}, u32[]{:S(2)}, u32[]{:S(2)}) collective-permute-start(bf16[96,3840]{1,0:T(8,128)(2,1)S(1)} %pad_maximum_fusion.rest_0_), channel_id=1, source_target_pairs={{0,1},{1,0},{2,3},{3,2},{4,5},{5,4},{6,7},{7,6},{8,9},{9,8},{10,11... | collective-permute-start | bytes 2211848 | tf_op jit(solution)/shard_map/ppermute | solution.py:722
  43.0 11.2 %collective-permute-start.15 = (bf16[96,3840]{1,0:T(8,128)(2,1)}, bf16[96,3840]{1,0:T(8,128)(2,1)S(1)}, u32[]{:S(2)}, u32[]{:S(2)}) collective-permute-start(bf16[96,3840]{1,0:T(8,128)(2,1)} %collective-permute-done.12.rest_2_), channel_id=1, source_target_pairs={{0,1},{1,0},{2,3},{3,2},{4,5},{5,4},{6,7},{7,6},{8,9},{9,8},{10,11... | collective-permute-start | bytes 2211848 | tf_op jit(solution)/shard_map/ppermute | solution.py:722
  43.3 10.9 %collective-permute-start.14 = (bf16[96,3840]{1,0:T(8,128)(2,1)}, bf16[96,3840]{1,0:T(8,128)(2,1)S(1)}, u32[]{:S(2)}, u32[]{:S(2)}) collective-permute-start(bf16[96,3840]{1,0:T(8,128)(2,1)} %collective-permute-done.11.rest_1_), channel_id=1, source_target_pairs={{0,1},{1,0},{2,3},{3,2},{4,5},{5,4},{6,7},{7,6},{8,9},{9,8},{10,11... | collective-permute-start | bytes 2211848 | tf_op jit(solution)/shard_map/ppermute | solution.py:722
  53.3 8.9 %collective-permute-start.17 = (bf16[96,3840]{1,0:T(8,128)(2,1)}, bf16[96,3840]{1,0:T(8,128)(2,1)}, u32[]{:S(2)}, u32[]{:S(2)}) collective-permute-start(bf16[96,3840]{1,0:T(8,128)(2,1)} %collective-permute-done.16.rest_3_), channel_id=1, source_target_pairs={{0,1},{1,0},{2,3},{3,2},{4,5},{5,4},{6,7},{7,6},{8,9},{9,8},{10,11... | collective-permute-start | bytes 2211848 | tf_op jit(solution)/shard_map/ppermute | solution.py:722
  54.2 15.8 %collective-permute-start.19 = (bf16[384,768]{1,0:T(8,128)(2,1)}, bf16[384,768]{1,0:T(8,128)(2,1)S(1)}, u32[]{:S(2)}, u32[]{:S(2)}) collective-permute-start(bf16[384,768]{1,0:T(8,128)(2,1)} %convert_element_type.290.rest_0_), channel_id=1, source_target_pairs={{0,4},{1,3},{2,6},{3,1},{4,0},{5,7},{6,2},{7,5},{8,12},{9,11},{10,... | collective-permute-start | bytes 1769480 | tf_op jit(solution)/shard_map/ppermute | solution.py:730
  55.5 14.8 %collective-permute-start.18 = (bf16[384,768]{1,0:T(8,128)(2,1)}, bf16[384,768]{1,0:T(8,128)(2,1)}, u32[]{:S(2)}, u32[]{:S(2)}) collective-permute-start(bf16[384,768]{1,0:T(8,128)(2,1)} %convert_element_type.290.rest_0_), channel_id=1, source_target_pairs={{0,2},{1,5},{2,0},{3,7},{4,6},{5,1},{6,4},{7,3},{8,10},{9,13},{10,... | collective-permute-start | bytes 1769480 | tf_op jit(solution)/shard_map/ppermute | solution.py:730
  69.9 12.1 %copy-start.27 = (bf16[384,768]{1,0:T(8,128)(2,1)}, bf16[384,768]{1,0:T(8,128)(2,1)S(1)}, u32[]{:S(2)}) copy-start(bf16[384,768]{1,0:T(8,128)(2,1)S(1)} %collective-permute-done.19.rest_2_) | copy-start | bytes 1769476
  70.3 11.8 %collective-permute-start.20 = (bf16[384,768]{1,0:T(8,128)(2,1)}, bf16[384,768]{1,0:T(8,128)(2,1)S(1)}, u32[]{:S(2)}, u32[]{:S(2)}) collective-permute-start(bf16[384,768]{1,0:T(8,128)(2,1)} %collective-permute-done.18.rest_1_), channel_id=1, source_target_pairs={{0,4},{1,3},{2,6},{3,1},{4,0},{5,7},{6,2},{7,5},{8,12},{9,11},{10,... | collective-permute-start | bytes 1769480 | tf_op jit(solution)/shard_map/ppermute | solution.py:730
  72.6 10.0 %collective-permute-start.21 = (bf16[384,768]{1,0:T(8,128)(2,1)}, bf16[384,768]{1,0:T(8,128)(2,1)S(1)}, u32[]{:S(2)}, u32[]{:S(2)}) collective-permute-start(bf16[384,768]{1,0:T(8,128)(2,1)} %convert_element_type.290.rest_0_), channel_id=1, source_target_pairs={{0,1},{1,0},{2,3},{3,2},{4,5},{5,4},{6,7},{7,6},{8,9},{9,8},{10,11... | collective-permute-start | bytes 1769480 | tf_op jit(solution)/shard_map/ppermute | solution.py:722
  72.7 9.9 %collective-permute-start.23 = (bf16[384,768]{1,0:T(8,128)(2,1)S(1)}, bf16[384,768]{1,0:T(8,128)(2,1)S(1)}, u32[]{:S(2)}, u32[]{:S(2)}) collective-permute-start(bf16[384,768]{1,0:T(8,128)(2,1)S(1)} %collective-permute-done.19.rest_2_), channel_id=1, source_target_pairs={{0,1},{1,0},{2,3},{3,2},{4,5},{5,4},{6,7},{7,6},{8,9},{9,8},{10,11... | collective-permute-start | bytes 1769480 | tf_op jit(solution)/shard_map/ppermute | solution.py:722
  73.2 9.4 %collective-permute-start.22 = (bf16[384,768]{1,0:T(8,128)(2,1)}, bf16[384,768]{1,0:T(8,128)(2,1)S(1)}, u32[]{:S(2)}, u32[]{:S(2)}) collective-permute-start(bf16[384,768]{1,0:T(8,128)(2,1)} %collective-permute-done.18.rest_1_), channel_id=1, source_target_pairs={{0,1},{1,0},{2,3},{3,2},{4,5},{5,4},{6,7},{7,6},{8,9},{9,8},{10,11... | collective-permute-start | bytes 1769480 | tf_op jit(solution)/shard_map/ppermute | solution.py:722
  73.2 11.8 %copy-start.3 = (bf16[1024,768]{1,0:T(8,128)(2,1)S(1)}, bf16[1024,768]{1,0:T(8,128)(2,1)}, u32[]{:S(2)}) copy-start(bf16[1024,768]{1,0:T(8,128)(2,1)} %g_ref.1) | copy-start | bytes 4718596
  82.1 2.1 collective-permute-start.24
  103.6 6.7 %collective-permute-start.25 = (bf16[4,384,768]{2,1,0:T(8,128)(2,1)}, bf16[4,384,768]{2,1,0:T(8,128)(2,1)S(1)}, u32[]{:S(2)}, u32[]{:S(2)}) collective-permute-start(bf16[4,384,768]{2,1,0:T(8,128)(2,1)} %get-tuple-element.130), channel_id=1, source_target_pairs={{0,1},{1,0},{2,3},{3,2},{4,5},{5,4},{6,7},{7,6},{8,9},{9,8},{10,11... | collective-permute-start | bytes 7077896 | tf_op jit(solution)/shard_map/ppermute | solution.py:722
  118.2 13.1 %collective-permute-start.27 = (bf16[4,96,3072]{2,1,0:T(8,128)(2,1)}, bf16[4,96,3072]{2,1,0:T(8,128)(2,1)S(1)}, u32[]{:S(2)}, u32[]{:S(2)}) collective-permute-start(bf16[4,96,3072]{2,1,0:T(8,128)(2,1)} %get-tuple-element.138), channel_id=1, source_target_pairs={{0,1},{1,0},{2,3},{3,2},{4,5},{5,4},{6,7},{7,6},{8,9},{9,8},{10,11... | collective-permute-start | bytes 7077896 | tf_op jit(solution)/shard_map/ppermute | solution.py:722
  118.3 16.2 %collective-permute-start.26 = (bf16[2,384,768]{2,1,0:T(8,128)(2,1)S(1)}, bf16[2,384,768]{2,1,0:T(8,128)(2,1)S(1)}, u32[]{:S(2)}, u32[]{:S(2)}) collective-permute-start(bf16[2,384,768]{2,1,0:T(8,128)(2,1)S(1)} %add_convert_fusion.1), channel_id=1, source_target_pairs={{0,2},{1,5},{2,0},{3,7},{4,6},{5,1},{6,4},{7,3},{8,10},{9,13},{10,... | collective-permute-start | bytes 3538952 | tf_op jit(solution)/shard_map/ppermute | solution.py:730
  118.9 12.4 %copy-start.6 = (bf16[4,96,3072]{2,1,0:T(8,128)(2,1)S(1)}, bf16[4,96,3072]{2,1,0:T(8,128)(2,1)}, u32[]{:S(2)}) copy-start(bf16[4,96,3072]{2,1,0:T(8,128)(2,1)} %get-tuple-element.139) | copy-start | bytes 7077892
  131.3 23.0 %copy-start.7 = (bf16[4,96,3072]{2,1,0:T(8,128)(2,1)}, bf16[4,96,3072]{2,1,0:T(8,128)(2,1)S(1)}, u32[]{:S(2)}) copy-start(bf16[4,96,3072]{2,1,0:T(8,128)(2,1)S(1)} %collective-permute-done.27) | copy-start | bytes 7077892
  131.8 22.6 %collective-permute-start.28 = (bf16[2,96,3072]{2,1,0:T(8,128)(2,1)S(1)}, bf16[2,96,3072]{2,1,0:T(8,128)(2,1)S(1)}, u32[]{:S(2)}, u32[]{:S(2)}) collective-permute-start(bf16[2,96,3072]{2,1,0:T(8,128)(2,1)S(1)} %add_convert_fusion), channel_id=1, source_target_pairs={{0,2},{1,5},{2,0},{3,7},{4,6},{5,1},{6,4},{7,3},{8,10},{9,13},{10,... | collective-permute-start | bytes 3538952 | tf_op jit(solution)/shard_map/ppermute | solution.py:730
  134.8 16.3 %collective-permute-start.29 = (bf16[384,768]{1,0:T(8,128)(2,1)S(1)}, bf16[384,768]{1,0:T(8,128)(2,1)S(1)}, u32[]{:S(2)}, u32[]{:S(2)}) collective-permute-start(bf16[384,768]{1,0:T(8,128)(2,1)S(1)} %fusion.6), channel_id=1, source_target_pairs={{0,4},{1,3},{2,6},{3,1},{4,0},{5,7},{6,2},{7,5},{8,12},{9,11},{10,... | collective-permute-start | bytes 1769480 | tf_op jit(solution)/shard_map/ppermute | solution.py:730
  145.4 26.4 %collective-permute-start.33 = (bf16[4,96,1920]{2,1,0:T(8,128)(2,1)}, bf16[4,96,1920]{2,1,0:T(8,128)(2,1)}, u32[]{:S(2)}, u32[]{:S(2)}) collective-permute-start(bf16[4,96,1920]{2,1,0:T(8,128)(2,1)} %get-tuple-element.151), channel_id=1, source_target_pairs={{0,1},{1,0},{2,3},{3,2},{4,5},{5,4},{6,7},{7,6},{8,9},{9,8},{10,11... | collective-permute-start | bytes 4423688 | tf_op jit(solution)/shard_map/ppermute | solution.py:722
  155.6 11.9 %collective-permute-start.30 = (bf16[96,3072]{1,0:T(8,128)(2,1)}, bf16[96,3072]{1,0:T(8,128)(2,1)}, u32[]{:S(2)}, u32[]{:S(2)}) collective-permute-start(bf16[96,3072]{1,0:T(8,128)(2,1)} %fusion.7), channel_id=1, source_target_pairs={{0,4},{1,3},{2,6},{3,1},{4,0},{5,7},{6,2},{7,5},{8,12},{9,11},{10,... | collective-permute-start | bytes 1769480 | tf_op jit(solution)/shard_map/ppermute | solution.py:730
  157.1 18.3 %collective-permute-start.36 = (bf16[384,768]{1,0:T(8,128)(2,1)S(1)}, bf16[384,768]{1,0:T(8,128)(2,1)S(1)}, u32[]{:S(2)}, u32[]{:S(2)}) collective-permute-start(bf16[384,768]{1,0:T(8,128)(2,1)S(1)} %fusion.4), channel_id=1, source_target_pairs={{0,8},{8,0},{16,24},{24,16},{1,9},{9,1},{17,25},{25,17},{2,10},{10... | collective-permute-start | bytes 1769480 | tf_op jit(solution)/shard_map/ppermute | solution.py:790
  167.4 6.8 %collective-permute-start.32 = (bf16[4,112,1152]{2,1,0:T(8,128)(2,1)}, bf16[4,112,1152]{2,1,0:T(8,128)(2,1)S(1)}, u32[]{:S(2)}, u32[]{:S(2)}) collective-permute-start(bf16[4,112,1152]{2,1,0:T(8,128)(2,1)} %get-tuple-element.162), channel_id=1, source_target_pairs={{0,1},{1,0},{2,3},{3,2},{4,5},{5,4},{6,7},{7,6},{8,9},{9,8},{10,11... | collective-permute-start | bytes 3096584 | tf_op jit(solution)/shard_map/ppermute | solution.py:722
  169.3 25.2 %collective-permute-start.31 = (bf16[96,3072]{1,0:T(8,128)(2,1)S(1)}, bf16[96,3072]{1,0:T(8,128)(2,1)S(1)}, u32[]{:S(2)}, u32[]{:S(2)}) collective-permute-start(bf16[96,3072]{1,0:T(8,128)(2,1)S(1)} %fusion.3), channel_id=1, source_target_pairs={{0,8},{24,16},{1,9},{25,17},{2,10},{26,18},{3,11},{27,19},{4,12},{... | collective-permute-start | bytes 1769480 | tf_op jit(solution)/shard_map/ppermute | solution.py:787
  173.1 11.5 %collective-permute-start.35 = (bf16[2,96,1920]{2,1,0:T(8,128)(2,1)S(1)}, bf16[2,96,1920]{2,1,0:T(8,128)(2,1)S(1)}, u32[]{:S(2)}, u32[]{:S(2)}) collective-permute-start(bf16[2,96,1920]{2,1,0:T(8,128)(2,1)S(1)} %add_convert_fusion.2), channel_id=1, source_target_pairs={{0,2},{1,5},{2,0},{3,7},{4,6},{5,1},{6,4},{7,3},{8,10},{9,13},{10,... | collective-permute-start | bytes 2211848 | tf_op jit(solution)/shard_map/ppermute | solution.py:730
  174.3 18.2 %collective-permute-start.34 = (bf16[2,112,1152]{2,1,0:T(8,128)(2,1)S(1)}, bf16[2,112,1152]{2,1,0:T(8,128)(2,1)S(1)}, u32[]{:S(2)}, u32[]{:S(2)}) collective-permute-start(bf16[2,112,1152]{2,1,0:T(8,128)(2,1)S(1)} %add_convert_fusion.8), channel_id=1, source_target_pairs={{0,2},{1,5},{2,0},{3,7},{4,6},{5,1},{6,4},{7,3},{8,10},{9,13},{10,... | collective-permute-start | bytes 1548296 | tf_op jit(solution)/shard_map/ppermute | solution.py:730
  175.6 30.3 %collective-permute-start.47 = (bf16[384,768]{1,0:T(8,128)(2,1)S(1)}, bf16[384,768]{1,0:T(8,128)(2,1)S(1)}, u32[]{:S(2)}, u32[]{:S(2)}) collective-permute-start(bf16[384,768]{1,0:T(8,128)(2,1)S(1)} %add_convert_fusion.5), channel_id=1, source_target_pairs={{0,16},{8,24},{16,0},{24,8},{1,17},{9,25},{17,1},{25,9},{2,18},{10... | collective-permute-start | bytes 1769480 | tf_op jit(solution)/shard_map/ppermute | solution.py:796
  185.8 17.6 %collective-permute-start.37 = (bf16[96,1920]{1,0:T(8,128)(2,1)S(1)}, bf16[96,1920]{1,0:T(8,128)(2,1)S(1)}, u32[]{:S(2)}, u32[]{:S(2)}) collective-permute-start(bf16[96,1920]{1,0:T(8,128)(2,1)S(1)} %fusion.9), channel_id=1, source_target_pairs={{0,4},{1,3},{2,6},{3,1},{4,0},{5,7},{6,2},{7,5},{8,12},{9,11},{10,... | collective-permute-start | bytes 1105928 | tf_op jit(solution)/shard_map/ppermute | solution.py:730
  192.6 6.9 %collective-permute-start.38 = (bf16[112,1152]{1,0:T(8,128)(2,1)S(1)}, bf16[112,1152]{1,0:T(8,128)(2,1)S(1)}, u32[]{:S(2)}, u32[]{:S(2)}) collective-permute-start(bf16[112,1152]{1,0:T(8,128)(2,1)S(1)} %fusion.10), channel_id=1, source_target_pairs={{0,4},{1,3},{2,6},{3,1},{4,0},{5,7},{6,2},{7,5},{8,12},{9,11},{10,... | collective-permute-start | bytes 774152 | tf_op jit(solution)/shard_map/ppermute | solution.py:730
  194.7 13.7 %collective-permute-start.41 = (bf16[96,3072]{1,0:T(8,128)(2,1)S(1)}, bf16[96,3072]{1,0:T(8,128)(2,1)S(1)}, u32[]{:S(2)}, u32[]{:S(2)}) collective-permute-start(bf16[96,3072]{1,0:T(8,128)(2,1)S(1)} %add_convert_fusion.4), channel_id=1, source_target_pairs={{8,16},{16,8},{9,17},{17,9},{10,18},{18,10},{11,19},{19,11},{12,20... | collective-permute-start | bytes 1769480 | tf_op jit(solution)/shard_map/ppermute | solution.py:798
  199.7 10.3 %collective-permute-start.40 = (bf16[112,1152]{1,0:T(8,128)(2,1)S(1)}, bf16[112,1152]{1,0:T(8,128)(2,1)S(1)}, u32[]{:S(2)}, u32[]{:S(2)}) collective-permute-start(bf16[112,1152]{1,0:T(8,128)(2,1)S(1)} %fusion.8), channel_id=1, source_target_pairs={{0,8},{24,16},{1,9},{25,17},{2,10},{26,18},{3,11},{27,19},{4,12},{... | collective-permute-start | bytes 774152 | tf_op jit(solution)/shard_map/ppermute | solution.py:787
  204.6 9.6 %collective-permute-start.39 = (bf16[96,1920]{1,0:T(8,128)(2,1)S(1)}, bf16[96,1920]{1,0:T(8,128)(2,1)S(1)}, u32[]{:S(2)}, u32[]{:S(2)}) collective-permute-start(bf16[96,1920]{1,0:T(8,128)(2,1)S(1)} %fusion.5), channel_id=1, source_target_pairs={{0,8},{24,16},{1,9},{25,17},{2,10},{26,18},{3,11},{27,19},{4,12},{... | collective-permute-start | bytes 1105928 | tf_op jit(solution)/shard_map/ppermute | solution.py:787
  208.5 29.6 %collective-permute-start.46 = (bf16[96,3072]{1,0:T(8,128)(2,1)S(1)}, bf16[96,3072]{1,0:T(8,128)(2,1)S(1)}, u32[]{:S(2)}, u32[]{:S(2)}) collective-permute-start(bf16[96,3072]{1,0:T(8,128)(2,1)S(1)} %add_convert_fusion.3), channel_id=1, source_target_pairs={{8,0},{16,24},{9,1},{17,25},{10,2},{18,26},{11,3},{19,27},{12,4},{... | collective-permute-start | bytes 1769480 | tf_op jit(solution)/shard_map/ppermute | solution.py:803
  210.1 5.1 %collective-permute-start.43 = (bf16[112,1152]{1,0:T(8,128)(2,1)S(1)}, bf16[112,1152]{1,0:T(8,128)(2,1)S(1)}, u32[]{:S(2)}, u32[]{:S(2)}) collective-permute-start(bf16[112,1152]{1,0:T(8,128)(2,1)S(1)} %add_convert_fusion.13), channel_id=1, source_target_pairs={{8,16},{16,8},{9,17},{17,9},{10,18},{18,10},{11,19},{19,11},{12,20... | collective-permute-start | bytes 774152 | tf_op jit(solution)/shard_map/ppermute | solution.py:798
  214.3 22.6 %copy-start.41 = (f32[384]{0:T(512)S(1)}, f32[384]{0:T(512)}, u32[]{:S(2)}) copy-start(f32[384]{0:T(512)} %param.31) | copy-start | bytes 4612
  214.3 22.6 %copy-start.42 = (f32[384]{0:T(512)S(1)}, f32[384]{0:T(512)}, u32[]{:S(2)}) copy-start(f32[384]{0:T(512)} %param.36) | copy-start | bytes 4612
  214.3 23.2 %copy-start.38 = (f32[8,96]{1,0:T(8,128)S(1)}, f32[8,96]{1,0:T(8,128)}, u32[]{:S(2)}) copy-start(f32[8,96]{1,0:T(8,128)} %param.32) | copy-start | bytes 9220
  214.3 23.2 %copy-start.39 = (f32[8,96]{1,0:T(8,128)S(1)}, f32[8,96]{1,0:T(8,128)}, u32[]{:S(2)}) copy-start(f32[8,96]{1,0:T(8,128)} %param.37) | copy-start | bytes 9220
  214.3 23.8 %copy-start.17 = (f32[96,3072]{1,0:T(8,128)S(1)}, f32[96,3072]{1,0:T(8,128)}, u32[]{:S(2)}) copy-start(f32[96,3072]{1,0:T(8,128)} %param.29) | copy-start | bytes 3538948
  214.3 23.8 %copy-start.18 = (f32[96,3072]{1,0:T(8,128)S(1)}, f32[96,3072]{1,0:T(8,128)}, u32[]{:S(2)}) copy-start(f32[96,3072]{1,0:T(8,128)} %param.34) | copy-start | bytes 3538948
  214.3 2.2 collective-permute-start.42
  215.3 21.5 %collective-permute-start.45 = (bf16[112,1152]{1,0:T(8,128)(2,1)S(1)}, bf16[112,1152]{1,0:T(8,128)(2,1)S(1)}, u32[]{:S(2)}, u32[]{:S(2)}) collective-permute-start(bf16[112,1152]{1,0:T(8,128)(2,1)S(1)} %add_convert_fusion.12), channel_id=1, source_target_pairs={{8,0},{16,24},{9,1},{17,25},{10,2},{18,26},{11,3},{19,27},{12,4},{... | collective-permute-start | bytes 774152 | tf_op jit(solution)/shard_map/ppermute | solution.py:803
  216.7 28.4 %collective-permute-start.44 = (bf16[96,1920]{1,0:T(8,128)(2,1)S(1)}, bf16[96,1920]{1,0:T(8,128)(2,1)S(1)}, u32[]{:S(2)}, u32[]{:S(2)}) collective-permute-start(bf16[96,1920]{1,0:T(8,128)(2,1)S(1)} %add_convert_fusion.9), channel_id=1, source_target_pairs={{8,0},{16,24},{9,1},{17,25},{10,2},{18,26},{11,3},{19,27},{12,4},{... | collective-permute-start | bytes 1105928 | tf_op jit(solution)/shard_map/ppermute | solution.py:803
  (29 other events, 103.5 us)
